TPU v7x, 32 devices: a whole 2x2x4 slice. The times are simulated.
32 devices in a mesh: grp: 2 (over y), psg: 8 (over z, x), qry: 2 (over core).
Axes of the slice: x: 2, y: 2, z: 4, core: 2. Of those that a mesh axis runs over, the one named last changes fastest.
Arguments:
- queries: bfloat16 [256, 32, 128], P(('grp', 'psg', 'qry')), parts along dimension 0, may hold values from -0.5 to 0.5
- passages: bfloat16 [2048, 64, 128], P(('grp', 'psg')), parts along dimension 0, may hold values from -6 to 6
- lengths: int32 [2048], P(('grp', 'psg')), parts along dimension 0, may hold values from 8 to 64
- candidates: int32 [2, 128, 32], P('qry', ('grp', 'psg')), parts along dimension 1, may hold values from 0 to 31, as said below
Outputs:
- scores: float32 [32, 8, 32, 2, 16], P(('grp', 'psg', 'qry')), parts along dimension 0
There are 2 independent parts, one for each index of `grp`. A program takes and returns all parts, laid end to end along the dimension named above; each array names one. Nothing has to cross between parts.
Inputs may be any that keep to these rules, and one draw needn't show every extreme that they name: `candidates`: in the 8 rows of one passage shard and one half, every owner id // 4 is named exactly 32 times, always with the same id.
All inputs are finite; a program needn't handle non-finite values.
Results may differ from a plain program's by a relative error of at most 0.0003.
Values may be sent and summed in bfloat16 or wider, within the bound.
No kernel may reach another device: no remote copies, remote signals or barrier semaphores. Data moves between devices by JAX's collectives and lax.ppermute only.
A program may use at most 64 MiB of HBM per device.

v0:
```python
import jax
import jax.numpy as jnp
from jax import lax
from jax.sharding import PartitionSpec as P

DIM = 128
QT = 32
PT = 64
QB = 2
QBD = 4
PBS = 16
KB = 32


def score_rows(query_sel, passages, lengths):
    block_rows = passages.shape[0] // PBS
    query_rows = query_sel.reshape(block_rows, KB * QB * QT, DIM)
    passage_rows = passages.reshape(block_rows, PBS * PT, DIM)
    valid = jnp.arange(PT, dtype=jnp.int32)[None, None, :] < lengths.reshape(block_rows, PBS, 1)

    def one_row(items):
        left, right, keep = items
        dots = jnp.einsum("ad,bd->ab", left, right, preferred_element_type=jnp.float32)
        dots = dots.reshape(KB * QB, QT, PBS, PT)
        dots = jnp.where(keep[None, None, :, :], dots, -jnp.inf)
        return jnp.sum(jnp.max(dots, axis=3), axis=1) * (1.0 / QT)

    tiles = lax.map(one_row, (query_rows, passage_rows, valid))
    return tiles.reshape(block_rows * KB, QB, PBS)


def per_device(queries, passages, lengths, candidates):
    shards = lax.axis_size("psg")
    rows = candidates.reshape(-1)
    entries = rows.shape[0]
    slots = entries // shards
    owners = rows // QBD
    blocks = rows % QBD
    gathered = lax.all_gather(queries, "psg", axis=0, tiled=True)
    start = owners * (QBD * QB) + blocks * QB
    picked = start[:, None] + jnp.arange(QB, dtype=jnp.int32)[None, :]
    query_sel = gathered[picked]
    tiles = score_rows(query_sel, passages, lengths)
    order = jnp.arange(entries, dtype=jnp.int32)
    same = owners[:, None] == owners[None, :]
    earlier = order[None, :] < order[:, None]
    rank = jnp.sum(jnp.where(same & earlier, 1, 0), axis=1).astype(jnp.int32)
    outgoing_tiles = jnp.zeros((shards, slots, QB, PBS), jnp.float32).at[owners, rank].set(tiles)
    received = lax.all_to_all(outgoing_tiles, "psg", split_axis=0, concat_axis=0, tiled=True)
    return received[None]


def solution(mesh):
    return jax.shard_map(
        per_device,
        mesh=mesh,
        in_specs=(
            P(("grp", "psg", "qry"), None, None),
            P(("grp", "psg"), None, None),
            P(("grp", "psg")),
            P("qry", ("grp", "psg"), None),
        ),
        out_specs=P(("grp", "psg", "qry"), None, None, None, None),
        check_vma=False,
    )
```

profile of v0, /device:TPU:0, one launch (start us, length us, event | category | flops | bytes accessed | tf_op | source)
XLA Modules:
  0.0 120.3 jit_solution(14168817770136057016)
XLA Ops:
  0.0 0.8 reshape.233
  0.8 0.8 reshape.232
  1.8 33.2 %all_gather.3 = bf16[64,32,128]{2,1,0:T(8,128)(2,1)S(1)} all-gather(bf16[8,32,128]{2,1,0:T(8,128)(2,1)} %param.6), channel_id=1, replica_groups=mesh['grp'=2,'psg'=8,'qry'=2] {'psg'}, dimensions={0}, use_global_device_ids=true | all-gather | bytes 589824 | tf_op jit(solution)/shard_map/all_gather | solution.py:39
  35.0 0.7 lt.76
  35.9 3.4 %gather_fusion = bf16[512,32,128]{2,1,0:T(8,128)(2,1)} fusion(bf16[64,32,128]{2,1,0:T(8,128)(2,1)S(1)} %all_gather.3, s32[1024]{0:T(1024)S(1)} %pad_clamp_fusion), kind=kCustom, calls=%fused_computation | custom fusion | bytes 8390656 | tf_op jit(solution)/shard_map/gather | solution.py:42
  39.3 56.4 %while.10 = (s32[]{:T(128)}, f32[8,64,16]{2,1,0:T(8,128)S(1)}, pred[8,16,64]{2,1,0:T(8,128)(4,1)S(1)}, bf16[8,2048,128]{2,1,0:T(8,128)(2,1)}, bf16[8,1024,128]{2,1,0:T(8,128)(2,1)}, /*index=5*/s32[]{:T(128)}, f32[]{:T(128)}) while((s32[]{:T(128)}, f32[8,64,16]{2,1,0:T(8,128)S(1)}, pred[8,16,64]{2,1,0:T(8,128)(4,1)S(1)}, ...), condition=%wide.region_4.5_spmd, body=%wide.region_1.4_spmd.sunk | while | flops 541065216 | bytes 2694241 | solution.py:28
  39.3 1.1 constant_dynamic-slice_fusion.4
  40.4 1.0 constant_dynamic-slice_fusion.5
  41.4 4.7 %select_reduce_fusion.3 = f32[64,32,16]{1,2,0:T(8,128)S(1)} fusion(bf16[64,32,128,1]{2,1,3,0:T(8,128)(2,1)S(1)} %bitcast.39, bf16[16,64,128,1]{2,1,0,3:T(8,128)(2,1)S(1)} %bitcast.41, pred[16,64]{1,0:T(8,128)(4,1)S(1)} %dynamic-slice_bitcast_fusion.2), kind=kOutput, calls=%fused_computation.2.clone.1 | convolution fusion | flops 541032448 | bytes 918528 | tf_op jit(solution)/shard_map/while/body/eval_jaxpr/ad,bd->ab/dot_general | solution.py:23
  46.4 1.1 constant_dynamic-slice_fusion.4
  47.4 1.0 constant_dynamic-slice_fusion.5
  48.4 4.7 %select_reduce_fusion.3 = f32[64,32,16]{1,2,0:T(8,128)S(1)} fusion(bf16[64,32,128,1]{2,1,3,0:T(8,128)(2,1)S(1)} %bitcast.39, bf16[16,64,128,1]{2,1,0,3:T(8,128)(2,1)S(1)} %bitcast.41, pred[16,64]{1,0:T(8,128)(4,1)S(1)} %dynamic-slice_bitcast_fusion.2), kind=kOutput, calls=%fused_computation.2.clone.1 | convolution fusion | flops 541032448 | bytes 918528 | tf_op jit(solution)/shard_map/while/body/eval_jaxpr/ad,bd->ab/dot_general | solution.py:23
  53.4 1.1 constant_dynamic-slice_fusion.4
  54.5 1.0 constant_dynamic-slice_fusion.5
  55.5 4.7 %select_reduce_fusion.3 = f32[64,32,16]{1,2,0:T(8,128)S(1)} fusion(bf16[64,32,128,1]{2,1,3,0:T(8,128)(2,1)S(1)} %bitcast.39, bf16[16,64,128,1]{2,1,0,3:T(8,128)(2,1)S(1)} %bitcast.41, pred[16,64]{1,0:T(8,128)(4,1)S(1)} %dynamic-slice_bitcast_fusion.2), kind=kOutput, calls=%fused_computation.2.clone.1 | convolution fusion | flops 541032448 | bytes 918528 | tf_op jit(solution)/shard_map/while/body/eval_jaxpr/ad,bd->ab/dot_general | solution.py:23
  60.5 1.1 constant_dynamic-slice_fusion.4
  61.6 1.0 constant_dynamic-slice_fusion.5
  62.5 4.7 %select_reduce_fusion.3 = f32[64,32,16]{1,2,0:T(8,128)S(1)} fusion(bf16[64,32,128,1]{2,1,3,0:T(8,128)(2,1)S(1)} %bitcast.39, bf16[16,64,128,1]{2,1,0,3:T(8,128)(2,1)S(1)} %bitcast.41, pred[16,64]{1,0:T(8,128)(4,1)S(1)} %dynamic-slice_bitcast_fusion.2), kind=kOutput, calls=%fused_computation.2.clone.1 | convolution fusion | flops 541032448 | bytes 918528 | tf_op jit(solution)/shard_map/while/body/eval_jaxpr/ad,bd->ab/dot_general | solution.py:23
  67.5 1.1 constant_dynamic-slice_fusion.4
  68.6 1.0 constant_dynamic-slice_fusion.5
  69.6 4.7 %select_reduce_fusion.3 = f32[64,32,16]{1,2,0:T(8,128)S(1)} fusion(bf16[64,32,128,1]{2,1,3,0:T(8,128)(2,1)S(1)} %bitcast.39, bf16[16,64,128,1]{2,1,0,3:T(8,128)(2,1)S(1)} %bitcast.41, pred[16,64]{1,0:T(8,128)(4,1)S(1)} %dynamic-slice_bitcast_fusion.2), kind=kOutput, calls=%fused_computation.2.clone.1 | convolution fusion | flops 541032448 | bytes 918528 | tf_op jit(solution)/shard_map/while/body/eval_jaxpr/ad,bd->ab/dot_general | solution.py:23
  74.6 1.1 constant_dynamic-slice_fusion.4
  75.7 1.0 constant_dynamic-slice_fusion.5
  76.7 4.7 %select_reduce_fusion.3 = f32[64,32,16]{1,2,0:T(8,128)S(1)} fusion(bf16[64,32,128,1]{2,1,3,0:T(8,128)(2,1)S(1)} %bitcast.39, bf16[16,64,128,1]{2,1,0,3:T(8,128)(2,1)S(1)} %bitcast.41, pred[16,64]{1,0:T(8,128)(4,1)S(1)} %dynamic-slice_bitcast_fusion.2), kind=kOutput, calls=%fused_computation.2.clone.1 | convolution fusion | flops 541032448 | bytes 918528 | tf_op jit(solution)/shard_map/while/body/eval_jaxpr/ad,bd->ab/dot_general | solution.py:23
  81.6 1.1 constant_dynamic-slice_fusion.4
  82.7 1.0 constant_dynamic-slice_fusion.5
  83.7 4.7 %select_reduce_fusion.3 = f32[64,32,16]{1,2,0:T(8,128)S(1)} fusion(bf16[64,32,128,1]{2,1,3,0:T(8,128)(2,1)S(1)} %bitcast.39, bf16[16,64,128,1]{2,1,0,3:T(8,128)(2,1)S(1)} %bitcast.41, pred[16,64]{1,0:T(8,128)(4,1)S(1)} %dynamic-slice_bitcast_fusion.2), kind=kOutput, calls=%fused_computation.2.clone.1 | convolution fusion | flops 541032448 | bytes 918528 | tf_op jit(solution)/shard_map/while/body/eval_jaxpr/ad,bd->ab/dot_general | solution.py:23
  88.7 1.1 constant_dynamic-slice_fusion.4
  89.8 1.0 constant_dynamic-slice_fusion.5
  90.8 4.7 %select_reduce_fusion.3 = f32[64,32,16]{1,2,0:T(8,128)S(1)} fusion(bf16[64,32,128,1]{2,1,3,0:T(8,128)(2,1)S(1)} %bitcast.39, bf16[16,64,128,1]{2,1,0,3:T(8,128)(2,1)S(1)} %bitcast.41, pred[16,64]{1,0:T(8,128)(4,1)S(1)} %dynamic-slice_bitcast_fusion.2), kind=kOutput, calls=%fused_computation.2.clone.1 | convolution fusion | flops 541032448 | bytes 918528 | tf_op jit(solution)/shard_map/while/body/eval_jaxpr/ad,bd->ab/dot_general | solution.py:23
  96.0 9.8 %scatter_fusion = f32[8,32,2,16]{3,2,1,0:T(2,128)S(1)} fusion(f32[8,32,2,16]{3,2,1,0:T(2,128)S(1)} %broadcast_in_dim.44, s32[256]{0:T(256)S(1)} %bitcast.38, f32[256,2,16]{2,1,0:T(2,128)S(1)} %bitcast.44), kind=kCustom, calls=%fused_computation.1 | custom fusion | bytes 100352 | tf_op jit(solution)/shard_map/scatter | solution.py:48
  106.1 12.2 %all_to_all.5 = f32[8,1,1024]{2,1,0:T(1,128)S(1)} all-to-all(f32[8,1,1024]{2,1,0:T(1,128)S(1)} %reshape.255), channel_id=1, replica_groups=mesh['grp'=2,'psg'=8,'qry'=2] {'psg'}, dimensions={0} | all-to-all | bytes 65536 | tf_op jit(solution)/shard_map/all_to_all | solution.py:49
  (39 shorter events, 4.7 us)
where the time goes:
time: 121 us; the launch traced here: 120 us
  blocking collectives  45.4 us (38%)
  matrix products  37.8 us (31%)
  local copies, waits for them, and re-layouts  33.7 us (28%)
  other arithmetic  2.88 us (2%)
    dot_general x8, matrix products, one_row(): jnp.einsum('ad,bd->ab', left, right, preferred_element_type=jnp.float32)  37.8 us
    all_gather x1, blocking collectives, per_device(): gathered = lax.all_gather(queries, 'psg', axis=0, tiled=True)  33.2 us
    dynamic_slice x16, local copies, waits for them, and re-layouts, score_rows(): tiles = lax.map(one_row, (query_rows, passage_rows, valid))  16.4 us
    all_to_all x1, blocking collectives, per_device(): lax.all_to_all(outgoing_tiles, 'psg', split_axis=0, concat_axis=0, tiled=...  12.2 us
    scatter x2, local copies, waits for them, and re-layouts, per_device(): jnp.zeros((shards, slots, QB, PBS), jnp.float32).at[owners, rank].set(tiles)  9.88 us
    gather x1, local copies, waits for them, and re-layouts, per_device(): query_sel = gathered[picked]  3.43 us

commit v1 on v0

v1 whole, which is shorter than its diff:
```python
import functools

import jax
import jax.numpy as jnp
from jax import lax
from jax.experimental import pallas as pl
from jax.experimental.pallas import tpu as pltpu
from jax.sharding import PartitionSpec as P

DIM = 128
QT = 32
PT = 64
QB = 2
QBD = 4
PBS = 16
KB = 32
LANES = 128
GROUP = 8


def score_kernel(first_ref, cand_ref, len_ref, q_ref, p_ref, out_ref, sel_ref, max_ref):
    shards = q_ref.shape[0]
    rows = cand_ref.shape[0]
    count = p_ref.shape[0]
    tokens = QB * QT
    cand = cand_ref[...]
    owner = cand // QBD
    block = cand - owner * QBD
    lane = lax.broadcasted_iota(jnp.int32, (rows, LANES), 1)
    sub = lax.broadcasted_iota(jnp.int32, (rows, LANES), 0)

    for o in range(shards):
        mine = owner == first_ref[0] + o
        named = jnp.max(jnp.where(mine, block, 0))
        sel_ref[o * tokens:(o + 1) * tokens, :] = q_ref[o, pl.ds(named * tokens, tokens), :]
        named_here = jnp.sum(jnp.where(mine, 1.0, 0.0), axis=1, keepdims=True)
        upto = jnp.broadcast_to(named_here, (rows, LANES))
        step = 1
        while step < rows:
            upto = upto + jnp.where(sub >= step, pltpu.roll(upto, step, 0), 0.0)
            step *= 2
        row_of_slot = jnp.sum(jnp.where(upto <= lane.astype(jnp.float32), 1.0, 0.0), axis=0, keepdims=True)
        out_ref[o, QB:QB + 1, :] = row_of_slot

    sel = sel_ref[...]
    u = lax.broadcasted_iota(jnp.int32, (PT, 1), 0)
    for g in range(count // GROUP):
        left = p_ref[g * GROUP:(g + 1) * GROUP].reshape(GROUP * PT, DIM)
        dots = lax.dot_general(left, sel, (((1,), (1,)), ((), ())), preferred_element_type=jnp.float32)
        for i in range(GROUP):
            live = u < len_ref[g * GROUP + i]
            best = jnp.where(live, dots[i * PT:(i + 1) * PT], -jnp.inf)
            max_ref[g * GROUP + i:g * GROUP + i + 1, :] = jnp.max(best, axis=0, keepdims=True)

    best = max_ref[...]
    high = best.astype(jnp.bfloat16)
    rest = best - high.astype(jnp.float32)
    mid = rest.astype(jnp.bfloat16)
    low = (rest - mid.astype(jnp.float32)).astype(jnp.bfloat16)
    query = lax.broadcasted_iota(jnp.int32, (shards * QB, shards * tokens), 0)
    token = lax.broadcasted_iota(jnp.int32, (shards * QB, shards * tokens), 1)
    ones = jnp.where(token // QT == query, 1.0, 0.0).astype(jnp.bfloat16)
    total = jnp.zeros((shards * QB, count), jnp.float32)
    for part in (low, mid, high):
        total = total + lax.dot_general(ones, part, (((1,), (1,)), ((), ())), preferred_element_type=jnp.float32)
    total = total * (1.0 / QT)
    for o in range(shards):
        out_ref[o, 0:QB, :] = total[o * QB:(o + 1) * QB]


def place_kernel(in_ref, out_ref):
    shards = in_ref.shape[0]
    slots = out_ref.shape[-1]
    m = lax.broadcasted_iota(jnp.int32, (PBS, LANES), 0)
    for j in range(shards):
        row = in_ref[j, QB:QB + 1, :].astype(jnp.int32)
        where = jnp.minimum(row * PBS, LANES - PBS) + m
        for i in range(QB):
            tile = jnp.broadcast_to(in_ref[j, i:i + 1, :], (PBS, LANES))
            out_ref[j, i] = jnp.take_along_axis(tile, where, axis=1)[:, :slots]


def per_device(queries, passages, lengths, candidates):
    shards = lax.axis_size("psg")
    count = passages.shape[0]
    rows = count // PBS
    slots = rows * KB // shards
    tokens = QB * QT
    mine = queries.reshape(1, QBD * tokens, DIM)
    gathered = lax.all_to_all(
        jnp.broadcast_to(mine, (shards, QBD * tokens, DIM)), "psg", split_axis=0, concat_axis=0, tiled=True
    )
    vmem = pl.BlockSpec(memory_space=pltpu.VMEM)
    some = min(shards, 8)
    smem = pl.BlockSpec(memory_space=pltpu.SMEM)
    score = pl.pallas_call(
        score_kernel,
        out_shape=jax.ShapeDtypeStruct((some, QB + 1, LANES), jnp.float32),
        in_specs=[smem, vmem, smem, vmem, vmem],
        out_specs=vmem,
        scratch_shapes=[
            pltpu.VMEM((some * tokens, DIM), jnp.bfloat16),
            pltpu.VMEM((count, some * tokens), jnp.float32),
        ],
        compiler_params=pltpu.CompilerParams(vmem_limit_bytes=40 * 1024 * 1024),
    )

    def score_some(items):
        first, some_queries = items
        return score(first, candidates.reshape(rows, KB), lengths, some_queries, passages)

    firsts = some * jnp.arange(shards // some, dtype=jnp.int32)[:, None]
    if shards == some:
        tiles = score_some((firsts[0], gathered))
    else:
        tiles = lax.map(score_some, (firsts, gathered.reshape(shards // some, some, QBD * tokens, DIM)))
        tiles = tiles.reshape(shards, QB + 1, LANES)
    received = lax.all_to_all(tiles, "psg", split_axis=0, concat_axis=0, tiled=True)
    placed = pl.pallas_call(
        place_kernel,
        out_shape=jax.ShapeDtypeStruct((shards, QB, PBS, slots), jnp.float32),
        in_specs=[vmem],
        out_specs=vmem,
    )(received)
    return placed.transpose(0, 3, 1, 2)[None]


def solution(mesh):
    return jax.shard_map(
        per_device,
        mesh=mesh,
        in_specs=(
            P(("grp", "psg", "qry"), None, None),
            P(("grp", "psg"), None, None),
            P(("grp", "psg")),
            P("qry", ("grp", "psg"), None),
        ),
        out_specs=P(("grp", "psg", "qry"), None, None, None, None),
        check_vma=False,
    )
```

time: 121 us -> 41 us (0.34)
  matrix products: 37.8 us -> 0 us
  local copies, waits for them, and re-layouts: 33.7 us -> 3.84 us
  blocking collectives: 45.4 us -> 31.6 us
  Pallas kernels: 0 us -> 5.19 us
  other arithmetic: 2.88 us -> 0 us
    dot_general x8 -> x0, matrix products: 37.8 us -> none  [one_row(): jnp.einsum('ad,bd->ab', left, right, preferred_element_type=jnp.float32)]
    all_gather x1 -> x0, blocking collectives: 33.2 us -> none  [per_device(): gathered = lax.all_gather(queries, 'psg', axis=0, tiled=True)]
    all_to_all x1 -> x2, blocking collectives: 12.2 us -> 31.6 us  [the longest x1 21.6 us: per_device(): lax.all_to_all(jnp.broadcast_to(mine, (shards, QBD * tokens, DIM)), 'psg'...]
    dynamic_slice x16 -> x0, local copies, waits for them, and re-layouts: 16.4 us -> none  [score_rows(): tiles = lax.map(one_row, (query_rows, passage_rows, valid))]
    scatter x2 -> x0, local copies, waits for them, and re-layouts: 9.88 us -> none  [per_device(): jnp.zeros((shards, slots, QB, PBS), jnp.float32).at[owners, rank].set(tiles)]
    pallas_call x0 -> x2, Pallas kernels: none -> 5.19 us  [the longest x1 3.67 us: score_some(): score(first, candidates.reshape(rows, KB), lengths, some_queries, passages)]
    gather x1 -> x0, local copies, waits for them, and re-layouts: 3.43 us -> none  [per_device(): query_sel = gathered[picked]]
    unnamed x2 -> x6, local copies, waits for them, and re-layouts: 0.23 us -> 2.93 us
where the time goes in v1:
time: 41 us; the launch traced here: 40.7 us
  blocking collectives  31.6 us (77%)
  Pallas kernels  5.19 us (13%)
  local copies, waits for them, and re-layouts  3.84 us (9%)
    all_to_all x1, blocking collectives, per_device(): lax.all_to_all(jnp.broadcast_to(mine, (shards, QBD * tokens, DIM)), 'psg'...  21.6 us
    all_to_all x1, blocking collectives, per_device(): lax.all_to_all(tiles, 'psg', split_axis=0, concat_axis=0, tiled=True)  10.1 us
    pallas_call x1, Pallas kernels, score_some(): score(first, candidates.reshape(rows, KB), lengths, some_queries, passages)  3.67 us
    unnamed x6, local copies, waits for them, and re-layouts  2.93 us
    pallas_call x1, Pallas kernels, per_device(): pl.pallas_call(place_kernel, out_shape=jax.ShapeDtypeStruct((shards, QB,...  1.52 us
    broadcast_in_dim x1, local copies, waits for them, and re-layouts, per_device(): jnp.broadcast_to(mine, (shards, QBD * tokens, DIM))  0.91 us

profile of v1, /device:TPU:0, one launch (start us, length us, event | category | flops | bytes accessed | tf_op | source)
XLA Modules:
  0.0 40.7 jit_solution(16084127227122640346)
XLA Ops:
  0.0 0.9 %broadcast_in_dim.11 = bf16[8,256,128]{2,1,0:T(8,128)(2,1)S(1)} broadcast(bf16[256,128]{1,0:T(8,128)(2,1)} %bitcast.6), dimensions={1,2} | broadcast | bytes 589824 | tf_op jit(solution)/shard_map/broadcast_in_dim | solution.py:91
  0.9 21.6 %all_to_all.10.q_ref = bf16[8,256,128]{2,1,0:T(8,128)(2,1)S(1)} all-to-all(bf16[8,256,128]{2,1,0:T(8,128)(2,1)S(1)} %broadcast_in_dim.11), channel_id=1, replica_groups=mesh['grp'=2,'psg'=8,'qry'=2] {'psg'}, dimensions={0} | all-to-all | bytes 1048576 | tf_op jit(solution)/shard_map/all_to_all | solution.py:90
  22.5 0.0 copy-start
  22.5 1.6 %copy-done = bf16[128,64,128]{2,1,0:T(8,128)(2,1)S(1)} copy-done((bf16[128,64,128]{2,1,0:T(8,128)(2,1)S(1)}, bf16[128,64,128]{2,1,0:T(8,128)(2,1)}, u32[]{:S(2)}) %copy-start) | copy-done | bytes 2097176
  24.1 0.0 copy-start.1
  24.1 0.7 %copy-done.1 = s32[1,8,32]{2,1,0:T(8,128)S(1)} copy-done((s32[1,8,32]{2,1,0:T(8,128)S(1)}, s32[1,8,32]{2,1,0:T(8,128)}, u32[]{:S(2)}) %copy-start.1) | copy-done | bytes 1048
  24.8 0.0 copy-start.2
  24.8 0.7 %copy-done.2 = s32[128]{0:T(128)S(1)} copy-done((s32[128]{0:T(128)S(1)}, s32[128]{0:T(128)}, u32[]{:S(2)}) %copy-start.2) | copy-done | bytes 536
  25.4 3.7 %shard_map.46 = f32[8,3,128]{2,1,0:T(4,128)S(1)} custom-call(s32[1]{0:T(128)} %constant.0.clone.1.first_ref, s32[8,32]{1,0:T(8,128)S(1)} %bitcast.5, s32[128]{0:T(128)S(1)} %copy-done.2, bf16[8,256,128]{2,1,0:T(8,128)(2,1)S(1)} %all_to_all.10.q_ref, bf16[128,64,128]{2,1,0:T(8,128)(2,1)S(1)} %copy-done), custom_call_target="tpu_custom_call" | custom-call | tf_op jit(solution)/shard_map/pallas_call | solution.py:110
  29.1 10.1 %all_to_all.11.in_ref = f32[8,3,128]{2,1,0:T(4,128)} all-to-all(f32[8,3,128]{2,1,0:T(4,128)S(1)} %shard_map.46), channel_id=1, replica_groups=mesh['grp'=2,'psg'=8,'qry'=2] {'psg'}, dimensions={0} | all-to-all | bytes 24576 | tf_op jit(solution)/shard_map/all_to_all | solution.py:118
  39.2 1.5 %shard_map.47 = f32[8,2,16,32]{3,2,1,0:T(8,128)} custom-call(f32[8,3,128]{2,1,0:T(4,128)} %all_to_all.11.in_ref), custom_call_target="tpu_custom_call" | custom-call | tf_op jit(solution)/shard_map/pallas_call | solution.py:119
Async XLA Ops:
  22.5 1.6 %copy-start = (bf16[128,64,128]{2,1,0:T(8,128)(2,1)S(1)}, bf16[128,64,128]{2,1,0:T(8,128)(2,1)}, u32[]{:S(2)}) copy-start(bf16[128,64,128]{2,1,0:T(8,128)(2,1)} %p_ref.1) | copy-start | bytes 6291460
  24.1 0.7 %copy-start.1 = (s32[1,8,32]{2,1,0:T(8,128)S(1)}, s32[1,8,32]{2,1,0:T(8,128)}, u32[]{:S(2)}) copy-start(s32[1,8,32]{2,1,0:T(8,128)} %param.7) | copy-start | bytes 3076
  24.8 0.7 %copy-start.2 = (s32[128]{0:T(128)S(1)}, s32[128]{0:T(128)}, u32[]{:S(2)}) copy-start(s32[128]{0:T(128)} %len_ref.1) | copy-start | bytes 1540

commit v2 on v1

v2 whole, which is shorter than its diff:
```python
import jax
import jax.numpy as jnp
from jax import lax
from jax.experimental import pallas as pl
from jax.experimental.pallas import tpu as pltpu
from jax.sharding import PartitionSpec as P

DIM = 128
QT = 32
PT = 64
QB = 2
QBD = 4
PBS = 16
KB = 32
LANES = 128
GROUP = 8


def score_kernel(owners_ref, cand_ref, len_ref, p_ref, *refs):
    some = (len(refs) - 2) // 2
    q_refs, out_refs = refs[:some], refs[some:2 * some]
    sel_ref, max_ref = refs[2 * some:]
    rows = cand_ref.shape[0]
    count = p_ref.shape[0]
    tokens = QB * QT
    cand = cand_ref[...]
    owner = cand // QBD
    block = cand - owner * QBD
    lane = lax.broadcasted_iota(jnp.int32, (rows, LANES), 1)
    sub = lax.broadcasted_iota(jnp.int32, (rows, LANES), 0)

    for k in range(some):
        mine = owner == owners_ref[k]
        named = jnp.max(jnp.where(mine, block, 0))
        sel_ref[k * tokens:(k + 1) * tokens, :] = q_refs[k][pl.ds(named * tokens, tokens), :]
        named_here = jnp.sum(jnp.where(mine, 1.0, 0.0), axis=1, keepdims=True)
        upto = jnp.broadcast_to(named_here, (rows, LANES))
        step = 1
        while step < rows:
            upto = upto + jnp.where(sub >= step, pltpu.roll(upto, step, 0), 0.0)
            step *= 2
        row_of_slot = jnp.sum(jnp.where(upto <= lane.astype(jnp.float32), 1.0, 0.0), axis=0, keepdims=True)
        out_refs[k][QB:QB + 1, :] = row_of_slot

    sel = sel_ref[...]
    u = lax.broadcasted_iota(jnp.int32, (PT, 1), 0)
    for g in range(count // GROUP):
        left = p_ref[g * GROUP:(g + 1) * GROUP].reshape(GROUP * PT, DIM)
        dots = lax.dot_general(left, sel, (((1,), (1,)), ((), ())), preferred_element_type=jnp.float32)
        for i in range(GROUP):
            live = u < len_ref[g * GROUP + i]
            best = jnp.where(live, dots[i * PT:(i + 1) * PT], -jnp.inf)
            max_ref[g * GROUP + i:g * GROUP + i + 1, :] = jnp.max(best, axis=0, keepdims=True)

    best = max_ref[...]
    high = best.astype(jnp.bfloat16)
    rest = best - high.astype(jnp.float32)
    mid = rest.astype(jnp.bfloat16)
    low = (rest - mid.astype(jnp.float32)).astype(jnp.bfloat16)
    query = lax.broadcasted_iota(jnp.int32, (some * QB, some * tokens), 0)
    token = lax.broadcasted_iota(jnp.int32, (some * QB, some * tokens), 1)
    ones = jnp.where(token // QT == query, 1.0, 0.0).astype(jnp.bfloat16)
    total = jnp.zeros((some * QB, count), jnp.float32)
    for part in (low, mid, high):
        total = total + lax.dot_general(ones, part, (((1,), (1,)), ((), ())), preferred_element_type=jnp.float32)
    total = total * (1.0 / QT)
    for k in range(some):
        out_refs[k][0:QB, :] = total[k * QB:(k + 1) * QB]


def score(owners, candidates, lengths, passages, blocks):
    some = len(blocks)
    count = passages.shape[0]
    smem = pl.BlockSpec(memory_space=pltpu.SMEM)
    vmem = pl.BlockSpec(memory_space=pltpu.VMEM)
    return pl.pallas_call(
        score_kernel,
        out_shape=[jax.ShapeDtypeStruct((QB + 1, LANES), jnp.float32)] * some,
        in_specs=[smem, vmem, smem, vmem] + [vmem] * some,
        out_specs=[vmem] * some,
        scratch_shapes=[
            pltpu.VMEM((some * QB * QT, DIM), jnp.bfloat16),
            pltpu.VMEM((count, some * QB * QT), jnp.float32),
        ],
        compiler_params=pltpu.CompilerParams(vmem_limit_bytes=40 * 1024 * 1024),
    )(owners, candidates, lengths, passages, *blocks)


def place_kernel(shards_ref, *refs):
    in_refs, out_ref = refs[:-1], refs[-1]
    slots = out_ref.shape[-1]
    m = lax.broadcasted_iota(jnp.int32, (PBS, LANES), 0)
    for k, in_ref in enumerate(in_refs):
        row = in_ref[QB:QB + 1, :].astype(jnp.int32)
        where = jnp.minimum(row * PBS, LANES - PBS) + m
        for i in range(QB):
            tile = jnp.broadcast_to(in_ref[i:i + 1, :], (PBS, LANES))
            out_ref[shards_ref[k], i] = jnp.take_along_axis(tile, where, axis=1)[:, :slots]


def place(shards, tiles, slots):
    vmem = pl.BlockSpec(memory_space=pltpu.VMEM)
    return pl.pallas_call(
        place_kernel,
        out_shape=jax.ShapeDtypeStruct((len(tiles), QB, PBS, slots), jnp.float32),
        in_specs=[pl.BlockSpec(memory_space=pltpu.SMEM)] + [vmem] * len(tiles),
        out_specs=vmem,
    )(shards, *tiles)


def swap(x, k, shards):
    return lax.ppermute(x, "psg", [(j, j ^ k) for j in range(shards)]) if k else x


def per_device(queries, passages, lengths, candidates):
    shards = lax.axis_size("psg")
    rows = passages.shape[0] // PBS
    slots = rows * KB // shards
    cand = candidates.reshape(rows, KB)
    own = queries.reshape(QBD * QB * QT, DIM)
    if shards <= 8:
        partners = lax.axis_index("psg") ^ jnp.arange(shards, dtype=jnp.int32)
        blocks = [swap(own, k, shards) for k in range(shards)]
        tiles = score(partners, cand, lengths, passages, blocks)
        received = [swap(tiles[k], k, shards) for k in range(shards)]
        placed = place(partners, received, slots)
    else:
        gathered = lax.all_gather(own, "psg", axis=0)
        some = 8

        def score_some(items):
            first, some_blocks = items
            owners = first + jnp.arange(some, dtype=jnp.int32)
            return jnp.stack(score(owners, cand, lengths, passages, [some_blocks[k] for k in range(some)]))

        firsts = jnp.arange(0, shards, some, dtype=jnp.int32)
        tiles = lax.map(score_some, (firsts, gathered.reshape(shards // some, some, *own.shape)))
        received = lax.all_to_all(
            tiles.reshape(shards, QB + 1, LANES), "psg", split_axis=0, concat_axis=0, tiled=True
        )
        placed = jnp.concatenate([
            place(jnp.arange(some, dtype=jnp.int32), [received[j + k] for k in range(some)], slots)
            for j in range(0, shards, some)
        ])
    return placed.transpose(0, 3, 1, 2)[None]


def solution(mesh):
    return jax.shard_map(
        per_device,
        mesh=mesh,
        in_specs=(
            P(("grp", "psg", "qry"), None, None),
            P(("grp", "psg"), None, None),
            P(("grp", "psg")),
            P("qry", ("grp", "psg"), None),
        ),
        out_specs=P(("grp", "psg", "qry"), None, None, None, None),
        check_vma=False,
    )
```

time: 41 us -> 45.1 us (1.10)
  blocking collectives: 31.6 us -> 0 us
  starting transfers between devices: 0 us -> 24.2 us
  waiting for transfers between devices: 0 us -> 10.3 us
  local copies, waits for them, and re-layouts: 3.84 us -> 4.91 us
    all_to_all x2 -> x0, blocking collectives: 31.6 us -> none  [the longest x1 21.6 us: per_device(): lax.all_to_all(jnp.broadcast_to(mine, (shards, QBD * tokens, DIM)), 'psg'...]
    ppermute x0 -> x14, starting transfers between devices: none -> 24.2 us  [swap(): lax.ppermute(x, 'psg', [(j, j ^ k) for j in range(shards)])]
    ppermute x0 -> x14, waiting for transfers between devices: none -> 10.3 us  [swap(): lax.ppermute(x, 'psg', [(j, j ^ k) for j in range(shards)])]
    unnamed x6 -> x26, local copies, waits for them, and re-layouts: 2.93 us -> 4.91 us
    broadcast_in_dim x1 -> x0, local copies, waits for them, and re-layouts: 0.91 us -> none  [per_device(): jnp.broadcast_to(mine, (shards, QBD * tokens, DIM))]
  transfers between devices with their start and end apart: 0 -> 14, of which waited for: 0 -> 7; matrix products, arithmetic and copies ran while one was open for 0% -> 0% of each run, Pallas kernels for 0% -> 0%
where the time goes in v2:
time: 45.1 us; the launch traced here: 44.8 us
  starting transfers between devices  24.2 us (54%)
  waiting for transfers between devices  10.3 us (23%)
  Pallas kernels  5.28 us (12%)
  local copies, waits for them, and re-layouts  4.91 us (11%)
    ppermute x14, starting transfers between devices, swap(): lax.ppermute(x, 'psg', [(j, j ^ k) for j in range(shards)])  24.2 us
    ppermute x14, waiting for transfers between devices, swap(): lax.ppermute(x, 'psg', [(j, j ^ k) for j in range(shards)])  10.3 us
    unnamed x26, local copies, waits for them, and re-layouts  4.91 us
    pallas_call x1, Pallas kernels, score(): pl.pallas_call(score_kernel, out_shape=[jax.ShapeDtypeStruct((QB + 1, LAN...  3.67 us
    pallas_call x1, Pallas kernels, place(): pl.pallas_call(place_kernel, out_shape=jax.ShapeDtypeStruct((len(tiles),...  1.61 us
  transfers between devices with their start and end apart: 14, of which 7 were waited for; matrix products, arithmetic and copies ran while one was open for 0% of the time, Pallas kernels for 0%

profile of v2, /device:TPU:0, one launch (start us, length us, event | category | flops | bytes accessed | tf_op | source)
XLA Modules:
  0.0 44.8 jit_solution(2576965312978783967)
XLA Ops:
  0.0 6.0 %collective-permute-start.6 = (bf16[256,128]{1,0:T(8,128)(2,1)}, bf16[256,128]{1,0:T(8,128)(2,1)S(1)}, u32[]{:S(2)}, u32[]{:S(2)}) collective-permute-start(bf16[256,128]{1,0:T(8,128)(2,1)} %bitcast.5), channel_id=1, source_target_pairs={{0,14},{2,12},{4,10},{6,8},{8,6},{10,4},{12,2},{14,0},{1,15},{3,13... | collective-permute-start | bytes 196616 | tf_op jit(solution)/shard_map/ppermute | solution.py:112
  6.0 0.2 collective-permute-start.5
  6.2 0.8 %collective-permute-start.4 = (bf16[256,128]{1,0:T(8,128)(2,1)}, bf16[256,128]{1,0:T(8,128)(2,1)S(1)}, u32[]{:S(2)}, u32[]{:S(2)}) collective-permute-start(bf16[256,128]{1,0:T(8,128)(2,1)} %bitcast.7), channel_id=1, source_target_pairs={{0,10},{2,8},{4,14},{6,12},{8,2},{10,0},{12,6},{14,4},{1,11},{3,9}... | collective-permute-start | bytes 196616 | tf_op jit(solution)/shard_map/ppermute | solution.py:112
  7.0 1.9 %collective-permute-start.3 = (bf16[256,128]{1,0:T(8,128)(2,1)}, bf16[256,128]{1,0:T(8,128)(2,1)S(1)}, u32[]{:S(2)}, u32[]{:S(2)}) collective-permute-start(bf16[256,128]{1,0:T(8,128)(2,1)} %bitcast.8), channel_id=1, source_target_pairs={{0,8},{2,10},{4,12},{6,14},{8,0},{10,2},{12,4},{14,6},{1,9},{3,11}... | collective-permute-start | bytes 196616 | tf_op jit(solution)/shard_map/ppermute | solution.py:112
  8.9 2.4 %collective-permute-start.2 = (bf16[256,128]{1,0:T(8,128)(2,1)}, bf16[256,128]{1,0:T(8,128)(2,1)S(1)}, u32[]{:S(2)}, u32[]{:S(2)}) collective-permute-start(bf16[256,128]{1,0:T(8,128)(2,1)} %bitcast.9), channel_id=1, source_target_pairs={{0,6},{2,4},{4,2},{6,0},{8,14},{10,12},{12,10},{14,8},{1,7},{3,5},... | collective-permute-start | bytes 196616 | tf_op jit(solution)/shard_map/ppermute | solution.py:112
  11.3 0.0 collective-permute-done.6.refs_7_
  11.3 0.8 %collective-permute-start.1 = (bf16[256,128]{1,0:T(8,128)(2,1)}, bf16[256,128]{1,0:T(8,128)(2,1)S(1)}, u32[]{:S(2)}, u32[]{:S(2)}) collective-permute-start(bf16[256,128]{1,0:T(8,128)(2,1)} %bitcast.10), channel_id=1, source_target_pairs={{0,4},{2,6},{4,0},{6,2},{8,12},{10,14},{12,8},{14,10},{1,5},{3,7},... | collective-permute-start | bytes 196616 | tf_op jit(solution)/shard_map/ppermute | solution.py:112
  12.1 0.4 collective-permute-done.5.refs_6_
  12.4 0.5 %collective-permute-start = (bf16[256,128]{1,0:T(8,128)(2,1)}, bf16[256,128]{1,0:T(8,128)(2,1)S(1)}, u32[]{:S(2)}, u32[]{:S(2)}) collective-permute-start(bf16[256,128]{1,0:T(8,128)(2,1)} %bitcast.11), channel_id=1, source_target_pairs={{0,2},{2,0},{4,6},{6,4},{8,10},{10,8},{12,14},{14,12},{1,3},{3,1},... | collective-permute-start | bytes 196616 | tf_op jit(solution)/shard_map/ppermute | solution.py:112
  13.0 2.8 %collective-permute-done.4.refs_5_ = bf16[256,128]{1,0:T(8,128)(2,1)S(1)} collective-permute-done((bf16[256,128]{1,0:T(8,128)(2,1)}, bf16[256,128]{1,0:T(8,128)(2,1)S(1)}, u32[]{:S(2)}, u32[]{:S(2)}) %collective-permute-start.4) | collective-permute-done | bytes 65568 | tf_op jit(solution)/shard_map/ppermute | solution.py:112
  15.8 1.7 %collective-permute-done.3.refs_4_ = bf16[256,128]{1,0:T(8,128)(2,1)S(1)} collective-permute-done((bf16[256,128]{1,0:T(8,128)(2,1)}, bf16[256,128]{1,0:T(8,128)(2,1)S(1)}, u32[]{:S(2)}, u32[]{:S(2)}) %collective-permute-start.3) | collective-permute-done | bytes 65568 | tf_op jit(solution)/shard_map/ppermute | solution.py:112
  17.4 0.0 collective-permute-done.2.refs_3_
  17.4 0.4 collective-permute-done.1.refs_2_
  17.8 0.0 collective-permute-done.refs_1_
  17.8 1.6 %copy-done = bf16[128,64,128]{2,1,0:T(8,128)(2,1)S(1)} copy-done((bf16[128,64,128]{2,1,0:T(8,128)(2,1)S(1)}, bf16[128,64,128]{2,1,0:T(8,128)(2,1)}, u32[]{:S(2)}) %copy-start) | copy-done | bytes 2097176
  19.4 0.8 %copy-done.1 = bf16[8,32,128]{2,1,0:T(8,128)(2,1)S(1)} copy-done((bf16[8,32,128]{2,1,0:T(8,128)(2,1)S(1)}, bf16[8,32,128]{2,1,0:T(8,128)(2,1)}, u32[]{:S(2)}) %copy-start.1) | copy-done | bytes 65560
  20.3 0.7 %copy-done.2 = s32[1,8,32]{2,1,0:T(8,128)S(1)} copy-done((s32[1,8,32]{2,1,0:T(8,128)S(1)}, s32[1,8,32]{2,1,0:T(8,128)}, u32[]{:S(2)}) %copy-start.2) | copy-done | bytes 1048
  20.9 0.7 %copy-done.5 = s32[128]{0:T(128)S(1)} copy-done((s32[128]{0:T(128)S(1)}, s32[128]{0:T(128)}, u32[]{:S(2)}) %copy-start.5) | copy-done | bytes 536
  21.6 3.7 %shard_map.46 = (f32[3,128]{1,0:T(4,128)S(1)}, f32[3,128]{1,0:T(4,128)S(1)}, f32[3,128]{1,0:T(4,128)S(1)}, f32[3,128]{1,0:T(4,128)S(1)}, f32[3,128]{1,0:T(4,128)...) custom-call(s32[8]{0:T(128)S(1)} %iota_xor_fusion.owners_ref.shards_ref, ...), custom_call_target="tpu_custom_call" | custom-call | tf_op jit(solution)/shard_map/pallas_call | solution.py:76
  25.3 0.6 %copy-done.3 = f32[3,128]{1,0:T(4,128)} copy-done((f32[3,128]{1,0:T(4,128)}, f32[3,128]{1,0:T(4,128)S(1)}, u32[]{:S(2)}) %copy-start.3) | copy-done | bytes 1560
  25.9 0.7 %collective-permute-start.7 = (f32[3,128]{1,0:T(4,128)S(1)}, f32[3,128]{1,0:T(4,128)S(1)}, u32[]{:S(2)}, u32[]{:S(2)}) collective-permute-start(f32[3,128]{1,0:T(4,128)S(1)} %get-tuple-element.14), channel_id=1, source_target_pairs={{0,2},{2,0},{4,6},{6,4},{8,10},{10,8},{12,14},{14,12},{1,3},{3,1},... | collective-permute-start | bytes 4616 | tf_op jit(solution)/shard_map/ppermute | solution.py:112
  26.5 1.3 %collective-permute-start.8 = (f32[3,128]{1,0:T(4,128)S(1)}, f32[3,128]{1,0:T(4,128)S(1)}, u32[]{:S(2)}, u32[]{:S(2)}) collective-permute-start(f32[3,128]{1,0:T(4,128)S(1)} %get-tuple-element.15), channel_id=1, source_target_pairs={{0,4},{2,6},{4,0},{6,2},{8,12},{10,14},{12,8},{14,10},{1,5},{3,7},... | collective-permute-start | bytes 4616 | tf_op jit(solution)/shard_map/ppermute | solution.py:112
  27.8 1.5 %collective-permute-start.9 = (f32[3,128]{1,0:T(4,128)S(1)}, f32[3,128]{1,0:T(4,128)S(1)}, u32[]{:S(2)}, u32[]{:S(2)}) collective-permute-start(f32[3,128]{1,0:T(4,128)S(1)} %get-tuple-element.16), channel_id=1, source_target_pairs={{0,6},{2,4},{4,2},{6,0},{8,14},{10,12},{12,10},{14,8},{1,7},{3,5},... | collective-permute-start | bytes 4616 | tf_op jit(solution)/shard_map/ppermute | solution.py:112
  29.3 3.4 %collective-permute-start.10 = (f32[3,128]{1,0:T(4,128)S(1)}, f32[3,128]{1,0:T(4,128)S(1)}, u32[]{:S(2)}, u32[]{:S(2)}) collective-permute-start(f32[3,128]{1,0:T(4,128)S(1)} %get-tuple-element.17), channel_id=1, source_target_pairs={{0,8},{2,10},{4,12},{6,14},{8,0},{10,2},{12,4},{14,6},{1,9},{3,11}... | collective-permute-start | bytes 4616 | tf_op jit(solution)/shard_map/ppermute | solution.py:112
  32.8 3.6 %collective-permute-start.12 = (f32[3,128]{1,0:T(4,128)S(1)}, f32[3,128]{1,0:T(4,128)S(1)}, u32[]{:S(2)}, u32[]{:S(2)}) collective-permute-start(f32[3,128]{1,0:T(4,128)S(1)} %get-tuple-element.19), channel_id=1, source_target_pairs={{0,12},{2,14},{4,8},{6,10},{8,4},{10,6},{12,0},{14,2},{1,13},{3,15... | collective-permute-start | bytes 4616 | tf_op jit(solution)/shard_map/ppermute | solution.py:112
  36.3 1.2 %collective-permute-start.13 = (f32[3,128]{1,0:T(4,128)S(1)}, f32[3,128]{1,0:T(4,128)S(1)}, u32[]{:S(2)}, u32[]{:S(2)}) collective-permute-start(f32[3,128]{1,0:T(4,128)S(1)} %get-tuple-element.20), channel_id=1, source_target_pairs={{0,14},{2,12},{4,10},{6,8},{8,6},{10,4},{12,2},{14,0},{1,15},{3,13... | collective-permute-start | bytes 4616 | tf_op jit(solution)/shard_map/ppermute | solution.py:112
  37.5 0.0 collective-permute-done.10.refs_4_
  37.5 0.6 %collective-permute-done.11.refs_5_ = f32[3,128]{1,0:T(4,128)S(1)} collective-permute-done((f32[3,128]{1,0:T(4,128)S(1)}, f32[3,128]{1,0:T(4,128)S(1)}, u32[]{:S(2)}, u32[]{:S(2)}) %collective-permute-start.11) | collective-permute-done | bytes 1568 | tf_op jit(solution)/shard_map/ppermute | solution.py:112
  38.1 0.1 collective-permute-done.12.refs_6_
  38.2 4.4 %collective-permute-done.13.refs_7_ = f32[3,128]{1,0:T(4,128)S(1)} collective-permute-done((f32[3,128]{1,0:T(4,128)S(1)}, f32[3,128]{1,0:T(4,128)S(1)}, u32[]{:S(2)}, u32[]{:S(2)}) %collective-permute-start.13) | collective-permute-done | bytes 1568 | tf_op jit(solution)/shard_map/ppermute | solution.py:112
  42.7 0.5 %copy-done.12 = f32[3,128]{1,0:T(4,128)} copy-done((f32[3,128]{1,0:T(4,128)}, f32[3,128]{1,0:T(4,128)S(1)}, u32[]{:S(2)}) %copy-start.12) | copy-done | bytes 1560
  43.2 1.6 %shard_map.47 = f32[8,2,16,32]{3,2,1,0:T(8,128)} custom-call(s32[8]{0:T(128)} %copy-done.4, f32[3,128]{1,0:T(4,128)} %copy-done.3, f32[3,128]{1,0:T(4,128)} %copy-done.6, f32[3,128]{1,0:T(4,128)} %copy-done.7, f32[3,128]{1,0:T(4,128)} %copy-done.8, f32[3,128]{1,0:T(4,128)} %copy-done.9, f32[3,128]{1,0:T(4,128)} %copy-done.10, f32[3,128]{1,0:T(4,128)} %copy-done.11, ...), custom_call_target="tpu_custom_call" | custom-call | tf_op jit(solution)/shard_map/pallas_call | solution.py:103
  (25 shorter events, 0.0 us)
Async XLA Ops:
  0.0 11.3 %collective-permute-start.6 = (bf16[256,128]{1,0:T(8,128)(2,1)}, bf16[256,128]{1,0:T(8,128)(2,1)S(1)}, u32[]{:S(2)}, u32[]{:S(2)}) collective-permute-start(bf16[256,128]{1,0:T(8,128)(2,1)} %bitcast.5), channel_id=1, source_target_pairs={{0,14},{2,12},{4,10},{6,8},{8,6},{10,4},{12,2},{14,0},{1,15},{3,13... | collective-permute-start | bytes 196616 | tf_op jit(solution)/shard_map/ppermute | solution.py:112
  6.0 6.5 %collective-permute-start.5 = (bf16[256,128]{1,0:T(8,128)(2,1)}, bf16[256,128]{1,0:T(8,128)(2,1)S(1)}, u32[]{:S(2)}, u32[]{:S(2)}) collective-permute-start(bf16[256,128]{1,0:T(8,128)(2,1)} %bitcast.6), channel_id=1, source_target_pairs={{0,12},{2,14},{4,8},{6,10},{8,4},{10,6},{12,0},{14,2},{1,13},{3,15... | collective-permute-start | bytes 196616 | tf_op jit(solution)/shard_map/ppermute | solution.py:112
  6.2 9.6 %collective-permute-start.4 = (bf16[256,128]{1,0:T(8,128)(2,1)}, bf16[256,128]{1,0:T(8,128)(2,1)S(1)}, u32[]{:S(2)}, u32[]{:S(2)}) collective-permute-start(bf16[256,128]{1,0:T(8,128)(2,1)} %bitcast.7), channel_id=1, source_target_pairs={{0,10},{2,8},{4,14},{6,12},{8,2},{10,0},{12,6},{14,4},{1,11},{3,9}... | collective-permute-start | bytes 196616 | tf_op jit(solution)/shard_map/ppermute | solution.py:112
  7.0 10.4 %collective-permute-start.3 = (bf16[256,128]{1,0:T(8,128)(2,1)}, bf16[256,128]{1,0:T(8,128)(2,1)S(1)}, u32[]{:S(2)}, u32[]{:S(2)}) collective-permute-start(bf16[256,128]{1,0:T(8,128)(2,1)} %bitcast.8), channel_id=1, source_target_pairs={{0,8},{2,10},{4,12},{6,14},{8,0},{10,2},{12,4},{14,6},{1,9},{3,11}... | collective-permute-start | bytes 196616 | tf_op jit(solution)/shard_map/ppermute | solution.py:112
  8.9 8.5 %collective-permute-start.2 = (bf16[256,128]{1,0:T(8,128)(2,1)}, bf16[256,128]{1,0:T(8,128)(2,1)S(1)}, u32[]{:S(2)}, u32[]{:S(2)}) collective-permute-start(bf16[256,128]{1,0:T(8,128)(2,1)} %bitcast.9), channel_id=1, source_target_pairs={{0,6},{2,4},{4,2},{6,0},{8,14},{10,12},{12,10},{14,8},{1,7},{3,5},... | collective-permute-start | bytes 196616 | tf_op jit(solution)/shard_map/ppermute | solution.py:112
  11.3 6.5 %collective-permute-start.1 = (bf16[256,128]{1,0:T(8,128)(2,1)}, bf16[256,128]{1,0:T(8,128)(2,1)S(1)}, u32[]{:S(2)}, u32[]{:S(2)}) collective-permute-start(bf16[256,128]{1,0:T(8,128)(2,1)} %bitcast.10), channel_id=1, source_target_pairs={{0,4},{2,6},{4,0},{6,2},{8,12},{10,14},{12,8},{14,10},{1,5},{3,7},... | collective-permute-start | bytes 196616 | tf_op jit(solution)/shard_map/ppermute | solution.py:112
  12.4 5.4 %collective-permute-start = (bf16[256,128]{1,0:T(8,128)(2,1)}, bf16[256,128]{1,0:T(8,128)(2,1)S(1)}, u32[]{:S(2)}, u32[]{:S(2)}) collective-permute-start(bf16[256,128]{1,0:T(8,128)(2,1)} %bitcast.11), channel_id=1, source_target_pairs={{0,2},{2,0},{4,6},{6,4},{8,10},{10,8},{12,14},{14,12},{1,3},{3,1},... | collective-permute-start | bytes 196616 | tf_op jit(solution)/shard_map/ppermute | solution.py:112
  13.0 29.6 %copy-start.4 = (s32[8]{0:T(128)}, s32[8]{0:T(128)S(1)}, u32[]{:S(2)}) copy-start(s32[8]{0:T(128)S(1)} %iota_xor_fusion.owners_ref.shards_ref) | copy-start | bytes 100
  17.8 1.6 %copy-start = (bf16[128,64,128]{2,1,0:T(8,128)(2,1)S(1)}, bf16[128,64,128]{2,1,0:T(8,128)(2,1)}, u32[]{:S(2)}) copy-start(bf16[128,64,128]{2,1,0:T(8,128)(2,1)} %p_ref.1) | copy-start | bytes 6291460
  19.4 0.8 %copy-start.1 = (bf16[8,32,128]{2,1,0:T(8,128)(2,1)S(1)}, bf16[8,32,128]{2,1,0:T(8,128)(2,1)}, u32[]{:S(2)}) copy-start(bf16[8,32,128]{2,1,0:T(8,128)(2,1)} %param.4) | copy-start | bytes 196612
  20.3 0.7 %copy-start.2 = (s32[1,8,32]{2,1,0:T(8,128)S(1)}, s32[1,8,32]{2,1,0:T(8,128)}, u32[]{:S(2)}) copy-start(s32[1,8,32]{2,1,0:T(8,128)} %param.7) | copy-start | bytes 3076
  20.9 0.7 %copy-start.5 = (s32[128]{0:T(128)S(1)}, s32[128]{0:T(128)}, u32[]{:S(2)}) copy-start(s32[128]{0:T(128)} %len_ref.1) | copy-start | bytes 1540
  25.3 0.6 %copy-start.3 = (f32[3,128]{1,0:T(4,128)}, f32[3,128]{1,0:T(4,128)S(1)}, u32[]{:S(2)}) copy-start(f32[3,128]{1,0:T(4,128)S(1)} %get-tuple-element.13.refs_0_) | copy-start | bytes 4612
  25.9 6.9 %collective-permute-start.7 = (f32[3,128]{1,0:T(4,128)S(1)}, f32[3,128]{1,0:T(4,128)S(1)}, u32[]{:S(2)}, u32[]{:S(2)}) collective-permute-start(f32[3,128]{1,0:T(4,128)S(1)} %get-tuple-element.14), channel_id=1, source_target_pairs={{0,2},{2,0},{4,6},{6,4},{8,10},{10,8},{12,14},{14,12},{1,3},{3,1},... | collective-permute-start | bytes 4616 | tf_op jit(solution)/shard_map/ppermute | solution.py:112
  26.5 9.8 %collective-permute-start.8 = (f32[3,128]{1,0:T(4,128)S(1)}, f32[3,128]{1,0:T(4,128)S(1)}, u32[]{:S(2)}, u32[]{:S(2)}) collective-permute-start(f32[3,128]{1,0:T(4,128)S(1)} %get-tuple-element.15), channel_id=1, source_target_pairs={{0,4},{2,6},{4,0},{6,2},{8,12},{10,14},{12,8},{14,10},{1,5},{3,7},... | collective-permute-start | bytes 4616 | tf_op jit(solution)/shard_map/ppermute | solution.py:112
  27.8 9.6 %collective-permute-start.9 = (f32[3,128]{1,0:T(4,128)S(1)}, f32[3,128]{1,0:T(4,128)S(1)}, u32[]{:S(2)}, u32[]{:S(2)}) collective-permute-start(f32[3,128]{1,0:T(4,128)S(1)} %get-tuple-element.16), channel_id=1, source_target_pairs={{0,6},{2,4},{4,2},{6,0},{8,14},{10,12},{12,10},{14,8},{1,7},{3,5},... | collective-permute-start | bytes 4616 | tf_op jit(solution)/shard_map/ppermute | solution.py:112
  29.3 8.2 %collective-permute-start.10 = (f32[3,128]{1,0:T(4,128)S(1)}, f32[3,128]{1,0:T(4,128)S(1)}, u32[]{:S(2)}, u32[]{:S(2)}) collective-permute-start(f32[3,128]{1,0:T(4,128)S(1)} %get-tuple-element.17), channel_id=1, source_target_pairs={{0,8},{2,10},{4,12},{6,14},{8,0},{10,2},{12,4},{14,6},{1,9},{3,11}... | collective-permute-start | bytes 4616 | tf_op jit(solution)/shard_map/ppermute | solution.py:112
  32.8 5.4 %collective-permute-start.11 = (f32[3,128]{1,0:T(4,128)S(1)}, f32[3,128]{1,0:T(4,128)S(1)}, u32[]{:S(2)}, u32[]{:S(2)}) collective-permute-start(f32[3,128]{1,0:T(4,128)S(1)} %get-tuple-element.18), channel_id=1, source_target_pairs={{0,10},{2,8},{4,14},{6,12},{8,2},{10,0},{12,6},{14,4},{1,11},{3,9}... | collective-permute-start | bytes 4616 | tf_op jit(solution)/shard_map/ppermute | solution.py:112
  32.8 9.9 %copy-start.6 = (f32[3,128]{1,0:T(4,128)}, f32[3,128]{1,0:T(4,128)S(1)}, u32[]{:S(2)}) copy-start(f32[3,128]{1,0:T(4,128)S(1)} %collective-permute-done.7.refs_1_) | copy-start | bytes 4612
  32.8 5.4 %collective-permute-start.12 = (f32[3,128]{1,0:T(4,128)S(1)}, f32[3,128]{1,0:T(4,128)S(1)}, u32[]{:S(2)}, u32[]{:S(2)}) collective-permute-start(f32[3,128]{1,0:T(4,128)S(1)} %get-tuple-element.19), channel_id=1, source_target_pairs={{0,12},{2,14},{4,8},{6,10},{8,4},{10,6},{12,0},{14,2},{1,13},{3,15... | collective-permute-start | bytes 4616 | tf_op jit(solution)/shard_map/ppermute | solution.py:112
  36.3 6.3 %copy-start.7 = (f32[3,128]{1,0:T(4,128)}, f32[3,128]{1,0:T(4,128)S(1)}, u32[]{:S(2)}) copy-start(f32[3,128]{1,0:T(4,128)S(1)} %collective-permute-done.8.refs_2_) | copy-start | bytes 4612
  36.3 6.3 %collective-permute-start.13 = (f32[3,128]{1,0:T(4,128)S(1)}, f32[3,128]{1,0:T(4,128)S(1)}, u32[]{:S(2)}, u32[]{:S(2)}) collective-permute-start(f32[3,128]{1,0:T(4,128)S(1)} %get-tuple-element.20), channel_id=1, source_target_pairs={{0,14},{2,12},{4,10},{6,8},{8,6},{10,4},{12,2},{14,0},{1,15},{3,13... | collective-permute-start | bytes 4616 | tf_op jit(solution)/shard_map/ppermute | solution.py:112
  37.5 5.1 %copy-start.8 = (f32[3,128]{1,0:T(4,128)}, f32[3,128]{1,0:T(4,128)S(1)}, u32[]{:S(2)}) copy-start(f32[3,128]{1,0:T(4,128)S(1)} %collective-permute-done.9.refs_3_) | copy-start | bytes 4612
  37.5 5.1 %copy-start.9 = (f32[3,128]{1,0:T(4,128)}, f32[3,128]{1,0:T(4,128)S(1)}, u32[]{:S(2)}) copy-start(f32[3,128]{1,0:T(4,128)S(1)} %collective-permute-done.10.refs_4_) | copy-start | bytes 4612
  38.1 4.5 %copy-start.10 = (f32[3,128]{1,0:T(4,128)}, f32[3,128]{1,0:T(4,128)S(1)}, u32[]{:S(2)}) copy-start(f32[3,128]{1,0:T(4,128)S(1)} %collective-permute-done.11.refs_5_) | copy-start | bytes 4612
  38.2 4.4 %copy-start.11 = (f32[3,128]{1,0:T(4,128)}, f32[3,128]{1,0:T(4,128)S(1)}, u32[]{:S(2)}) copy-start(f32[3,128]{1,0:T(4,128)S(1)} %collective-permute-done.12.refs_6_) | copy-start | bytes 4612
  42.6 0.6 %copy-start.12 = (f32[3,128]{1,0:T(4,128)}, f32[3,128]{1,0:T(4,128)S(1)}, u32[]{:S(2)}) copy-start(f32[3,128]{1,0:T(4,128)S(1)} %collective-permute-done.13.refs_7_) | copy-start | bytes 4612

commit v3 on v2

v3 whole, which is shorter than its diff:
```python
import functools

import jax
import jax.numpy as jnp
from jax import lax
from jax.experimental import pallas as pl
from jax.experimental.pallas import tpu as pltpu
from jax.sharding import PartitionSpec as P

DIM = 128
QT = 32
PT = 64
QB = 2
QBD = 4
PBS = 16
KB = 32
LANES = 128
GROUP = 8


def prepare_kernel(cand_ref, len_ref, p_hbm, slots_ref, picks_ref, clean_ref, raw_ref, sems):
    rows = cand_ref.shape[0]
    shards = slots_ref.shape[0]
    count = p_hbm.shape[0]

    def fetch(g):
        part = pl.ds(g * GROUP, GROUP)
        return pltpu.make_async_copy(p_hbm.at[part], raw_ref.at[part], sems.at[g])

    for g in range(count // GROUP):
        fetch(g).start()

    cand = cand_ref[...]
    owner = cand // QBD
    block = cand - owner * QBD
    lane = lax.broadcasted_iota(jnp.int32, (rows, LANES), 1).astype(jnp.float32)
    sub = lax.broadcasted_iota(jnp.int32, (rows, LANES), 0)
    for o in range(shards):
        mine = owner == o
        named_here = jnp.sum(jnp.where(mine, 1.0, 0.0), axis=1, keepdims=True)
        upto = jnp.broadcast_to(named_here, (rows, LANES))
        step = 1
        while step < rows:
            upto = upto + jnp.where(sub >= step, pltpu.roll(upto, step, 0), 0.0)
            step *= 2
        slots_ref[o:o + 1, :] = jnp.sum(jnp.where(upto <= lane, 1.0, 0.0), axis=0, keepdims=True)
        named = jnp.max(jnp.where(mine, block, 0), axis=1, keepdims=True)
        picks_ref[o:o + 1, :] = jnp.broadcast_to(jnp.max(named, axis=0, keepdims=True), (1, LANES))

    u = lax.broadcasted_iota(jnp.int32, (PT, LANES), 0)
    for g in range(count // GROUP):
        fetch(g).wait()
        for p in range(g * GROUP, (g + 1) * GROUP):
            tokens = raw_ref[p].astype(jnp.float32)
            clean_ref[p] = jnp.where(u < len_ref[p], tokens, tokens[0:1]).astype(jnp.bfloat16)


def prepare(shards, candidates, lengths, passages):
    smem = pl.BlockSpec(memory_space=pltpu.SMEM)
    vmem = pl.BlockSpec(memory_space=pltpu.VMEM)
    return pl.pallas_call(
        prepare_kernel,
        out_shape=[
            jax.ShapeDtypeStruct((shards, LANES), jnp.float32),
            jax.ShapeDtypeStruct((shards, LANES), jnp.int32),
            jax.ShapeDtypeStruct(passages.shape, passages.dtype),
        ],
        in_specs=[vmem, smem, pl.BlockSpec(memory_space=pl.ANY)],
        out_specs=[vmem] * 3,
        scratch_shapes=[
            pltpu.VMEM(passages.shape, passages.dtype),
            pltpu.SemaphoreType.DMA((passages.shape[0] // GROUP,)),
        ],
        compiler_params=pltpu.CompilerParams(vmem_limit_bytes=24 * 1024 * 1024),
        cost_estimate=pl.CostEstimate(flops=passages.size, bytes_accessed=2 * passages.size, transcendentals=0),
    )(candidates, lengths, passages)


def score_kernel(paired, slots_ref, picks_ref, p_ref, *refs):
    some = len(refs) - 3
    q_refs, (out_ref, sel_ref, max_ref) = refs[:some], refs[some:]
    count = p_ref.shape[0]
    tokens = QB * QT
    me = lax.axis_index("psg") if paired else 0

    for k in range(some):
        pick = jnp.max(picks_ref[pl.ds(me ^ k, 1), :])
        sel_ref[k * tokens:(k + 1) * tokens, :] = q_refs[k][pl.ds(pick * tokens, tokens), :]

    sel = sel_ref[...]
    for g in range(count // GROUP):
        left = p_ref[g * GROUP:(g + 1) * GROUP].reshape(GROUP * PT, DIM)
        dots = lax.dot_general(left, sel, (((1,), (1,)), ((), ())), preferred_element_type=jnp.float32)
        best = jnp.max(dots.reshape(GROUP, PT, some * tokens), axis=1)
        max_ref[g * GROUP:(g + 1) * GROUP, :] = best

    best = max_ref[...]
    high = best.astype(jnp.bfloat16)
    rest = best - high.astype(jnp.float32)
    mid = rest.astype(jnp.bfloat16)
    low = (rest - mid.astype(jnp.float32)).astype(jnp.bfloat16)
    query = lax.broadcasted_iota(jnp.int32, (some * QB, some * tokens), 0)
    token = lax.broadcasted_iota(jnp.int32, (some * QB, some * tokens), 1)
    ones = jnp.where(token // QT == query, 1.0, 0.0).astype(jnp.bfloat16)
    total = jnp.zeros((some * QB, count), jnp.float32)
    for part in (low, mid, high):
        total = total + lax.dot_general(ones, part, (((1,), (1,)), ((), ())), preferred_element_type=jnp.float32)
    total = total * (1.0 / QT)
    for k in range(some):
        out_ref[me ^ k, 0:QB, :] = total[k * QB:(k + 1) * QB]
        out_ref[k, QB:QB + 1, :] = slots_ref[k:k + 1, :]


def score(paired, slots, picks, passages, blocks):
    some = len(blocks)
    count = passages.shape[0]
    vmem = pl.BlockSpec(memory_space=pltpu.VMEM)
    return pl.pallas_call(
        functools.partial(score_kernel, paired),
        out_shape=jax.ShapeDtypeStruct((some, QB + 1, LANES), jnp.float32),
        in_specs=[vmem] * (3 + some),
        out_specs=vmem,
        scratch_shapes=[
            pltpu.VMEM((some * QB * QT, DIM), jnp.bfloat16),
            pltpu.VMEM((count, some * QB * QT), jnp.float32),
        ],
        compiler_params=pltpu.CompilerParams(vmem_limit_bytes=40 * 1024 * 1024),
    )(slots, picks, passages, *blocks)


def place_kernel(in_ref, out_ref):
    slots = out_ref.shape[-1]
    m = lax.broadcasted_iota(jnp.int32, (PBS, LANES), 0)
    for j in range(in_ref.shape[0]):
        row = in_ref[j, QB:QB + 1, :].astype(jnp.int32)
        where = jnp.minimum(row * PBS, LANES - PBS) + m
        for i in range(QB):
            tile = jnp.broadcast_to(in_ref[j, i:i + 1, :], (PBS, LANES))
            out_ref[j, i] = jnp.take_along_axis(tile, where, axis=1)[:, :slots]


def place(tiles, slots):
    vmem = pl.BlockSpec(memory_space=pltpu.VMEM)
    return pl.pallas_call(
        place_kernel,
        out_shape=jax.ShapeDtypeStruct((tiles.shape[0], QB, PBS, slots), jnp.float32),
        in_specs=[vmem],
        out_specs=vmem,
    )(tiles)


def relay(own, shards):
    blocks = {0: own}

    def swap(source, k):
        blocks[source ^ k] = lax.ppermute(blocks[source], "psg", [(j, j ^ k) for j in range(shards)])

    for source, k in ((0, 4), (0, 2), (0, 1), (4, 2), (1, 2), (4, 1), (6, 1)):
        if source ^ k < shards:
            swap(source, k)
    return [blocks[k] for k in range(shards)]


def per_device(queries, passages, lengths, candidates):
    shards = lax.axis_size("psg")
    rows = passages.shape[0] // PBS
    slots = rows * KB // shards
    own = queries.reshape(QBD * QB * QT, DIM)
    slot_rows, picks, clean = prepare(shards, candidates.reshape(rows, KB), lengths, passages)
    if shards in (2, 4, 8):
        tiles = score(True, slot_rows, picks, clean, relay(own, shards))
    else:
        gathered = lax.all_gather(own, "psg", axis=0)
        some = 8

        def score_some(items):
            some_rows, some_picks, some_blocks = items
            return score(False, some_rows, some_picks, clean, [some_blocks[k] for k in range(some)])

        parts = shards // some
        tiles = lax.map(score_some, (
            slot_rows.reshape(parts, some, LANES),
            picks.reshape(parts, some, LANES),
            gathered.reshape(parts, some, *own.shape),
        )).reshape(shards, QB + 1, LANES)
    received = lax.all_to_all(tiles, "psg", split_axis=0, concat_axis=0, tiled=True)
    return place(received, slots).transpose(0, 3, 1, 2)[None]


def solution(mesh):
    return jax.shard_map(
        per_device,
        mesh=mesh,
        in_specs=(
            P(("grp", "psg", "qry"), None, None),
            P(("grp", "psg"), None, None),
            P(("grp", "psg")),
            P("qry", ("grp", "psg"), None),
        ),
        out_specs=P(("grp", "psg", "qry"), None, None, None, None),
        check_vma=False,
    )
```

time: 45.1 us -> 37.2 us (0.82)
  starting transfers between devices: 24.2 us -> 11.3 us
  blocking collectives: 0 us -> 11.1 us
  waiting for transfers between devices: 10.3 us -> 2.94 us
  Pallas kernels: 5.28 us -> 8.59 us
  local copies, waits for them, and re-layouts: 4.91 us -> 2.94 us
    ppermute x14 -> x7, starting transfers between devices: 24.2 us -> 11.3 us  [swap(): lax.ppermute(blocks[source], 'psg', [(j, j ^ k) for j in range(shards)])]
    all_to_all x0 -> x1, blocking collectives: none -> 11.1 us  [per_device(): lax.all_to_all(tiles, 'psg', split_axis=0, concat_axis=0, tiled=True)]
    ppermute x14 -> x7, waiting for transfers between devices: 10.3 us -> 2.94 us  [swap(): lax.ppermute(blocks[source], 'psg', [(j, j ^ k) for j in range(shards)])]
    pallas_call x2 -> x3, Pallas kernels: 5.28 us -> 8.59 us  [the longest x1 4.13 us: prepare(): pl.pallas_call(prepare_kernel, out_shape=[jax.ShapeDtypeStruct((shards, L...]
    unnamed x26 -> x8, local copies, waits for them, and re-layouts: 4.91 us -> 2.94 us
  transfers between devices with their start and end apart: 14 -> 7, of which waited for: 7 -> 2; matrix products, arithmetic and copies ran while one was open for 0% -> 0% of each run, Pallas kernels for 0% -> 11%
where the time goes in v3:
time: 37.2 us; the launch traced here: 36.9 us
  starting transfers between devices  11.3 us (30%)
  blocking collectives  11.1 us (30%)
  Pallas kernels  8.59 us (23%)
  waiting for transfers between devices  2.94 us (8%)
  local copies, waits for them, and re-layouts  2.94 us (8%)
    ppermute x7, starting transfers between devices, swap(): lax.ppermute(blocks[source], 'psg', [(j, j ^ k) for j in range(shards)])  11.3 us
    all_to_all x1, blocking collectives, per_device(): lax.all_to_all(tiles, 'psg', split_axis=0, concat_axis=0, tiled=True)  11.1 us
    pallas_call x1, Pallas kernels, prepare(): pl.pallas_call(prepare_kernel, out_shape=[jax.ShapeDtypeStruct((shards, L...  4.13 us
    ppermute x7, waiting for transfers between devices, swap(): lax.ppermute(blocks[source], 'psg', [(j, j ^ k) for j in range(shards)])  2.94 us
    unnamed x8, local copies, waits for them, and re-layouts  2.94 us
    pallas_call x1, Pallas kernels, score(): pl.pallas_call(functools.partial(score_kernel, paired), out_shape=jax.Sha...  2.93 us
    pallas_call x1, Pallas kernels, place(): pl.pallas_call(place_kernel, out_shape=jax.ShapeDtypeStruct((tiles.shape[...  1.52 us
  transfers between devices with their start and end apart: 7, of which 2 were waited for; matrix products, arithmetic and copies ran while one was open for 0% of the time, Pallas kernels for 11%

profile of v3, /device:TPU:0, one launch (start us, length us, event | category | flops | bytes accessed | tf_op | source)
XLA Modules:
  0.0 36.9 jit_solution(10769727043131819229)
XLA Ops:
  0.0 4.0 %collective-permute-start.3 = (bf16[256,128]{1,0:T(8,128)(2,1)}, bf16[256,128]{1,0:T(8,128)(2,1)S(1)}, u32[]{:S(2)}, u32[]{:S(2)}) collective-permute-start(bf16[256,128]{1,0:T(8,128)(2,1)} %bitcast.5), channel_id=1, source_target_pairs={{0,8},{2,10},{4,12},{6,14},{8,0},{10,2},{12,4},{14,6},{1,9},{3,11}... | collective-permute-start | bytes 196616 | tf_op jit(solution)/shard_map/ppermute | solution.py:156
  4.0 1.5 %collective-permute-start = (bf16[256,128]{1,0:T(8,128)(2,1)}, bf16[256,128]{1,0:T(8,128)(2,1)S(1)}, u32[]{:S(2)}, u32[]{:S(2)}) collective-permute-start(bf16[256,128]{1,0:T(8,128)(2,1)} %bitcast.6), channel_id=1, source_target_pairs={{0,2},{2,0},{4,6},{6,4},{8,10},{10,8},{12,14},{14,12},{1,3},{3,1},... | collective-permute-start | bytes 196616 | tf_op jit(solution)/shard_map/ppermute | solution.py:156
  5.5 2.4 %collective-permute-done.3.refs_4_ = bf16[256,128]{1,0:T(8,128)(2,1)S(1)} collective-permute-done((bf16[256,128]{1,0:T(8,128)(2,1)}, bf16[256,128]{1,0:T(8,128)(2,1)S(1)}, u32[]{:S(2)}, u32[]{:S(2)}) %collective-permute-start.3) | collective-permute-done | bytes 65568 | tf_op jit(solution)/shard_map/ppermute | solution.py:156
  7.9 0.7 %collective-permute-start.5 = (bf16[256,128]{1,0:T(8,128)(2,1)S(1)}, bf16[256,128]{1,0:T(8,128)(2,1)S(1)}, u32[]{:S(2)}, u32[]{:S(2)}) collective-permute-start(bf16[256,128]{1,0:T(8,128)(2,1)S(1)} %collective-permute-done.3.refs_4_), channel_id=1, source_target_pairs={{0,4},{2,6},{4,0},{6,2},{8,12},{10,14},{12,8},{14,10},{1,5},{3,7},... | collective-permute-start | bytes 196616 | tf_op jit(solution)/shard_map/ppermute | solution.py:156
  8.6 1.3 %collective-permute-start.1 = (bf16[256,128]{1,0:T(8,128)(2,1)}, bf16[256,128]{1,0:T(8,128)(2,1)S(1)}, u32[]{:S(2)}, u32[]{:S(2)}) collective-permute-start(bf16[256,128]{1,0:T(8,128)(2,1)} %bitcast.7), channel_id=1, source_target_pairs={{0,4},{2,6},{4,0},{6,2},{8,12},{10,14},{12,8},{14,10},{1,5},{3,7},... | collective-permute-start | bytes 196616 | tf_op jit(solution)/shard_map/ppermute | solution.py:156
  9.9 1.7 %collective-permute-start.4 = (bf16[256,128]{1,0:T(8,128)(2,1)S(1)}, bf16[256,128]{1,0:T(8,128)(2,1)S(1)}, u32[]{:S(2)}, u32[]{:S(2)}) collective-permute-start(bf16[256,128]{1,0:T(8,128)(2,1)S(1)} %collective-permute-done.3.refs_4_), channel_id=1, source_target_pairs={{0,2},{2,0},{4,6},{6,4},{8,10},{10,8},{12,14},{14,12},{1,3},{3,1},... | collective-permute-start | bytes 196616 | tf_op jit(solution)/shard_map/ppermute | solution.py:156
  11.6 0.0 collective-permute-done.refs_1_
  11.6 0.5 %collective-permute-start.2 = (bf16[256,128]{1,0:T(8,128)(2,1)S(1)}, bf16[256,128]{1,0:T(8,128)(2,1)S(1)}, u32[]{:S(2)}, u32[]{:S(2)}) collective-permute-start(bf16[256,128]{1,0:T(8,128)(2,1)S(1)} %collective-permute-done.refs_1_), channel_id=1, source_target_pairs={{0,4},{2,6},{4,0},{6,2},{8,12},{10,14},{12,8},{14,10},{1,5},{3,7},... | collective-permute-start | bytes 196616 | tf_op jit(solution)/shard_map/ppermute | solution.py:156
  12.1 0.6 %collective-permute-done.5.refs_6_ = bf16[256,128]{1,0:T(8,128)(2,1)S(1)} collective-permute-done((bf16[256,128]{1,0:T(8,128)(2,1)S(1)}, bf16[256,128]{1,0:T(8,128)(2,1)S(1)}, u32[]{:S(2)}, u32[]{:S(2)}) %collective-permute-start.5) | collective-permute-done | bytes 65568 | tf_op jit(solution)/shard_map/ppermute | solution.py:156
  12.7 1.6 %collective-permute-start.6 = (bf16[256,128]{1,0:T(8,128)(2,1)S(1)}, bf16[256,128]{1,0:T(8,128)(2,1)S(1)}, u32[]{:S(2)}, u32[]{:S(2)}) collective-permute-start(bf16[256,128]{1,0:T(8,128)(2,1)S(1)} %collective-permute-done.5.refs_6_), channel_id=1, source_target_pairs={{0,2},{2,0},{4,6},{6,4},{8,10},{10,8},{12,14},{14,12},{1,3},{3,1},... | collective-permute-start | bytes 196616 | tf_op jit(solution)/shard_map/ppermute | solution.py:156
  14.2 0.0 copy-start
  14.2 1.6 %copy-done = bf16[128,64,128]{2,1,0:T(8,128)(2,1)S(1)} copy-done((bf16[128,64,128]{2,1,0:T(8,128)(2,1)S(1)}, bf16[128,64,128]{2,1,0:T(8,128)(2,1)}, u32[]{:S(2)}) %copy-start) | copy-done | bytes 2097176
  15.8 0.0 copy-start.2
  15.8 0.7 %copy-done.2 = s32[1,8,32]{2,1,0:T(8,128)S(1)} copy-done((s32[1,8,32]{2,1,0:T(8,128)S(1)}, s32[1,8,32]{2,1,0:T(8,128)}, u32[]{:S(2)}) %copy-start.2) | copy-done | bytes 1048
  16.5 0.0 copy-start.3
  16.5 0.7 %copy-done.3 = s32[128]{0:T(128)S(1)} copy-done((s32[128]{0:T(128)S(1)}, s32[128]{0:T(128)}, u32[]{:S(2)}) %copy-start.3) | copy-done | bytes 536
  17.2 0.0 copy-start.1
  17.2 4.1 %shard_map.46 = (f32[8,128]{1,0:T(8,128)S(1)}, s32[8,128]{1,0:T(8,128)S(1)}, bf16[128,64,128]{2,1,0:T(8,128)(2,1)S(1)}) custom-call(s32[8,32]{1,0:T(8,128)S(1)} %bitcast.9, s32[128]{0:T(128)S(1)} %copy-done.3, bf16[128,64,128]{2,1,0:T(8,128)(2,1)S(1)} %copy-done), custom_call_target="tpu_custom_call" | custom-call | flops 1048576 | bytes 2097152 | tf_op jit(solution)/shard_map/pallas_call | solution.py:61
  21.3 0.0 collective-permute-done.1.refs_2_
  21.3 0.0 collective-permute-done.4.refs_5_
  21.3 0.0 collective-permute-done.2.refs_3_
  21.3 0.0 collective-permute-done.6.refs_7_
  21.3 0.0 copy-done.1
  21.3 2.9 %shard_map.47 = f32[8,3,128]{2,1,0:T(4,128)S(1)} custom-call(f32[8,128]{1,0:T(8,128)S(1)} %get-tuple-element.8.slots_ref, s32[8,128]{1,0:T(8,128)S(1)} %get-tuple-element.9.picks_ref, bf16[128,64,128]{2,1,0:T(8,128)(2,1)S(1)} %get-tuple-element.10.p_ref, bf16[256,128]{1,0:T(8,128)(2,1)S(1)} %bitcast.8, bf16[256,128]{1,0:T(8,128)(2,1)S(1)} %collective-permute-done.refs_1_, ...), custom_call_target="tpu_custom_call" | custom-call | tf_op jit(solution)/shard_map/pallas_call | solution.py:118
  24.3 11.1 %all_to_all.5.in_ref = f32[8,3,128]{2,1,0:T(4,128)} all-to-all(f32[8,3,128]{2,1,0:T(4,128)S(1)} %shard_map.47), channel_id=1, replica_groups=mesh['grp'=2,'psg'=8,'qry'=2] {'psg'}, dimensions={0} | all-to-all | bytes 24576 | tf_op jit(solution)/shard_map/all_to_all | solution.py:186
  35.3 1.5 %shard_map.48 = f32[8,2,16,32]{3,2,1,0:T(8,128)} custom-call(f32[8,3,128]{2,1,0:T(4,128)} %all_to_all.5.in_ref), custom_call_target="tpu_custom_call" | custom-call | tf_op jit(solution)/shard_map/pallas_call | solution.py:144
Async XLA Ops:
  0.0 7.9 %collective-permute-start.3 = (bf16[256,128]{1,0:T(8,128)(2,1)}, bf16[256,128]{1,0:T(8,128)(2,1)S(1)}, u32[]{:S(2)}, u32[]{:S(2)}) collective-permute-start(bf16[256,128]{1,0:T(8,128)(2,1)} %bitcast.5), channel_id=1, source_target_pairs={{0,8},{2,10},{4,12},{6,14},{8,0},{10,2},{12,4},{14,6},{1,9},{3,11}... | collective-permute-start | bytes 196616 | tf_op jit(solution)/shard_map/ppermute | solution.py:156
  4.0 7.6 %collective-permute-start = (bf16[256,128]{1,0:T(8,128)(2,1)}, bf16[256,128]{1,0:T(8,128)(2,1)S(1)}, u32[]{:S(2)}, u32[]{:S(2)}) collective-permute-start(bf16[256,128]{1,0:T(8,128)(2,1)} %bitcast.6), channel_id=1, source_target_pairs={{0,2},{2,0},{4,6},{6,4},{8,10},{10,8},{12,14},{14,12},{1,3},{3,1},... | collective-permute-start | bytes 196616 | tf_op jit(solution)/shard_map/ppermute | solution.py:156
  7.9 4.8 %collective-permute-start.5 = (bf16[256,128]{1,0:T(8,128)(2,1)S(1)}, bf16[256,128]{1,0:T(8,128)(2,1)S(1)}, u32[]{:S(2)}, u32[]{:S(2)}) collective-permute-start(bf16[256,128]{1,0:T(8,128)(2,1)S(1)} %collective-permute-done.3.refs_4_), channel_id=1, source_target_pairs={{0,4},{2,6},{4,0},{6,2},{8,12},{10,14},{12,8},{14,10},{1,5},{3,7},... | collective-permute-start | bytes 196616 | tf_op jit(solution)/shard_map/ppermute | solution.py:156
  8.6 12.7 %collective-permute-start.1 = (bf16[256,128]{1,0:T(8,128)(2,1)}, bf16[256,128]{1,0:T(8,128)(2,1)S(1)}, u32[]{:S(2)}, u32[]{:S(2)}) collective-permute-start(bf16[256,128]{1,0:T(8,128)(2,1)} %bitcast.7), channel_id=1, source_target_pairs={{0,4},{2,6},{4,0},{6,2},{8,12},{10,14},{12,8},{14,10},{1,5},{3,7},... | collective-permute-start | bytes 196616 | tf_op jit(solution)/shard_map/ppermute | solution.py:156
  9.9 11.4 %collective-permute-start.4 = (bf16[256,128]{1,0:T(8,128)(2,1)S(1)}, bf16[256,128]{1,0:T(8,128)(2,1)S(1)}, u32[]{:S(2)}, u32[]{:S(2)}) collective-permute-start(bf16[256,128]{1,0:T(8,128)(2,1)S(1)} %collective-permute-done.3.refs_4_), channel_id=1, source_target_pairs={{0,2},{2,0},{4,6},{6,4},{8,10},{10,8},{12,14},{14,12},{1,3},{3,1},... | collective-permute-start | bytes 196616 | tf_op jit(solution)/shard_map/ppermute | solution.py:156
  11.6 9.7 %collective-permute-start.2 = (bf16[256,128]{1,0:T(8,128)(2,1)S(1)}, bf16[256,128]{1,0:T(8,128)(2,1)S(1)}, u32[]{:S(2)}, u32[]{:S(2)}) collective-permute-start(bf16[256,128]{1,0:T(8,128)(2,1)S(1)} %collective-permute-done.refs_1_), channel_id=1, source_target_pairs={{0,4},{2,6},{4,0},{6,2},{8,12},{10,14},{12,8},{14,10},{1,5},{3,7},... | collective-permute-start | bytes 196616 | tf_op jit(solution)/shard_map/ppermute | solution.py:156
  12.7 8.7 %collective-permute-start.6 = (bf16[256,128]{1,0:T(8,128)(2,1)S(1)}, bf16[256,128]{1,0:T(8,128)(2,1)S(1)}, u32[]{:S(2)}, u32[]{:S(2)}) collective-permute-start(bf16[256,128]{1,0:T(8,128)(2,1)S(1)} %collective-permute-done.5.refs_6_), channel_id=1, source_target_pairs={{0,2},{2,0},{4,6},{6,4},{8,10},{10,8},{12,14},{14,12},{1,3},{3,1},... | collective-permute-start | bytes 196616 | tf_op jit(solution)/shard_map/ppermute | solution.py:156
  14.2 1.6 %copy-start = (bf16[128,64,128]{2,1,0:T(8,128)(2,1)S(1)}, bf16[128,64,128]{2,1,0:T(8,128)(2,1)}, u32[]{:S(2)}) copy-start(bf16[128,64,128]{2,1,0:T(8,128)(2,1)} %p_hbm.1) | copy-start | bytes 6291460
  15.8 0.7 %copy-start.2 = (s32[1,8,32]{2,1,0:T(8,128)S(1)}, s32[1,8,32]{2,1,0:T(8,128)}, u32[]{:S(2)}) copy-start(s32[1,8,32]{2,1,0:T(8,128)} %param.7) | copy-start | bytes 3076
  16.5 0.7 %copy-start.3 = (s32[128]{0:T(128)S(1)}, s32[128]{0:T(128)}, u32[]{:S(2)}) copy-start(s32[128]{0:T(128)} %len_ref.1) | copy-start | bytes 1540
  17.2 4.2 %copy-start.1 = (bf16[8,32,128]{2,1,0:T(8,128)(2,1)S(1)}, bf16[8,32,128]{2,1,0:T(8,128)(2,1)}, u32[]{:S(2)}) copy-start(bf16[8,32,128]{2,1,0:T(8,128)(2,1)} %param.4) | copy-start | bytes 196612

commit v4 on v3

--- a/solution.py
+++ b/solution.py
@@ -18,18 +18,23 @@
 GROUP = 8
 
 
-def prepare_kernel(cand_ref, len_ref, p_hbm, slots_ref, picks_ref, clean_ref, raw_ref, sems):
+def prepare_kernel(cand_hbm, len_hbm, p_hbm, slots_ref, picks_ref, clean_ref, cand_ref, len_ref, raw_ref, sems):
     rows = cand_ref.shape[0]
     shards = slots_ref.shape[0]
-    count = p_hbm.shape[0]
+    groups = p_hbm.shape[0] // GROUP
 
     def fetch(g):
         part = pl.ds(g * GROUP, GROUP)
         return pltpu.make_async_copy(p_hbm.at[part], raw_ref.at[part], sems.at[g])
 
-    for g in range(count // GROUP):
+    fetch_cand = pltpu.make_async_copy(cand_hbm, cand_ref, sems.at[groups])
+    fetch_len = pltpu.make_async_copy(len_hbm, len_ref, sems.at[groups + 1])
+    fetch_cand.start()
+    fetch_len.start()
+    for g in range(groups):
         fetch(g).start()
 
+    fetch_cand.wait()
     cand = cand_ref[...]
     owner = cand // QBD
     block = cand - owner * QBD
@@ -47,16 +52,20 @@
         named = jnp.max(jnp.where(mine, block, 0), axis=1, keepdims=True)
         picks_ref[o:o + 1, :] = jnp.broadcast_to(jnp.max(named, axis=0, keepdims=True), (1, LANES))
 
+    fetch_len.wait()
     u = lax.broadcasted_iota(jnp.int32, (PT, LANES), 0)
-    for g in range(count // GROUP):
+
+    @pl.loop(0, groups)
+    def _(g):
         fetch(g).wait()
-        for p in range(g * GROUP, (g + 1) * GROUP):
+        for i in range(GROUP):
+            p = g * GROUP + i
             tokens = raw_ref[p].astype(jnp.float32)
             clean_ref[p] = jnp.where(u < len_ref[p], tokens, tokens[0:1]).astype(jnp.bfloat16)
 
 
 def prepare(shards, candidates, lengths, passages):
-    smem = pl.BlockSpec(memory_space=pltpu.SMEM)
+    hbm = pl.BlockSpec(memory_space=pltpu.HBM)
     vmem = pl.BlockSpec(memory_space=pltpu.VMEM)
     return pl.pallas_call(
         prepare_kernel,
@@ -65,27 +74,30 @@
             jax.ShapeDtypeStruct((shards, LANES), jnp.int32),
             jax.ShapeDtypeStruct(passages.shape, passages.dtype),
         ],
-        in_specs=[vmem, smem, pl.BlockSpec(memory_space=pl.ANY)],
+        in_specs=[hbm] * 3,
         out_specs=[vmem] * 3,
         scratch_shapes=[
+            pltpu.VMEM(candidates.shape, candidates.dtype),
+            pltpu.SMEM(lengths.shape, lengths.dtype),
             pltpu.VMEM(passages.shape, passages.dtype),
-            pltpu.SemaphoreType.DMA((passages.shape[0] // GROUP,)),
+            pltpu.SemaphoreType.DMA((passages.shape[0] // GROUP + 2,)),
         ],
         compiler_params=pltpu.CompilerParams(vmem_limit_bytes=24 * 1024 * 1024),
         cost_estimate=pl.CostEstimate(flops=passages.size, bytes_accessed=2 * passages.size, transcendentals=0),
     )(candidates, lengths, passages)
 
 
-def score_kernel(paired, slots_ref, picks_ref, p_ref, *refs):
-    some = len(refs) - 3
-    q_refs, (out_ref, sel_ref, max_ref) = refs[:some], refs[some:]
+def score_kernel(partners, shards, slots_ref, picks_ref, p_ref, *refs):
+    some = len(partners)
+    q_refs, (out_ref, sel_ref, max_ref) = refs[:some], refs[-3:]
+    earlier_refs = refs[some:-3]
     count = p_ref.shape[0]
     tokens = QB * QT
-    me = lax.axis_index("psg") if paired else 0
-
-    for k in range(some):
+    me = lax.axis_index("psg") if some < shards or len(earlier_refs) else 0
+
+    for n, k in enumerate(partners):
         pick = jnp.max(picks_ref[pl.ds(me ^ k, 1), :])
-        sel_ref[k * tokens:(k + 1) * tokens, :] = q_refs[k][pl.ds(pick * tokens, tokens), :]
+        sel_ref[n * tokens:(n + 1) * tokens, :] = q_refs[n][pl.ds(pick * tokens, tokens), :]
 
     sel = sel_ref[...]
     for g in range(count // GROUP):
@@ -106,26 +118,32 @@
     for part in (low, mid, high):
         total = total + lax.dot_general(ones, part, (((1,), (1,)), ((), ())), preferred_element_type=jnp.float32)
     total = total * (1.0 / QT)
-    for k in range(some):
-        out_ref[me ^ k, 0:QB, :] = total[k * QB:(k + 1) * QB]
-        out_ref[k, QB:QB + 1, :] = slots_ref[k:k + 1, :]
-
-
-def score(paired, slots, picks, passages, blocks):
+    if earlier_refs:
+        out_ref[...] = earlier_refs[0][...]
+    for n, k in enumerate(partners):
+        out_ref[me ^ k, 0:QB, :] = total[n * QB:(n + 1) * QB]
+        out_ref[me ^ k, QB:QB + 1, :] = slots_ref[pl.ds(me ^ k, 1), :]
+
+
+def score(partners, slots, picks, passages, blocks, *earlier):
     some = len(blocks)
+    shards = slots.shape[0]
     count = passages.shape[0]
     vmem = pl.BlockSpec(memory_space=pltpu.VMEM)
     return pl.pallas_call(
-        functools.partial(score_kernel, paired),
-        out_shape=jax.ShapeDtypeStruct((some, QB + 1, LANES), jnp.float32),
-        in_specs=[vmem] * (3 + some),
+        functools.partial(score_kernel, partners, shards),
+        out_shape=jax.ShapeDtypeStruct((shards, QB + 1, LANES), jnp.float32),
+        in_specs=[vmem] * (3 + some + len(earlier)),
         out_specs=vmem,
         scratch_shapes=[
             pltpu.VMEM((some * QB * QT, DIM), jnp.bfloat16),
             pltpu.VMEM((count, some * QB * QT), jnp.float32),
         ],
-        compiler_params=pltpu.CompilerParams(vmem_limit_bytes=40 * 1024 * 1024),
-    )(slots, picks, passages, *blocks)
+        compiler_params=pltpu.CompilerParams(vmem_limit_bytes=32 * 1024 * 1024),
+        cost_estimate=pl.CostEstimate(
+            flops=2 * passages.size * some * QB * QT, bytes_accessed=2 * passages.size, transcendentals=0
+        ),
+    )(slots, picks, passages, *blocks, *earlier)
 
 
 def place_kernel(in_ref, out_ref):
@@ -149,16 +167,21 @@
     )(tiles)
 
 
-def relay(own, shards):
-    blocks = {0: own}
-
-    def swap(source, k):
-        blocks[source ^ k] = lax.ppermute(blocks[source], "psg", [(j, j ^ k) for j in range(shards)])
-
-    for source, k in ((0, 4), (0, 2), (0, 1), (4, 2), (1, 2), (4, 1), (6, 1)):
-        if source ^ k < shards:
-            swap(source, k)
-    return [blocks[k] for k in range(shards)]
+def relay_and_score(own, shards, candidates, lengths, passages):
+    def swap(x, k):
+        return lax.ppermute(x, "psg", [(j, j ^ k) for j in range(shards)])
+
+    queries = {0: own, 4: swap(own, 4), 1: swap(own, 1), 2: swap(own, 2)}
+    slots, picks, clean = prepare(shards, candidates, lengths, passages)
+    queries[4], queries[1], clean = lax.optimization_barrier((queries[4], queries[1], clean))
+    queries[6] = swap(queries[4], 2)
+    queries[5] = swap(queries[4], 1)
+    queries[3] = swap(queries[1], 2)
+    first, second = (0, 1, 2, 4), (3, 5, 6, 7)
+    tiles = score(first, slots, picks, clean, [queries[k] for k in first])
+    queries[6], tiles = lax.optimization_barrier((queries[6], tiles))
+    queries[7] = swap(queries[6], 1)
+    return score(second, slots, picks, clean, [queries[k] for k in second], tiles)
 
 
 def per_device(queries, passages, lengths, candidates):
@@ -166,16 +189,17 @@
     rows = passages.shape[0] // PBS
     slots = rows * KB // shards
     own = queries.reshape(QBD * QB * QT, DIM)
-    slot_rows, picks, clean = prepare(shards, candidates.reshape(rows, KB), lengths, passages)
-    if shards in (2, 4, 8):
-        tiles = score(True, slot_rows, picks, clean, relay(own, shards))
+    candidates = candidates.reshape(rows, KB)
+    if shards == 8:
+        tiles = relay_and_score(own, shards, candidates, lengths, passages)
     else:
+        slot_rows, picks, clean = prepare(shards, candidates, lengths, passages)
         gathered = lax.all_gather(own, "psg", axis=0)
         some = 8
 
         def score_some(items):
             some_rows, some_picks, some_blocks = items
-            return score(False, some_rows, some_picks, clean, [some_blocks[k] for k in range(some)])
+            return score(range(some), some_rows, some_picks, clean, [some_blocks[k] for k in range(some)])
 
         parts = shards // some
         tiles = lax.map(score_some, (

time: 37.2 us -> 35.5 us (0.954)
  blocking collectives: 11.1 us -> 9.64 us
    all_to_all x1, blocking collectives: 11.1 us -> 9.64 us  [per_device(): lax.all_to_all(tiles, 'psg', split_axis=0, concat_axis=0, tiled=True)]
    pallas_call x1, Pallas kernels: 4.13 us -> 3.62 us  [prepare(): pl.pallas_call(prepare_kernel, out_shape=[jax.ShapeDtypeStruct((shards, L...]
    pallas_call x1 -> x2, Pallas kernels: 2.93 us -> 3.34 us  [score(): pl.pallas_call(functools.partial(score_kernel, partners, shards), out_sha...]
  transfers between devices with their start and end apart: 7 -> 7, of which waited for: 2 -> 1; matrix products, arithmetic and copies ran while one was open for 0% -> 0% of each run, Pallas kernels for 11% -> 15%
where the time goes in v4:
time: 35.5 us; the launch traced here: 35.2 us
  starting transfers between devices  11.3 us (32%)
  blocking collectives  9.64 us (27%)
  Pallas kernels  8.49 us (24%)
  local copies, waits for them, and re-layouts  2.94 us (8%)
  waiting for transfers between devices  2.8 us (8%)
    ppermute x7, starting transfers between devices, swap(): return lax.ppermute(x, 'psg', [(j, j ^ k) for j in range(shards)])  11.3 us
    all_to_all x1, blocking collectives, per_device(): lax.all_to_all(tiles, 'psg', split_axis=0, concat_axis=0, tiled=True)  9.64 us
    pallas_call x1, Pallas kernels, prepare(): pl.pallas_call(prepare_kernel, out_shape=[jax.ShapeDtypeStruct((shards, L...  3.62 us
    pallas_call x2, Pallas kernels, score(): pl.pallas_call(functools.partial(score_kernel, partners, shards), out_sha...  3.34 us
    unnamed x8, local copies, waits for them, and re-layouts  2.94 us
    ppermute x7, waiting for transfers between devices, swap(): return lax.ppermute(x, 'psg', [(j, j ^ k) for j in range(shards)])  2.8 us
    pallas_call x1, Pallas kernels, place(): pl.pallas_call(place_kernel, out_shape=jax.ShapeDtypeStruct((tiles.shape[...  1.52 us
  transfers between devices with their start and end apart: 7, of which 1 were waited for; matrix products, arithmetic and copies ran while one was open for 0% of the time, Pallas kernels for 15%

profile of v4, /device:TPU:0, one launch (start us, length us, event | category | flops | bytes accessed | tf_op | source)
XLA Modules:
  0.0 35.2 jit_solution(5815315520124126737)
XLA Ops:
  0.0 2.9 %collective-permute-start.1 = (bf16[256,128]{1,0:T(8,128)(2,1)}, bf16[256,128]{1,0:T(8,128)(2,1)S(1)}, u32[]{:S(2)}, u32[]{:S(2)}) collective-permute-start(bf16[256,128]{1,0:T(8,128)(2,1)} %bitcast.5), channel_id=1, source_target_pairs={{0,2},{2,0},{4,6},{6,4},{8,10},{10,8},{12,14},{14,12},{1,3},{3,1},... | collective-permute-start | bytes 196616 | tf_op jit(solution)/shard_map/ppermute | solution.py:172
  2.9 2.6 %collective-permute-start = (bf16[256,128]{1,0:T(8,128)(2,1)}, bf16[256,128]{1,0:T(8,128)(2,1)S(1)}, u32[]{:S(2)}, u32[]{:S(2)}) collective-permute-start(bf16[256,128]{1,0:T(8,128)(2,1)} %bitcast.6), channel_id=1, source_target_pairs={{0,8},{2,10},{4,12},{6,14},{8,0},{10,2},{12,4},{14,6},{1,9},{3,11}... | collective-permute-start | bytes 196616 | tf_op jit(solution)/shard_map/ppermute | solution.py:172
  5.5 1.6 %collective-permute-start.5 = (bf16[256,128]{1,0:T(8,128)(2,1)}, bf16[256,128]{1,0:T(8,128)(2,1)S(1)}, u32[]{:S(2)}, u32[]{:S(2)}) collective-permute-start(bf16[256,128]{1,0:T(8,128)(2,1)} %bitcast.7), channel_id=1, source_target_pairs={{0,4},{2,6},{4,0},{6,2},{8,12},{10,14},{12,8},{14,10},{1,5},{3,7},... | collective-permute-start | bytes 196616 | tf_op jit(solution)/shard_map/ppermute | solution.py:172
  7.1 0.0 copy-start
  7.1 1.6 %copy-done = bf16[128,64,128]{2,1,0:T(8,128)(2,1)S(1)} copy-done((bf16[128,64,128]{2,1,0:T(8,128)(2,1)S(1)}, bf16[128,64,128]{2,1,0:T(8,128)(2,1)}, u32[]{:S(2)}) %copy-start) | copy-done | bytes 2097176
  8.7 0.0 copy-start.2
  8.7 0.7 %copy-done.2 = s32[1,8,32]{2,1,0:T(8,128)S(1)} copy-done((s32[1,8,32]{2,1,0:T(8,128)S(1)}, s32[1,8,32]{2,1,0:T(8,128)}, u32[]{:S(2)}) %copy-start.2) | copy-done | bytes 1048
  9.4 0.0 copy-start.3
  9.4 0.7 %copy-done.3 = s32[128]{0:T(128)S(1)} copy-done((s32[128]{0:T(128)S(1)}, s32[128]{0:T(128)}, u32[]{:S(2)}) %copy-start.3) | copy-done | bytes 536
  10.0 0.0 copy-start.1
  10.0 3.6 %shard_map.46 = (f32[8,128]{1,0:T(8,128)S(1)}, s32[8,128]{1,0:T(8,128)S(1)}, bf16[128,64,128]{2,1,0:T(8,128)(2,1)S(1)}) custom-call(s32[8,32]{1,0:T(8,128)S(1)} %bitcast.9, s32[128]{0:T(128)S(1)} %copy-done.3, bf16[128,64,128]{2,1,0:T(8,128)(2,1)S(1)} %copy-done), custom_call_target="tpu_custom_call" | custom-call | flops 1048576 | bytes 2097152 | tf_op jit(solution)/shard_map/pallas_call | solution.py:70
  13.7 0.0 collective-permute-done.1.refs_1_
  13.7 0.0 collective-permute-done.refs_3_
  13.7 0.5 %collective-permute-start.4 = (bf16[256,128]{1,0:T(8,128)(2,1)S(1)}, bf16[256,128]{1,0:T(8,128)(2,1)S(1)}, u32[]{:S(2)}, u32[]{:S(2)}) collective-permute-start(bf16[256,128]{1,0:T(8,128)(2,1)S(1)} %collective-permute-done.refs_3_), channel_id=1, source_target_pairs={{0,4},{2,6},{4,0},{6,2},{8,12},{10,14},{12,8},{14,10},{1,5},{3,7},... | collective-permute-start | bytes 196616 | tf_op jit(solution)/shard_map/ppermute | solution.py:172
  14.2 0.5 %collective-permute-start.3 = (bf16[256,128]{1,0:T(8,128)(2,1)S(1)}, bf16[256,128]{1,0:T(8,128)(2,1)S(1)}, u32[]{:S(2)}, u32[]{:S(2)}) collective-permute-start(bf16[256,128]{1,0:T(8,128)(2,1)S(1)} %collective-permute-done.refs_3_), channel_id=1, source_target_pairs={{0,2},{2,0},{4,6},{6,4},{8,10},{10,8},{12,14},{14,12},{1,3},{3,1},... | collective-permute-start | bytes 196616 | tf_op jit(solution)/shard_map/ppermute | solution.py:172
  14.7 1.6 %collective-permute-start.2 = (bf16[256,128]{1,0:T(8,128)(2,1)S(1)}, bf16[256,128]{1,0:T(8,128)(2,1)S(1)}, u32[]{:S(2)}, u32[]{:S(2)}) collective-permute-start(bf16[256,128]{1,0:T(8,128)(2,1)S(1)} %collective-permute-done.1.refs_1_), channel_id=1, source_target_pairs={{0,4},{2,6},{4,0},{6,2},{8,12},{10,14},{12,8},{14,10},{1,5},{3,7},... | collective-permute-start | bytes 196616 | tf_op jit(solution)/shard_map/ppermute | solution.py:172
  16.3 0.0 collective-permute-done.5.refs_2_
  16.3 0.0 copy-done.1
  16.3 1.7 %shard_map.47.refs_4_ = f32[8,3,128]{2,1,0:T(4,128)S(1)} custom-call(f32[8,128]{1,0:T(8,128)S(1)} %get-tuple-element.13.slots_ref, s32[8,128]{1,0:T(8,128)S(1)} %get-tuple-element.14.picks_ref, bf16[128,64,128]{2,1,0:T(8,128)(2,1)S(1)} %get-tuple-element.16.p_ref, bf16[256,128]{1,0:T(8,128)(2,1)S(1)} %bitcast.8, ...), custom_call_target="tpu_custom_call" | custom-call | flops 536870912 | bytes 2097152 | tf_op jit(solution)/shard_map/pallas_call | solution.py:133
  18.0 0.0 collective-permute-done.4.refs_2_
  18.0 1.5 %collective-permute-start.6 = (bf16[256,128]{1,0:T(8,128)(2,1)S(1)}, bf16[256,128]{1,0:T(8,128)(2,1)S(1)}, u32[]{:S(2)}, u32[]{:S(2)}) collective-permute-start(bf16[256,128]{1,0:T(8,128)(2,1)S(1)} %collective-permute-done.4.refs_2_), channel_id=1, source_target_pairs={{0,2},{2,0},{4,6},{6,4},{8,10},{10,8},{12,14},{14,12},{1,3},{3,1},... | collective-permute-start | bytes 196616 | tf_op jit(solution)/shard_map/ppermute | solution.py:172
  19.5 0.0 collective-permute-done.2.refs_0_
  19.5 0.0 collective-permute-done.3.refs_1_
  19.5 2.8 %collective-permute-done.6.refs_3_ = bf16[256,128]{1,0:T(8,128)(2,1)S(1)} collective-permute-done((bf16[256,128]{1,0:T(8,128)(2,1)S(1)}, bf16[256,128]{1,0:T(8,128)(2,1)S(1)}, u32[]{:S(2)}, u32[]{:S(2)}) %collective-permute-start.6) | collective-permute-done | bytes 65568 | tf_op jit(solution)/shard_map/ppermute | solution.py:172
  22.3 1.7 %shard_map.48 = f32[8,3,128]{2,1,0:T(4,128)S(1)} custom-call(f32[8,128]{1,0:T(8,128)S(1)} %get-tuple-element.13.slots_ref, s32[8,128]{1,0:T(8,128)S(1)} %get-tuple-element.14.picks_ref, bf16[128,64,128]{2,1,0:T(8,128)(2,1)S(1)} %get-tuple-element.16.p_ref, bf16[256,128]{1,0:T(8,128)(2,1)S(1)} %collective-permute-done.2.refs_0_, ...), custom_call_target="tpu_custom_call" | custom-call | flops 536870912 | bytes 2097152 | tf_op jit(solution)/shard_map/pallas_call | solution.py:133
  24.0 9.6 %all_to_all.5.in_ref = f32[8,3,128]{2,1,0:T(4,128)} all-to-all(f32[8,3,128]{2,1,0:T(4,128)S(1)} %shard_map.48), channel_id=1, replica_groups=mesh['grp'=2,'psg'=8,'qry'=2] {'psg'}, dimensions={0} | all-to-all | bytes 24576 | tf_op jit(solution)/shard_map/all_to_all | solution.py:210
  33.6 1.5 %shard_map.49 = f32[8,2,16,32]{3,2,1,0:T(8,128)} custom-call(f32[8,3,128]{2,1,0:T(4,128)} %all_to_all.5.in_ref), custom_call_target="tpu_custom_call" | custom-call | tf_op jit(solution)/shard_map/pallas_call | solution.py:162
Async XLA Ops:
  0.0 13.7 %collective-permute-start.1 = (bf16[256,128]{1,0:T(8,128)(2,1)}, bf16[256,128]{1,0:T(8,128)(2,1)S(1)}, u32[]{:S(2)}, u32[]{:S(2)}) collective-permute-start(bf16[256,128]{1,0:T(8,128)(2,1)} %bitcast.5), channel_id=1, source_target_pairs={{0,2},{2,0},{4,6},{6,4},{8,10},{10,8},{12,14},{14,12},{1,3},{3,1},... | collective-permute-start | bytes 196616 | tf_op jit(solution)/shard_map/ppermute | solution.py:172
  2.9 10.7 %collective-permute-start = (bf16[256,128]{1,0:T(8,128)(2,1)}, bf16[256,128]{1,0:T(8,128)(2,1)S(1)}, u32[]{:S(2)}, u32[]{:S(2)}) collective-permute-start(bf16[256,128]{1,0:T(8,128)(2,1)} %bitcast.6), channel_id=1, source_target_pairs={{0,8},{2,10},{4,12},{6,14},{8,0},{10,2},{12,4},{14,6},{1,9},{3,11}... | collective-permute-start | bytes 196616 | tf_op jit(solution)/shard_map/ppermute | solution.py:172
  5.5 10.8 %collective-permute-start.5 = (bf16[256,128]{1,0:T(8,128)(2,1)}, bf16[256,128]{1,0:T(8,128)(2,1)S(1)}, u32[]{:S(2)}, u32[]{:S(2)}) collective-permute-start(bf16[256,128]{1,0:T(8,128)(2,1)} %bitcast.7), channel_id=1, source_target_pairs={{0,4},{2,6},{4,0},{6,2},{8,12},{10,14},{12,8},{14,10},{1,5},{3,7},... | collective-permute-start | bytes 196616 | tf_op jit(solution)/shard_map/ppermute | solution.py:172
  7.1 1.6 %copy-start = (bf16[128,64,128]{2,1,0:T(8,128)(2,1)S(1)}, bf16[128,64,128]{2,1,0:T(8,128)(2,1)}, u32[]{:S(2)}) copy-start(bf16[128,64,128]{2,1,0:T(8,128)(2,1)} %p_hbm.1) | copy-start | bytes 6291460
  8.7 0.7 %copy-start.2 = (s32[1,8,32]{2,1,0:T(8,128)S(1)}, s32[1,8,32]{2,1,0:T(8,128)}, u32[]{:S(2)}) copy-start(s32[1,8,32]{2,1,0:T(8,128)} %param.7) | copy-start | bytes 3076
  9.4 0.7 %copy-start.3 = (s32[128]{0:T(128)S(1)}, s32[128]{0:T(128)}, u32[]{:S(2)}) copy-start(s32[128]{0:T(128)} %len_hbm.1) | copy-start | bytes 1540
  10.0 6.3 %copy-start.1 = (bf16[8,32,128]{2,1,0:T(8,128)(2,1)S(1)}, bf16[8,32,128]{2,1,0:T(8,128)(2,1)}, u32[]{:S(2)}) copy-start(bf16[8,32,128]{2,1,0:T(8,128)(2,1)} %param.4) | copy-start | bytes 196612
  13.7 4.3 %collective-permute-start.4 = (bf16[256,128]{1,0:T(8,128)(2,1)S(1)}, bf16[256,128]{1,0:T(8,128)(2,1)S(1)}, u32[]{:S(2)}, u32[]{:S(2)}) collective-permute-start(bf16[256,128]{1,0:T(8,128)(2,1)S(1)} %collective-permute-done.refs_3_), channel_id=1, source_target_pairs={{0,4},{2,6},{4,0},{6,2},{8,12},{10,14},{12,8},{14,10},{1,5},{3,7},... | collective-permute-start | bytes 196616 | tf_op jit(solution)/shard_map/ppermute | solution.py:172
  14.2 5.3 %collective-permute-start.3 = (bf16[256,128]{1,0:T(8,128)(2,1)S(1)}, bf16[256,128]{1,0:T(8,128)(2,1)S(1)}, u32[]{:S(2)}, u32[]{:S(2)}) collective-permute-start(bf16[256,128]{1,0:T(8,128)(2,1)S(1)} %collective-permute-done.refs_3_), channel_id=1, source_target_pairs={{0,2},{2,0},{4,6},{6,4},{8,10},{10,8},{12,14},{14,12},{1,3},{3,1},... | collective-permute-start | bytes 196616 | tf_op jit(solution)/shard_map/ppermute | solution.py:172
  14.7 4.8 %collective-permute-start.2 = (bf16[256,128]{1,0:T(8,128)(2,1)S(1)}, bf16[256,128]{1,0:T(8,128)(2,1)S(1)}, u32[]{:S(2)}, u32[]{:S(2)}) collective-permute-start(bf16[256,128]{1,0:T(8,128)(2,1)S(1)} %collective-permute-done.1.refs_1_), channel_id=1, source_target_pairs={{0,4},{2,6},{4,0},{6,2},{8,12},{10,14},{12,8},{14,10},{1,5},{3,7},... | collective-permute-start | bytes 196616 | tf_op jit(solution)/shard_map/ppermute | solution.py:172
  18.0 4.3 %collective-permute-start.6 = (bf16[256,128]{1,0:T(8,128)(2,1)S(1)}, bf16[256,128]{1,0:T(8,128)(2,1)S(1)}, u32[]{:S(2)}, u32[]{:S(2)}) collective-permute-start(bf16[256,128]{1,0:T(8,128)(2,1)S(1)} %collective-permute-done.4.refs_2_), channel_id=1, source_target_pairs={{0,2},{2,0},{4,6},{6,4},{8,10},{10,8},{12,14},{14,12},{1,3},{3,1},... | collective-permute-start | bytes 196616 | tf_op jit(solution)/shard_map/ppermute | solution.py:172

commit v5 on v4

--- a/solution.py
+++ b/solution.py
@@ -67,6 +67,7 @@
 def prepare(shards, candidates, lengths, passages):
     hbm = pl.BlockSpec(memory_space=pltpu.HBM)
     vmem = pl.BlockSpec(memory_space=pltpu.VMEM)
+    operands = [pltpu.with_memory_space_constraint(x, pltpu.HBM) for x in (candidates, lengths, passages)]
     return pl.pallas_call(
         prepare_kernel,
         out_shape=[
@@ -84,17 +85,13 @@
         ],
         compiler_params=pltpu.CompilerParams(vmem_limit_bytes=24 * 1024 * 1024),
         cost_estimate=pl.CostEstimate(flops=passages.size, bytes_accessed=2 * passages.size, transcendentals=0),
-    )(candidates, lengths, passages)
-
-
-def score_kernel(partners, shards, slots_ref, picks_ref, p_ref, *refs):
+    )(*operands)
+
+
+def score_blocks(partners, me, slots_ref, picks_ref, p_ref, q_refs, sel_ref, max_ref):
     some = len(partners)
-    q_refs, (out_ref, sel_ref, max_ref) = refs[:some], refs[-3:]
-    earlier_refs = refs[some:-3]
     count = p_ref.shape[0]
     tokens = QB * QT
-    me = lax.axis_index("psg") if some < shards or len(earlier_refs) else 0
-
     for n, k in enumerate(partners):
         pick = jnp.max(picks_ref[pl.ds(me ^ k, 1), :])
         sel_ref[n * tokens:(n + 1) * tokens, :] = q_refs[n][pl.ds(pick * tokens, tokens), :]
@@ -118,23 +115,38 @@
     for part in (low, mid, high):
         total = total + lax.dot_general(ones, part, (((1,), (1,)), ((), ())), preferred_element_type=jnp.float32)
     total = total * (1.0 / QT)
-    if earlier_refs:
-        out_ref[...] = earlier_refs[0][...]
-    for n, k in enumerate(partners):
-        out_ref[me ^ k, 0:QB, :] = total[n * QB:(n + 1) * QB]
-        out_ref[me ^ k, QB:QB + 1, :] = slots_ref[pl.ds(me ^ k, 1), :]
-
-
-def score(partners, slots, picks, passages, blocks, *earlier):
+    return [
+        jnp.concatenate([total[n * QB:(n + 1) * QB], slots_ref[pl.ds(me ^ k, 1), :]]) for n, k in enumerate(partners)
+    ]
+
+
+def score_kernel(partners, paired, slots_ref, picks_ref, p_ref, *refs):
+    q_refs, (out_ref, sel_ref, max_ref) = refs[:-3], refs[-3:]
+    me = lax.axis_index("psg") if paired else 0
+    tiles = score_blocks(partners, me, slots_ref, picks_ref, p_ref, q_refs, sel_ref, max_ref)
+    for n, tile in enumerate(tiles):
+        out_ref[n] = tile
+
+
+def join_kernel(partners, slots_ref, picks_ref, p_ref, *refs):
+    some = len(partners)
+    q_refs, theirs_ref, out_refs, (sel_ref, max_ref) = refs[:some], refs[some], refs[some + 1:-2], refs[-2:]
+    me = lax.axis_index("psg")
+    tiles = score_blocks(partners, me, slots_ref, picks_ref, p_ref, q_refs, sel_ref, max_ref)
+    for n, tile in enumerate(tiles):
+        out_refs[n][0] = tile
+        out_refs[n][1] = theirs_ref[n]
+
+
+def score(kernel, out_shape, slots, picks, passages, blocks, *more):
     some = len(blocks)
-    shards = slots.shape[0]
     count = passages.shape[0]
     vmem = pl.BlockSpec(memory_space=pltpu.VMEM)
     return pl.pallas_call(
-        functools.partial(score_kernel, partners, shards),
-        out_shape=jax.ShapeDtypeStruct((shards, QB + 1, LANES), jnp.float32),
-        in_specs=[vmem] * (3 + some + len(earlier)),
-        out_specs=vmem,
+        kernel,
+        out_shape=out_shape,
+        in_specs=[vmem] * (3 + some + len(more)),
+        out_specs=jax.tree.map(lambda _: vmem, out_shape),
         scratch_shapes=[
             pltpu.VMEM((some * QB * QT, DIM), jnp.bfloat16),
             pltpu.VMEM((count, some * QB * QT), jnp.float32),
@@ -143,72 +155,102 @@
         cost_estimate=pl.CostEstimate(
             flops=2 * passages.size * some * QB * QT, bytes_accessed=2 * passages.size, transcendentals=0
         ),
-    )(slots, picks, passages, *blocks, *earlier)
-
-
-def place_kernel(in_ref, out_ref):
+    )(slots, picks, passages, *blocks, *more)
+
+
+def place_kernel(sources, in_refs, out_ref):
     slots = out_ref.shape[-1]
     m = lax.broadcasted_iota(jnp.int32, (PBS, LANES), 0)
-    for j in range(in_ref.shape[0]):
-        row = in_ref[j, QB:QB + 1, :].astype(jnp.int32)
+    for j, tile_ref in zip(sources, in_refs):
+        row = tile_ref[QB:QB + 1, :].astype(jnp.int32)
         where = jnp.minimum(row * PBS, LANES - PBS) + m
         for i in range(QB):
-            tile = jnp.broadcast_to(in_ref[j, i:i + 1, :], (PBS, LANES))
+            tile = jnp.broadcast_to(tile_ref[i:i + 1, :], (PBS, LANES))
             out_ref[j, i] = jnp.take_along_axis(tile, where, axis=1)[:, :slots]
 
 
-def place(tiles, slots):
+def place_all_kernel(in_ref, out_ref):
+    shards = in_ref.shape[0]
+    place_kernel(range(shards), [in_ref.at[j] for j in range(shards)], out_ref)
+
+
+def place_pairs_kernel(partners, *refs):
+    me = lax.axis_index("psg")
+    in_refs = [ref.at[n] for ref in refs[:-1] for n in range(2)]
+    place_kernel([me ^ k ^ n for k in partners for n in range(2)], in_refs, refs[-1])
+
+
+def place(kernel, shards, slots, *tiles):
     vmem = pl.BlockSpec(memory_space=pltpu.VMEM)
     return pl.pallas_call(
-        place_kernel,
-        out_shape=jax.ShapeDtypeStruct((tiles.shape[0], QB, PBS, slots), jnp.float32),
-        in_specs=[vmem],
+        kernel,
+        out_shape=jax.ShapeDtypeStruct((shards, QB, PBS, slots), jnp.float32),
+        in_specs=[vmem] * len(tiles),
         out_specs=vmem,
-    )(tiles)
-
-
-def relay_and_score(own, shards, candidates, lengths, passages):
+    )(*tiles)
+
+
+def by_partners(own, shards, slots, candidates, lengths, passages):
     def swap(x, k):
         return lax.ppermute(x, "psg", [(j, j ^ k) for j in range(shards)])
 
-    queries = {0: own, 4: swap(own, 4), 1: swap(own, 1), 2: swap(own, 2)}
-    slots, picks, clean = prepare(shards, candidates, lengths, passages)
-    queries[4], queries[1], clean = lax.optimization_barrier((queries[4], queries[1], clean))
-    queries[6] = swap(queries[4], 2)
-    queries[5] = swap(queries[4], 1)
-    queries[3] = swap(queries[1], 2)
-    first, second = (0, 1, 2, 4), (3, 5, 6, 7)
-    tiles = score(first, slots, picks, clean, [queries[k] for k in first])
-    queries[6], tiles = lax.optimization_barrier((queries[6], tiles))
-    queries[7] = swap(queries[6], 1)
-    return score(second, slots, picks, clean, [queries[k] for k in second], tiles)
+    near = list(range(0, shards, 2))
+    far = [k + 1 for k in near]
+    tile = (QB + 1, LANES)
+    queries = {0: own} | {k: swap(own, k) for k in reversed(far)}
+    rows, picks, clean = prepare(shards, candidates, lengths, passages)
+    *arrived, clean = lax.optimization_barrier((*[queries[k] for k in far], clean))
+    queries |= dict(zip(far, arrived))
+    queries |= {k: swap(queries[k + 1], 1) for k in near[1:]}
+    theirs = swap(
+        score(
+            functools.partial(score_kernel, far, True),
+            jax.ShapeDtypeStruct((len(far), *tile), jnp.float32),
+            rows, picks, clean, [queries[k] for k in far],
+        ), 1,
+    )
+    pairs = score(
+        functools.partial(join_kernel, near),
+        [jax.ShapeDtypeStruct((2, *tile), jnp.float32)] * len(near),
+        rows, picks, clean, [queries[k] for k in near], theirs,
+    )
+    pairs = [swap(pair, k) if k else pair for pair, k in zip(pairs, near)]
+    return place(functools.partial(place_pairs_kernel, near), shards, slots, *pairs)
+
+
+def by_collectives(own, shards, slots, candidates, lengths, passages):
+    rows, picks, clean = prepare(shards, candidates, lengths, passages)
+    gathered = lax.all_gather(own, "psg", axis=0)
+    some = min(shards, 8)
+    tile = (QB + 1, LANES)
+
+    def score_some(items):
+        some_rows, some_picks, some_blocks = items
+        return score(
+            functools.partial(score_kernel, range(some), False),
+            jax.ShapeDtypeStruct((some, *tile), jnp.float32),
+            some_rows, some_picks, clean, [some_blocks[k] for k in range(some)],
+        )
+
+    parts = shards // some
+    tiles = lax.map(score_some, (
+        rows.reshape(parts, some, LANES),
+        picks.reshape(parts, some, LANES),
+        gathered.reshape(parts, some, *own.shape),
+    ))
+    tiles = lax.all_to_all(tiles.reshape(shards, *tile), "psg", split_axis=0, concat_axis=0, tiled=True)
+    return place(place_all_kernel, shards, slots, tiles)
 
 
 def per_device(queries, passages, lengths, candidates):
     shards = lax.axis_size("psg")
     rows = passages.shape[0] // PBS
-    slots = rows * KB // shards
-    own = queries.reshape(QBD * QB * QT, DIM)
-    candidates = candidates.reshape(rows, KB)
-    if shards == 8:
-        tiles = relay_and_score(own, shards, candidates, lengths, passages)
-    else:
-        slot_rows, picks, clean = prepare(shards, candidates, lengths, passages)
-        gathered = lax.all_gather(own, "psg", axis=0)
-        some = 8
-
-        def score_some(items):
-            some_rows, some_picks, some_blocks = items
-            return score(range(some), some_rows, some_picks, clean, [some_blocks[k] for k in range(some)])
-
-        parts = shards // some
-        tiles = lax.map(score_some, (
-            slot_rows.reshape(parts, some, LANES),
-            picks.reshape(parts, some, LANES),
-            gathered.reshape(parts, some, *own.shape),
-        )).reshape(shards, QB + 1, LANES)
-    received = lax.all_to_all(tiles, "psg", split_axis=0, concat_axis=0, tiled=True)
-    return place(received, slots).transpose(0, 3, 1, 2)[None]
+    form = by_partners if shards in (4, 8) else by_collectives
+    placed = form(
+        queries.reshape(QBD * QB * QT, DIM), shards, rows * KB // shards,
+        candidates.reshape(rows, KB), lengths, passages,
+    )
+    return placed.transpose(0, 3, 1, 2)[None]
 
 
 def solution(mesh):

time: 35.5 us -> 35 us (0.986)
  blocking collectives: 9.64 us -> 0 us
  waiting for transfers between devices: 2.8 us -> 10.4 us
  starting transfers between devices: 11.3 us -> 16.5 us
  Pallas kernels: 8.49 us -> 6.71 us
  local copies, waits for them, and re-layouts: 2.94 us -> 1.22 us
    all_to_all x1 -> x0, blocking collectives: 9.64 us -> none  [per_device(): lax.all_to_all(tiles, 'psg', split_axis=0, concat_axis=0, tiled=True)]
    ppermute x7 -> x11, waiting for transfers between devices: 2.8 us -> 10.4 us  [swap(): return lax.ppermute(x, 'psg', [(j, j ^ k) for j in range(shards)])]
    ppermute x7 -> x11, starting transfers between devices: 11.3 us -> 16.5 us  [swap(): return lax.ppermute(x, 'psg', [(j, j ^ k) for j in range(shards)])]
    pallas_call x1, Pallas kernels: 3.62 us -> 1.82 us  [prepare(): pl.pallas_call(prepare_kernel, out_shape=[jax.ShapeDtypeStruct((shards, L...]
    unnamed x8 -> x10, local copies, waits for them, and re-layouts: 2.94 us -> 1.22 us
  transfers between devices with their start and end apart: 7 -> 11, of which waited for: 1 -> 5; matrix products, arithmetic and copies ran while one was open for 0% -> 0% of each run, Pallas kernels for 15% -> 10%
where the time goes in v5:
time: 35 us; the launch traced here: 34.8 us
  starting transfers between devices  16.5 us (47%)
  waiting for transfers between devices  10.4 us (30%)
  Pallas kernels  6.71 us (19%)
  local copies, waits for them, and re-layouts  1.22 us (3%)
    ppermute x11, starting transfers between devices, swap(): return lax.ppermute(x, 'psg', [(j, j ^ k) for j in range(shards)])  16.5 us
    ppermute x11, waiting for transfers between devices, swap(): return lax.ppermute(x, 'psg', [(j, j ^ k) for j in range(shards)])  10.4 us
    pallas_call x2, Pallas kernels, score(): pl.pallas_call(kernel, out_shape=out_shape, in_specs=[vmem] * (3 + some +...  3.36 us
    pallas_call x1, Pallas kernels, prepare(): pl.pallas_call(prepare_kernel, out_shape=[jax.ShapeDtypeStruct((shards, L...  1.82 us
    pallas_call x1, Pallas kernels, place(): pl.pallas_call(kernel, out_shape=jax.ShapeDtypeStruct((shards, QB, PBS, s...  1.53 us
    unnamed x10, local copies, waits for them, and re-layouts  1.22 us
  transfers between devices with their start and end apart: 11, of which 5 were waited for; matrix products, arithmetic and copies ran while one was open for 0% of the time, Pallas kernels for 10%

profile of v5, /device:TPU:0, one launch (start us, length us, event | category | flops | bytes accessed | tf_op | source)
XLA Modules:
  0.0 34.8 jit_solution(9546242866883850411)
XLA Ops:
  0.0 6.0 %collective-permute-start.3 = (bf16[256,128]{1,0:T(8,128)(2,1)}, bf16[256,128]{1,0:T(8,128)(2,1)S(1)}, u32[]{:S(2)}, u32[]{:S(2)}) collective-permute-start(bf16[256,128]{1,0:T(8,128)(2,1)} %bitcast.5), channel_id=1, source_target_pairs={{0,14},{2,12},{4,10},{6,8},{8,6},{10,4},{12,2},{14,0},{1,15},{3,13... | collective-permute-start | bytes 196616 | tf_op jit(solution)/shard_map/ppermute | solution.py:195
  6.0 0.0 collective-permute-start.2
  6.0 1.7 %collective-permute-start.1 = (bf16[256,128]{1,0:T(8,128)(2,1)}, bf16[256,128]{1,0:T(8,128)(2,1)S(1)}, u32[]{:S(2)}, u32[]{:S(2)}) collective-permute-start(bf16[256,128]{1,0:T(8,128)(2,1)} %bitcast.7), channel_id=1, source_target_pairs={{0,6},{2,4},{4,2},{6,0},{8,14},{10,12},{12,10},{14,8},{1,7},{3,5},... | collective-permute-start | bytes 196616 | tf_op jit(solution)/shard_map/ppermute | solution.py:195
  7.7 0.3 collective-permute-start
  8.0 0.0 copy-start
  8.0 1.8 %shard_map.46 = (f32[8,128]{1,0:T(8,128)S(1)}, s32[8,128]{1,0:T(8,128)S(1)}, bf16[128,64,128]{2,1,0:T(8,128)(2,1)S(1)}) custom-call(s32[8,32]{1,0:T(8,128)} %bitcast.10, s32[128]{0:T(128)} %len_hbm.1, bf16[128,64,128]{2,1,0:T(8,128)(2,1)} %p_hbm.1), custom_call_target="tpu_custom_call" | custom-call | flops 1048576 | bytes 2097152 | tf_op jit(solution)/shard_map/pallas_call | solution.py:71
  9.8 0.0 collective-permute-done.3.refs_3_
  9.9 2.5 %collective-permute-done.2.refs_2_ = bf16[256,128]{1,0:T(8,128)(2,1)S(1)} collective-permute-done((bf16[256,128]{1,0:T(8,128)(2,1)}, bf16[256,128]{1,0:T(8,128)(2,1)S(1)}, u32[]{:S(2)}, u32[]{:S(2)}) %collective-permute-start.2) | collective-permute-done | bytes 65568 | tf_op jit(solution)/shard_map/ppermute | solution.py:195
  12.3 0.0 collective-permute-done.1.refs_1_
  12.3 1.1 %collective-permute-done.refs_0_ = bf16[256,128]{1,0:T(8,128)(2,1)S(1)} collective-permute-done((bf16[256,128]{1,0:T(8,128)(2,1)}, bf16[256,128]{1,0:T(8,128)(2,1)S(1)}, u32[]{:S(2)}, u32[]{:S(2)}) %collective-permute-start) | collective-permute-done | bytes 65568 | tf_op jit(solution)/shard_map/ppermute | solution.py:195
  13.5 1.0 %collective-permute-start.4 = (bf16[256,128]{1,0:T(8,128)(2,1)S(1)}, bf16[256,128]{1,0:T(8,128)(2,1)S(1)}, u32[]{:S(2)}, u32[]{:S(2)}) collective-permute-start(bf16[256,128]{1,0:T(8,128)(2,1)S(1)} %collective-permute-done.1.refs_1_), channel_id=1, source_target_pairs={{0,2},{2,0},{4,6},{6,4},{8,10},{10,8},{12,14},{14,12},{1,3},{3,1},... | collective-permute-start | bytes 196616 | tf_op jit(solution)/shard_map/ppermute | solution.py:195
  14.4 1.1 %collective-permute-start.5 = (bf16[256,128]{1,0:T(8,128)(2,1)S(1)}, bf16[256,128]{1,0:T(8,128)(2,1)S(1)}, u32[]{:S(2)}, u32[]{:S(2)}) collective-permute-start(bf16[256,128]{1,0:T(8,128)(2,1)S(1)} %collective-permute-done.2.refs_2_), channel_id=1, source_target_pairs={{0,2},{2,0},{4,6},{6,4},{8,10},{10,8},{12,14},{14,12},{1,3},{3,1},... | collective-permute-start | bytes 196616 | tf_op jit(solution)/shard_map/ppermute | solution.py:195
  15.5 1.0 %collective-permute-start.6 = (bf16[256,128]{1,0:T(8,128)(2,1)S(1)}, bf16[256,128]{1,0:T(8,128)(2,1)S(1)}, u32[]{:S(2)}, u32[]{:S(2)}) collective-permute-start(bf16[256,128]{1,0:T(8,128)(2,1)S(1)} %collective-permute-done.3.refs_3_), channel_id=1, source_target_pairs={{0,2},{2,0},{4,6},{6,4},{8,10},{10,8},{12,14},{14,12},{1,3},{3,1},... | collective-permute-start | bytes 196616 | tf_op jit(solution)/shard_map/ppermute | solution.py:195
  16.5 1.7 %shard_map.47 = f32[4,3,128]{2,1,0:T(4,128)S(1)} custom-call(f32[8,128]{1,0:T(8,128)S(1)} %get-tuple-element.17.slots_ref, s32[8,128]{1,0:T(8,128)S(1)} %get-tuple-element.18.picks_ref, bf16[128,64,128]{2,1,0:T(8,128)(2,1)S(1)} %get-tuple-element.20.p_ref, bf16[256,128]{1,0:T(8,128)(2,1)S(1)} %collective-permute-done.refs_0_, ...), custom_call_target="tpu_custom_call" | custom-call | flops 536870912 | bytes 2097152 | tf_op jit(solution)/shard_map/pallas_call | solution.py:145
  18.1 1.1 %collective-permute-start.7 = (f32[4,3,128]{2,1,0:T(4,128)S(1)}, f32[4,3,128]{2,1,0:T(4,128)S(1)}, u32[]{:S(2)}, u32[]{:S(2)}) collective-permute-start(f32[4,3,128]{2,1,0:T(4,128)S(1)} %shard_map.47), channel_id=1, source_target_pairs={{0,2},{2,0},{4,6},{6,4},{8,10},{10,8},{12,14},{14,12},{1,3},{3,1},... | collective-permute-start | bytes 18440 | tf_op jit(solution)/shard_map/ppermute | solution.py:195
  19.2 2.6 %collective-permute-done.7.refs_4_ = f32[4,3,128]{2,1,0:T(4,128)S(1)} collective-permute-done((f32[4,3,128]{2,1,0:T(4,128)S(1)}, f32[4,3,128]{2,1,0:T(4,128)S(1)}, u32[]{:S(2)}, u32[]{:S(2)}) %collective-permute-start.7) | collective-permute-done | bytes 6176 | tf_op jit(solution)/shard_map/ppermute | solution.py:195
  21.8 0.0 collective-permute-done.4.refs_1_
  21.8 0.0 collective-permute-done.5.refs_2_
  21.8 0.0 collective-permute-done.6.refs_3_
  21.8 0.0 copy-done
  21.8 1.7 %shard_map.48 = (f32[2,3,128]{2,1,0:T(4,128)S(1)}, f32[2,3,128]{2,1,0:T(4,128)S(1)}, f32[2,3,128]{2,1,0:T(4,128)S(1)}, f32[2,3,128]{2,1,0:T(4,128)S(1)}) custom-call(f32[8,128]{1,0:T(8,128)S(1)} %get-tuple-element.17.slots_ref, s32[8,128]{1,0:T(8,128)S(1)} %get-tuple-element.18.picks_ref, bf16[128,64,128]{2,1,0:T(8,128)(2,1)S(1)} %get-tuple-element.20.p_ref, ...), custom_call_target="tpu_custom_call" | custom-call | flops 536870912 | bytes 2097152 | tf_op jit(solution)/shard_map/pallas_call | solution.py:145
  23.5 0.6 %copy-done.1 = f32[2,3,128]{2,1,0:T(4,128)} copy-done((f32[2,3,128]{2,1,0:T(4,128)}, f32[2,3,128]{2,1,0:T(4,128)S(1)}, u32[]{:S(2)}) %copy-start.1) | copy-done | bytes 3096
  24.1 0.8 %collective-permute-start.8 = (f32[2,3,128]{2,1,0:T(4,128)S(1)}, f32[2,3,128]{2,1,0:T(4,128)S(1)}, u32[]{:S(2)}, u32[]{:S(2)}) collective-permute-start(f32[2,3,128]{2,1,0:T(4,128)S(1)} %get-tuple-element.26), channel_id=1, source_target_pairs={{0,4},{2,6},{4,0},{6,2},{8,12},{10,14},{12,8},{14,10},{1,5},{3,7},... | collective-permute-start | bytes 9224 | tf_op jit(solution)/shard_map/ppermute | solution.py:195
  24.9 2.4 %collective-permute-start.9 = (f32[2,3,128]{2,1,0:T(4,128)S(1)}, f32[2,3,128]{2,1,0:T(4,128)S(1)}, u32[]{:S(2)}, u32[]{:S(2)}) collective-permute-start(f32[2,3,128]{2,1,0:T(4,128)S(1)} %get-tuple-element.27), channel_id=1, source_target_pairs={{0,8},{2,10},{4,12},{6,14},{8,0},{10,2},{12,4},{14,6},{1,9},{3,11}... | collective-permute-start | bytes 9224 | tf_op jit(solution)/shard_map/ppermute | solution.py:195
  27.3 1.2 %collective-permute-start.10 = (f32[2,3,128]{2,1,0:T(4,128)S(1)}, f32[2,3,128]{2,1,0:T(4,128)S(1)}, u32[]{:S(2)}, u32[]{:S(2)}) collective-permute-start(f32[2,3,128]{2,1,0:T(4,128)S(1)} %get-tuple-element.28), channel_id=1, source_target_pairs={{0,12},{2,14},{4,8},{6,10},{8,4},{10,6},{12,0},{14,2},{1,13},{3,15... | collective-permute-start | bytes 9224 | tf_op jit(solution)/shard_map/ppermute | solution.py:195
  28.5 0.0 collective-permute-done.8.refs_1_
  28.5 0.9 %collective-permute-done.9.refs_2_ = f32[2,3,128]{2,1,0:T(4,128)S(1)} collective-permute-done((f32[2,3,128]{2,1,0:T(4,128)S(1)}, f32[2,3,128]{2,1,0:T(4,128)S(1)}, u32[]{:S(2)}, u32[]{:S(2)}) %collective-permute-start.9) | collective-permute-done | bytes 3104 | tf_op jit(solution)/shard_map/ppermute | solution.py:195
  29.4 3.3 %collective-permute-done.10.refs_3_ = f32[2,3,128]{2,1,0:T(4,128)S(1)} collective-permute-done((f32[2,3,128]{2,1,0:T(4,128)S(1)}, f32[2,3,128]{2,1,0:T(4,128)S(1)}, u32[]{:S(2)}, u32[]{:S(2)}) %collective-permute-start.10) | collective-permute-done | bytes 3104 | tf_op jit(solution)/shard_map/ppermute | solution.py:195
  32.7 0.0 copy-done.2
  32.7 0.0 copy-done.3
  32.7 0.6 %copy-done.4 = f32[2,3,128]{2,1,0:T(4,128)} copy-done((f32[2,3,128]{2,1,0:T(4,128)}, f32[2,3,128]{2,1,0:T(4,128)S(1)}, u32[]{:S(2)}) %copy-start.4) | copy-done | bytes 3096
  33.3 1.5 %shard_map.49 = f32[8,2,16,32]{3,2,1,0:T(8,128)} custom-call(f32[2,3,128]{2,1,0:T(4,128)} %copy-done.1, f32[2,3,128]{2,1,0:T(4,128)} %copy-done.2, f32[2,3,128]{2,1,0:T(4,128)} %copy-done.3, f32[2,3,128]{2,1,0:T(4,128)} %copy-done.4), custom_call_target="tpu_custom_call" | custom-call | tf_op jit(solution)/shard_map/pallas_call | solution.py:185
  (4 shorter events, 0.0 us)
Async XLA Ops:
  0.0 9.8 %collective-permute-start.3 = (bf16[256,128]{1,0:T(8,128)(2,1)}, bf16[256,128]{1,0:T(8,128)(2,1)S(1)}, u32[]{:S(2)}, u32[]{:S(2)}) collective-permute-start(bf16[256,128]{1,0:T(8,128)(2,1)} %bitcast.5), channel_id=1, source_target_pairs={{0,14},{2,12},{4,10},{6,8},{8,6},{10,4},{12,2},{14,0},{1,15},{3,13... | collective-permute-start | bytes 196616 | tf_op jit(solution)/shard_map/ppermute | solution.py:195
  6.0 6.3 %collective-permute-start.2 = (bf16[256,128]{1,0:T(8,128)(2,1)}, bf16[256,128]{1,0:T(8,128)(2,1)S(1)}, u32[]{:S(2)}, u32[]{:S(2)}) collective-permute-start(bf16[256,128]{1,0:T(8,128)(2,1)} %bitcast.6), channel_id=1, source_target_pairs={{0,10},{2,8},{4,14},{6,12},{8,2},{10,0},{12,6},{14,4},{1,11},{3,9}... | collective-permute-start | bytes 196616 | tf_op jit(solution)/shard_map/ppermute | solution.py:195
  6.0 6.3 %collective-permute-start.1 = (bf16[256,128]{1,0:T(8,128)(2,1)}, bf16[256,128]{1,0:T(8,128)(2,1)S(1)}, u32[]{:S(2)}, u32[]{:S(2)}) collective-permute-start(bf16[256,128]{1,0:T(8,128)(2,1)} %bitcast.7), channel_id=1, source_target_pairs={{0,6},{2,4},{4,2},{6,0},{8,14},{10,12},{12,10},{14,8},{1,7},{3,5},... | collective-permute-start | bytes 196616 | tf_op jit(solution)/shard_map/ppermute | solution.py:195
  7.7 5.8 %collective-permute-start = (bf16[256,128]{1,0:T(8,128)(2,1)}, bf16[256,128]{1,0:T(8,128)(2,1)S(1)}, u32[]{:S(2)}, u32[]{:S(2)}) collective-permute-start(bf16[256,128]{1,0:T(8,128)(2,1)} %bitcast.8), channel_id=1, source_target_pairs={{0,2},{2,0},{4,6},{6,4},{8,10},{10,8},{12,14},{14,12},{1,3},{3,1},... | collective-permute-start | bytes 196616 | tf_op jit(solution)/shard_map/ppermute | solution.py:195
  8.0 13.8 %copy-start = (bf16[8,32,128]{2,1,0:T(8,128)(2,1)S(1)}, bf16[8,32,128]{2,1,0:T(8,128)(2,1)}, u32[]{:S(2)}) copy-start(bf16[8,32,128]{2,1,0:T(8,128)(2,1)} %param.4) | copy-start | bytes 196612
  13.5 8.4 %collective-permute-start.4 = (bf16[256,128]{1,0:T(8,128)(2,1)S(1)}, bf16[256,128]{1,0:T(8,128)(2,1)S(1)}, u32[]{:S(2)}, u32[]{:S(2)}) collective-permute-start(bf16[256,128]{1,0:T(8,128)(2,1)S(1)} %collective-permute-done.1.refs_1_), channel_id=1, source_target_pairs={{0,2},{2,0},{4,6},{6,4},{8,10},{10,8},{12,14},{14,12},{1,3},{3,1},... | collective-permute-start | bytes 196616 | tf_op jit(solution)/shard_map/ppermute | solution.py:195
  14.4 7.4 %collective-permute-start.5 = (bf16[256,128]{1,0:T(8,128)(2,1)S(1)}, bf16[256,128]{1,0:T(8,128)(2,1)S(1)}, u32[]{:S(2)}, u32[]{:S(2)}) collective-permute-start(bf16[256,128]{1,0:T(8,128)(2,1)S(1)} %collective-permute-done.2.refs_2_), channel_id=1, source_target_pairs={{0,2},{2,0},{4,6},{6,4},{8,10},{10,8},{12,14},{14,12},{1,3},{3,1},... | collective-permute-start | bytes 196616 | tf_op jit(solution)/shard_map/ppermute | solution.py:195
  15.5 6.3 %collective-permute-start.6 = (bf16[256,128]{1,0:T(8,128)(2,1)S(1)}, bf16[256,128]{1,0:T(8,128)(2,1)S(1)}, u32[]{:S(2)}, u32[]{:S(2)}) collective-permute-start(bf16[256,128]{1,0:T(8,128)(2,1)S(1)} %collective-permute-done.3.refs_3_), channel_id=1, source_target_pairs={{0,2},{2,0},{4,6},{6,4},{8,10},{10,8},{12,14},{14,12},{1,3},{3,1},... | collective-permute-start | bytes 196616 | tf_op jit(solution)/shard_map/ppermute | solution.py:195
  18.1 3.7 %collective-permute-start.7 = (f32[4,3,128]{2,1,0:T(4,128)S(1)}, f32[4,3,128]{2,1,0:T(4,128)S(1)}, u32[]{:S(2)}, u32[]{:S(2)}) collective-permute-start(f32[4,3,128]{2,1,0:T(4,128)S(1)} %shard_map.47), channel_id=1, source_target_pairs={{0,2},{2,0},{4,6},{6,4},{8,10},{10,8},{12,14},{14,12},{1,3},{3,1},... | collective-permute-start | bytes 18440 | tf_op jit(solution)/shard_map/ppermute | solution.py:195
  23.5 0.6 %copy-start.1 = (f32[2,3,128]{2,1,0:T(4,128)}, f32[2,3,128]{2,1,0:T(4,128)S(1)}, u32[]{:S(2)}) copy-start(f32[2,3,128]{2,1,0:T(4,128)S(1)} %get-tuple-element.25.refs_0_) | copy-start | bytes 9220
  24.1 4.4 %collective-permute-start.8 = (f32[2,3,128]{2,1,0:T(4,128)S(1)}, f32[2,3,128]{2,1,0:T(4,128)S(1)}, u32[]{:S(2)}, u32[]{:S(2)}) collective-permute-start(f32[2,3,128]{2,1,0:T(4,128)S(1)} %get-tuple-element.26), channel_id=1, source_target_pairs={{0,4},{2,6},{4,0},{6,2},{8,12},{10,14},{12,8},{14,10},{1,5},{3,7},... | collective-permute-start | bytes 9224 | tf_op jit(solution)/shard_map/ppermute | solution.py:195
  24.9 4.5 %collective-permute-start.9 = (f32[2,3,128]{2,1,0:T(4,128)S(1)}, f32[2,3,128]{2,1,0:T(4,128)S(1)}, u32[]{:S(2)}, u32[]{:S(2)}) collective-permute-start(f32[2,3,128]{2,1,0:T(4,128)S(1)} %get-tuple-element.27), channel_id=1, source_target_pairs={{0,8},{2,10},{4,12},{6,14},{8,0},{10,2},{12,4},{14,6},{1,9},{3,11}... | collective-permute-start | bytes 9224 | tf_op jit(solution)/shard_map/ppermute | solution.py:195
  27.3 5.4 %collective-permute-start.10 = (f32[2,3,128]{2,1,0:T(4,128)S(1)}, f32[2,3,128]{2,1,0:T(4,128)S(1)}, u32[]{:S(2)}, u32[]{:S(2)}) collective-permute-start(f32[2,3,128]{2,1,0:T(4,128)S(1)} %get-tuple-element.28), channel_id=1, source_target_pairs={{0,12},{2,14},{4,8},{6,10},{8,4},{10,6},{12,0},{14,2},{1,13},{3,15... | collective-permute-start | bytes 9224 | tf_op jit(solution)/shard_map/ppermute | solution.py:195
  28.5 4.2 %copy-start.2 = (f32[2,3,128]{2,1,0:T(4,128)}, f32[2,3,128]{2,1,0:T(4,128)S(1)}, u32[]{:S(2)}) copy-start(f32[2,3,128]{2,1,0:T(4,128)S(1)} %collective-permute-done.8.refs_1_) | copy-start | bytes 9220
  29.4 3.3 %copy-start.3 = (f32[2,3,128]{2,1,0:T(4,128)}, f32[2,3,128]{2,1,0:T(4,128)S(1)}, u32[]{:S(2)}) copy-start(f32[2,3,128]{2,1,0:T(4,128)S(1)} %collective-permute-done.9.refs_2_) | copy-start | bytes 9220
  32.7 0.6 %copy-start.4 = (f32[2,3,128]{2,1,0:T(4,128)}, f32[2,3,128]{2,1,0:T(4,128)S(1)}, u32[]{:S(2)}) copy-start(f32[2,3,128]{2,1,0:T(4,128)S(1)} %collective-permute-done.10.refs_3_) | copy-start | bytes 9220

commit v6 on v4

v6 whole, which is shorter than its diff:
```python
import functools

import jax
import jax.numpy as jnp
from jax import lax
from jax.experimental import pallas as pl
from jax.experimental.pallas import tpu as pltpu
from jax.sharding import PartitionSpec as P

DIM = 128
QT = 32
PT = 64
QB = 2
QBD = 4
PBS = 16
KB = 32
LANES = 128
GROUP = 8


def prepare_kernel(*refs):
    several = (len(refs) - 8) // 2
    *cand_refs, len_hbm, p_hbm, slots_ref = refs[:several + 3]
    picks_refs = refs[several + 3:-5]
    clean_ref, len_ref, raw_ref, cand_ref, sems = refs[-5:]
    rows = cand_ref.shape[0]
    shards = slots_ref.shape[0]
    groups = p_hbm.shape[0] // GROUP

    def fetch(g):
        part = pl.ds(g * GROUP, GROUP)
        return pltpu.make_async_copy(p_hbm.at[part], raw_ref.at[part], sems.at[g])

    fetch_cand = pltpu.make_async_copy(cand_refs[0], cand_ref, sems.at[groups])
    fetch_len = pltpu.make_async_copy(len_hbm, len_ref, sems.at[groups + 1])
    fetch_cand.start()
    fetch_len.start()
    for g in range(groups):
        fetch(g).start()

    fetch_cand.wait()
    lane = lax.broadcasted_iota(jnp.int32, (rows, LANES), 1).astype(jnp.float32)
    sub = lax.broadcasted_iota(jnp.int32, (rows, LANES), 0)
    for n, picks_ref in enumerate(picks_refs):
        cand = (cand_refs[n] if n else cand_ref)[...]
        owner = cand // QBD
        block = cand - owner * QBD
        for o in range(shards):
            mine = owner == o
            named = jnp.max(jnp.where(mine, block, 0), axis=1, keepdims=True)
            picks_ref[o:o + 1, :] = jnp.broadcast_to(jnp.max(named, axis=0, keepdims=True), (1, LANES))
            if n:
                continue
            named_here = jnp.sum(jnp.where(mine, 1.0, 0.0), axis=1, keepdims=True)
            upto = jnp.broadcast_to(named_here, (rows, LANES))
            step = 1
            while step < rows:
                upto = upto + jnp.where(sub >= step, pltpu.roll(upto, step, 0), 0.0)
                step *= 2
            slots_ref[o:o + 1, :] = jnp.sum(jnp.where(upto <= lane, 1.0, 0.0), axis=0, keepdims=True)

    fetch_len.wait()
    u = lax.broadcasted_iota(jnp.int32, (PT, LANES), 0)

    @pl.loop(0, groups)
    def _(g):
        fetch(g).wait()
        for i in range(GROUP):
            p = g * GROUP + i
            tokens = raw_ref[p].astype(jnp.float32)
            clean_ref[p] = jnp.where(u < len_ref[p], tokens, tokens[0:1]).astype(jnp.bfloat16)


def prepare(shards, lengths, passages, *candidates):
    hbm = pl.BlockSpec(memory_space=pltpu.HBM)
    vmem = pl.BlockSpec(memory_space=pltpu.VMEM)
    kept = [pltpu.with_memory_space_constraint(x, pltpu.HBM) for x in (candidates[0], lengths, passages)]
    more = candidates[1:]
    return pl.pallas_call(
        prepare_kernel,
        out_shape=[
            jax.ShapeDtypeStruct((shards, LANES), jnp.float32),
            *[jax.ShapeDtypeStruct((shards, LANES), jnp.int32) for _ in candidates],
            jax.ShapeDtypeStruct(passages.shape, passages.dtype),
        ],
        in_specs=[hbm] + [vmem] * len(more) + [hbm] * 2,
        out_specs=[vmem] * (2 + len(candidates)),
        scratch_shapes=[
            pltpu.SMEM(lengths.shape, lengths.dtype),
            pltpu.VMEM(passages.shape, passages.dtype),
            pltpu.VMEM(candidates[0].shape, candidates[0].dtype),
            pltpu.SemaphoreType.DMA((passages.shape[0] // GROUP + 2,)),
        ],
        compiler_params=pltpu.CompilerParams(vmem_limit_bytes=24 * 1024 * 1024),
        cost_estimate=pl.CostEstimate(flops=passages.size, bytes_accessed=2 * passages.size, transcendentals=0),
    )(kept[0], *more, *kept[1:])


def picked(picks_ref, owner, q_ref):
    pick = jnp.max(picks_ref[pl.ds(owner, 1), :])
    return q_ref[pl.ds(pick * QB * QT, QB * QT), :]


def pack_kernel(partners, picks_ref, *refs):
    q_refs, out_ref = refs[:-1], refs[-1]
    me = lax.axis_index("psg")
    for n, k in enumerate(partners):
        out_ref[n * QB * QT:(n + 1) * QB * QT, :] = picked(picks_ref, me ^ k, q_refs[n])


def pack(partners, picks, blocks):
    vmem = pl.BlockSpec(memory_space=pltpu.VMEM)
    return pl.pallas_call(
        functools.partial(pack_kernel, partners),
        out_shape=jax.ShapeDtypeStruct((len(partners) * QB * QT, DIM), blocks[0].dtype),
        in_specs=[vmem] * (1 + len(blocks)),
        out_specs=vmem,
        compiler_params=pltpu.CompilerParams(vmem_limit_bytes=4 * 1024 * 1024),
    )(picks, *blocks)


def score_picked(sel_ref, p_ref, max_ref):
    count = p_ref.shape[0]
    sel = sel_ref[...]
    tokens = sel.shape[0]
    for g in range(count // GROUP):
        left = p_ref[g * GROUP:(g + 1) * GROUP].reshape(GROUP * PT, DIM)
        dots = lax.dot_general(left, sel, (((1,), (1,)), ((), ())), preferred_element_type=jnp.float32)
        best = jnp.max(dots.reshape(GROUP, PT, tokens), axis=1)
        max_ref[g * GROUP:(g + 1) * GROUP, :] = best

    best = max_ref[...]
    high = best.astype(jnp.bfloat16)
    rest = best - high.astype(jnp.float32)
    mid = rest.astype(jnp.bfloat16)
    low = (rest - mid.astype(jnp.float32)).astype(jnp.bfloat16)
    query = lax.broadcasted_iota(jnp.int32, (tokens // QT, tokens), 0)
    token = lax.broadcasted_iota(jnp.int32, (tokens // QT, tokens), 1)
    ones = jnp.where(token // QT == query, 1.0, 0.0).astype(jnp.bfloat16)
    total = jnp.zeros((tokens // QT, count), jnp.float32)
    for part in (low, mid, high):
        total = total + lax.dot_general(ones, part, (((1,), (1,)), ((), ())), preferred_element_type=jnp.float32)
    return total * (1.0 / QT)


def score_kernel(partners, slots_ref, picks_ref, p_ref, *refs):
    q_refs, (out_ref, sel_ref, max_ref) = refs[:-3], refs[-3:]
    me = lax.axis_index("psg")
    for n, k in enumerate(partners):
        sel_ref[n * QB * QT:(n + 1) * QB * QT, :] = picked(picks_ref, me ^ k, q_refs[n])
    total = score_picked(sel_ref, p_ref, max_ref)
    for n, k in enumerate(partners):
        out_ref[n, 0:QB, :] = total[n * QB:(n + 1) * QB]
        out_ref[n, QB:QB + 1, :] = slots_ref[pl.ds(me ^ k, 1), :]


def join_kernel(partners, slots_ref, p_ref, sel_ref, earlier_ref, out_ref, max_ref):
    me = lax.axis_index("psg")
    total = score_picked(sel_ref, p_ref, max_ref)
    for n, k in enumerate(partners):
        out_ref[me ^ k, 0:QB, :] = total[n * QB:(n + 1) * QB]
        out_ref[me ^ k, QB:QB + 1, :] = slots_ref[pl.ds(me ^ k, 1), :]
        out_ref[me ^ k ^ 1] = earlier_ref[n]


def all_kernel(slots_ref, picks_ref, p_ref, q_ref, out_ref, sel_ref, max_ref):
    some = q_ref.shape[0]
    for n in range(some):
        sel_ref[n * QB * QT:(n + 1) * QB * QT, :] = picked(picks_ref, n, q_ref.at[n])
    total = score_picked(sel_ref, p_ref, max_ref)
    for n in range(some):
        out_ref[n, 0:QB, :] = total[n * QB:(n + 1) * QB]
        out_ref[n, QB:QB + 1, :] = slots_ref[n:n + 1, :]


def score(kernel, tiles, some, selects, passages, *more):
    count = passages.shape[0]
    vmem = pl.BlockSpec(memory_space=pltpu.VMEM)
    return pl.pallas_call(
        kernel,
        out_shape=jax.ShapeDtypeStruct((tiles, QB + 1, LANES), jnp.float32),
        in_specs=[vmem] * len(more),
        out_specs=vmem,
        scratch_shapes=[pltpu.VMEM((some * QB * QT, DIM), jnp.bfloat16)] * selects + [
            pltpu.VMEM((count, some * QB * QT), jnp.float32),
        ],
        compiler_params=pltpu.CompilerParams(vmem_limit_bytes=32 * 1024 * 1024),
        cost_estimate=pl.CostEstimate(
            flops=2 * passages.size * some * QB * QT, bytes_accessed=2 * passages.size, transcendentals=0
        ),
    )(*more)


def place_kernel(in_ref, out_ref):
    slots = out_ref.shape[-1]
    m = lax.broadcasted_iota(jnp.int32, (PBS, LANES), 0)
    for j in range(in_ref.shape[0]):
        row = in_ref[j, QB:QB + 1, :].astype(jnp.int32)
        where = jnp.minimum(row * PBS, LANES - PBS) + m
        for i in range(QB):
            tile = jnp.broadcast_to(in_ref[j, i:i + 1, :], (PBS, LANES))
            out_ref[j, i] = jnp.take_along_axis(tile, where, axis=1)[:, :slots]


def place(tiles, slots):
    vmem = pl.BlockSpec(memory_space=pltpu.VMEM)
    shards = tiles.shape[0]
    return pl.pallas_call(
        place_kernel,
        out_shape=jax.ShapeDtypeStruct((shards, QB, PBS, slots), jnp.float32),
        in_specs=[vmem],
        out_specs=vmem,
        compiler_params=pltpu.CompilerParams(vmem_limit_bytes=8 * 1024 * 1024),
    )(tiles)


def by_partners(own, shards, candidates, lengths, passages):
    def swap(x, k):
        return lax.ppermute(x, "psg", [(j, j ^ k) for j in range(shards)])

    near = list(range(0, shards, 2))
    theirs = swap(candidates, 1)
    queries = {0: own} | {k: swap(own, k) for k in reversed(near[1:])}
    slots, picks, their_picks, clean = prepare(shards, lengths, passages, candidates, theirs)
    *arrived, clean = lax.optimization_barrier((*[queries[k] for k in near[1:]], clean))
    blocks = [own, *arrived]
    far = swap(pack(near, their_picks, blocks), 1)
    tiles = score(
        functools.partial(score_kernel, near), len(near), len(near), 1, clean, slots, picks, clean, *blocks
    )
    far, tiles = lax.optimization_barrier((far, tiles))
    return score(
        functools.partial(join_kernel, [k + 1 for k in near]), shards, len(near), 0, clean, slots, clean, far, tiles
    )


def by_gather(own, shards, candidates, lengths, passages):
    slots, picks, clean = prepare(shards, lengths, passages, candidates)
    gathered = lax.all_gather(own, "psg", axis=0)
    some = min(shards, 8)

    def score_some(items):
        return score(all_kernel, some, some, 1, clean, items[0], items[1], clean, items[2])

    parts = [x.reshape(shards // some, some, *x.shape[1:]) for x in (slots, picks, gathered)]
    return lax.map(score_some, parts).reshape(shards, QB + 1, LANES)


def per_device(queries, passages, lengths, candidates):
    shards = lax.axis_size("psg")
    rows = passages.shape[0] // PBS
    form = by_partners if shards in (4, 8) else by_gather
    tiles = form(
        queries.reshape(QBD * QB * QT, DIM), shards, candidates.reshape(rows, KB), lengths, passages
    )
    tiles = lax.all_to_all(tiles, "psg", split_axis=0, concat_axis=0, tiled=True)
    return place(tiles, rows * KB // shards).transpose(0, 3, 1, 2)[None]


def solution(mesh):
    return jax.shard_map(
        per_device,
        mesh=mesh,
        in_specs=(
            P(("grp", "psg", "qry"), None, None),
            P(("grp", "psg"), None, None),
            P(("grp", "psg")),
            P("qry", ("grp", "psg"), None),
        ),
        out_specs=P(("grp", "psg", "qry"), None, None, None, None),
        check_vma=False,
    )
```

time: 35.5 us -> 30.7 us (0.86)
  local copies, waits for them, and re-layouts: 2.94 us -> 0.01 us
  blocking collectives: 9.64 us -> 12.4 us
  Pallas kernels: 8.49 us -> 5.95 us
  starting transfers between devices: 11.3 us -> 9.04 us
    unnamed x8 -> x2, local copies, waits for them, and re-layouts: 2.94 us -> 0.01 us
    all_to_all x1, blocking collectives: 9.64 us -> 12.4 us  [per_device(): lax.all_to_all(tiles, 'psg', split_axis=0, concat_axis=0, tiled=True)]
    ppermute x7 -> x5, starting transfers between devices: 11.3 us -> 9.04 us  [swap(): return lax.ppermute(x, 'psg', [(j, j ^ k) for j in range(shards)])]
    pallas_call x1, Pallas kernels: 3.62 us -> 1.8 us  [prepare(): pl.pallas_call(prepare_kernel, out_shape=[jax.ShapeDtypeStruct((shards, L...]
    pallas_call x3 -> x4, Pallas kernels: 4.87 us -> 4.15 us  [the longest x2 3.13 us: score(): pl.pallas_call(kernel, out_shape=jax.ShapeDtypeStruct((tiles, QB + 1, LAN...]
    ppermute x7 -> x5, waiting for transfers between devices: 2.8 us -> 3.12 us  [swap(): return lax.ppermute(x, 'psg', [(j, j ^ k) for j in range(shards)])]
  transfers between devices with their start and end apart: 7 -> 5, of which waited for: 1 -> 2; matrix products, arithmetic and copies ran while one was open for 0% -> 0% of each run, Pallas kernels for 15% -> 11%
where the time goes in v6:
time: 30.7 us; the launch traced here: 30.5 us
  blocking collectives  12.4 us (40%)
  starting transfers between devices  9.04 us (29%)
  Pallas kernels  5.95 us (19%)
  waiting for transfers between devices  3.12 us (10%)
    all_to_all x1, blocking collectives, per_device(): lax.all_to_all(tiles, 'psg', split_axis=0, concat_axis=0, tiled=True)  12.4 us
    ppermute x5, starting transfers between devices, swap(): return lax.ppermute(x, 'psg', [(j, j ^ k) for j in range(shards)])  9.04 us
    pallas_call x2, Pallas kernels, score(): pl.pallas_call(kernel, out_shape=jax.ShapeDtypeStruct((tiles, QB + 1, LAN...  3.13 us
    ppermute x5, waiting for transfers between devices, swap(): return lax.ppermute(x, 'psg', [(j, j ^ k) for j in range(shards)])  3.12 us
    pallas_call x1, Pallas kernels, prepare(): pl.pallas_call(prepare_kernel, out_shape=[jax.ShapeDtypeStruct((shards, L...  1.8 us
    pallas_call x1, Pallas kernels, place(): pl.pallas_call(place_kernel, out_shape=jax.ShapeDtypeStruct((shards, QB,...  0.81 us
  transfers between devices with their start and end apart: 5, of which 2 were waited for; matrix products, arithmetic and copies ran while one was open for 0% of the time, Pallas kernels for 11%

profile of v6, /device:TPU:0, one launch (start us, length us, event | category | flops | bytes accessed | tf_op | source)
XLA Modules:
  0.0 30.5 jit_solution(11605263837726927801)
XLA Ops:
  0.0 0.0 copy-start
  0.0 5.0 %collective-permute-start.3 = (bf16[256,128]{1,0:T(8,128)(2,1)}, bf16[256,128]{1,0:T(8,128)(2,1)S(1)}, u32[]{:S(2)}, u32[]{:S(2)}) collective-permute-start(bf16[256,128]{1,0:T(8,128)(2,1)} %bitcast.5), channel_id=1, source_target_pairs={{0,12},{2,14},{4,8},{6,10},{8,4},{10,6},{12,0},{14,2},{1,13},{3,15... | collective-permute-start | bytes 196616 | tf_op jit(solution)/shard_map/ppermute | solution.py:219
  5.1 0.0 collective-permute-start.2
  5.1 0.6 %collective-permute-start.1 = (bf16[256,128]{1,0:T(8,128)(2,1)}, bf16[256,128]{1,0:T(8,128)(2,1)S(1)}, u32[]{:S(2)}, u32[]{:S(2)}) collective-permute-start(bf16[256,128]{1,0:T(8,128)(2,1)} %bitcast.7), channel_id=1, source_target_pairs={{0,4},{2,6},{4,0},{6,2},{8,12},{10,14},{12,8},{14,10},{1,5},{3,7},... | collective-permute-start | bytes 196616 | tf_op jit(solution)/shard_map/ppermute | solution.py:219
  5.7 1.6 %collective-permute-start = (s32[8,32]{1,0:T(8,128)}, s32[8,32]{1,0:T(8,128)S(1)}, u32[]{:S(2)}, u32[]{:S(2)}) collective-permute-start(s32[8,32]{1,0:T(8,128)} %bitcast.10), channel_id=1, source_target_pairs={{0,2},{2,0},{4,6},{6,4},{8,10},{10,8},{12,14},{14,12},{1,3},{3,1},... | collective-permute-start | bytes 3080 | tf_op jit(solution)/shard_map/ppermute | solution.py:219
  7.3 2.2 %collective-permute-done.refs_1_ = s32[8,32]{1,0:T(8,128)S(1)} collective-permute-done((s32[8,32]{1,0:T(8,128)}, s32[8,32]{1,0:T(8,128)S(1)}, u32[]{:S(2)}, u32[]{:S(2)}) %collective-permute-start) | collective-permute-done | bytes 1056 | tf_op jit(solution)/shard_map/ppermute | solution.py:219
  9.5 1.8 %shard_map.46 = (f32[8,128]{1,0:T(8,128)S(1)}, s32[8,128]{1,0:T(8,128)S(1)}, s32[8,128]{1,0:T(8,128)S(1)}, bf16[128,64,128]{2,1,0:T(8,128)(2,1)S(1)}) custom-call(s32[8,32]{1,0:T(8,128)} %bitcast.11, s32[8,32]{1,0:T(8,128)S(1)} %collective-permute-done.refs_1_, s32[128]{0:T(128)} %refs_2_.1, bf16[128,64,128]{2,1,0:T(8,128)(2,1)} %refs_3_.1), custom_call_target="tpu_custom_call" | custom-call | flops 1048576 | bytes 2097152 | tf_op jit(solution)/shard_map/pallas_call | solution.py:79
  11.3 0.0 collective-permute-done.3.refs_3_
  11.3 0.0 collective-permute-done.2.refs_2_
  11.3 0.0 collective-permute-done.1.refs_1_
  11.3 0.0 copy-done
  11.3 0.2 shard_map.47
  11.6 1.7 %collective-permute-start.4 = (bf16[256,128]{1,0:T(8,128)(2,1)S(1)}, bf16[256,128]{1,0:T(8,128)(2,1)S(1)}, u32[]{:S(2)}, u32[]{:S(2)}) collective-permute-start(bf16[256,128]{1,0:T(8,128)(2,1)S(1)} %shard_map.47), channel_id=1, source_target_pairs={{0,2},{2,0},{4,6},{6,4},{8,10},{10,8},{12,14},{14,12},{1,3},{3,1},... | collective-permute-start | bytes 196616 | tf_op jit(solution)/shard_map/ppermute | solution.py:219
  13.3 1.7 %shard_map.48.earlier_ref = f32[4,3,128]{2,1,0:T(4,128)S(1)} custom-call(f32[8,128]{1,0:T(8,128)S(1)} %get-tuple-element.15.slots_ref, s32[8,128]{1,0:T(8,128)S(1)} %get-tuple-element.22.picks_ref, bf16[128,64,128]{2,1,0:T(8,128)(2,1)S(1)} %get-tuple-element.17.p_ref, bf16[256,128]{1,0:T(8,128)(2,1)S(1)} %bitcast.9, ...), custom_call_target="tpu_custom_call" | custom-call | flops 536870912 | bytes 2097152 | tf_op jit(solution)/shard_map/pallas_call | solution.py:179
  15.0 0.9 %collective-permute-done.4.sel_ref = bf16[256,128]{1,0:T(8,128)(2,1)S(1)} collective-permute-done((bf16[256,128]{1,0:T(8,128)(2,1)S(1)}, bf16[256,128]{1,0:T(8,128)(2,1)S(1)}, u32[]{:S(2)}, u32[]{:S(2)}) %collective-permute-start.4) | collective-permute-done | bytes 65568 | tf_op jit(solution)/shard_map/ppermute | solution.py:219
  15.9 1.5 %shard_map.49 = f32[8,3,128]{2,1,0:T(4,128)S(1)} custom-call(f32[8,128]{1,0:T(8,128)S(1)} %get-tuple-element.15.slots_ref, bf16[128,64,128]{2,1,0:T(8,128)(2,1)S(1)} %get-tuple-element.17.p_ref, bf16[256,128]{1,0:T(8,128)(2,1)S(1)} %collective-permute-done.4.sel_ref, f32[4,3,128]{2,1,0:T(4,128)S(1)} %shard_map.48.earlier_ref), custom_call_target="tpu_custom_call" | custom-call | flops 536870912 | bytes 2097152 | tf_op jit(solution)/shard_map/pallas_call | solution.py:179
  17.4 12.4 %all_to_all.5.in_ref = f32[8,3,128]{2,1,0:T(4,128)S(1)} all-to-all(f32[8,3,128]{2,1,0:T(4,128)S(1)} %shard_map.49), channel_id=1, replica_groups=mesh['grp'=2,'psg'=8,'qry'=2] {'psg'}, dimensions={0} | all-to-all | bytes 24576 | tf_op jit(solution)/shard_map/all_to_all | solution.py:256
  29.7 0.8 %shard_map.50 = f32[8,2,16,32]{3,2,1,0:T(8,128)} custom-call(f32[8,3,128]{2,1,0:T(4,128)S(1)} %all_to_all.5.in_ref), custom_call_target="tpu_custom_call" | custom-call | tf_op jit(solution)/shard_map/pallas_call | solution.py:208
Async XLA Ops:
  0.0 11.3 %copy-start = (bf16[8,32,128]{2,1,0:T(8,128)(2,1)S(1)}, bf16[8,32,128]{2,1,0:T(8,128)(2,1)}, u32[]{:S(2)}) copy-start(bf16[8,32,128]{2,1,0:T(8,128)(2,1)} %param.4) | copy-start | bytes 196612
  0.0 11.3 %collective-permute-start.3 = (bf16[256,128]{1,0:T(8,128)(2,1)}, bf16[256,128]{1,0:T(8,128)(2,1)S(1)}, u32[]{:S(2)}, u32[]{:S(2)}) collective-permute-start(bf16[256,128]{1,0:T(8,128)(2,1)} %bitcast.5), channel_id=1, source_target_pairs={{0,12},{2,14},{4,8},{6,10},{8,4},{10,6},{12,0},{14,2},{1,13},{3,15... | collective-permute-start | bytes 196616 | tf_op jit(solution)/shard_map/ppermute | solution.py:219
  5.1 6.3 %collective-permute-start.2 = (bf16[256,128]{1,0:T(8,128)(2,1)}, bf16[256,128]{1,0:T(8,128)(2,1)S(1)}, u32[]{:S(2)}, u32[]{:S(2)}) collective-permute-start(bf16[256,128]{1,0:T(8,128)(2,1)} %bitcast.6), channel_id=1, source_target_pairs={{0,8},{2,10},{4,12},{6,14},{8,0},{10,2},{12,4},{14,6},{1,9},{3,11}... | collective-permute-start | bytes 196616 | tf_op jit(solution)/shard_map/ppermute | solution.py:219
  5.1 6.3 %collective-permute-start.1 = (bf16[256,128]{1,0:T(8,128)(2,1)}, bf16[256,128]{1,0:T(8,128)(2,1)S(1)}, u32[]{:S(2)}, u32[]{:S(2)}) collective-permute-start(bf16[256,128]{1,0:T(8,128)(2,1)} %bitcast.7), channel_id=1, source_target_pairs={{0,4},{2,6},{4,0},{6,2},{8,12},{10,14},{12,8},{14,10},{1,5},{3,7},... | collective-permute-start | bytes 196616 | tf_op jit(solution)/shard_map/ppermute | solution.py:219
  5.7 3.8 %collective-permute-start = (s32[8,32]{1,0:T(8,128)}, s32[8,32]{1,0:T(8,128)S(1)}, u32[]{:S(2)}, u32[]{:S(2)}) collective-permute-start(s32[8,32]{1,0:T(8,128)} %bitcast.10), channel_id=1, source_target_pairs={{0,2},{2,0},{4,6},{6,4},{8,10},{10,8},{12,14},{14,12},{1,3},{3,1},... | collective-permute-start | bytes 3080 | tf_op jit(solution)/shard_map/ppermute | solution.py:219
  11.6 4.3 %collective-permute-start.4 = (bf16[256,128]{1,0:T(8,128)(2,1)S(1)}, bf16[256,128]{1,0:T(8,128)(2,1)S(1)}, u32[]{:S(2)}, u32[]{:S(2)}) collective-permute-start(bf16[256,128]{1,0:T(8,128)(2,1)S(1)} %shard_map.47), channel_id=1, source_target_pairs={{0,2},{2,0},{4,6},{6,4},{8,10},{10,8},{12,14},{14,12},{1,3},{3,1},... | collective-permute-start | bytes 196616 | tf_op jit(solution)/shard_map/ppermute | solution.py:219

commit v7 on v6

--- a/solution.py
+++ b/solution.py
@@ -18,11 +18,9 @@
 GROUP = 8
 
 
-def prepare_kernel(*refs):
-    several = (len(refs) - 8) // 2
-    *cand_refs, len_hbm, p_hbm, slots_ref = refs[:several + 3]
-    picks_refs = refs[several + 3:-5]
-    clean_ref, len_ref, raw_ref, cand_ref, sems = refs[-5:]
+def prepare_kernel(
+    cand_hbm, len_hbm, p_hbm, slots_ref, picks_ref, clean_ref, cand_ref, len_ref, raw_ref, sems
+):
     rows = cand_ref.shape[0]
     shards = slots_ref.shape[0]
     groups = p_hbm.shape[0] // GROUP
@@ -31,7 +29,7 @@
         part = pl.ds(g * GROUP, GROUP)
         return pltpu.make_async_copy(p_hbm.at[part], raw_ref.at[part], sems.at[g])
 
-    fetch_cand = pltpu.make_async_copy(cand_refs[0], cand_ref, sems.at[groups])
+    fetch_cand = pltpu.make_async_copy(cand_hbm, cand_ref, sems.at[groups])
     fetch_len = pltpu.make_async_copy(len_hbm, len_ref, sems.at[groups + 1])
     fetch_cand.start()
     fetch_len.start()
@@ -39,25 +37,22 @@
         fetch(g).start()
 
     fetch_cand.wait()
+    cand = cand_ref[...]
+    owner = cand // QBD
+    block = cand - owner * QBD
     lane = lax.broadcasted_iota(jnp.int32, (rows, LANES), 1).astype(jnp.float32)
     sub = lax.broadcasted_iota(jnp.int32, (rows, LANES), 0)
-    for n, picks_ref in enumerate(picks_refs):
-        cand = (cand_refs[n] if n else cand_ref)[...]
-        owner = cand // QBD
-        block = cand - owner * QBD
-        for o in range(shards):
-            mine = owner == o
-            named = jnp.max(jnp.where(mine, block, 0), axis=1, keepdims=True)
-            picks_ref[o:o + 1, :] = jnp.broadcast_to(jnp.max(named, axis=0, keepdims=True), (1, LANES))
-            if n:
-                continue
-            named_here = jnp.sum(jnp.where(mine, 1.0, 0.0), axis=1, keepdims=True)
-            upto = jnp.broadcast_to(named_here, (rows, LANES))
-            step = 1
-            while step < rows:
-                upto = upto + jnp.where(sub >= step, pltpu.roll(upto, step, 0), 0.0)
-                step *= 2
-            slots_ref[o:o + 1, :] = jnp.sum(jnp.where(upto <= lane, 1.0, 0.0), axis=0, keepdims=True)
+    for o in range(shards):
+        mine = owner == o
+        named = jnp.max(jnp.where(mine, block, 0), axis=1, keepdims=True)
+        picks_ref[o:o + 1, :] = jnp.broadcast_to(jnp.max(named, axis=0, keepdims=True), (1, LANES))
+        named_here = jnp.sum(jnp.where(mine, 1.0, 0.0), axis=1, keepdims=True)
+        upto = jnp.broadcast_to(named_here, (rows, LANES))
+        step = 1
+        while step < rows:
+            upto = upto + jnp.where(sub >= step, pltpu.roll(upto, step, 0), 0.0)
+            step *= 2
+        slots_ref[o:o + 1, :] = jnp.sum(jnp.where(upto <= lane, 1.0, 0.0), axis=0, keepdims=True)
 
     fetch_len.wait()
     u = lax.broadcasted_iota(jnp.int32, (PT, LANES), 0)
@@ -71,29 +66,28 @@
             clean_ref[p] = jnp.where(u < len_ref[p], tokens, tokens[0:1]).astype(jnp.bfloat16)
 
 
-def prepare(shards, lengths, passages, *candidates):
+def prepare(shards, candidates, lengths, passages):
     hbm = pl.BlockSpec(memory_space=pltpu.HBM)
     vmem = pl.BlockSpec(memory_space=pltpu.VMEM)
-    kept = [pltpu.with_memory_space_constraint(x, pltpu.HBM) for x in (candidates[0], lengths, passages)]
-    more = candidates[1:]
+    operands = [pltpu.with_memory_space_constraint(x, pltpu.HBM) for x in (candidates, lengths, passages)]
     return pl.pallas_call(
         prepare_kernel,
         out_shape=[
             jax.ShapeDtypeStruct((shards, LANES), jnp.float32),
-            *[jax.ShapeDtypeStruct((shards, LANES), jnp.int32) for _ in candidates],
+            jax.ShapeDtypeStruct((shards, LANES), jnp.int32),
             jax.ShapeDtypeStruct(passages.shape, passages.dtype),
         ],
-        in_specs=[hbm] + [vmem] * len(more) + [hbm] * 2,
-        out_specs=[vmem] * (2 + len(candidates)),
+        in_specs=[hbm] * 3,
+        out_specs=[vmem] * 3,
         scratch_shapes=[
+            pltpu.VMEM(candidates.shape, candidates.dtype),
             pltpu.SMEM(lengths.shape, lengths.dtype),
             pltpu.VMEM(passages.shape, passages.dtype),
-            pltpu.VMEM(candidates[0].shape, candidates[0].dtype),
             pltpu.SemaphoreType.DMA((passages.shape[0] // GROUP + 2,)),
         ],
         compiler_params=pltpu.CompilerParams(vmem_limit_bytes=24 * 1024 * 1024),
         cost_estimate=pl.CostEstimate(flops=passages.size, bytes_accessed=2 * passages.size, transcendentals=0),
-    )(kept[0], *more, *kept[1:])
+    )(*operands)
 
 
 def picked(picks_ref, owner, q_ref):
@@ -101,14 +95,18 @@
     return q_ref[pl.ds(pick * QB * QT, QB * QT), :]
 
 
-def pack_kernel(partners, picks_ref, *refs):
+def pack_kernel(partners, cand_ref, *refs):
     q_refs, out_ref = refs[:-1], refs[-1]
     me = lax.axis_index("psg")
-    for n, k in enumerate(partners):
-        out_ref[n * QB * QT:(n + 1) * QB * QT, :] = picked(picks_ref, me ^ k, q_refs[n])
-
-
-def pack(partners, picks, blocks):
+    cand = cand_ref[...]
+    owner = cand // QBD
+    block = cand - owner * QBD
+    for n, k in enumerate(partners):
+        pick = jnp.max(jnp.where(owner == me ^ k, block, 0))
+        out_ref[n * QB * QT:(n + 1) * QB * QT, :] = q_refs[n][pl.ds(pick * QB * QT, QB * QT), :]
+
+
+def pack(partners, candidates, blocks):
     vmem = pl.BlockSpec(memory_space=pltpu.VMEM)
     return pl.pallas_call(
         functools.partial(pack_kernel, partners),
@@ -116,7 +114,7 @@
         in_specs=[vmem] * (1 + len(blocks)),
         out_specs=vmem,
         compiler_params=pltpu.CompilerParams(vmem_limit_bytes=4 * 1024 * 1024),
-    )(picks, *blocks)
+    )(candidates, *blocks)
 
 
 def score_picked(sel_ref, p_ref, max_ref):
@@ -221,10 +219,10 @@
     near = list(range(0, shards, 2))
     theirs = swap(candidates, 1)
     queries = {0: own} | {k: swap(own, k) for k in reversed(near[1:])}
-    slots, picks, their_picks, clean = prepare(shards, lengths, passages, candidates, theirs)
+    slots, picks, clean = prepare(shards, candidates, lengths, passages)
     *arrived, clean = lax.optimization_barrier((*[queries[k] for k in near[1:]], clean))
     blocks = [own, *arrived]
-    far = swap(pack(near, their_picks, blocks), 1)
+    far = swap(pack(near, theirs, blocks), 1)
     tiles = score(
         functools.partial(score_kernel, near), len(near), len(near), 1, clean, slots, picks, clean, *blocks
     )
@@ -235,7 +233,7 @@
 
 
 def by_gather(own, shards, candidates, lengths, passages):
-    slots, picks, clean = prepare(shards, lengths, passages, candidates)
+    slots, picks, clean = prepare(shards, candidates, lengths, passages)
     gathered = lax.all_gather(own, "psg", axis=0)
     some = min(shards, 8)
 

time: 30.7 us -> 29.2 us (0.951)
  blocking collectives: 12.4 us -> 11.2 us
    all_to_all x1, blocking collectives: 12.4 us -> 11.2 us  [per_device(): lax.all_to_all(tiles, 'psg', split_axis=0, concat_axis=0, tiled=True)]
  transfers between devices with their start and end apart: 5 -> 5, of which waited for: 2 -> 2; matrix products, arithmetic and copies ran while one was open for 0% -> 0% of each run, Pallas kernels for 11% -> 12%
where the time goes in v7:
time: 29.2 us; the launch traced here: 29 us
  blocking collectives  11.2 us (38%)
  starting transfers between devices  8.88 us (30%)
  Pallas kernels  5.95 us (20%)
  waiting for transfers between devices  2.91 us (10%)
    all_to_all x1, blocking collectives, per_device(): lax.all_to_all(tiles, 'psg', split_axis=0, concat_axis=0, tiled=True)  11.2 us
    ppermute x5, starting transfers between devices, swap(): return lax.ppermute(x, 'psg', [(j, j ^ k) for j in range(shards)])  8.88 us
    pallas_call x2, Pallas kernels, score(): pl.pallas_call(kernel, out_shape=jax.ShapeDtypeStruct((tiles, QB + 1, LAN...  3.13 us
    ppermute x5, waiting for transfers between devices, swap(): return lax.ppermute(x, 'psg', [(j, j ^ k) for j in range(shards)])  2.91 us
    pallas_call x1, Pallas kernels, prepare(): pl.pallas_call(prepare_kernel, out_shape=[jax.ShapeDtypeStruct((shards, L...  1.8 us
    pallas_call x1, Pallas kernels, place(): pl.pallas_call(place_kernel, out_shape=jax.ShapeDtypeStruct((shards, QB,...  0.81 us
  transfers between devices with their start and end apart: 5, of which 2 were waited for; matrix products, arithmetic and copies ran while one was open for 0% of the time, Pallas kernels for 12%

profile of v7, /device:TPU:0, one launch (start us, length us, event | category | flops | bytes accessed | tf_op | source)
XLA Modules:
  0.0 29.0 jit_solution(6649319566706439143)
XLA Ops:
  0.0 0.0 copy-start
  0.0 5.0 %collective-permute-start.2 = (bf16[256,128]{1,0:T(8,128)(2,1)}, bf16[256,128]{1,0:T(8,128)(2,1)S(1)}, u32[]{:S(2)}, u32[]{:S(2)}) collective-permute-start(bf16[256,128]{1,0:T(8,128)(2,1)} %bitcast.5), channel_id=1, source_target_pairs={{0,12},{2,14},{4,8},{6,10},{8,4},{10,6},{12,0},{14,2},{1,13},{3,15... | collective-permute-start | bytes 196616 | tf_op jit(solution)/shard_map/ppermute | solution.py:217
  5.1 0.0 collective-permute-start.1
  5.1 0.6 %collective-permute-start = (bf16[256,128]{1,0:T(8,128)(2,1)}, bf16[256,128]{1,0:T(8,128)(2,1)S(1)}, u32[]{:S(2)}, u32[]{:S(2)}) collective-permute-start(bf16[256,128]{1,0:T(8,128)(2,1)} %bitcast.7), channel_id=1, source_target_pairs={{0,4},{2,6},{4,0},{6,2},{8,12},{10,14},{12,8},{14,10},{1,5},{3,7},... | collective-permute-start | bytes 196616 | tf_op jit(solution)/shard_map/ppermute | solution.py:217
  5.7 1.6 %collective-permute-start.3 = (s32[8,32]{1,0:T(8,128)}, s32[8,32]{1,0:T(8,128)S(1)}, u32[]{:S(2)}, u32[]{:S(2)}) collective-permute-start(s32[8,32]{1,0:T(8,128)} %bitcast.10), channel_id=1, source_target_pairs={{0,2},{2,0},{4,6},{6,4},{8,10},{10,8},{12,14},{14,12},{1,3},{3,1},... | collective-permute-start | bytes 3080 | tf_op jit(solution)/shard_map/ppermute | solution.py:217
  7.3 1.8 %shard_map.46 = (f32[8,128]{1,0:T(8,128)S(1)}, s32[8,128]{1,0:T(8,128)S(1)}, bf16[128,64,128]{2,1,0:T(8,128)(2,1)S(1)}) custom-call(s32[8,32]{1,0:T(8,128)} %bitcast.11, s32[128]{0:T(128)} %len_hbm.1, bf16[128,64,128]{2,1,0:T(8,128)(2,1)} %p_hbm.1), custom_call_target="tpu_custom_call" | custom-call | flops 1048576 | bytes 2097152 | tf_op jit(solution)/shard_map/pallas_call | solution.py:73
  9.1 0.0 collective-permute-done.2.refs_3_
  9.1 1.8 %collective-permute-done.1.refs_2_ = bf16[256,128]{1,0:T(8,128)(2,1)S(1)} collective-permute-done((bf16[256,128]{1,0:T(8,128)(2,1)}, bf16[256,128]{1,0:T(8,128)(2,1)S(1)}, u32[]{:S(2)}, u32[]{:S(2)}) %collective-permute-start.1) | collective-permute-done | bytes 65568 | tf_op jit(solution)/shard_map/ppermute | solution.py:217
  10.9 0.0 collective-permute-done.refs_1_
  10.9 0.0 collective-permute-done.3.cand_ref
  10.9 0.0 copy-done
  10.9 0.2 shard_map.47
  11.2 1.6 %collective-permute-start.4 = (bf16[256,128]{1,0:T(8,128)(2,1)S(1)}, bf16[256,128]{1,0:T(8,128)(2,1)S(1)}, u32[]{:S(2)}, u32[]{:S(2)}) collective-permute-start(bf16[256,128]{1,0:T(8,128)(2,1)S(1)} %shard_map.47), channel_id=1, source_target_pairs={{0,2},{2,0},{4,6},{6,4},{8,10},{10,8},{12,14},{14,12},{1,3},{3,1},... | collective-permute-start | bytes 196616 | tf_op jit(solution)/shard_map/ppermute | solution.py:217
  12.7 1.7 %shard_map.48.earlier_ref = f32[4,3,128]{2,1,0:T(4,128)S(1)} custom-call(f32[8,128]{1,0:T(8,128)S(1)} %get-tuple-element.14.slots_ref, s32[8,128]{1,0:T(8,128)S(1)} %get-tuple-element.20.picks_ref, bf16[128,64,128]{2,1,0:T(8,128)(2,1)S(1)} %get-tuple-element.16.p_ref, bf16[256,128]{1,0:T(8,128)(2,1)S(1)} %bitcast.9, ...), custom_call_target="tpu_custom_call" | custom-call | flops 536870912 | bytes 2097152 | tf_op jit(solution)/shard_map/pallas_call | solution.py:177
  14.4 1.1 %collective-permute-done.4.sel_ref = bf16[256,128]{1,0:T(8,128)(2,1)S(1)} collective-permute-done((bf16[256,128]{1,0:T(8,128)(2,1)S(1)}, bf16[256,128]{1,0:T(8,128)(2,1)S(1)}, u32[]{:S(2)}, u32[]{:S(2)}) %collective-permute-start.4) | collective-permute-done | bytes 65568 | tf_op jit(solution)/shard_map/ppermute | solution.py:217
  15.5 1.5 %shard_map.49 = f32[8,3,128]{2,1,0:T(4,128)S(1)} custom-call(f32[8,128]{1,0:T(8,128)S(1)} %get-tuple-element.14.slots_ref, bf16[128,64,128]{2,1,0:T(8,128)(2,1)S(1)} %get-tuple-element.16.p_ref, bf16[256,128]{1,0:T(8,128)(2,1)S(1)} %collective-permute-done.4.sel_ref, f32[4,3,128]{2,1,0:T(4,128)S(1)} %shard_map.48.earlier_ref), custom_call_target="tpu_custom_call" | custom-call | flops 536870912 | bytes 2097152 | tf_op jit(solution)/shard_map/pallas_call | solution.py:177
  17.0 11.2 %all_to_all.5.in_ref = f32[8,3,128]{2,1,0:T(4,128)S(1)} all-to-all(f32[8,3,128]{2,1,0:T(4,128)S(1)} %shard_map.49), channel_id=1, replica_groups=mesh['grp'=2,'psg'=8,'qry'=2] {'psg'}, dimensions={0} | all-to-all | bytes 24576 | tf_op jit(solution)/shard_map/all_to_all | solution.py:254
  28.2 0.8 %shard_map.50 = f32[8,2,16,32]{3,2,1,0:T(8,128)} custom-call(f32[8,3,128]{2,1,0:T(4,128)S(1)} %all_to_all.5.in_ref), custom_call_target="tpu_custom_call" | custom-call | tf_op jit(solution)/shard_map/pallas_call | solution.py:206
Async XLA Ops:
  0.0 10.9 %copy-start = (bf16[8,32,128]{2,1,0:T(8,128)(2,1)S(1)}, bf16[8,32,128]{2,1,0:T(8,128)(2,1)}, u32[]{:S(2)}) copy-start(bf16[8,32,128]{2,1,0:T(8,128)(2,1)} %param.4) | copy-start | bytes 196612
  0.0 9.1 %collective-permute-start.2 = (bf16[256,128]{1,0:T(8,128)(2,1)}, bf16[256,128]{1,0:T(8,128)(2,1)S(1)}, u32[]{:S(2)}, u32[]{:S(2)}) collective-permute-start(bf16[256,128]{1,0:T(8,128)(2,1)} %bitcast.5), channel_id=1, source_target_pairs={{0,12},{2,14},{4,8},{6,10},{8,4},{10,6},{12,0},{14,2},{1,13},{3,15... | collective-permute-start | bytes 196616 | tf_op jit(solution)/shard_map/ppermute | solution.py:217
  5.1 5.9 %collective-permute-start.1 = (bf16[256,128]{1,0:T(8,128)(2,1)}, bf16[256,128]{1,0:T(8,128)(2,1)S(1)}, u32[]{:S(2)}, u32[]{:S(2)}) collective-permute-start(bf16[256,128]{1,0:T(8,128)(2,1)} %bitcast.6), channel_id=1, source_target_pairs={{0,8},{2,10},{4,12},{6,14},{8,0},{10,2},{12,4},{14,6},{1,9},{3,11}... | collective-permute-start | bytes 196616 | tf_op jit(solution)/shard_map/ppermute | solution.py:217
  5.1 5.9 %collective-permute-start = (bf16[256,128]{1,0:T(8,128)(2,1)}, bf16[256,128]{1,0:T(8,128)(2,1)S(1)}, u32[]{:S(2)}, u32[]{:S(2)}) collective-permute-start(bf16[256,128]{1,0:T(8,128)(2,1)} %bitcast.7), channel_id=1, source_target_pairs={{0,4},{2,6},{4,0},{6,2},{8,12},{10,14},{12,8},{14,10},{1,5},{3,7},... | collective-permute-start | bytes 196616 | tf_op jit(solution)/shard_map/ppermute | solution.py:217
  5.7 5.3 %collective-permute-start.3 = (s32[8,32]{1,0:T(8,128)}, s32[8,32]{1,0:T(8,128)S(1)}, u32[]{:S(2)}, u32[]{:S(2)}) collective-permute-start(s32[8,32]{1,0:T(8,128)} %bitcast.10), channel_id=1, source_target_pairs={{0,2},{2,0},{4,6},{6,4},{8,10},{10,8},{12,14},{14,12},{1,3},{3,1},... | collective-permute-start | bytes 3080 | tf_op jit(solution)/shard_map/ppermute | solution.py:217
  11.2 4.3 %collective-permute-start.4 = (bf16[256,128]{1,0:T(8,128)(2,1)S(1)}, bf16[256,128]{1,0:T(8,128)(2,1)S(1)}, u32[]{:S(2)}, u32[]{:S(2)}) collective-permute-start(bf16[256,128]{1,0:T(8,128)(2,1)S(1)} %shard_map.47), channel_id=1, source_target_pairs={{0,2},{2,0},{4,6},{6,4},{8,10},{10,8},{12,14},{14,12},{1,3},{3,1},... | collective-permute-start | bytes 196616 | tf_op jit(solution)/shard_map/ppermute | solution.py:217

commit v8 on v7

--- a/solution.py
+++ b/solution.py
@@ -152,13 +152,12 @@
         out_ref[n, QB:QB + 1, :] = slots_ref[pl.ds(me ^ k, 1), :]
 
 
-def join_kernel(partners, slots_ref, p_ref, sel_ref, earlier_ref, out_ref, max_ref):
+def score_far_kernel(partners, slots_ref, p_ref, sel_ref, out_ref, max_ref):
     me = lax.axis_index("psg")
     total = score_picked(sel_ref, p_ref, max_ref)
     for n, k in enumerate(partners):
-        out_ref[me ^ k, 0:QB, :] = total[n * QB:(n + 1) * QB]
-        out_ref[me ^ k, QB:QB + 1, :] = slots_ref[pl.ds(me ^ k, 1), :]
-        out_ref[me ^ k ^ 1] = earlier_ref[n]
+        out_ref[n, 0:QB, :] = total[n * QB:(n + 1) * QB]
+        out_ref[n, QB:QB + 1, :] = slots_ref[pl.ds(me ^ k, 1), :]
 
 
 def all_kernel(slots_ref, picks_ref, p_ref, q_ref, out_ref, sel_ref, max_ref):
@@ -189,30 +188,56 @@
     )(*more)
 
 
-def place_kernel(in_ref, out_ref):
+def collect(tiles):
+    arrays = {id(array): array for array, _, _ in tiles}
+    places = {key: n for n, key in enumerate(arrays)}
+    return list(arrays.values()), [(places[id(array)], n, source) for array, n, source in tiles]
+
+
+def join_kernel(tiles, *refs):
+    for n, (array, index, _) in enumerate(tiles):
+        refs[-1][n] = refs[array][index]
+
+
+def join(tiles):
+    arrays, tiles = collect(tiles)
+    vmem = pl.BlockSpec(memory_space=pltpu.VMEM)
+    return pl.pallas_call(
+        functools.partial(join_kernel, tiles),
+        out_shape=jax.ShapeDtypeStruct((len(tiles), QB + 1, LANES), jnp.float32),
+        in_specs=[vmem] * len(arrays),
+        out_specs=vmem,
+        compiler_params=pltpu.CompilerParams(vmem_limit_bytes=4 * 1024 * 1024),
+    )(*arrays)
+
+
+def place_kernel(tiles, paired, *refs):
+    out_ref = refs[-1]
     slots = out_ref.shape[-1]
+    me = lax.axis_index("psg") if paired else 0
     m = lax.broadcasted_iota(jnp.int32, (PBS, LANES), 0)
-    for j in range(in_ref.shape[0]):
-        row = in_ref[j, QB:QB + 1, :].astype(jnp.int32)
+    for array, index, source in tiles:
+        tile_ref = refs[array].at[index]
+        row = tile_ref[QB:QB + 1, :].astype(jnp.int32)
         where = jnp.minimum(row * PBS, LANES - PBS) + m
         for i in range(QB):
-            tile = jnp.broadcast_to(in_ref[j, i:i + 1, :], (PBS, LANES))
-            out_ref[j, i] = jnp.take_along_axis(tile, where, axis=1)[:, :slots]
-
-
-def place(tiles, slots):
-    vmem = pl.BlockSpec(memory_space=pltpu.VMEM)
-    shards = tiles.shape[0]
-    return pl.pallas_call(
-        place_kernel,
-        out_shape=jax.ShapeDtypeStruct((shards, QB, PBS, slots), jnp.float32),
-        in_specs=[vmem],
+            tile = jnp.broadcast_to(tile_ref[i:i + 1, :], (PBS, LANES))
+            out_ref[me ^ source, i] = jnp.take_along_axis(tile, where, axis=1)[:, :slots]
+
+
+def place(tiles, paired, slots):
+    arrays, tiles = collect(tiles)
+    vmem = pl.BlockSpec(memory_space=pltpu.VMEM)
+    return pl.pallas_call(
+        functools.partial(place_kernel, tiles, paired),
+        out_shape=jax.ShapeDtypeStruct((len(tiles), QB, PBS, slots), jnp.float32),
+        in_specs=[vmem] * len(arrays),
         out_specs=vmem,
         compiler_params=pltpu.CompilerParams(vmem_limit_bytes=8 * 1024 * 1024),
-    )(tiles)
-
-
-def by_partners(own, shards, candidates, lengths, passages):
+    )(*arrays)
+
+
+def by_partners(own, shards, slot_count, candidates, lengths, passages):
     def swap(x, k):
         return lax.ppermute(x, "psg", [(j, j ^ k) for j in range(shards)])
 
@@ -223,16 +248,27 @@
     *arrived, clean = lax.optimization_barrier((*[queries[k] for k in near[1:]], clean))
     blocks = [own, *arrived]
     far = swap(pack(near, theirs, blocks), 1)
-    tiles = score(
+    near_tiles = score(
         functools.partial(score_kernel, near), len(near), len(near), 1, clean, slots, picks, clean, *blocks
     )
-    far, tiles = lax.optimization_barrier((far, tiles))
-    return score(
-        functools.partial(join_kernel, [k + 1 for k in near]), shards, len(near), 0, clean, slots, clean, far, tiles
+    far, near_tiles = lax.optimization_barrier((far, near_tiles))
+    far_tiles = score(
+        functools.partial(score_far_kernel, [k + 1 for k in near]), len(near), len(near), 0, clean, slots, clean, far
     )
-
-
-def by_gather(own, shards, candidates, lengths, passages):
+    joined = swap(far_tiles, 1)
+    tiles = {k: [(near_tiles, n, 0), (joined, n, 1)] for n, k in enumerate(near)}
+    step = 2
+    while step < shards:
+        across = [k for k in tiles if k & step]
+        handed = [(k ^ step, source ^ step) for k in across for _, _, source in tiles[k]]
+        joined = swap(join([tile for k in across for tile in tiles.pop(k)]), step)
+        for n, (k, source) in enumerate(handed):
+            tiles[k].append((joined, n, source))
+        step *= 2
+    return place(tiles[0], True, slot_count)
+
+
+def by_gather(own, shards, slot_count, candidates, lengths, passages):
     slots, picks, clean = prepare(shards, candidates, lengths, passages)
     gathered = lax.all_gather(own, "psg", axis=0)
     some = min(shards, 8)
@@ -241,18 +277,20 @@
         return score(all_kernel, some, some, 1, clean, items[0], items[1], clean, items[2])
 
     parts = [x.reshape(shards // some, some, *x.shape[1:]) for x in (slots, picks, gathered)]
-    return lax.map(score_some, parts).reshape(shards, QB + 1, LANES)
+    tiles = lax.map(score_some, parts).reshape(shards, QB + 1, LANES)
+    tiles = lax.all_to_all(tiles, "psg", split_axis=0, concat_axis=0, tiled=True)
+    return place([(tiles, n, n) for n in range(shards)], False, slot_count)
 
 
 def per_device(queries, passages, lengths, candidates):
     shards = lax.axis_size("psg")
     rows = passages.shape[0] // PBS
     form = by_partners if shards in (4, 8) else by_gather
-    tiles = form(
-        queries.reshape(QBD * QB * QT, DIM), shards, candidates.reshape(rows, KB), lengths, passages
+    placed = form(
+        queries.reshape(QBD * QB * QT, DIM), shards, rows * KB // shards,
+        candidates.reshape(rows, KB), lengths, passages,
     )
-    tiles = lax.all_to_all(tiles, "psg", split_axis=0, concat_axis=0, tiled=True)
-    return place(tiles, rows * KB // shards).transpose(0, 3, 1, 2)[None]
+    return placed.transpose(0, 3, 1, 2)[None]
 
 
 def solution(mesh):

time: 29.2 us -> 29.8 us (1.021)
  blocking collectives: 11.2 us -> 0 us
  waiting for transfers between devices: 2.91 us -> 10.8 us
  starting transfers between devices: 8.88 us -> 12.9 us
    all_to_all x1 -> x0, blocking collectives: 11.2 us -> none  [per_device(): lax.all_to_all(tiles, 'psg', split_axis=0, concat_axis=0, tiled=True)]
    ppermute x5 -> x8, waiting for transfers between devices: 2.91 us -> 10.8 us  [swap(): return lax.ppermute(x, 'psg', [(j, j ^ k) for j in range(shards)])]
    ppermute x5 -> x8, starting transfers between devices: 8.88 us -> 12.9 us  [swap(): return lax.ppermute(x, 'psg', [(j, j ^ k) for j in range(shards)])]
    pallas_call x1 -> x3, Pallas kernels: 0.81 us -> 0.81 us  [the longest x1 0.81 us: place(): pl.pallas_call(functools.partial(place_kernel, tiles, paired), out_shape=...]
  transfers between devices with their start and end apart: 5 -> 8, of which waited for: 2 -> 5; matrix products, arithmetic and copies ran while one was open for 0% -> 0% of each run, Pallas kernels for 12% -> 12%
where the time goes in v8:
time: 29.8 us; the launch traced here: 29.7 us
  starting transfers between devices  12.9 us (43%)
  waiting for transfers between devices  10.8 us (36%)
  Pallas kernels  5.95 us (20%)
    ppermute x8, starting transfers between devices, swap(): return lax.ppermute(x, 'psg', [(j, j ^ k) for j in range(shards)])  12.9 us
    ppermute x8, waiting for transfers between devices, swap(): return lax.ppermute(x, 'psg', [(j, j ^ k) for j in range(shards)])  10.8 us
    pallas_call x2, Pallas kernels, score(): pl.pallas_call(kernel, out_shape=jax.ShapeDtypeStruct((tiles, QB + 1, LAN...  3.13 us
    pallas_call x1, Pallas kernels, prepare(): pl.pallas_call(prepare_kernel, out_shape=[jax.ShapeDtypeStruct((shards, L...  1.8 us
    pallas_call x1, Pallas kernels, place(): pl.pallas_call(functools.partial(place_kernel, tiles, paired), out_shape=...  0.81 us
  transfers between devices with their start and end apart: 8, of which 5 were waited for; matrix products, arithmetic and copies ran while one was open for 0% of the time, Pallas kernels for 12%

profile of v8, /device:TPU:0, one launch (start us, length us, event | category | flops | bytes accessed | tf_op | source)
XLA Modules:
  0.0 29.7 jit_solution(14651386912608296850)
XLA Ops:
  0.0 0.0 copy-start
  0.0 5.0 %collective-permute-start.3 = (bf16[256,128]{1,0:T(8,128)(2,1)}, bf16[256,128]{1,0:T(8,128)(2,1)S(1)}, u32[]{:S(2)}, u32[]{:S(2)}) collective-permute-start(bf16[256,128]{1,0:T(8,128)(2,1)} %bitcast.5), channel_id=1, source_target_pairs={{0,12},{2,14},{4,8},{6,10},{8,4},{10,6},{12,0},{14,2},{1,13},{3,15... | collective-permute-start | bytes 196616 | tf_op jit(solution)/shard_map/ppermute | solution.py:242
  5.1 0.0 collective-permute-start.2
  5.1 0.6 %collective-permute-start.1 = (bf16[256,128]{1,0:T(8,128)(2,1)}, bf16[256,128]{1,0:T(8,128)(2,1)S(1)}, u32[]{:S(2)}, u32[]{:S(2)}) collective-permute-start(bf16[256,128]{1,0:T(8,128)(2,1)} %bitcast.7), channel_id=1, source_target_pairs={{0,4},{2,6},{4,0},{6,2},{8,12},{10,14},{12,8},{14,10},{1,5},{3,7},... | collective-permute-start | bytes 196616 | tf_op jit(solution)/shard_map/ppermute | solution.py:242
  5.7 1.6 %collective-permute-start = (s32[8,32]{1,0:T(8,128)}, s32[8,32]{1,0:T(8,128)S(1)}, u32[]{:S(2)}, u32[]{:S(2)}) collective-permute-start(s32[8,32]{1,0:T(8,128)} %bitcast.10), channel_id=1, source_target_pairs={{0,2},{2,0},{4,6},{6,4},{8,10},{10,8},{12,14},{14,12},{1,3},{3,1},... | collective-permute-start | bytes 3080 | tf_op jit(solution)/shard_map/ppermute | solution.py:242
  7.3 1.8 %shard_map.46 = (f32[8,128]{1,0:T(8,128)S(1)}, s32[8,128]{1,0:T(8,128)S(1)}, bf16[128,64,128]{2,1,0:T(8,128)(2,1)S(1)}) custom-call(s32[8,32]{1,0:T(8,128)} %bitcast.11, s32[128]{0:T(128)} %len_hbm.1, bf16[128,64,128]{2,1,0:T(8,128)(2,1)} %p_hbm.1), custom_call_target="tpu_custom_call" | custom-call | flops 1048576 | bytes 2097152 | tf_op jit(solution)/shard_map/pallas_call | solution.py:73
  9.1 0.0 collective-permute-done.3.refs_3_
  9.1 1.8 %collective-permute-done.2.refs_2_ = bf16[256,128]{1,0:T(8,128)(2,1)S(1)} collective-permute-done((bf16[256,128]{1,0:T(8,128)(2,1)}, bf16[256,128]{1,0:T(8,128)(2,1)S(1)}, u32[]{:S(2)}, u32[]{:S(2)}) %collective-permute-start.2) | collective-permute-done | bytes 65568 | tf_op jit(solution)/shard_map/ppermute | solution.py:242
  10.9 0.0 collective-permute-done.1.refs_1_
  10.9 0.0 collective-permute-done.cand_ref
  10.9 0.0 copy-done
  10.9 0.2 shard_map.47
  11.2 1.6 %collective-permute-start.4 = (bf16[256,128]{1,0:T(8,128)(2,1)S(1)}, bf16[256,128]{1,0:T(8,128)(2,1)S(1)}, u32[]{:S(2)}, u32[]{:S(2)}) collective-permute-start(bf16[256,128]{1,0:T(8,128)(2,1)S(1)} %shard_map.47), channel_id=1, source_target_pairs={{0,2},{2,0},{4,6},{6,4},{8,10},{10,8},{12,14},{14,12},{1,3},{3,1},... | collective-permute-start | bytes 196616 | tf_op jit(solution)/shard_map/ppermute | solution.py:242
  12.7 1.7 %shard_map.48.refs_0_ = f32[4,3,128]{2,1,0:T(4,128)S(1)} custom-call(f32[8,128]{1,0:T(8,128)S(1)} %get-tuple-element.18.slots_ref, s32[8,128]{1,0:T(8,128)S(1)} %get-tuple-element.19.picks_ref, bf16[128,64,128]{2,1,0:T(8,128)(2,1)S(1)} %get-tuple-element.20.p_ref, bf16[256,128]{1,0:T(8,128)(2,1)S(1)} %bitcast.9, ...), custom_call_target="tpu_custom_call" | custom-call | flops 536870912 | bytes 2097152 | tf_op jit(solution)/shard_map/pallas_call | solution.py:176
  14.4 1.1 %collective-permute-done.4.sel_ref = bf16[256,128]{1,0:T(8,128)(2,1)S(1)} collective-permute-done((bf16[256,128]{1,0:T(8,128)(2,1)S(1)}, bf16[256,128]{1,0:T(8,128)(2,1)S(1)}, u32[]{:S(2)}, u32[]{:S(2)}) %collective-permute-start.4) | collective-permute-done | bytes 65568 | tf_op jit(solution)/shard_map/ppermute | solution.py:242
  15.5 1.5 %shard_map.49 = f32[4,3,128]{2,1,0:T(4,128)S(1)} custom-call(f32[8,128]{1,0:T(8,128)S(1)} %get-tuple-element.18.slots_ref, bf16[128,64,128]{2,1,0:T(8,128)(2,1)S(1)} %get-tuple-element.20.p_ref, bf16[256,128]{1,0:T(8,128)(2,1)S(1)} %collective-permute-done.4.sel_ref), custom_call_target="tpu_custom_call" | custom-call | flops 536870912 | bytes 2097152 | tf_op jit(solution)/shard_map/pallas_call | solution.py:176
  17.0 1.5 %collective-permute-start.5 = (f32[4,3,128]{2,1,0:T(4,128)S(1)}, f32[4,3,128]{2,1,0:T(4,128)S(1)}, u32[]{:S(2)}, u32[]{:S(2)}) collective-permute-start(f32[4,3,128]{2,1,0:T(4,128)S(1)} %shard_map.49), channel_id=1, source_target_pairs={{0,2},{2,0},{4,6},{6,4},{8,10},{10,8},{12,14},{14,12},{1,3},{3,1},... | collective-permute-start | bytes 18440 | tf_op jit(solution)/shard_map/ppermute | solution.py:242
  18.5 2.2 %collective-permute-done.5.refs_1_ = f32[4,3,128]{2,1,0:T(4,128)S(1)} collective-permute-done((f32[4,3,128]{2,1,0:T(4,128)S(1)}, f32[4,3,128]{2,1,0:T(4,128)S(1)}, u32[]{:S(2)}, u32[]{:S(2)}) %collective-permute-start.5) | collective-permute-done | bytes 6176 | tf_op jit(solution)/shard_map/ppermute | solution.py:242
  20.7 1.0 %collective-permute-start.6 = (f32[4,3,128]{2,1,0:T(4,128)S(1)}, f32[4,3,128]{2,1,0:T(4,128)S(1)}, u32[]{:S(2)}, u32[]{:S(2)}) collective-permute-start(f32[4,3,128]{2,1,0:T(4,128)S(1)} %shard_map.50), channel_id=1, source_target_pairs={{0,4},{2,6},{4,0},{6,2},{8,12},{10,14},{12,8},{14,10},{1,5},{3,7},... | collective-permute-start | bytes 18440 | tf_op jit(solution)/shard_map/ppermute | solution.py:242
  21.7 2.7 %collective-permute-done.6.refs_2_ = f32[4,3,128]{2,1,0:T(4,128)S(1)} collective-permute-done((f32[4,3,128]{2,1,0:T(4,128)S(1)}, f32[4,3,128]{2,1,0:T(4,128)S(1)}, u32[]{:S(2)}, u32[]{:S(2)}) %collective-permute-start.6) | collective-permute-done | bytes 6176 | tf_op jit(solution)/shard_map/ppermute | solution.py:242
  24.3 1.5 %collective-permute-start.7 = (f32[4,3,128]{2,1,0:T(4,128)S(1)}, f32[4,3,128]{2,1,0:T(4,128)S(1)}, u32[]{:S(2)}, u32[]{:S(2)}) collective-permute-start(f32[4,3,128]{2,1,0:T(4,128)S(1)} %shard_map.51), channel_id=1, source_target_pairs={{0,8},{2,10},{4,12},{6,14},{8,0},{10,2},{12,4},{14,6},{1,9},{3,11}... | collective-permute-start | bytes 18440 | tf_op jit(solution)/shard_map/ppermute | solution.py:242
  25.8 3.0 %collective-permute-done.7.refs_3_ = f32[4,3,128]{2,1,0:T(4,128)S(1)} collective-permute-done((f32[4,3,128]{2,1,0:T(4,128)S(1)}, f32[4,3,128]{2,1,0:T(4,128)S(1)}, u32[]{:S(2)}, u32[]{:S(2)}) %collective-permute-start.7) | collective-permute-done | bytes 6176 | tf_op jit(solution)/shard_map/ppermute | solution.py:242
  28.9 0.8 %shard_map.52 = f32[8,2,16,32]{3,2,1,0:T(8,128)} custom-call(f32[4,3,128]{2,1,0:T(4,128)S(1)} %shard_map.48.refs_0_, f32[4,3,128]{2,1,0:T(4,128)S(1)} %collective-permute-done.5.refs_1_, f32[4,3,128]{2,1,0:T(4,128)S(1)} %collective-permute-done.6.refs_2_, f32[4,3,128]{2,1,0:T(4,128)S(1)} %collective-permute-done.7.refs_3_), custom_call_target="tpu_custom_call" | custom-call | tf_op jit(solution)/shard_map/pallas_call | solution.py:231
  (2 shorter events, 0.0 us)
Async XLA Ops:
  0.0 10.9 %copy-start = (bf16[8,32,128]{2,1,0:T(8,128)(2,1)S(1)}, bf16[8,32,128]{2,1,0:T(8,128)(2,1)}, u32[]{:S(2)}) copy-start(bf16[8,32,128]{2,1,0:T(8,128)(2,1)} %param.4) | copy-start | bytes 196612
  0.0 9.1 %collective-permute-start.3 = (bf16[256,128]{1,0:T(8,128)(2,1)}, bf16[256,128]{1,0:T(8,128)(2,1)S(1)}, u32[]{:S(2)}, u32[]{:S(2)}) collective-permute-start(bf16[256,128]{1,0:T(8,128)(2,1)} %bitcast.5), channel_id=1, source_target_pairs={{0,12},{2,14},{4,8},{6,10},{8,4},{10,6},{12,0},{14,2},{1,13},{3,15... | collective-permute-start | bytes 196616 | tf_op jit(solution)/shard_map/ppermute | solution.py:242
  5.1 5.9 %collective-permute-start.2 = (bf16[256,128]{1,0:T(8,128)(2,1)}, bf16[256,128]{1,0:T(8,128)(2,1)S(1)}, u32[]{:S(2)}, u32[]{:S(2)}) collective-permute-start(bf16[256,128]{1,0:T(8,128)(2,1)} %bitcast.6), channel_id=1, source_target_pairs={{0,8},{2,10},{4,12},{6,14},{8,0},{10,2},{12,4},{14,6},{1,9},{3,11}... | collective-permute-start | bytes 196616 | tf_op jit(solution)/shard_map/ppermute | solution.py:242
  5.1 5.9 %collective-permute-start.1 = (bf16[256,128]{1,0:T(8,128)(2,1)}, bf16[256,128]{1,0:T(8,128)(2,1)S(1)}, u32[]{:S(2)}, u32[]{:S(2)}) collective-permute-start(bf16[256,128]{1,0:T(8,128)(2,1)} %bitcast.7), channel_id=1, source_target_pairs={{0,4},{2,6},{4,0},{6,2},{8,12},{10,14},{12,8},{14,10},{1,5},{3,7},... | collective-permute-start | bytes 196616 | tf_op jit(solution)/shard_map/ppermute | solution.py:242
  5.7 5.3 %collective-permute-start = (s32[8,32]{1,0:T(8,128)}, s32[8,32]{1,0:T(8,128)S(1)}, u32[]{:S(2)}, u32[]{:S(2)}) collective-permute-start(s32[8,32]{1,0:T(8,128)} %bitcast.10), channel_id=1, source_target_pairs={{0,2},{2,0},{4,6},{6,4},{8,10},{10,8},{12,14},{14,12},{1,3},{3,1},... | collective-permute-start | bytes 3080 | tf_op jit(solution)/shard_map/ppermute | solution.py:242
  11.2 4.3 %collective-permute-start.4 = (bf16[256,128]{1,0:T(8,128)(2,1)S(1)}, bf16[256,128]{1,0:T(8,128)(2,1)S(1)}, u32[]{:S(2)}, u32[]{:S(2)}) collective-permute-start(bf16[256,128]{1,0:T(8,128)(2,1)S(1)} %shard_map.47), channel_id=1, source_target_pairs={{0,2},{2,0},{4,6},{6,4},{8,10},{10,8},{12,14},{14,12},{1,3},{3,1},... | collective-permute-start | bytes 196616 | tf_op jit(solution)/shard_map/ppermute | solution.py:242
  17.0 3.7 %collective-permute-start.5 = (f32[4,3,128]{2,1,0:T(4,128)S(1)}, f32[4,3,128]{2,1,0:T(4,128)S(1)}, u32[]{:S(2)}, u32[]{:S(2)}) collective-permute-start(f32[4,3,128]{2,1,0:T(4,128)S(1)} %shard_map.49), channel_id=1, source_target_pairs={{0,2},{2,0},{4,6},{6,4},{8,10},{10,8},{12,14},{14,12},{1,3},{3,1},... | collective-permute-start | bytes 18440 | tf_op jit(solution)/shard_map/ppermute | solution.py:242
  20.7 3.7 %collective-permute-start.6 = (f32[4,3,128]{2,1,0:T(4,128)S(1)}, f32[4,3,128]{2,1,0:T(4,128)S(1)}, u32[]{:S(2)}, u32[]{:S(2)}) collective-permute-start(f32[4,3,128]{2,1,0:T(4,128)S(1)} %shard_map.50), channel_id=1, source_target_pairs={{0,4},{2,6},{4,0},{6,2},{8,12},{10,14},{12,8},{14,10},{1,5},{3,7},... | collective-permute-start | bytes 18440 | tf_op jit(solution)/shard_map/ppermute | solution.py:242
  24.3 4.5 %collective-permute-start.7 = (f32[4,3,128]{2,1,0:T(4,128)S(1)}, f32[4,3,128]{2,1,0:T(4,128)S(1)}, u32[]{:S(2)}, u32[]{:S(2)}) collective-permute-start(f32[4,3,128]{2,1,0:T(4,128)S(1)} %shard_map.51), channel_id=1, source_target_pairs={{0,8},{2,10},{4,12},{6,14},{8,0},{10,2},{12,4},{14,6},{1,9},{3,11}... | collective-permute-start | bytes 18440 | tf_op jit(solution)/shard_map/ppermute | solution.py:242

commit v9 on v7

--- a/solution.py
+++ b/solution.py
@@ -117,15 +117,14 @@
     )(candidates, *blocks)
 
 
-def score_picked(sel_ref, p_ref, max_ref):
+def score_picked(sel_ref, p_ref, max_ref, piece):
     count = p_ref.shape[0]
     sel = sel_ref[...]
     tokens = sel.shape[0]
-    for g in range(count // GROUP):
-        left = p_ref[g * GROUP:(g + 1) * GROUP].reshape(GROUP * PT, DIM)
+    for g in range(0, count, piece):
+        left = p_ref[g:g + piece].reshape(piece * PT, DIM)
         dots = lax.dot_general(left, sel, (((1,), (1,)), ((), ())), preferred_element_type=jnp.float32)
-        best = jnp.max(dots.reshape(GROUP, PT, tokens), axis=1)
-        max_ref[g * GROUP:(g + 1) * GROUP, :] = best
+        max_ref[g:g + piece, :] = jnp.max(dots.reshape(piece, PT, tokens), axis=1)
 
     best = max_ref[...]
     high = best.astype(jnp.bfloat16)
@@ -146,7 +145,7 @@
     me = lax.axis_index("psg")
     for n, k in enumerate(partners):
         sel_ref[n * QB * QT:(n + 1) * QB * QT, :] = picked(picks_ref, me ^ k, q_refs[n])
-    total = score_picked(sel_ref, p_ref, max_ref)
+    total = score_picked(sel_ref, p_ref, max_ref, 16)
     for n, k in enumerate(partners):
         out_ref[n, 0:QB, :] = total[n * QB:(n + 1) * QB]
         out_ref[n, QB:QB + 1, :] = slots_ref[pl.ds(me ^ k, 1), :]
@@ -154,7 +153,7 @@
 
 def join_kernel(partners, slots_ref, p_ref, sel_ref, earlier_ref, out_ref, max_ref):
     me = lax.axis_index("psg")
-    total = score_picked(sel_ref, p_ref, max_ref)
+    total = score_picked(sel_ref, p_ref, max_ref, 32)
     for n, k in enumerate(partners):
         out_ref[me ^ k, 0:QB, :] = total[n * QB:(n + 1) * QB]
         out_ref[me ^ k, QB:QB + 1, :] = slots_ref[pl.ds(me ^ k, 1), :]
@@ -165,7 +164,7 @@
     some = q_ref.shape[0]
     for n in range(some):
         sel_ref[n * QB * QT:(n + 1) * QB * QT, :] = picked(picks_ref, n, q_ref.at[n])
-    total = score_picked(sel_ref, p_ref, max_ref)
+    total = score_picked(sel_ref, p_ref, max_ref, GROUP)
     for n in range(some):
         out_ref[n, 0:QB, :] = total[n * QB:(n + 1) * QB]
         out_ref[n, QB:QB + 1, :] = slots_ref[n:n + 1, :]
@@ -218,10 +217,10 @@
 
     near = list(range(0, shards, 2))
     theirs = swap(candidates, 1)
-    queries = {0: own} | {k: swap(own, k) for k in reversed(near[1:])}
+    queries = {0: own} | {k: swap(own, k) for k in near[1:]}
     slots, picks, clean = prepare(shards, candidates, lengths, passages)
-    *arrived, clean = lax.optimization_barrier((*[queries[k] for k in near[1:]], clean))
-    blocks = [own, *arrived]
+    clean, *arrived = lax.optimization_barrier((clean, *[queries[k] for k in reversed(near[1:])]))
+    blocks = [own, *reversed(arrived)]
     far = swap(pack(near, theirs, blocks), 1)
     tiles = score(
         functools.partial(score_kernel, near), len(near), len(near), 1, clean, slots, picks, clean, *blocks

time: 29.2 us -> 29.3 us (level)
  waiting for transfers between devices: 2.91 us -> 3.89 us
  blocking collectives: 11.2 us -> 10.4 us
    ppermute x5, waiting for transfers between devices: 2.91 us -> 3.89 us  [swap(): return lax.ppermute(x, 'psg', [(j, j ^ k) for j in range(shards)])]
    all_to_all x1, blocking collectives: 11.2 us -> 10.4 us  [per_device(): lax.all_to_all(tiles, 'psg', split_axis=0, concat_axis=0, tiled=True)]
  transfers between devices with their start and end apart: 5 -> 5, of which waited for: 2 -> 3; matrix products, arithmetic and copies ran while one was open for 0% -> 0% of each run, Pallas kernels for 12% -> 12%
where the time goes in v9:
time: 29.3 us; the launch traced here: 29.1 us
  blocking collectives  10.4 us (35%)
  starting transfers between devices  8.88 us (30%)
  Pallas kernels  5.95 us (20%)
  waiting for transfers between devices  3.89 us (13%)
    all_to_all x1, blocking collectives, per_device(): lax.all_to_all(tiles, 'psg', split_axis=0, concat_axis=0, tiled=True)  10.4 us
    ppermute x5, starting transfers between devices, swap(): return lax.ppermute(x, 'psg', [(j, j ^ k) for j in range(shards)])  8.88 us
    ppermute x5, waiting for transfers between devices, swap(): return lax.ppermute(x, 'psg', [(j, j ^ k) for j in range(shards)])  3.89 us
    pallas_call x2, Pallas kernels, score(): pl.pallas_call(kernel, out_shape=jax.ShapeDtypeStruct((tiles, QB + 1, LAN...  3.13 us
    pallas_call x1, Pallas kernels, prepare(): pl.pallas_call(prepare_kernel, out_shape=[jax.ShapeDtypeStruct((shards, L...  1.8 us
    pallas_call x1, Pallas kernels, place(): pl.pallas_call(place_kernel, out_shape=jax.ShapeDtypeStruct((shards, QB,...  0.81 us
  transfers between devices with their start and end apart: 5, of which 3 were waited for; matrix products, arithmetic and copies ran while one was open for 0% of the time, Pallas kernels for 12%

profile of v9, /device:TPU:0, one launch (start us, length us, event | category | flops | bytes accessed | tf_op | source)
XLA Modules:
  0.0 29.1 jit_solution(1324321155942657081)
XLA Ops:
  0.0 0.0 copy-start
  0.0 3.0 %collective-permute-start.2 = (bf16[256,128]{1,0:T(8,128)(2,1)}, bf16[256,128]{1,0:T(8,128)(2,1)S(1)}, u32[]{:S(2)}, u32[]{:S(2)}) collective-permute-start(bf16[256,128]{1,0:T(8,128)(2,1)} %bitcast.5), channel_id=1, source_target_pairs={{0,4},{2,6},{4,0},{6,2},{8,12},{10,14},{12,8},{14,10},{1,5},{3,7},... | collective-permute-start | bytes 196616 | tf_op jit(solution)/shard_map/ppermute | solution.py:216
  3.0 2.6 %collective-permute-start.1 = (bf16[256,128]{1,0:T(8,128)(2,1)}, bf16[256,128]{1,0:T(8,128)(2,1)S(1)}, u32[]{:S(2)}, u32[]{:S(2)}) collective-permute-start(bf16[256,128]{1,0:T(8,128)(2,1)} %bitcast.6), channel_id=1, source_target_pairs={{0,8},{2,10},{4,12},{6,14},{8,0},{10,2},{12,4},{14,6},{1,9},{3,11}... | collective-permute-start | bytes 196616 | tf_op jit(solution)/shard_map/ppermute | solution.py:216
  5.6 0.0 collective-permute-start
  5.6 1.7 %collective-permute-start.3 = (s32[8,32]{1,0:T(8,128)}, s32[8,32]{1,0:T(8,128)S(1)}, u32[]{:S(2)}, u32[]{:S(2)}) collective-permute-start(s32[8,32]{1,0:T(8,128)} %bitcast.10), channel_id=1, source_target_pairs={{0,2},{2,0},{4,6},{6,4},{8,10},{10,8},{12,14},{14,12},{1,3},{3,1},... | collective-permute-start | bytes 3080 | tf_op jit(solution)/shard_map/ppermute | solution.py:216
  7.3 1.8 %shard_map.46 = (f32[8,128]{1,0:T(8,128)S(1)}, s32[8,128]{1,0:T(8,128)S(1)}, bf16[128,64,128]{2,1,0:T(8,128)(2,1)S(1)}) custom-call(s32[8,32]{1,0:T(8,128)} %bitcast.11, s32[128]{0:T(128)} %len_hbm.1, bf16[128,64,128]{2,1,0:T(8,128)(2,1)} %p_hbm.1), custom_call_target="tpu_custom_call" | custom-call | flops 1048576 | bytes 2097152 | tf_op jit(solution)/shard_map/pallas_call | solution.py:73
  9.1 0.0 collective-permute-done.2.refs_1_
  9.1 1.4 %collective-permute-done.1.refs_2_ = bf16[256,128]{1,0:T(8,128)(2,1)S(1)} collective-permute-done((bf16[256,128]{1,0:T(8,128)(2,1)}, bf16[256,128]{1,0:T(8,128)(2,1)S(1)}, u32[]{:S(2)}, u32[]{:S(2)}) %collective-permute-start.1) | collective-permute-done | bytes 65568 | tf_op jit(solution)/shard_map/ppermute | solution.py:216
  10.5 1.4 %collective-permute-done.refs_3_ = bf16[256,128]{1,0:T(8,128)(2,1)S(1)} collective-permute-done((bf16[256,128]{1,0:T(8,128)(2,1)}, bf16[256,128]{1,0:T(8,128)(2,1)S(1)}, u32[]{:S(2)}, u32[]{:S(2)}) %collective-permute-start) | collective-permute-done | bytes 65568 | tf_op jit(solution)/shard_map/ppermute | solution.py:216
  11.9 0.0 collective-permute-done.3.cand_ref
  11.9 0.0 copy-done
  11.9 0.2 shard_map.47
  12.2 1.6 %collective-permute-start.4 = (bf16[256,128]{1,0:T(8,128)(2,1)S(1)}, bf16[256,128]{1,0:T(8,128)(2,1)S(1)}, u32[]{:S(2)}, u32[]{:S(2)}) collective-permute-start(bf16[256,128]{1,0:T(8,128)(2,1)S(1)} %shard_map.47), channel_id=1, source_target_pairs={{0,2},{2,0},{4,6},{6,4},{8,10},{10,8},{12,14},{14,12},{1,3},{3,1},... | collective-permute-start | bytes 196616 | tf_op jit(solution)/shard_map/ppermute | solution.py:216
  13.7 1.7 %shard_map.48.earlier_ref = f32[4,3,128]{2,1,0:T(4,128)S(1)} custom-call(f32[8,128]{1,0:T(8,128)S(1)} %get-tuple-element.14.slots_ref, s32[8,128]{1,0:T(8,128)S(1)} %get-tuple-element.20.picks_ref, bf16[128,64,128]{2,1,0:T(8,128)(2,1)S(1)} %get-tuple-element.16.p_ref, bf16[256,128]{1,0:T(8,128)(2,1)S(1)} %bitcast.9, ...), custom_call_target="tpu_custom_call" | custom-call | flops 536870912 | bytes 2097152 | tf_op jit(solution)/shard_map/pallas_call | solution.py:176
  15.4 1.1 %collective-permute-done.4.sel_ref = bf16[256,128]{1,0:T(8,128)(2,1)S(1)} collective-permute-done((bf16[256,128]{1,0:T(8,128)(2,1)S(1)}, bf16[256,128]{1,0:T(8,128)(2,1)S(1)}, u32[]{:S(2)}, u32[]{:S(2)}) %collective-permute-start.4) | collective-permute-done | bytes 65568 | tf_op jit(solution)/shard_map/ppermute | solution.py:216
  16.5 1.5 %shard_map.49 = f32[8,3,128]{2,1,0:T(4,128)S(1)} custom-call(f32[8,128]{1,0:T(8,128)S(1)} %get-tuple-element.14.slots_ref, bf16[128,64,128]{2,1,0:T(8,128)(2,1)S(1)} %get-tuple-element.16.p_ref, bf16[256,128]{1,0:T(8,128)(2,1)S(1)} %collective-permute-done.4.sel_ref, f32[4,3,128]{2,1,0:T(4,128)S(1)} %shard_map.48.earlier_ref), custom_call_target="tpu_custom_call" | custom-call | flops 536870912 | bytes 2097152 | tf_op jit(solution)/shard_map/pallas_call | solution.py:176
  17.9 10.4 %all_to_all.5.in_ref = f32[8,3,128]{2,1,0:T(4,128)S(1)} all-to-all(f32[8,3,128]{2,1,0:T(4,128)S(1)} %shard_map.49), channel_id=1, replica_groups=mesh['grp'=2,'psg'=8,'qry'=2] {'psg'}, dimensions={0} | all-to-all | bytes 24576 | tf_op jit(solution)/shard_map/all_to_all | solution.py:253
  28.3 0.8 %shard_map.50 = f32[8,2,16,32]{3,2,1,0:T(8,128)} custom-call(f32[8,3,128]{2,1,0:T(4,128)S(1)} %all_to_all.5.in_ref), custom_call_target="tpu_custom_call" | custom-call | tf_op jit(solution)/shard_map/pallas_call | solution.py:205
Async XLA Ops:
  0.0 11.9 %copy-start = (bf16[8,32,128]{2,1,0:T(8,128)(2,1)S(1)}, bf16[8,32,128]{2,1,0:T(8,128)(2,1)}, u32[]{:S(2)}) copy-start(bf16[8,32,128]{2,1,0:T(8,128)(2,1)} %param.4) | copy-start | bytes 196612
  0.0 9.1 %collective-permute-start.2 = (bf16[256,128]{1,0:T(8,128)(2,1)}, bf16[256,128]{1,0:T(8,128)(2,1)S(1)}, u32[]{:S(2)}, u32[]{:S(2)}) collective-permute-start(bf16[256,128]{1,0:T(8,128)(2,1)} %bitcast.5), channel_id=1, source_target_pairs={{0,4},{2,6},{4,0},{6,2},{8,12},{10,14},{12,8},{14,10},{1,5},{3,7},... | collective-permute-start | bytes 196616 | tf_op jit(solution)/shard_map/ppermute | solution.py:216
  3.0 7.5 %collective-permute-start.1 = (bf16[256,128]{1,0:T(8,128)(2,1)}, bf16[256,128]{1,0:T(8,128)(2,1)S(1)}, u32[]{:S(2)}, u32[]{:S(2)}) collective-permute-start(bf16[256,128]{1,0:T(8,128)(2,1)} %bitcast.6), channel_id=1, source_target_pairs={{0,8},{2,10},{4,12},{6,14},{8,0},{10,2},{12,4},{14,6},{1,9},{3,11}... | collective-permute-start | bytes 196616 | tf_op jit(solution)/shard_map/ppermute | solution.py:216
  5.6 6.3 %collective-permute-start = (bf16[256,128]{1,0:T(8,128)(2,1)}, bf16[256,128]{1,0:T(8,128)(2,1)S(1)}, u32[]{:S(2)}, u32[]{:S(2)}) collective-permute-start(bf16[256,128]{1,0:T(8,128)(2,1)} %bitcast.7), channel_id=1, source_target_pairs={{0,12},{2,14},{4,8},{6,10},{8,4},{10,6},{12,0},{14,2},{1,13},{3,15... | collective-permute-start | bytes 196616 | tf_op jit(solution)/shard_map/ppermute | solution.py:216
  5.6 6.3 %collective-permute-start.3 = (s32[8,32]{1,0:T(8,128)}, s32[8,32]{1,0:T(8,128)S(1)}, u32[]{:S(2)}, u32[]{:S(2)}) collective-permute-start(s32[8,32]{1,0:T(8,128)} %bitcast.10), channel_id=1, source_target_pairs={{0,2},{2,0},{4,6},{6,4},{8,10},{10,8},{12,14},{14,12},{1,3},{3,1},... | collective-permute-start | bytes 3080 | tf_op jit(solution)/shard_map/ppermute | solution.py:216
  12.2 4.3 %collective-permute-start.4 = (bf16[256,128]{1,0:T(8,128)(2,1)S(1)}, bf16[256,128]{1,0:T(8,128)(2,1)S(1)}, u32[]{:S(2)}, u32[]{:S(2)}) collective-permute-start(bf16[256,128]{1,0:T(8,128)(2,1)S(1)} %shard_map.47), channel_id=1, source_target_pairs={{0,2},{2,0},{4,6},{6,4},{8,10},{10,8},{12,14},{14,12},{1,3},{3,1},... | collective-permute-start | bytes 196616 | tf_op jit(solution)/shard_map/ppermute | solution.py:216

commit v10 on v7

--- a/solution.py
+++ b/solution.py
@@ -18,31 +18,38 @@
 GROUP = 8
 
 
-def prepare_kernel(
-    cand_hbm, len_hbm, p_hbm, slots_ref, picks_ref, clean_ref, cand_ref, len_ref, raw_ref, sems
-):
-    rows = cand_ref.shape[0]
-    shards = slots_ref.shape[0]
+def clean_passages(len_hbm, p_hbm, clean_ref, len_ref, raw_ref, sems, meanwhile=lambda: None):
     groups = p_hbm.shape[0] // GROUP
 
     def fetch(g):
         part = pl.ds(g * GROUP, GROUP)
         return pltpu.make_async_copy(p_hbm.at[part], raw_ref.at[part], sems.at[g])
 
-    fetch_cand = pltpu.make_async_copy(cand_hbm, cand_ref, sems.at[groups])
-    fetch_len = pltpu.make_async_copy(len_hbm, len_ref, sems.at[groups + 1])
-    fetch_cand.start()
+    fetch_len = pltpu.make_async_copy(len_hbm, len_ref, sems.at[groups])
     fetch_len.start()
     for g in range(groups):
         fetch(g).start()
-
-    fetch_cand.wait()
+    meanwhile()
+    fetch_len.wait()
+    u = lax.broadcasted_iota(jnp.int32, (PT, LANES), 0)
+
+    @pl.loop(0, groups)
+    def _(g):
+        fetch(g).wait()
+        for i in range(GROUP):
+            p = g * GROUP + i
+            tokens = raw_ref[p].astype(jnp.float32)
+            clean_ref[p] = jnp.where(u < len_ref[p], tokens, tokens[0:1]).astype(jnp.bfloat16)
+
+
+def read_candidates(cand_ref, slots_ref, picks_ref):
+    rows = cand_ref.shape[0]
     cand = cand_ref[...]
     owner = cand // QBD
     block = cand - owner * QBD
     lane = lax.broadcasted_iota(jnp.int32, (rows, LANES), 1).astype(jnp.float32)
     sub = lax.broadcasted_iota(jnp.int32, (rows, LANES), 0)
-    for o in range(shards):
+    for o in range(slots_ref.shape[0]):
         mine = owner == o
         named = jnp.max(jnp.where(mine, block, 0), axis=1, keepdims=True)
         picks_ref[o:o + 1, :] = jnp.broadcast_to(jnp.max(named, axis=0, keepdims=True), (1, LANES))
@@ -54,40 +61,78 @@
             step *= 2
         slots_ref[o:o + 1, :] = jnp.sum(jnp.where(upto <= lane, 1.0, 0.0), axis=0, keepdims=True)
 
-    fetch_len.wait()
-    u = lax.broadcasted_iota(jnp.int32, (PT, LANES), 0)
-
-    @pl.loop(0, groups)
-    def _(g):
-        fetch(g).wait()
-        for i in range(GROUP):
-            p = g * GROUP + i
-            tokens = raw_ref[p].astype(jnp.float32)
-            clean_ref[p] = jnp.where(u < len_ref[p], tokens, tokens[0:1]).astype(jnp.bfloat16)
-
-
-def prepare(shards, candidates, lengths, passages):
+
+def prepare_early_kernel(len_hbm, p_hbm, clean_ref, *scratch):
+    @pl.when(lax.axis_index("qry") % 2 == 1)
+    def _():
+        clean_passages(len_hbm, p_hbm, clean_ref, *scratch)
+
+
+def prepare_kernel(early, cand_hbm, len_hbm, p_hbm, *refs):
+    early_refs, (slots_ref, picks_ref, clean_ref, len_ref, raw_ref, sems, cand_ref) = refs[:early], refs[early:]
+    fetch_cand = pltpu.make_async_copy(cand_hbm, cand_ref, sems.at[sems.shape[0] - 1])
+    fetch_cand.start()
+
+    def candidates():
+        fetch_cand.wait()
+        read_candidates(cand_ref, slots_ref, picks_ref)
+
+    def now():
+        clean_passages(len_hbm, p_hbm, clean_ref, len_ref, raw_ref, sems, candidates)
+
+    if not early:
+        now()
+        return
+    odd = lax.axis_index("qry") % 2 == 1
+    pl.when(jnp.logical_not(odd))(now)
+
+    @pl.when(odd)
+    def _():
+        candidates()
+
+        @pl.loop(0, clean_ref.shape[0] // GROUP)
+        def _(g):
+            part = pl.ds(g * GROUP, GROUP)
+            clean_ref[part] = early_refs[0][part]
+
+
+def prepare_scratch(lengths, passages):
+    return [
+        pltpu.SMEM(lengths.shape, lengths.dtype),
+        pltpu.VMEM(passages.shape, passages.dtype),
+        pltpu.SemaphoreType.DMA((passages.shape[0] // GROUP + 2,)),
+    ]
+
+
+def prepare_early(lengths, passages):
+    hbm = pl.BlockSpec(memory_space=pltpu.HBM)
+    return pl.pallas_call(
+        prepare_early_kernel,
+        out_shape=jax.ShapeDtypeStruct(passages.shape, passages.dtype),
+        in_specs=[hbm] * 2,
+        out_specs=pl.BlockSpec(memory_space=pltpu.VMEM),
+        scratch_shapes=prepare_scratch(lengths, passages),
+        compiler_params=pltpu.CompilerParams(vmem_limit_bytes=24 * 1024 * 1024),
+    )(*[pltpu.with_memory_space_constraint(x, pltpu.HBM) for x in (lengths, passages)])
+
+
+def prepare(shards, candidates, lengths, passages, *early):
     hbm = pl.BlockSpec(memory_space=pltpu.HBM)
     vmem = pl.BlockSpec(memory_space=pltpu.VMEM)
     operands = [pltpu.with_memory_space_constraint(x, pltpu.HBM) for x in (candidates, lengths, passages)]
     return pl.pallas_call(
-        prepare_kernel,
+        functools.partial(prepare_kernel, len(early)),
         out_shape=[
             jax.ShapeDtypeStruct((shards, LANES), jnp.float32),
             jax.ShapeDtypeStruct((shards, LANES), jnp.int32),
             jax.ShapeDtypeStruct(passages.shape, passages.dtype),
         ],
-        in_specs=[hbm] * 3,
+        in_specs=[hbm] * 3 + [vmem] * len(early),
         out_specs=[vmem] * 3,
-        scratch_shapes=[
-            pltpu.VMEM(candidates.shape, candidates.dtype),
-            pltpu.SMEM(lengths.shape, lengths.dtype),
-            pltpu.VMEM(passages.shape, passages.dtype),
-            pltpu.SemaphoreType.DMA((passages.shape[0] // GROUP + 2,)),
-        ],
+        scratch_shapes=prepare_scratch(lengths, passages) + [pltpu.VMEM(candidates.shape, candidates.dtype)],
         compiler_params=pltpu.CompilerParams(vmem_limit_bytes=24 * 1024 * 1024),
         cost_estimate=pl.CostEstimate(flops=passages.size, bytes_accessed=2 * passages.size, transcendentals=0),
-    )(*operands)
+    )(*operands, *early)
 
 
 def picked(picks_ref, owner, q_ref):
@@ -121,11 +166,10 @@
     count = p_ref.shape[0]
     sel = sel_ref[...]
     tokens = sel.shape[0]
-    for g in range(count // GROUP):
-        left = p_ref[g * GROUP:(g + 1) * GROUP].reshape(GROUP * PT, DIM)
+    for g in range(0, count, 2 * GROUP):
+        left = p_ref[g:g + 2 * GROUP].reshape(2 * GROUP * PT, DIM)
         dots = lax.dot_general(left, sel, (((1,), (1,)), ((), ())), preferred_element_type=jnp.float32)
-        best = jnp.max(dots.reshape(GROUP, PT, tokens), axis=1)
-        max_ref[g * GROUP:(g + 1) * GROUP, :] = best
+        max_ref[g:g + 2 * GROUP, :] = jnp.max(dots.reshape(2 * GROUP, PT, tokens), axis=1)
 
     best = max_ref[...]
     high = best.astype(jnp.bfloat16)
@@ -218,10 +262,11 @@
 
     near = list(range(0, shards, 2))
     theirs = swap(candidates, 1)
-    queries = {0: own} | {k: swap(own, k) for k in reversed(near[1:])}
-    slots, picks, clean = prepare(shards, candidates, lengths, passages)
-    *arrived, clean = lax.optimization_barrier((*[queries[k] for k in near[1:]], clean))
-    blocks = [own, *arrived]
+    own, early = lax.optimization_barrier((own, prepare_early(lengths, passages)))
+    queries = {0: own} | {k: swap(own, k) for k in near[1:]}
+    slots, picks, clean = prepare(shards, candidates, lengths, passages, early)
+    clean, *arrived = lax.optimization_barrier((clean, *[queries[k] for k in reversed(near[1:])]))
+    blocks = [own, *reversed(arrived)]
     far = swap(pack(near, theirs, blocks), 1)
     tiles = score(
         functools.partial(score_kernel, near), len(near), len(near), 1, clean, slots, picks, clean, *blocks

time: 29.2 us -> 30.5 us (1.045)
  local copies, waits for them, and re-layouts: 0.01 us -> 0.67 us
  waiting for transfers between devices: 2.91 us -> 3.53 us
    unnamed x2 -> x4, local copies, waits for them, and re-layouts: 0.01 us -> 0.67 us
    ppermute x5, waiting for transfers between devices: 2.91 us -> 3.53 us  [swap(): return lax.ppermute(x, 'psg', [(j, j ^ k) for j in range(shards)])]
    pallas_call x1 -> x2, Pallas kernels: 1.8 us -> 1.96 us  [the longest x1 1.8 us: prepare(): pl.pallas_call(functools.partial(prepare_kernel, len(early)), out_shape=[...]
  transfers between devices with their start and end apart: 5 -> 5, of which waited for: 2 -> 2; matrix products, arithmetic and copies ran while one was open for 0% -> 0% of each run, Pallas kernels for 12% -> 11%
where the time goes in v10:
time: 30.5 us; the launch traced here: 30.3 us
  blocking collectives  11.1 us (36%)
  starting transfers between devices  8.88 us (29%)
  Pallas kernels  6.12 us (20%)
  waiting for transfers between devices  3.53 us (12%)
  local copies, waits for them, and re-layouts  0.67 us (2%)
    all_to_all x1, blocking collectives, per_device(): lax.all_to_all(tiles, 'psg', split_axis=0, concat_axis=0, tiled=True)  11.1 us
    ppermute x5, starting transfers between devices, swap(): return lax.ppermute(x, 'psg', [(j, j ^ k) for j in range(shards)])  8.88 us
    ppermute x5, waiting for transfers between devices, swap(): return lax.ppermute(x, 'psg', [(j, j ^ k) for j in range(shards)])  3.53 us
    pallas_call x2, Pallas kernels, score(): pl.pallas_call(kernel, out_shape=jax.ShapeDtypeStruct((tiles, QB + 1, LAN...  3.14 us
    pallas_call x1, Pallas kernels, prepare(): pl.pallas_call(functools.partial(prepare_kernel, len(early)), out_shape=[...  1.8 us
    pallas_call x1, Pallas kernels, place(): pl.pallas_call(place_kernel, out_shape=jax.ShapeDtypeStruct((shards, QB,...  0.81 us
    unnamed x4, local copies, waits for them, and re-layouts  0.67 us
  transfers between devices with their start and end apart: 5, of which 2 were waited for; matrix products, arithmetic and copies ran while one was open for 0% of the time, Pallas kernels for 11%

profile of v10, /device:TPU:0, one launch (start us, length us, event | category | flops | bytes accessed | tf_op | source)
XLA Modules:
  0.0 30.3 jit_solution(16973097297680577685)
XLA Ops:
  0.0 0.0 copy-start
  0.0 0.0 copy-start.1
  0.0 0.2 shard_map.46.refs_0_
  0.2 0.7 %copy-done = bf16[8,32,128]{2,1,0:T(8,128)(2,1)S(1)} copy-done((bf16[8,32,128]{2,1,0:T(8,128)(2,1)S(1)}, bf16[8,32,128]{2,1,0:T(8,128)(2,1)}, u32[]{:S(2)}) %copy-start) | copy-done | bytes 65560
  0.8 5.0 %collective-permute-start = (bf16[256,128]{1,0:T(8,128)(2,1)S(1)}, bf16[256,128]{1,0:T(8,128)(2,1)S(1)}, u32[]{:S(2)}, u32[]{:S(2)}) collective-permute-start(bf16[256,128]{1,0:T(8,128)(2,1)S(1)} %bitcast.5), channel_id=1, source_target_pairs={{0,12},{2,14},{4,8},{6,10},{8,4},{10,6},{12,0},{14,2},{1,13},{3,15... | collective-permute-start | bytes 196616 | tf_op jit(solution)/shard_map/ppermute | solution.py:261
  5.9 0.0 collective-permute-start.1
  5.9 0.6 %collective-permute-start.2 = (bf16[256,128]{1,0:T(8,128)(2,1)S(1)}, bf16[256,128]{1,0:T(8,128)(2,1)S(1)}, u32[]{:S(2)}, u32[]{:S(2)}) collective-permute-start(bf16[256,128]{1,0:T(8,128)(2,1)S(1)} %bitcast.7), channel_id=1, source_target_pairs={{0,4},{2,6},{4,0},{6,2},{8,12},{10,14},{12,8},{14,10},{1,5},{3,7},... | collective-permute-start | bytes 196616 | tf_op jit(solution)/shard_map/ppermute | solution.py:261
  6.5 0.0 copy-done.1
  6.5 1.7 %collective-permute-start.3 = (s32[8,32]{1,0:T(8,128)S(1)}, s32[8,32]{1,0:T(8,128)S(1)}, u32[]{:S(2)}, u32[]{:S(2)}) collective-permute-start(s32[8,32]{1,0:T(8,128)S(1)} %bitcast.11), channel_id=1, source_target_pairs={{0,2},{2,0},{4,6},{6,4},{8,10},{10,8},{12,14},{14,12},{1,3},{3,1},... | collective-permute-start | bytes 3080 | tf_op jit(solution)/shard_map/ppermute | solution.py:261
  8.2 1.8 %shard_map.47 = (f32[8,128]{1,0:T(8,128)S(1)}, s32[8,128]{1,0:T(8,128)S(1)}, bf16[128,64,128]{2,1,0:T(8,128)(2,1)S(1)}) custom-call(s32[8,32]{1,0:T(8,128)} %bitcast.10, s32[128]{0:T(128)} %len_hbm.3, bf16[128,64,128]{2,1,0:T(8,128)(2,1)} %p_hbm.3, bf16[128,64,128]{2,1,0:T(8,128)(2,1)S(1)} %shard_map.46.refs_0_), custom_call_target="tpu_custom_call" | custom-call | flops 1048576 | bytes 2097152 | tf_op jit(solution)/shard_map/pallas_call | solution.py:123
  10.0 0.0 collective-permute-done.refs_3_
  10.0 2.4 %collective-permute-done.1.refs_2_ = bf16[256,128]{1,0:T(8,128)(2,1)S(1)} collective-permute-done((bf16[256,128]{1,0:T(8,128)(2,1)S(1)}, bf16[256,128]{1,0:T(8,128)(2,1)S(1)}, u32[]{:S(2)}, u32[]{:S(2)}) %collective-permute-start.1) | collective-permute-done | bytes 65568 | tf_op jit(solution)/shard_map/ppermute | solution.py:261
  12.4 0.0 collective-permute-done.2.refs_1_
  12.4 0.0 collective-permute-done.3.cand_ref
  12.4 0.2 shard_map.48
  12.6 1.6 %collective-permute-start.4 = (bf16[256,128]{1,0:T(8,128)(2,1)S(1)}, bf16[256,128]{1,0:T(8,128)(2,1)S(1)}, u32[]{:S(2)}, u32[]{:S(2)}) collective-permute-start(bf16[256,128]{1,0:T(8,128)(2,1)S(1)} %shard_map.48), channel_id=1, source_target_pairs={{0,2},{2,0},{4,6},{6,4},{8,10},{10,8},{12,14},{14,12},{1,3},{3,1},... | collective-permute-start | bytes 196616 | tf_op jit(solution)/shard_map/ppermute | solution.py:261
  14.2 1.7 %shard_map.49.earlier_ref = f32[4,3,128]{2,1,0:T(4,128)S(1)} custom-call(f32[8,128]{1,0:T(8,128)S(1)} %get-tuple-element.17.slots_ref, s32[8,128]{1,0:T(8,128)S(1)} %get-tuple-element.24.picks_ref, bf16[128,64,128]{2,1,0:T(8,128)(2,1)S(1)} %get-tuple-element.20.p_ref, bf16[256,128]{1,0:T(8,128)(2,1)S(1)} %bitcast.9, ...), custom_call_target="tpu_custom_call" | custom-call | flops 536870912 | bytes 2097152 | tf_op jit(solution)/shard_map/pallas_call | solution.py:221
  15.9 1.1 %collective-permute-done.4.sel_ref = bf16[256,128]{1,0:T(8,128)(2,1)S(1)} collective-permute-done((bf16[256,128]{1,0:T(8,128)(2,1)S(1)}, bf16[256,128]{1,0:T(8,128)(2,1)S(1)}, u32[]{:S(2)}, u32[]{:S(2)}) %collective-permute-start.4) | collective-permute-done | bytes 65568 | tf_op jit(solution)/shard_map/ppermute | solution.py:261
  17.0 1.5 %shard_map.50 = f32[8,3,128]{2,1,0:T(4,128)S(1)} custom-call(f32[8,128]{1,0:T(8,128)S(1)} %get-tuple-element.17.slots_ref, bf16[128,64,128]{2,1,0:T(8,128)(2,1)S(1)} %get-tuple-element.20.p_ref, bf16[256,128]{1,0:T(8,128)(2,1)S(1)} %collective-permute-done.4.sel_ref, f32[4,3,128]{2,1,0:T(4,128)S(1)} %shard_map.49.earlier_ref), custom_call_target="tpu_custom_call" | custom-call | flops 536870912 | bytes 2097152 | tf_op jit(solution)/shard_map/pallas_call | solution.py:221
  18.4 11.1 %all_to_all.5.in_ref = f32[8,3,128]{2,1,0:T(4,128)S(1)} all-to-all(f32[8,3,128]{2,1,0:T(4,128)S(1)} %shard_map.50), channel_id=1, replica_groups=mesh['grp'=2,'psg'=8,'qry'=2] {'psg'}, dimensions={0} | all-to-all | bytes 24576 | tf_op jit(solution)/shard_map/all_to_all | solution.py:299
  29.5 0.8 %shard_map.51 = f32[8,2,16,32]{3,2,1,0:T(8,128)} custom-call(f32[8,3,128]{2,1,0:T(4,128)S(1)} %all_to_all.5.in_ref), custom_call_target="tpu_custom_call" | custom-call | tf_op jit(solution)/shard_map/pallas_call | solution.py:250
Async XLA Ops:
  0.0 0.8 %copy-start = (bf16[8,32,128]{2,1,0:T(8,128)(2,1)S(1)}, bf16[8,32,128]{2,1,0:T(8,128)(2,1)}, u32[]{:S(2)}) copy-start(bf16[8,32,128]{2,1,0:T(8,128)(2,1)} %param.4) | copy-start | bytes 196612
  0.0 6.5 %copy-start.1 = (s32[1,8,32]{2,1,0:T(8,128)S(1)}, s32[1,8,32]{2,1,0:T(8,128)}, u32[]{:S(2)}) copy-start(s32[1,8,32]{2,1,0:T(8,128)} %param.7) | copy-start | bytes 3076
  0.8 9.1 %collective-permute-start = (bf16[256,128]{1,0:T(8,128)(2,1)S(1)}, bf16[256,128]{1,0:T(8,128)(2,1)S(1)}, u32[]{:S(2)}, u32[]{:S(2)}) collective-permute-start(bf16[256,128]{1,0:T(8,128)(2,1)S(1)} %bitcast.5), channel_id=1, source_target_pairs={{0,12},{2,14},{4,8},{6,10},{8,4},{10,6},{12,0},{14,2},{1,13},{3,15... | collective-permute-start | bytes 196616 | tf_op jit(solution)/shard_map/ppermute | solution.py:261
  5.9 6.5 %collective-permute-start.1 = (bf16[256,128]{1,0:T(8,128)(2,1)S(1)}, bf16[256,128]{1,0:T(8,128)(2,1)S(1)}, u32[]{:S(2)}, u32[]{:S(2)}) collective-permute-start(bf16[256,128]{1,0:T(8,128)(2,1)S(1)} %bitcast.6), channel_id=1, source_target_pairs={{0,8},{2,10},{4,12},{6,14},{8,0},{10,2},{12,4},{14,6},{1,9},{3,11}... | collective-permute-start | bytes 196616 | tf_op jit(solution)/shard_map/ppermute | solution.py:261
  5.9 6.5 %collective-permute-start.2 = (bf16[256,128]{1,0:T(8,128)(2,1)S(1)}, bf16[256,128]{1,0:T(8,128)(2,1)S(1)}, u32[]{:S(2)}, u32[]{:S(2)}) collective-permute-start(bf16[256,128]{1,0:T(8,128)(2,1)S(1)} %bitcast.7), channel_id=1, source_target_pairs={{0,4},{2,6},{4,0},{6,2},{8,12},{10,14},{12,8},{14,10},{1,5},{3,7},... | collective-permute-start | bytes 196616 | tf_op jit(solution)/shard_map/ppermute | solution.py:261
  6.5 6.0 %collective-permute-start.3 = (s32[8,32]{1,0:T(8,128)S(1)}, s32[8,32]{1,0:T(8,128)S(1)}, u32[]{:S(2)}, u32[]{:S(2)}) collective-permute-start(s32[8,32]{1,0:T(8,128)S(1)} %bitcast.11), channel_id=1, source_target_pairs={{0,2},{2,0},{4,6},{6,4},{8,10},{10,8},{12,14},{14,12},{1,3},{3,1},... | collective-permute-start | bytes 3080 | tf_op jit(solution)/shard_map/ppermute | solution.py:261
  12.6 4.3 %collective-permute-start.4 = (bf16[256,128]{1,0:T(8,128)(2,1)S(1)}, bf16[256,128]{1,0:T(8,128)(2,1)S(1)}, u32[]{:S(2)}, u32[]{:S(2)}) collective-permute-start(bf16[256,128]{1,0:T(8,128)(2,1)S(1)} %shard_map.48), channel_id=1, source_target_pairs={{0,2},{2,0},{4,6},{6,4},{8,10},{10,8},{12,14},{14,12},{1,3},{3,1},... | collective-permute-start | bytes 196616 | tf_op jit(solution)/shard_map/ppermute | solution.py:261

commit v11 on v7

--- a/solution.py
+++ b/solution.py
@@ -90,9 +90,15 @@
     )(*operands)
 
 
-def picked(picks_ref, owner, q_ref):
-    pick = jnp.max(picks_ref[pl.ds(owner, 1), :])
-    return q_ref[pl.ds(pick * QB * QT, QB * QT), :]
+def picked(pick, takes_first, q_refs):
+    parts = [ref[pl.ds(pick * QB * QT, QB * QT), :] for ref in q_refs]
+    return jnp.where(takes_first, *parts) if len(parts) == 2 else parts[0]
+
+
+def by_partner(partners, me, refs):
+    refs = iter(refs)
+    lowest = me >> 1 == 0
+    return [(lowest | (me >> 1 == k >> 1), [next(refs) for _ in range(2 if k else 1)]) for k in partners]
 
 
 def pack_kernel(partners, cand_ref, *refs):
@@ -101,9 +107,9 @@
     cand = cand_ref[...]
     owner = cand // QBD
     block = cand - owner * QBD
-    for n, k in enumerate(partners):
+    for n, (k, (takes_first, some_refs)) in enumerate(zip(partners, by_partner(partners, me, q_refs))):
         pick = jnp.max(jnp.where(owner == me ^ k, block, 0))
-        out_ref[n * QB * QT:(n + 1) * QB * QT, :] = q_refs[n][pl.ds(pick * QB * QT, QB * QT), :]
+        out_ref[n * QB * QT:(n + 1) * QB * QT, :] = picked(pick, takes_first, some_refs)
 
 
 def pack(partners, candidates, blocks):
@@ -121,11 +127,11 @@
     count = p_ref.shape[0]
     sel = sel_ref[...]
     tokens = sel.shape[0]
-    for g in range(count // GROUP):
-        left = p_ref[g * GROUP:(g + 1) * GROUP].reshape(GROUP * PT, DIM)
+    piece = 2 * GROUP
+    for g in range(0, count, piece):
+        left = p_ref[g:g + piece].reshape(piece * PT, DIM)
         dots = lax.dot_general(left, sel, (((1,), (1,)), ((), ())), preferred_element_type=jnp.float32)
-        best = jnp.max(dots.reshape(GROUP, PT, tokens), axis=1)
-        max_ref[g * GROUP:(g + 1) * GROUP, :] = best
+        max_ref[g:g + piece, :] = jnp.max(dots.reshape(piece, PT, tokens), axis=1)
 
     best = max_ref[...]
     high = best.astype(jnp.bfloat16)
@@ -144,8 +150,9 @@
 def score_kernel(partners, slots_ref, picks_ref, p_ref, *refs):
     q_refs, (out_ref, sel_ref, max_ref) = refs[:-3], refs[-3:]
     me = lax.axis_index("psg")
-    for n, k in enumerate(partners):
-        sel_ref[n * QB * QT:(n + 1) * QB * QT, :] = picked(picks_ref, me ^ k, q_refs[n])
+    for n, (k, (takes_first, some_refs)) in enumerate(zip(partners, by_partner(partners, me, q_refs))):
+        pick = jnp.max(picks_ref[pl.ds(me ^ k, 1), :])
+        sel_ref[n * QB * QT:(n + 1) * QB * QT, :] = picked(pick, takes_first, some_refs)
     total = score_picked(sel_ref, p_ref, max_ref)
     for n, k in enumerate(partners):
         out_ref[n, 0:QB, :] = total[n * QB:(n + 1) * QB]
@@ -164,7 +171,7 @@
 def all_kernel(slots_ref, picks_ref, p_ref, q_ref, out_ref, sel_ref, max_ref):
     some = q_ref.shape[0]
     for n in range(some):
-        sel_ref[n * QB * QT:(n + 1) * QB * QT, :] = picked(picks_ref, n, q_ref.at[n])
+        sel_ref[n * QB * QT:(n + 1) * QB * QT, :] = picked(jnp.max(picks_ref[n:n + 1, :]), True, [q_ref.at[n]])
     total = score_picked(sel_ref, p_ref, max_ref)
     for n in range(some):
         out_ref[n, 0:QB, :] = total[n * QB:(n + 1) * QB]
@@ -216,12 +223,20 @@
     def swap(x, k):
         return lax.ppermute(x, "psg", [(j, j ^ k) for j in range(shards)])
 
+    def swap_planes(x, low, high):
+        ends = [(2 * low + j, 2 * high + j) for j in range(2)]
+        return lax.ppermute(x, "psg", ends + [(high, low) for low, high in ends])
+
     near = list(range(0, shards, 2))
     theirs = swap(candidates, 1)
-    queries = {0: own} | {k: swap(own, k) for k in reversed(near[1:])}
+    pairs = [(low, high) for high in range(shards // 2) for low in range(high)]
+    arrived = {pair: swap_planes(own, *pair) for pair in pairs}
     slots, picks, clean = prepare(shards, candidates, lengths, passages)
-    *arrived, clean = lax.optimization_barrier((*[queries[k] for k in near[1:]], clean))
-    blocks = [own, *arrived]
+    clean, *swapped = lax.optimization_barrier((clean, *[arrived[pair] for pair in reversed(pairs)]))
+    arrived = dict(zip(reversed(pairs), swapped))
+    blocks = [own]
+    for k in near[1:]:
+        blocks += [arrived[pair] for pair in sorted(pairs) if pair[0] ^ pair[1] == k >> 1]
     far = swap(pack(near, theirs, blocks), 1)
     tiles = score(
         functools.partial(score_kernel, near), len(near), len(near), 1, clean, slots, picks, clean, *blocks
@@ -247,7 +262,7 @@
 def per_device(queries, passages, lengths, candidates):
     shards = lax.axis_size("psg")
     rows = passages.shape[0] // PBS
-    form = by_partners if shards in (4, 8) else by_gather
+    form = by_partners if shards == 8 else by_gather
     tiles = form(
         queries.reshape(QBD * QB * QT, DIM), shards, candidates.reshape(rows, KB), lengths, passages
     )

time: 29.2 us -> 39.5 us (1.35)
  starting transfers between devices: 8.88 us -> 13.9 us
  blocking collectives: 11.2 us -> 15.9 us
    ppermute x0 -> x6, starting transfers between devices: none -> 10.9 us  [swap_planes(): return lax.ppermute(x, 'psg', ends + [(high, low) for low, high in ends])]
    ppermute x5 -> x2, starting transfers between devices: 8.88 us -> 3.05 us  [swap(): return lax.ppermute(x, 'psg', [(j, j ^ k) for j in range(shards)])]
    all_to_all x1, blocking collectives: 11.2 us -> 15.9 us  [per_device(): lax.all_to_all(tiles, 'psg', split_axis=0, concat_axis=0, tiled=True)]
    ppermute x0 -> x6, waiting for transfers between devices: none -> 1.66 us  [swap_planes(): return lax.ppermute(x, 'psg', ends + [(high, low) for low, high in ends])]
    ppermute x5 -> x2, waiting for transfers between devices: 2.91 us -> 1.58 us  [swap(): return lax.ppermute(x, 'psg', [(j, j ^ k) for j in range(shards)])]
  transfers between devices with their start and end apart: 5 -> 8, of which waited for: 2 -> 3; matrix products, arithmetic and copies ran while one was open for 0% -> 0% of each run, Pallas kernels for 12% -> 9%
where the time goes in v11:
time: 39.5 us; the launch traced here: 39.2 us
  blocking collectives  15.9 us (40%)
  starting transfers between devices  13.9 us (35%)
  Pallas kernels  5.96 us (15%)
  waiting for transfers between devices  3.24 us (8%)
    all_to_all x1, blocking collectives, per_device(): lax.all_to_all(tiles, 'psg', split_axis=0, concat_axis=0, tiled=True)  15.9 us
    ppermute x6, starting transfers between devices, swap_planes(): return lax.ppermute(x, 'psg', ends + [(high, low) for low, high in ends])  10.9 us
    pallas_call x2, Pallas kernels, score(): pl.pallas_call(kernel, out_shape=jax.ShapeDtypeStruct((tiles, QB + 1, LAN...  3.13 us
    ppermute x2, starting transfers between devices, swap(): return lax.ppermute(x, 'psg', [(j, j ^ k) for j in range(shards)])  3.05 us
    pallas_call x1, Pallas kernels, prepare(): pl.pallas_call(prepare_kernel, out_shape=[jax.ShapeDtypeStruct((shards, L...  1.8 us
    ppermute x6, waiting for transfers between devices, swap_planes(): return lax.ppermute(x, 'psg', ends + [(high, low) for low, high in ends])  1.66 us
    ppermute x2, waiting for transfers between devices, swap(): return lax.ppermute(x, 'psg', [(j, j ^ k) for j in range(shards)])  1.58 us
    pallas_call x1, Pallas kernels, place(): pl.pallas_call(place_kernel, out_shape=jax.ShapeDtypeStruct((shards, QB,...  0.81 us
  transfers between devices with their start and end apart: 8, of which 3 were waited for; matrix products, arithmetic and copies ran while one was open for 0% of the time, Pallas kernels for 9%

profile of v11, /device:TPU:0, one launch (start us, length us, event | category | flops | bytes accessed | tf_op | source)
XLA Modules:
  0.0 39.2 jit_solution(8605770369729555277)
XLA Ops:
  0.0 0.0 copy-start
  0.0 5.1 %collective-permute-start.5 = (bf16[256,128]{1,0:T(8,128)(2,1)}, bf16[256,128]{1,0:T(8,128)(2,1)S(1)}, u32[]{:S(2)}, u32[]{:S(2)}) collective-permute-start(bf16[256,128]{1,0:T(8,128)(2,1)} %bitcast.5), channel_id=1, source_target_pairs={{0,4},{2,6},{4,0},{6,2},{1,5},{3,7},{5,1},{7,3},{16,20},{18,22},{2... | collective-permute-start | bytes 196616 | tf_op jit(solution)/shard_map/ppermute | solution.py:228
  5.1 1.9 %collective-permute-start.4 = (bf16[256,128]{1,0:T(8,128)(2,1)}, bf16[256,128]{1,0:T(8,128)(2,1)S(1)}, u32[]{:S(2)}, u32[]{:S(2)}) collective-permute-start(bf16[256,128]{1,0:T(8,128)(2,1)} %bitcast.6), channel_id=1, source_target_pairs={{0,8},{2,10},{8,0},{10,2},{1,9},{3,11},{9,1},{11,3},{16,24},{18,26... | collective-permute-start | bytes 196616 | tf_op jit(solution)/shard_map/ppermute | solution.py:228
  7.0 0.7 %collective-permute-start.3 = (bf16[256,128]{1,0:T(8,128)(2,1)}, bf16[256,128]{1,0:T(8,128)(2,1)S(1)}, u32[]{:S(2)}, u32[]{:S(2)}) collective-permute-start(bf16[256,128]{1,0:T(8,128)(2,1)} %bitcast.7), channel_id=1, source_target_pairs={{4,8},{6,10},{8,4},{10,6},{5,9},{7,11},{9,5},{11,7},{20,24},{22,26... | collective-permute-start | bytes 196616 | tf_op jit(solution)/shard_map/ppermute | solution.py:228
  7.7 1.9 %collective-permute-start.2 = (bf16[256,128]{1,0:T(8,128)(2,1)}, bf16[256,128]{1,0:T(8,128)(2,1)S(1)}, u32[]{:S(2)}, u32[]{:S(2)}) collective-permute-start(bf16[256,128]{1,0:T(8,128)(2,1)} %bitcast.8), channel_id=1, source_target_pairs={{0,12},{2,14},{12,0},{14,2},{1,13},{3,15},{13,1},{15,3},{16,28},{1... | collective-permute-start | bytes 196616 | tf_op jit(solution)/shard_map/ppermute | solution.py:228
  9.6 0.7 %collective-permute-start.1 = (bf16[256,128]{1,0:T(8,128)(2,1)}, bf16[256,128]{1,0:T(8,128)(2,1)S(1)}, u32[]{:S(2)}, u32[]{:S(2)}) collective-permute-start(bf16[256,128]{1,0:T(8,128)(2,1)} %bitcast.9), channel_id=1, source_target_pairs={{4,12},{6,14},{12,4},{14,6},{5,13},{7,15},{13,5},{15,7},{20,28},{2... | collective-permute-start | bytes 196616 | tf_op jit(solution)/shard_map/ppermute | solution.py:228
  10.3 0.0 collective-permute-done.5.refs_1_
  10.3 0.7 %collective-permute-start = (bf16[256,128]{1,0:T(8,128)(2,1)}, bf16[256,128]{1,0:T(8,128)(2,1)S(1)}, u32[]{:S(2)}, u32[]{:S(2)}) collective-permute-start(bf16[256,128]{1,0:T(8,128)(2,1)} %bitcast.10), channel_id=1, source_target_pairs={{8,12},{10,14},{12,8},{14,10},{9,13},{11,15},{13,9},{15,11},{24,28... | collective-permute-start | bytes 196616 | tf_op jit(solution)/shard_map/ppermute | solution.py:228
  10.9 1.6 %collective-permute-done.4.refs_3_ = bf16[256,128]{1,0:T(8,128)(2,1)S(1)} collective-permute-done((bf16[256,128]{1,0:T(8,128)(2,1)}, bf16[256,128]{1,0:T(8,128)(2,1)S(1)}, u32[]{:S(2)}, u32[]{:S(2)}) %collective-permute-start.4) | collective-permute-done | bytes 65568 | tf_op jit(solution)/shard_map/ppermute | solution.py:228
  12.6 1.5 %collective-permute-start.6 = (s32[8,32]{1,0:T(8,128)}, s32[8,32]{1,0:T(8,128)S(1)}, u32[]{:S(2)}, u32[]{:S(2)}) collective-permute-start(s32[8,32]{1,0:T(8,128)} %bitcast.13), channel_id=1, source_target_pairs={{0,2},{2,0},{4,6},{6,4},{8,10},{10,8},{12,14},{14,12},{1,3},{3,1},... | collective-permute-start | bytes 3080 | tf_op jit(solution)/shard_map/ppermute | solution.py:224
  14.1 1.8 %shard_map.46 = (f32[8,128]{1,0:T(8,128)S(1)}, s32[8,128]{1,0:T(8,128)S(1)}, bf16[128,64,128]{2,1,0:T(8,128)(2,1)S(1)}) custom-call(s32[8,32]{1,0:T(8,128)} %bitcast.14, s32[128]{0:T(128)} %len_hbm.1, bf16[128,64,128]{2,1,0:T(8,128)(2,1)} %p_hbm.1), custom_call_target="tpu_custom_call" | custom-call | flops 1048576 | bytes 2097152 | tf_op jit(solution)/shard_map/pallas_call | solution.py:73
  15.9 0.0 collective-permute-done.3.refs_6_
  15.9 0.0 collective-permute-done.2.refs_5_
  15.9 0.0 collective-permute-done.1.refs_4_
  15.9 0.0 collective-permute-done.refs_2_
  15.9 0.5 %collective-permute-done.6.cand_ref = s32[8,32]{1,0:T(8,128)S(1)} collective-permute-done((s32[8,32]{1,0:T(8,128)}, s32[8,32]{1,0:T(8,128)S(1)}, u32[]{:S(2)}, u32[]{:S(2)}) %collective-permute-start.6) | collective-permute-done | bytes 1056 | tf_op jit(solution)/shard_map/ppermute | solution.py:224
  16.4 0.0 copy-done
  16.4 0.2 shard_map.47
  16.6 1.6 %collective-permute-start.7 = (bf16[256,128]{1,0:T(8,128)(2,1)S(1)}, bf16[256,128]{1,0:T(8,128)(2,1)S(1)}, u32[]{:S(2)}, u32[]{:S(2)}) collective-permute-start(bf16[256,128]{1,0:T(8,128)(2,1)S(1)} %shard_map.47), channel_id=1, source_target_pairs={{0,2},{2,0},{4,6},{6,4},{8,10},{10,8},{12,14},{14,12},{1,3},{3,1},... | collective-permute-start | bytes 196616 | tf_op jit(solution)/shard_map/ppermute | solution.py:224
  18.2 1.7 %shard_map.48.earlier_ref = f32[4,3,128]{2,1,0:T(4,128)S(1)} custom-call(f32[8,128]{1,0:T(8,128)S(1)} %get-tuple-element.17.slots_ref, s32[8,128]{1,0:T(8,128)S(1)} %get-tuple-element.26.picks_ref, bf16[128,64,128]{2,1,0:T(8,128)(2,1)S(1)} %get-tuple-element.19.p_ref, bf16[256,128]{1,0:T(8,128)(2,1)S(1)} %bitcast.12, ...), custom_call_target="tpu_custom_call" | custom-call | flops 536870912 | bytes 2097152 | tf_op jit(solution)/shard_map/pallas_call | solution.py:184
  19.9 1.1 %collective-permute-done.7.sel_ref = bf16[256,128]{1,0:T(8,128)(2,1)S(1)} collective-permute-done((bf16[256,128]{1,0:T(8,128)(2,1)S(1)}, bf16[256,128]{1,0:T(8,128)(2,1)S(1)}, u32[]{:S(2)}, u32[]{:S(2)}) %collective-permute-start.7) | collective-permute-done | bytes 65568 | tf_op jit(solution)/shard_map/ppermute | solution.py:224
  21.0 1.5 %shard_map.49 = f32[8,3,128]{2,1,0:T(4,128)S(1)} custom-call(f32[8,128]{1,0:T(8,128)S(1)} %get-tuple-element.17.slots_ref, bf16[128,64,128]{2,1,0:T(8,128)(2,1)S(1)} %get-tuple-element.19.p_ref, bf16[256,128]{1,0:T(8,128)(2,1)S(1)} %collective-permute-done.7.sel_ref, f32[4,3,128]{2,1,0:T(4,128)S(1)} %shard_map.48.earlier_ref), custom_call_target="tpu_custom_call" | custom-call | flops 536870912 | bytes 2097152 | tf_op jit(solution)/shard_map/pallas_call | solution.py:184
  22.4 15.9 %all_to_all.5.in_ref = f32[8,3,128]{2,1,0:T(4,128)S(1)} all-to-all(f32[8,3,128]{2,1,0:T(4,128)S(1)} %shard_map.49), channel_id=1, replica_groups=mesh['grp'=2,'psg'=8,'qry'=2] {'psg'}, dimensions={0} | all-to-all | bytes 24576 | tf_op jit(solution)/shard_map/all_to_all | solution.py:269
  38.3 0.8 %shard_map.50 = f32[8,2,16,32]{3,2,1,0:T(8,128)} custom-call(f32[8,3,128]{2,1,0:T(4,128)S(1)} %all_to_all.5.in_ref), custom_call_target="tpu_custom_call" | custom-call | tf_op jit(solution)/shard_map/pallas_call | solution.py:213
Async XLA Ops:
  0.0 16.4 %copy-start = (bf16[8,32,128]{2,1,0:T(8,128)(2,1)S(1)}, bf16[8,32,128]{2,1,0:T(8,128)(2,1)}, u32[]{:S(2)}) copy-start(bf16[8,32,128]{2,1,0:T(8,128)(2,1)} %param.4) | copy-start | bytes 196612
  0.0 10.3 %collective-permute-start.5 = (bf16[256,128]{1,0:T(8,128)(2,1)}, bf16[256,128]{1,0:T(8,128)(2,1)S(1)}, u32[]{:S(2)}, u32[]{:S(2)}) collective-permute-start(bf16[256,128]{1,0:T(8,128)(2,1)} %bitcast.5), channel_id=1, source_target_pairs={{0,4},{2,6},{4,0},{6,2},{1,5},{3,7},{5,1},{7,3},{16,20},{18,22},{2... | collective-permute-start | bytes 196616 | tf_op jit(solution)/shard_map/ppermute | solution.py:228
  5.1 7.5 %collective-permute-start.4 = (bf16[256,128]{1,0:T(8,128)(2,1)}, bf16[256,128]{1,0:T(8,128)(2,1)S(1)}, u32[]{:S(2)}, u32[]{:S(2)}) collective-permute-start(bf16[256,128]{1,0:T(8,128)(2,1)} %bitcast.6), channel_id=1, source_target_pairs={{0,8},{2,10},{8,0},{10,2},{1,9},{3,11},{9,1},{11,3},{16,24},{18,26... | collective-permute-start | bytes 196616 | tf_op jit(solution)/shard_map/ppermute | solution.py:228
  7.0 8.9 %collective-permute-start.3 = (bf16[256,128]{1,0:T(8,128)(2,1)}, bf16[256,128]{1,0:T(8,128)(2,1)S(1)}, u32[]{:S(2)}, u32[]{:S(2)}) collective-permute-start(bf16[256,128]{1,0:T(8,128)(2,1)} %bitcast.7), channel_id=1, source_target_pairs={{4,8},{6,10},{8,4},{10,6},{5,9},{7,11},{9,5},{11,7},{20,24},{22,26... | collective-permute-start | bytes 196616 | tf_op jit(solution)/shard_map/ppermute | solution.py:228
  7.7 8.2 %collective-permute-start.2 = (bf16[256,128]{1,0:T(8,128)(2,1)}, bf16[256,128]{1,0:T(8,128)(2,1)S(1)}, u32[]{:S(2)}, u32[]{:S(2)}) collective-permute-start(bf16[256,128]{1,0:T(8,128)(2,1)} %bitcast.8), channel_id=1, source_target_pairs={{0,12},{2,14},{12,0},{14,2},{1,13},{3,15},{13,1},{15,3},{16,28},{1... | collective-permute-start | bytes 196616 | tf_op jit(solution)/shard_map/ppermute | solution.py:228
  9.6 6.3 %collective-permute-start.1 = (bf16[256,128]{1,0:T(8,128)(2,1)}, bf16[256,128]{1,0:T(8,128)(2,1)S(1)}, u32[]{:S(2)}, u32[]{:S(2)}) collective-permute-start(bf16[256,128]{1,0:T(8,128)(2,1)} %bitcast.9), channel_id=1, source_target_pairs={{4,12},{6,14},{12,4},{14,6},{5,13},{7,15},{13,5},{15,7},{20,28},{2... | collective-permute-start | bytes 196616 | tf_op jit(solution)/shard_map/ppermute | solution.py:228
  10.3 5.6 %collective-permute-start = (bf16[256,128]{1,0:T(8,128)(2,1)}, bf16[256,128]{1,0:T(8,128)(2,1)S(1)}, u32[]{:S(2)}, u32[]{:S(2)}) collective-permute-start(bf16[256,128]{1,0:T(8,128)(2,1)} %bitcast.10), channel_id=1, source_target_pairs={{8,12},{10,14},{12,8},{14,10},{9,13},{11,15},{13,9},{15,11},{24,28... | collective-permute-start | bytes 196616 | tf_op jit(solution)/shard_map/ppermute | solution.py:228
  12.6 3.8 %collective-permute-start.6 = (s32[8,32]{1,0:T(8,128)}, s32[8,32]{1,0:T(8,128)S(1)}, u32[]{:S(2)}, u32[]{:S(2)}) collective-permute-start(s32[8,32]{1,0:T(8,128)} %bitcast.13), channel_id=1, source_target_pairs={{0,2},{2,0},{4,6},{6,4},{8,10},{10,8},{12,14},{14,12},{1,3},{3,1},... | collective-permute-start | bytes 3080 | tf_op jit(solution)/shard_map/ppermute | solution.py:224
  16.6 4.3 %collective-permute-start.7 = (bf16[256,128]{1,0:T(8,128)(2,1)S(1)}, bf16[256,128]{1,0:T(8,128)(2,1)S(1)}, u32[]{:S(2)}, u32[]{:S(2)}) collective-permute-start(bf16[256,128]{1,0:T(8,128)(2,1)S(1)} %shard_map.47), channel_id=1, source_target_pairs={{0,2},{2,0},{4,6},{6,4},{8,10},{10,8},{12,14},{14,12},{1,3},{3,1},... | collective-permute-start | bytes 196616 | tf_op jit(solution)/shard_map/ppermute | solution.py:224

commit v12 on v9

--- a/solution.py
+++ b/solution.py
@@ -117,10 +117,11 @@
     )(candidates, *blocks)
 
 
-def score_picked(sel_ref, p_ref, max_ref, piece):
+def score_picked(sel_ref, p_ref, max_ref):
     count = p_ref.shape[0]
     sel = sel_ref[...]
     tokens = sel.shape[0]
+    piece = 2 * GROUP
     for g in range(0, count, piece):
         left = p_ref[g:g + piece].reshape(piece * PT, DIM)
         dots = lax.dot_general(left, sel, (((1,), (1,)), ((), ())), preferred_element_type=jnp.float32)
@@ -145,26 +146,25 @@
     me = lax.axis_index("psg")
     for n, k in enumerate(partners):
         sel_ref[n * QB * QT:(n + 1) * QB * QT, :] = picked(picks_ref, me ^ k, q_refs[n])
-    total = score_picked(sel_ref, p_ref, max_ref, 16)
+    total = score_picked(sel_ref, p_ref, max_ref)
     for n, k in enumerate(partners):
         out_ref[n, 0:QB, :] = total[n * QB:(n + 1) * QB]
         out_ref[n, QB:QB + 1, :] = slots_ref[pl.ds(me ^ k, 1), :]
 
 
-def join_kernel(partners, slots_ref, p_ref, sel_ref, earlier_ref, out_ref, max_ref):
+def score_far_kernel(partners, slots_ref, p_ref, sel_ref, out_ref, max_ref):
     me = lax.axis_index("psg")
-    total = score_picked(sel_ref, p_ref, max_ref, 32)
-    for n, k in enumerate(partners):
-        out_ref[me ^ k, 0:QB, :] = total[n * QB:(n + 1) * QB]
-        out_ref[me ^ k, QB:QB + 1, :] = slots_ref[pl.ds(me ^ k, 1), :]
-        out_ref[me ^ k ^ 1] = earlier_ref[n]
+    total = score_picked(sel_ref, p_ref, max_ref)
+    for n, k in enumerate(partners):
+        out_ref[n, 0:QB, :] = total[n * QB:(n + 1) * QB]
+        out_ref[n, QB:QB + 1, :] = slots_ref[pl.ds(me ^ k, 1), :]
 
 
 def all_kernel(slots_ref, picks_ref, p_ref, q_ref, out_ref, sel_ref, max_ref):
     some = q_ref.shape[0]
     for n in range(some):
         sel_ref[n * QB * QT:(n + 1) * QB * QT, :] = picked(picks_ref, n, q_ref.at[n])
-    total = score_picked(sel_ref, p_ref, max_ref, GROUP)
+    total = score_picked(sel_ref, p_ref, max_ref)
     for n in range(some):
         out_ref[n, 0:QB, :] = total[n * QB:(n + 1) * QB]
         out_ref[n, QB:QB + 1, :] = slots_ref[n:n + 1, :]
@@ -188,22 +188,41 @@
     )(*more)
 
 
-def place_kernel(in_ref, out_ref):
+def join_kernel(partners, near_ref, theirs_ref, out_ref):
+    plane = lax.axis_index("psg") >> 1
+    for n, k in enumerate(partners):
+        out_ref[plane ^ k >> 1, 0:QB + 1, :] = near_ref[n]
+        out_ref[plane ^ k >> 1, QB + 1:2 * QB + 2, :] = theirs_ref[n]
+
+
+def join(partners, near_tiles, their_tiles):
+    vmem = pl.BlockSpec(memory_space=pltpu.VMEM)
+    return pl.pallas_call(
+        functools.partial(join_kernel, partners),
+        out_shape=jax.ShapeDtypeStruct((len(partners), 2 * QB + 2, LANES), jnp.float32),
+        in_specs=[vmem] * 2,
+        out_specs=vmem,
+        compiler_params=pltpu.CompilerParams(vmem_limit_bytes=4 * 1024 * 1024),
+    )(near_tiles, their_tiles)
+
+
+def place_kernel(paired, in_ref, out_ref):
     slots = out_ref.shape[-1]
+    side = lax.axis_index("psg") & 1 if paired else 0
     m = lax.broadcasted_iota(jnp.int32, (PBS, LANES), 0)
-    for j in range(in_ref.shape[0]):
-        row = in_ref[j, QB:QB + 1, :].astype(jnp.int32)
+    for j in range(out_ref.shape[0]):
+        tile_ref = in_ref.at[j // 2, pl.ds(j % 2 * (QB + 1), QB + 1)] if paired else in_ref.at[j]
+        row = tile_ref[QB:QB + 1, :].astype(jnp.int32)
         where = jnp.minimum(row * PBS, LANES - PBS) + m
         for i in range(QB):
-            tile = jnp.broadcast_to(in_ref[j, i:i + 1, :], (PBS, LANES))
-            out_ref[j, i] = jnp.take_along_axis(tile, where, axis=1)[:, :slots]
-
-
-def place(tiles, slots):
-    vmem = pl.BlockSpec(memory_space=pltpu.VMEM)
-    shards = tiles.shape[0]
-    return pl.pallas_call(
-        place_kernel,
+            tile = jnp.broadcast_to(tile_ref[i:i + 1, :], (PBS, LANES))
+            out_ref[j ^ side, i] = jnp.take_along_axis(tile, where, axis=1)[:, :slots]
+
+
+def place(paired, tiles, shards, slots):
+    vmem = pl.BlockSpec(memory_space=pltpu.VMEM)
+    return pl.pallas_call(
+        functools.partial(place_kernel, paired),
         out_shape=jax.ShapeDtypeStruct((shards, QB, PBS, slots), jnp.float32),
         in_specs=[vmem],
         out_specs=vmem,
@@ -211,7 +230,7 @@
     )(tiles)
 
 
-def by_partners(own, shards, candidates, lengths, passages):
+def by_partners(own, shards, slot_count, candidates, lengths, passages):
     def swap(x, k):
         return lax.ppermute(x, "psg", [(j, j ^ k) for j in range(shards)])
 
@@ -222,16 +241,22 @@
     clean, *arrived = lax.optimization_barrier((clean, *[queries[k] for k in reversed(near[1:])]))
     blocks = [own, *reversed(arrived)]
     far = swap(pack(near, theirs, blocks), 1)
-    tiles = score(
+    far_tiles = score(
+        functools.partial(score_far_kernel, [k + 1 for k in near]), len(near), len(near), 0, clean, slots, clean, far
+    )
+    theirs = swap(far_tiles, 1)
+    *blocks, far_tiles = lax.optimization_barrier((*blocks, far_tiles))
+    near_tiles = score(
         functools.partial(score_kernel, near), len(near), len(near), 1, clean, slots, picks, clean, *blocks
     )
-    far, tiles = lax.optimization_barrier((far, tiles))
-    return score(
-        functools.partial(join_kernel, [k + 1 for k in near]), shards, len(near), 0, clean, slots, clean, far, tiles
-    )
-
-
-def by_gather(own, shards, candidates, lengths, passages):
+    planes = [[j + side for j in near] for side in range(2)]
+    tiles = lax.all_to_all(
+        join(near, near_tiles, theirs), "psg", split_axis=0, concat_axis=0, tiled=True, axis_index_groups=planes
+    )
+    return place(True, tiles, shards, slot_count)
+
+
+def by_gather(own, shards, slot_count, candidates, lengths, passages):
     slots, picks, clean = prepare(shards, candidates, lengths, passages)
     gathered = lax.all_gather(own, "psg", axis=0)
     some = min(shards, 8)
@@ -240,18 +265,20 @@
         return score(all_kernel, some, some, 1, clean, items[0], items[1], clean, items[2])
 
     parts = [x.reshape(shards // some, some, *x.shape[1:]) for x in (slots, picks, gathered)]
-    return lax.map(score_some, parts).reshape(shards, QB + 1, LANES)
+    tiles = lax.map(score_some, parts).reshape(shards, QB + 1, LANES)
+    tiles = lax.all_to_all(tiles, "psg", split_axis=0, concat_axis=0, tiled=True)
+    return place(False, tiles, shards, slot_count)
 
 
 def per_device(queries, passages, lengths, candidates):
     shards = lax.axis_size("psg")
     rows = passages.shape[0] // PBS
-    form = by_partners if shards in (4, 8) else by_gather
-    tiles = form(
-        queries.reshape(QBD * QB * QT, DIM), shards, candidates.reshape(rows, KB), lengths, passages
-    )
-    tiles = lax.all_to_all(tiles, "psg", split_axis=0, concat_axis=0, tiled=True)
-    return place(tiles, rows * KB // shards).transpose(0, 3, 1, 2)[None]
+    form = by_partners if shards == 8 else by_gather
+    placed = form(
+        queries.reshape(QBD * QB * QT, DIM), shards, rows * KB // shards,
+        candidates.reshape(rows, KB), lengths, passages,
+    )
+    return placed.transpose(0, 3, 1, 2)[None]
 
 
 def solution(mesh):

time: 29.3 us -> 31.1 us (1.061)
  waiting for transfers between devices: 3.89 us -> 6.05 us
  blocking collectives: 10.4 us -> 8.43 us
  starting transfers between devices: 8.88 us -> 10.4 us
    ppermute x5 -> x6, waiting for transfers between devices: 3.89 us -> 6.05 us  [swap(): return lax.ppermute(x, 'psg', [(j, j ^ k) for j in range(shards)])]
    all_to_all x1, blocking collectives: 10.4 us -> 8.43 us  [by_partners(): lax.all_to_all(join(near, near_tiles, theirs), 'psg', split_axis=0, conca...]
    ppermute x5 -> x6, starting transfers between devices: 8.88 us -> 10.4 us  [swap(): return lax.ppermute(x, 'psg', [(j, j ^ k) for j in range(shards)])]
    pallas_call x1 -> x2, Pallas kernels: 0.81 us -> 0.81 us  [the longest x1 0.81 us: place(): pl.pallas_call(functools.partial(place_kernel, paired), out_shape=jax.Sha...]
  transfers between devices with their start and end apart: 5 -> 6, of which waited for: 3 -> 4; matrix products, arithmetic and copies ran while one was open for 0% -> 0% of each run, Pallas kernels for 12% -> 11%
where the time goes in v12:
time: 31.1 us; the launch traced here: 30.9 us
  starting transfers between devices  10.4 us (33%)
  blocking collectives  8.43 us (27%)
  waiting for transfers between devices  6.05 us (19%)
  Pallas kernels  5.95 us (19%)
    ppermute x6, starting transfers between devices, swap(): return lax.ppermute(x, 'psg', [(j, j ^ k) for j in range(shards)])  10.4 us
    all_to_all x1, blocking collectives, by_partners(): lax.all_to_all(join(near, near_tiles, theirs), 'psg', split_axis=0, conca...  8.43 us
    ppermute x6, waiting for transfers between devices, swap(): return lax.ppermute(x, 'psg', [(j, j ^ k) for j in range(shards)])  6.05 us
    pallas_call x2, Pallas kernels, score(): pl.pallas_call(kernel, out_shape=jax.ShapeDtypeStruct((tiles, QB + 1, LAN...  3.13 us
    pallas_call x1, Pallas kernels, prepare(): pl.pallas_call(prepare_kernel, out_shape=[jax.ShapeDtypeStruct((shards, L...  1.8 us
    pallas_call x1, Pallas kernels, place(): pl.pallas_call(functools.partial(place_kernel, paired), out_shape=jax.Sha...  0.81 us
  transfers between devices with their start and end apart: 6, of which 4 were waited for; matrix products, arithmetic and copies ran while one was open for 0% of the time, Pallas kernels for 11%

profile of v12, /device:TPU:0, one launch (start us, length us, event | category | flops | bytes accessed | tf_op | source)
XLA Modules:
  0.0 30.9 jit_solution(17338676219118730590)
XLA Ops:
  0.0 0.0 copy-start
  0.0 3.0 %collective-permute-start.2 = (bf16[256,128]{1,0:T(8,128)(2,1)}, bf16[256,128]{1,0:T(8,128)(2,1)S(1)}, u32[]{:S(2)}, u32[]{:S(2)}) collective-permute-start(bf16[256,128]{1,0:T(8,128)(2,1)} %bitcast.5), channel_id=1, source_target_pairs={{0,4},{2,6},{4,0},{6,2},{8,12},{10,14},{12,8},{14,10},{1,5},{3,7},... | collective-permute-start | bytes 196616 | tf_op jit(solution)/shard_map/ppermute | solution.py:235
  3.0 2.6 %collective-permute-start.1 = (bf16[256,128]{1,0:T(8,128)(2,1)}, bf16[256,128]{1,0:T(8,128)(2,1)S(1)}, u32[]{:S(2)}, u32[]{:S(2)}) collective-permute-start(bf16[256,128]{1,0:T(8,128)(2,1)} %bitcast.6), channel_id=1, source_target_pairs={{0,8},{2,10},{4,12},{6,14},{8,0},{10,2},{12,4},{14,6},{1,9},{3,11}... | collective-permute-start | bytes 196616 | tf_op jit(solution)/shard_map/ppermute | solution.py:235
  5.6 0.0 collective-permute-start
  5.6 1.7 %collective-permute-start.3 = (s32[8,32]{1,0:T(8,128)}, s32[8,32]{1,0:T(8,128)S(1)}, u32[]{:S(2)}, u32[]{:S(2)}) collective-permute-start(s32[8,32]{1,0:T(8,128)} %bitcast.10), channel_id=1, source_target_pairs={{0,2},{2,0},{4,6},{6,4},{8,10},{10,8},{12,14},{14,12},{1,3},{3,1},... | collective-permute-start | bytes 3080 | tf_op jit(solution)/shard_map/ppermute | solution.py:235
  7.3 1.8 %shard_map.46 = (f32[8,128]{1,0:T(8,128)S(1)}, s32[8,128]{1,0:T(8,128)S(1)}, bf16[128,64,128]{2,1,0:T(8,128)(2,1)S(1)}) custom-call(s32[8,32]{1,0:T(8,128)} %bitcast.11, s32[128]{0:T(128)} %len_hbm.1, bf16[128,64,128]{2,1,0:T(8,128)(2,1)} %p_hbm.1), custom_call_target="tpu_custom_call" | custom-call | flops 1048576 | bytes 2097152 | tf_op jit(solution)/shard_map/pallas_call | solution.py:73
  9.1 0.0 collective-permute-done.2.refs_1_
  9.1 1.4 %collective-permute-done.1.refs_2_ = bf16[256,128]{1,0:T(8,128)(2,1)S(1)} collective-permute-done((bf16[256,128]{1,0:T(8,128)(2,1)}, bf16[256,128]{1,0:T(8,128)(2,1)S(1)}, u32[]{:S(2)}, u32[]{:S(2)}) %collective-permute-start.1) | collective-permute-done | bytes 65568 | tf_op jit(solution)/shard_map/ppermute | solution.py:235
  10.5 1.4 %collective-permute-done.refs_3_ = bf16[256,128]{1,0:T(8,128)(2,1)S(1)} collective-permute-done((bf16[256,128]{1,0:T(8,128)(2,1)}, bf16[256,128]{1,0:T(8,128)(2,1)S(1)}, u32[]{:S(2)}, u32[]{:S(2)}) %collective-permute-start) | collective-permute-done | bytes 65568 | tf_op jit(solution)/shard_map/ppermute | solution.py:235
  11.9 0.0 collective-permute-done.3.cand_ref
  11.9 0.0 copy-done
  11.9 0.2 shard_map.47
  12.2 1.6 %collective-permute-start.4 = (bf16[256,128]{1,0:T(8,128)(2,1)S(1)}, bf16[256,128]{1,0:T(8,128)(2,1)S(1)}, u32[]{:S(2)}, u32[]{:S(2)}) collective-permute-start(bf16[256,128]{1,0:T(8,128)(2,1)S(1)} %shard_map.47), channel_id=1, source_target_pairs={{0,2},{2,0},{4,6},{6,4},{8,10},{10,8},{12,14},{14,12},{1,3},{3,1},... | collective-permute-start | bytes 196616 | tf_op jit(solution)/shard_map/ppermute | solution.py:235
  13.7 2.8 %collective-permute-done.4.sel_ref = bf16[256,128]{1,0:T(8,128)(2,1)S(1)} collective-permute-done((bf16[256,128]{1,0:T(8,128)(2,1)S(1)}, bf16[256,128]{1,0:T(8,128)(2,1)S(1)}, u32[]{:S(2)}, u32[]{:S(2)}) %collective-permute-start.4) | collective-permute-done | bytes 65568 | tf_op jit(solution)/shard_map/ppermute | solution.py:235
  16.5 1.5 %shard_map.48 = f32[4,3,128]{2,1,0:T(4,128)S(1)} custom-call(f32[8,128]{1,0:T(8,128)S(1)} %get-tuple-element.16.slots_ref, bf16[128,64,128]{2,1,0:T(8,128)(2,1)S(1)} %get-tuple-element.19.p_ref, bf16[256,128]{1,0:T(8,128)(2,1)S(1)} %collective-permute-done.4.sel_ref), custom_call_target="tpu_custom_call" | custom-call | flops 536870912 | bytes 2097152 | tf_op jit(solution)/shard_map/pallas_call | solution.py:176
  17.9 1.5 %collective-permute-start.5 = (f32[4,3,128]{2,1,0:T(4,128)S(1)}, f32[4,3,128]{2,1,0:T(4,128)S(1)}, u32[]{:S(2)}, u32[]{:S(2)}) collective-permute-start(f32[4,3,128]{2,1,0:T(4,128)S(1)} %shard_map.48), channel_id=1, source_target_pairs={{0,2},{2,0},{4,6},{6,4},{8,10},{10,8},{12,14},{14,12},{1,3},{3,1},... | collective-permute-start | bytes 18440 | tf_op jit(solution)/shard_map/ppermute | solution.py:235
  19.5 1.7 %shard_map.49.near_ref = f32[4,3,128]{2,1,0:T(4,128)S(1)} custom-call(f32[8,128]{1,0:T(8,128)S(1)} %get-tuple-element.16.slots_ref, s32[8,128]{1,0:T(8,128)S(1)} %get-tuple-element.17.picks_ref, bf16[128,64,128]{2,1,0:T(8,128)(2,1)S(1)} %get-tuple-element.19.p_ref, bf16[256,128]{1,0:T(8,128)(2,1)S(1)} %bitcast.9, ...), custom_call_target="tpu_custom_call" | custom-call | flops 536870912 | bytes 2097152 | tf_op jit(solution)/shard_map/pallas_call | solution.py:176
  21.1 0.5 %collective-permute-done.5.theirs_ref = f32[4,3,128]{2,1,0:T(4,128)S(1)} collective-permute-done((f32[4,3,128]{2,1,0:T(4,128)S(1)}, f32[4,3,128]{2,1,0:T(4,128)S(1)}, u32[]{:S(2)}, u32[]{:S(2)}) %collective-permute-start.5) | collective-permute-done | bytes 6176 | tf_op jit(solution)/shard_map/ppermute | solution.py:235
  21.6 8.4 %all_to_all.5.in_ref = f32[4,6,128]{2,1,0:T(8,128)S(1)} all-to-all(f32[4,6,128]{2,1,0:T(8,128)S(1)} %shard_map.50), channel_id=1, replica_groups={{0,4,8,12},{2,6,10,14},{1,5,9,13},{3,7,11,15},{16,20,24,28},{18,22,26,3..., dimensions={0} | all-to-all | bytes 24576 | tf_op jit(solution)/shard_map/all_to_all | solution.py:253
  30.1 0.8 %shard_map.51 = f32[8,2,16,32]{3,2,1,0:T(8,128)} custom-call(f32[4,6,128]{2,1,0:T(8,128)S(1)} %all_to_all.5.in_ref), custom_call_target="tpu_custom_call" | custom-call | tf_op jit(solution)/shard_map/pallas_call | solution.py:224
  (1 shorter events, 0.0 us)
Async XLA Ops:
  0.0 11.9 %copy-start = (bf16[8,32,128]{2,1,0:T(8,128)(2,1)S(1)}, bf16[8,32,128]{2,1,0:T(8,128)(2,1)}, u32[]{:S(2)}) copy-start(bf16[8,32,128]{2,1,0:T(8,128)(2,1)} %param.4) | copy-start | bytes 196612
  0.0 9.1 %collective-permute-start.2 = (bf16[256,128]{1,0:T(8,128)(2,1)}, bf16[256,128]{1,0:T(8,128)(2,1)S(1)}, u32[]{:S(2)}, u32[]{:S(2)}) collective-permute-start(bf16[256,128]{1,0:T(8,128)(2,1)} %bitcast.5), channel_id=1, source_target_pairs={{0,4},{2,6},{4,0},{6,2},{8,12},{10,14},{12,8},{14,10},{1,5},{3,7},... | collective-permute-start | bytes 196616 | tf_op jit(solution)/shard_map/ppermute | solution.py:235
  3.0 7.5 %collective-permute-start.1 = (bf16[256,128]{1,0:T(8,128)(2,1)}, bf16[256,128]{1,0:T(8,128)(2,1)S(1)}, u32[]{:S(2)}, u32[]{:S(2)}) collective-permute-start(bf16[256,128]{1,0:T(8,128)(2,1)} %bitcast.6), channel_id=1, source_target_pairs={{0,8},{2,10},{4,12},{6,14},{8,0},{10,2},{12,4},{14,6},{1,9},{3,11}... | collective-permute-start | bytes 196616 | tf_op jit(solution)/shard_map/ppermute | solution.py:235
  5.6 6.3 %collective-permute-start = (bf16[256,128]{1,0:T(8,128)(2,1)}, bf16[256,128]{1,0:T(8,128)(2,1)S(1)}, u32[]{:S(2)}, u32[]{:S(2)}) collective-permute-start(bf16[256,128]{1,0:T(8,128)(2,1)} %bitcast.7), channel_id=1, source_target_pairs={{0,12},{2,14},{4,8},{6,10},{8,4},{10,6},{12,0},{14,2},{1,13},{3,15... | collective-permute-start | bytes 196616 | tf_op jit(solution)/shard_map/ppermute | solution.py:235
  5.6 6.3 %collective-permute-start.3 = (s32[8,32]{1,0:T(8,128)}, s32[8,32]{1,0:T(8,128)S(1)}, u32[]{:S(2)}, u32[]{:S(2)}) collective-permute-start(s32[8,32]{1,0:T(8,128)} %bitcast.10), channel_id=1, source_target_pairs={{0,2},{2,0},{4,6},{6,4},{8,10},{10,8},{12,14},{14,12},{1,3},{3,1},... | collective-permute-start | bytes 3080 | tf_op jit(solution)/shard_map/ppermute | solution.py:235
  12.2 4.3 %collective-permute-start.4 = (bf16[256,128]{1,0:T(8,128)(2,1)S(1)}, bf16[256,128]{1,0:T(8,128)(2,1)S(1)}, u32[]{:S(2)}, u32[]{:S(2)}) collective-permute-start(bf16[256,128]{1,0:T(8,128)(2,1)S(1)} %shard_map.47), channel_id=1, source_target_pairs={{0,2},{2,0},{4,6},{6,4},{8,10},{10,8},{12,14},{14,12},{1,3},{3,1},... | collective-permute-start | bytes 196616 | tf_op jit(solution)/shard_map/ppermute | solution.py:235
  17.9 3.7 %collective-permute-start.5 = (f32[4,3,128]{2,1,0:T(4,128)S(1)}, f32[4,3,128]{2,1,0:T(4,128)S(1)}, u32[]{:S(2)}, u32[]{:S(2)}) collective-permute-start(f32[4,3,128]{2,1,0:T(4,128)S(1)} %shard_map.48), channel_id=1, source_target_pairs={{0,2},{2,0},{4,6},{6,4},{8,10},{10,8},{12,14},{14,12},{1,3},{3,1},... | collective-permute-start | bytes 18440 | tf_op jit(solution)/shard_map/ppermute | solution.py:235

commit v13 on v7

--- a/solution.py
+++ b/solution.py
@@ -90,27 +90,32 @@
     )(*operands)
 
 
+def near_owner(me, step, planes):
+    return lax.rem((me >> 1) + planes - step, planes) << 1 | me & 1
+
+
 def picked(picks_ref, owner, q_ref):
     pick = jnp.max(picks_ref[pl.ds(owner, 1), :])
     return q_ref[pl.ds(pick * QB * QT, QB * QT), :]
 
 
-def pack_kernel(partners, cand_ref, *refs):
+def pack_kernel(cand_ref, *refs):
     q_refs, out_ref = refs[:-1], refs[-1]
     me = lax.axis_index("psg")
+    planes = len(q_refs)
     cand = cand_ref[...]
     owner = cand // QBD
     block = cand - owner * QBD
-    for n, k in enumerate(partners):
-        pick = jnp.max(jnp.where(owner == me ^ k, block, 0))
+    for n in range(planes):
+        pick = jnp.max(jnp.where(owner == near_owner(me, n, planes), block, 0))
         out_ref[n * QB * QT:(n + 1) * QB * QT, :] = q_refs[n][pl.ds(pick * QB * QT, QB * QT), :]
 
 
-def pack(partners, candidates, blocks):
+def pack(candidates, blocks):
     vmem = pl.BlockSpec(memory_space=pltpu.VMEM)
     return pl.pallas_call(
-        functools.partial(pack_kernel, partners),
-        out_shape=jax.ShapeDtypeStruct((len(partners) * QB * QT, DIM), blocks[0].dtype),
+        pack_kernel,
+        out_shape=jax.ShapeDtypeStruct((len(blocks) * QB * QT, DIM), blocks[0].dtype),
         in_specs=[vmem] * (1 + len(blocks)),
         out_specs=vmem,
         compiler_params=pltpu.CompilerParams(vmem_limit_bytes=4 * 1024 * 1024),
@@ -121,44 +126,48 @@
     count = p_ref.shape[0]
     sel = sel_ref[...]
     tokens = sel.shape[0]
-    for g in range(count // GROUP):
-        left = p_ref[g * GROUP:(g + 1) * GROUP].reshape(GROUP * PT, DIM)
+    piece = 2 * GROUP
+    for g in range(0, count, piece):
+        left = p_ref[g:g + piece].reshape(piece * PT, DIM)
         dots = lax.dot_general(left, sel, (((1,), (1,)), ((), ())), preferred_element_type=jnp.float32)
-        best = jnp.max(dots.reshape(GROUP, PT, tokens), axis=1)
-        max_ref[g * GROUP:(g + 1) * GROUP, :] = best
+        max_ref[g:g + piece, :] = jnp.max(dots.reshape(piece, PT, tokens), axis=1)
 
     best = max_ref[...]
     high = best.astype(jnp.bfloat16)
     rest = best - high.astype(jnp.float32)
     mid = rest.astype(jnp.bfloat16)
     low = (rest - mid.astype(jnp.float32)).astype(jnp.bfloat16)
+    parts = jnp.concatenate([low, mid, high], axis=1)
     query = lax.broadcasted_iota(jnp.int32, (tokens // QT, tokens), 0)
     token = lax.broadcasted_iota(jnp.int32, (tokens // QT, tokens), 1)
     ones = jnp.where(token // QT == query, 1.0, 0.0).astype(jnp.bfloat16)
-    total = jnp.zeros((tokens // QT, count), jnp.float32)
-    for part in (low, mid, high):
-        total = total + lax.dot_general(ones, part, (((1,), (1,)), ((), ())), preferred_element_type=jnp.float32)
+    total = lax.dot_general(
+        jnp.concatenate([ones] * 3, axis=1), parts, (((1,), (1,)), ((), ())), preferred_element_type=jnp.float32
+    )
     return total * (1.0 / QT)
 
 
-def score_kernel(partners, slots_ref, picks_ref, p_ref, *refs):
+def near_kernel(slots_ref, picks_ref, p_ref, *refs):
     q_refs, (out_ref, sel_ref, max_ref) = refs[:-3], refs[-3:]
     me = lax.axis_index("psg")
-    for n, k in enumerate(partners):
-        sel_ref[n * QB * QT:(n + 1) * QB * QT, :] = picked(picks_ref, me ^ k, q_refs[n])
+    owners = [near_owner(me, n, len(q_refs)) for n in range(len(q_refs))]
+    for n, owner in enumerate(owners):
+        sel_ref[n * QB * QT:(n + 1) * QB * QT, :] = picked(picks_ref, owner, q_refs[n])
     total = score_picked(sel_ref, p_ref, max_ref)
-    for n, k in enumerate(partners):
+    for n, owner in enumerate(owners):
         out_ref[n, 0:QB, :] = total[n * QB:(n + 1) * QB]
-        out_ref[n, QB:QB + 1, :] = slots_ref[pl.ds(me ^ k, 1), :]
-
-
-def join_kernel(partners, slots_ref, p_ref, sel_ref, earlier_ref, out_ref, max_ref):
+        out_ref[n, QB:QB + 1, :] = slots_ref[pl.ds(owner, 1), :]
+
+
+def far_kernel(slots_ref, p_ref, sel_ref, earlier_ref, out_ref, max_ref):
     me = lax.axis_index("psg")
+    planes = earlier_ref.shape[0]
     total = score_picked(sel_ref, p_ref, max_ref)
-    for n, k in enumerate(partners):
-        out_ref[me ^ k, 0:QB, :] = total[n * QB:(n + 1) * QB]
-        out_ref[me ^ k, QB:QB + 1, :] = slots_ref[pl.ds(me ^ k, 1), :]
-        out_ref[me ^ k ^ 1] = earlier_ref[n]
+    for n in range(planes):
+        owner = near_owner(me, n, planes)
+        out_ref[owner] = earlier_ref[n]
+        out_ref[owner ^ 1, 0:QB, :] = total[n * QB:(n + 1) * QB]
+        out_ref[owner ^ 1, QB:QB + 1, :] = slots_ref[pl.ds(owner ^ 1, 1), :]
 
 
 def all_kernel(slots_ref, picks_ref, p_ref, q_ref, out_ref, sel_ref, max_ref):
@@ -189,47 +198,54 @@
     )(*more)
 
 
-def place_kernel(in_ref, out_ref):
-    slots = out_ref.shape[-1]
+def place_kernel(in_ref, out_hbm, placed_ref, sems):
+    shards, _, _, slots = placed_ref.shape
     m = lax.broadcasted_iota(jnp.int32, (PBS, LANES), 0)
-    for j in range(in_ref.shape[0]):
+
+    def send(j):
+        return pltpu.make_async_copy(placed_ref.at[j], out_hbm.at[j], sems.at[j])
+
+    for j in range(shards):
         row = in_ref[j, QB:QB + 1, :].astype(jnp.int32)
         where = jnp.minimum(row * PBS, LANES - PBS) + m
         for i in range(QB):
             tile = jnp.broadcast_to(in_ref[j, i:i + 1, :], (PBS, LANES))
-            out_ref[j, i] = jnp.take_along_axis(tile, where, axis=1)[:, :slots]
+            placed_ref[j, i] = jnp.take_along_axis(tile, where, axis=1)[:, :slots]
+        send(j).start()
+    for j in range(shards):
+        send(j).wait()
 
 
 def place(tiles, slots):
-    vmem = pl.BlockSpec(memory_space=pltpu.VMEM)
-    shards = tiles.shape[0]
+    shape = (tiles.shape[0], QB, PBS, slots)
     return pl.pallas_call(
         place_kernel,
-        out_shape=jax.ShapeDtypeStruct((shards, QB, PBS, slots), jnp.float32),
-        in_specs=[vmem],
-        out_specs=vmem,
-        compiler_params=pltpu.CompilerParams(vmem_limit_bytes=8 * 1024 * 1024),
+        out_shape=jax.ShapeDtypeStruct(shape, jnp.float32),
+        in_specs=[pl.BlockSpec(memory_space=pltpu.VMEM)],
+        out_specs=pl.BlockSpec(memory_space=pltpu.HBM),
+        scratch_shapes=[pltpu.VMEM(shape, jnp.float32), pltpu.SemaphoreType.DMA((shape[0],))],
+        compiler_params=pltpu.CompilerParams(vmem_limit_bytes=16 * 1024 * 1024),
     )(tiles)
 
 
-def by_partners(own, shards, candidates, lengths, passages):
-    def swap(x, k):
-        return lax.ppermute(x, "psg", [(j, j ^ k) for j in range(shards)])
-
-    near = list(range(0, shards, 2))
-    theirs = swap(candidates, 1)
-    queries = {0: own} | {k: swap(own, k) for k in reversed(near[1:])}
+def by_planes(own, shards, candidates, lengths, passages):
+    planes = shards // 2
+
+    def swap_sides(x):
+        return lax.ppermute(x, "psg", [(j, j ^ 1) for j in range(shards)])
+
+    def shift(x, step):
+        return lax.ppermute(x, "psg", [(j, (j + 2 * step) % shards) for j in range(shards)])
+
+    theirs = swap_sides(candidates)
+    shifted = [shift(own, step) for step in range(1, planes)]
     slots, picks, clean = prepare(shards, candidates, lengths, passages)
-    *arrived, clean = lax.optimization_barrier((*[queries[k] for k in near[1:]], clean))
-    blocks = [own, *arrived]
-    far = swap(pack(near, theirs, blocks), 1)
-    tiles = score(
-        functools.partial(score_kernel, near), len(near), len(near), 1, clean, slots, picks, clean, *blocks
-    )
+    clean, *shifted = lax.optimization_barrier((clean, *reversed(shifted)))
+    blocks = [own, *reversed(shifted)]
+    far = swap_sides(pack(theirs, blocks))
+    tiles = score(near_kernel, planes, planes, 1, clean, slots, picks, clean, *blocks)
     far, tiles = lax.optimization_barrier((far, tiles))
-    return score(
-        functools.partial(join_kernel, [k + 1 for k in near]), shards, len(near), 0, clean, slots, clean, far, tiles
-    )
+    return score(far_kernel, shards, planes, 0, clean, slots, clean, far, tiles)
 
 
 def by_gather(own, shards, candidates, lengths, passages):
@@ -247,7 +263,7 @@
 def per_device(queries, passages, lengths, candidates):
     shards = lax.axis_size("psg")
     rows = passages.shape[0] // PBS
-    form = by_partners if shards in (4, 8) else by_gather
+    form = by_planes if shards in (4, 8) else by_gather
     tiles = form(
         queries.reshape(QBD * QB * QT, DIM), shards, candidates.reshape(rows, KB), lengths, passages
     )

time: 29.2 us -> 29.2 us (level)
  waiting for transfers between devices: 2.91 us -> 1.62 us
  starting transfers between devices: 8.88 us -> 10 us
    ppermute x5, waiting for transfers between devices: 2.91 us -> 1.62 us  [the longest x2 1.34 us: swap_sides(): return lax.ppermute(x, 'psg', [(j, j ^ 1) for j in range(shards)])]
    ppermute x5, starting transfers between devices: 8.88 us -> 10 us  [the longest x3 6.96 us: shift(): lax.ppermute(x, 'psg', [(j, (j + 2 * step) % shards) for j in range(shard...]
  transfers between devices with their start and end apart: 5 -> 5, of which waited for: 2 -> 4; matrix products, arithmetic and copies ran while one was open for 0% -> 0% of each run, Pallas kernels for 12% -> 12%
where the time goes in v13:
time: 29.2 us; the launch traced here: 29 us
  blocking collectives  11.4 us (39%)
  starting transfers between devices  10 us (34%)
  Pallas kernels  5.99 us (21%)
  waiting for transfers between devices  1.62 us (6%)
    all_to_all x1, blocking collectives, per_device(): lax.all_to_all(tiles, 'psg', split_axis=0, concat_axis=0, tiled=True)  11.4 us
    ppermute x3, starting transfers between devices, shift(): lax.ppermute(x, 'psg', [(j, (j + 2 * step) % shards) for j in range(shard...  6.96 us
    pallas_call x2, Pallas kernels, score(): pl.pallas_call(kernel, out_shape=jax.ShapeDtypeStruct((tiles, QB + 1, LAN...  3.15 us
    ppermute x2, starting transfers between devices, swap_sides(): return lax.ppermute(x, 'psg', [(j, j ^ 1) for j in range(shards)])  3.05 us
    pallas_call x1, Pallas kernels, prepare(): pl.pallas_call(prepare_kernel, out_shape=[jax.ShapeDtypeStruct((shards, L...  1.8 us
    ppermute x2, waiting for transfers between devices, swap_sides(): return lax.ppermute(x, 'psg', [(j, j ^ 1) for j in range(shards)])  1.34 us
    pallas_call x1, Pallas kernels, place(): pl.pallas_call(place_kernel, out_shape=jax.ShapeDtypeStruct(shape, jnp.fl...  0.83 us
  transfers between devices with their start and end apart: 5, of which 4 were waited for; matrix products, arithmetic and copies ran while one was open for 0% of the time, Pallas kernels for 12%

profile of v13, /device:TPU:0, one launch (start us, length us, event | category | flops | bytes accessed | tf_op | source)
XLA Modules:
  0.0 29.0 jit_solution(5595829723921546835)
XLA Ops:
  0.0 0.0 copy-start
  0.0 3.0 %collective-permute-start.2 = (bf16[256,128]{1,0:T(8,128)(2,1)}, bf16[256,128]{1,0:T(8,128)(2,1)S(1)}, u32[]{:S(2)}, u32[]{:S(2)}) collective-permute-start(bf16[256,128]{1,0:T(8,128)(2,1)} %bitcast.5), channel_id=1, source_target_pairs={{0,4},{2,6},{4,8},{6,10},{8,12},{10,14},{12,0},{14,2},{1,5},{3,7},... | collective-permute-start | bytes 196616 | tf_op jit(solution)/shard_map/ppermute | solution.py:238
  3.0 2.6 %collective-permute-start.1 = (bf16[256,128]{1,0:T(8,128)(2,1)}, bf16[256,128]{1,0:T(8,128)(2,1)S(1)}, u32[]{:S(2)}, u32[]{:S(2)}) collective-permute-start(bf16[256,128]{1,0:T(8,128)(2,1)} %bitcast.6), channel_id=1, source_target_pairs={{0,8},{2,10},{4,12},{6,14},{8,0},{10,2},{12,4},{14,6},{1,9},{3,11}... | collective-permute-start | bytes 196616 | tf_op jit(solution)/shard_map/ppermute | solution.py:238
  5.6 1.3 %collective-permute-start = (bf16[256,128]{1,0:T(8,128)(2,1)}, bf16[256,128]{1,0:T(8,128)(2,1)S(1)}, u32[]{:S(2)}, u32[]{:S(2)}) collective-permute-start(bf16[256,128]{1,0:T(8,128)(2,1)} %bitcast.7), channel_id=1, source_target_pairs={{0,12},{2,14},{4,0},{6,2},{8,4},{10,6},{12,8},{14,10},{1,13},{3,15... | collective-permute-start | bytes 196616 | tf_op jit(solution)/shard_map/ppermute | solution.py:238
  7.0 1.5 %collective-permute-start.3 = (s32[8,32]{1,0:T(8,128)}, s32[8,32]{1,0:T(8,128)S(1)}, u32[]{:S(2)}, u32[]{:S(2)}) collective-permute-start(s32[8,32]{1,0:T(8,128)} %bitcast.10), channel_id=1, source_target_pairs={{0,2},{2,0},{4,6},{6,4},{8,10},{10,8},{12,14},{14,12},{1,3},{3,1},... | collective-permute-start | bytes 3080 | tf_op jit(solution)/shard_map/ppermute | solution.py:235
  8.5 1.8 %shard_map.46 = (f32[8,128]{1,0:T(8,128)S(1)}, s32[8,128]{1,0:T(8,128)S(1)}, bf16[128,64,128]{2,1,0:T(8,128)(2,1)S(1)}) custom-call(s32[8,32]{1,0:T(8,128)} %bitcast.11, s32[128]{0:T(128)} %len_hbm.1, bf16[128,64,128]{2,1,0:T(8,128)(2,1)} %p_hbm.1), custom_call_target="tpu_custom_call" | custom-call | flops 1048576 | bytes 2097152 | tf_op jit(solution)/shard_map/pallas_call | solution.py:73
  10.3 0.0 collective-permute-done.2.refs_1_
  10.3 0.1 collective-permute-done.1.refs_2_
  10.4 0.2 collective-permute-done.refs_3_
  10.5 0.2 collective-permute-done.3.cand_ref
  10.8 0.0 copy-done
  10.8 0.2 shard_map.47
  11.0 1.6 %collective-permute-start.4 = (bf16[256,128]{1,0:T(8,128)(2,1)S(1)}, bf16[256,128]{1,0:T(8,128)(2,1)S(1)}, u32[]{:S(2)}, u32[]{:S(2)}) collective-permute-start(bf16[256,128]{1,0:T(8,128)(2,1)S(1)} %shard_map.47), channel_id=1, source_target_pairs={{0,2},{2,0},{4,6},{6,4},{8,10},{10,8},{12,14},{14,12},{1,3},{3,1},... | collective-permute-start | bytes 196616 | tf_op jit(solution)/shard_map/ppermute | solution.py:235
  12.6 1.7 %shard_map.48.earlier_ref = f32[4,3,128]{2,1,0:T(4,128)S(1)} custom-call(f32[8,128]{1,0:T(8,128)S(1)} %get-tuple-element.14.slots_ref, s32[8,128]{1,0:T(8,128)S(1)} %get-tuple-element.20.picks_ref, bf16[128,64,128]{2,1,0:T(8,128)(2,1)S(1)} %get-tuple-element.16.p_ref, bf16[256,128]{1,0:T(8,128)(2,1)S(1)} %bitcast.9, ...), custom_call_target="tpu_custom_call" | custom-call | flops 536870912 | bytes 2097152 | tf_op jit(solution)/shard_map/pallas_call | solution.py:186
  14.2 1.1 %collective-permute-done.4.sel_ref = bf16[256,128]{1,0:T(8,128)(2,1)S(1)} collective-permute-done((bf16[256,128]{1,0:T(8,128)(2,1)S(1)}, bf16[256,128]{1,0:T(8,128)(2,1)S(1)}, u32[]{:S(2)}, u32[]{:S(2)}) %collective-permute-start.4) | collective-permute-done | bytes 65568 | tf_op jit(solution)/shard_map/ppermute | solution.py:235
  15.3 1.5 %shard_map.49 = f32[8,3,128]{2,1,0:T(4,128)S(1)} custom-call(f32[8,128]{1,0:T(8,128)S(1)} %get-tuple-element.14.slots_ref, bf16[128,64,128]{2,1,0:T(8,128)(2,1)S(1)} %get-tuple-element.16.p_ref, bf16[256,128]{1,0:T(8,128)(2,1)S(1)} %collective-permute-done.4.sel_ref, f32[4,3,128]{2,1,0:T(4,128)S(1)} %shard_map.48.earlier_ref), custom_call_target="tpu_custom_call" | custom-call | flops 536870912 | bytes 2097152 | tf_op jit(solution)/shard_map/pallas_call | solution.py:186
  16.8 11.4 %all_to_all.5.in_ref = f32[8,3,128]{2,1,0:T(4,128)S(1)} all-to-all(f32[8,3,128]{2,1,0:T(4,128)S(1)} %shard_map.49), channel_id=1, replica_groups=mesh['grp'=2,'psg'=8,'qry'=2] {'psg'}, dimensions={0} | all-to-all | bytes 24576 | tf_op jit(solution)/shard_map/all_to_all | solution.py:270
  28.2 0.8 %shard_map.50 = f32[8,2,16,32]{3,2,1,0:T(8,128)} custom-call(f32[8,3,128]{2,1,0:T(4,128)S(1)} %all_to_all.5.in_ref), custom_call_target="tpu_custom_call" | custom-call | tf_op jit(solution)/shard_map/pallas_call | solution.py:221
Async XLA Ops:
  0.0 10.8 %copy-start = (bf16[8,32,128]{2,1,0:T(8,128)(2,1)S(1)}, bf16[8,32,128]{2,1,0:T(8,128)(2,1)}, u32[]{:S(2)}) copy-start(bf16[8,32,128]{2,1,0:T(8,128)(2,1)} %param.4) | copy-start | bytes 196612
  0.0 10.3 %collective-permute-start.2 = (bf16[256,128]{1,0:T(8,128)(2,1)}, bf16[256,128]{1,0:T(8,128)(2,1)S(1)}, u32[]{:S(2)}, u32[]{:S(2)}) collective-permute-start(bf16[256,128]{1,0:T(8,128)(2,1)} %bitcast.5), channel_id=1, source_target_pairs={{0,4},{2,6},{4,8},{6,10},{8,12},{10,14},{12,0},{14,2},{1,5},{3,7},... | collective-permute-start | bytes 196616 | tf_op jit(solution)/shard_map/ppermute | solution.py:238
  3.0 7.4 %collective-permute-start.1 = (bf16[256,128]{1,0:T(8,128)(2,1)}, bf16[256,128]{1,0:T(8,128)(2,1)S(1)}, u32[]{:S(2)}, u32[]{:S(2)}) collective-permute-start(bf16[256,128]{1,0:T(8,128)(2,1)} %bitcast.6), channel_id=1, source_target_pairs={{0,8},{2,10},{4,12},{6,14},{8,0},{10,2},{12,4},{14,6},{1,9},{3,11}... | collective-permute-start | bytes 196616 | tf_op jit(solution)/shard_map/ppermute | solution.py:238
  5.6 4.9 %collective-permute-start = (bf16[256,128]{1,0:T(8,128)(2,1)}, bf16[256,128]{1,0:T(8,128)(2,1)S(1)}, u32[]{:S(2)}, u32[]{:S(2)}) collective-permute-start(bf16[256,128]{1,0:T(8,128)(2,1)} %bitcast.7), channel_id=1, source_target_pairs={{0,12},{2,14},{4,0},{6,2},{8,4},{10,6},{12,8},{14,10},{1,13},{3,15... | collective-permute-start | bytes 196616 | tf_op jit(solution)/shard_map/ppermute | solution.py:238
  7.0 3.8 %collective-permute-start.3 = (s32[8,32]{1,0:T(8,128)}, s32[8,32]{1,0:T(8,128)S(1)}, u32[]{:S(2)}, u32[]{:S(2)}) collective-permute-start(s32[8,32]{1,0:T(8,128)} %bitcast.10), channel_id=1, source_target_pairs={{0,2},{2,0},{4,6},{6,4},{8,10},{10,8},{12,14},{14,12},{1,3},{3,1},... | collective-permute-start | bytes 3080 | tf_op jit(solution)/shard_map/ppermute | solution.py:235
  11.0 4.3 %collective-permute-start.4 = (bf16[256,128]{1,0:T(8,128)(2,1)S(1)}, bf16[256,128]{1,0:T(8,128)(2,1)S(1)}, u32[]{:S(2)}, u32[]{:S(2)}) collective-permute-start(bf16[256,128]{1,0:T(8,128)(2,1)S(1)} %shard_map.47), channel_id=1, source_target_pairs={{0,2},{2,0},{4,6},{6,4},{8,10},{10,8},{12,14},{14,12},{1,3},{3,1},... | collective-permute-start | bytes 196616 | tf_op jit(solution)/shard_map/ppermute | solution.py:235

commit v14 on v13

--- a/solution.py
+++ b/solution.py
@@ -198,33 +198,26 @@
     )(*more)
 
 
-def place_kernel(in_ref, out_hbm, placed_ref, sems):
-    shards, _, _, slots = placed_ref.shape
+def place_kernel(in_ref, out_ref):
+    slots = out_ref.shape[-1]
     m = lax.broadcasted_iota(jnp.int32, (PBS, LANES), 0)
-
-    def send(j):
-        return pltpu.make_async_copy(placed_ref.at[j], out_hbm.at[j], sems.at[j])
-
-    for j in range(shards):
+    for j in range(in_ref.shape[0]):
         row = in_ref[j, QB:QB + 1, :].astype(jnp.int32)
         where = jnp.minimum(row * PBS, LANES - PBS) + m
         for i in range(QB):
             tile = jnp.broadcast_to(in_ref[j, i:i + 1, :], (PBS, LANES))
-            placed_ref[j, i] = jnp.take_along_axis(tile, where, axis=1)[:, :slots]
-        send(j).start()
-    for j in range(shards):
-        send(j).wait()
+            out_ref[j, i] = jnp.take_along_axis(tile, where, axis=1)[:, :slots]
 
 
 def place(tiles, slots):
-    shape = (tiles.shape[0], QB, PBS, slots)
+    vmem = pl.BlockSpec(memory_space=pltpu.VMEM)
+    shards = tiles.shape[0]
     return pl.pallas_call(
         place_kernel,
-        out_shape=jax.ShapeDtypeStruct(shape, jnp.float32),
-        in_specs=[pl.BlockSpec(memory_space=pltpu.VMEM)],
-        out_specs=pl.BlockSpec(memory_space=pltpu.HBM),
-        scratch_shapes=[pltpu.VMEM(shape, jnp.float32), pltpu.SemaphoreType.DMA((shape[0],))],
-        compiler_params=pltpu.CompilerParams(vmem_limit_bytes=16 * 1024 * 1024),
+        out_shape=jax.ShapeDtypeStruct((shards, QB, PBS, slots), jnp.float32),
+        in_specs=[vmem],
+        out_specs=vmem,
+        compiler_params=pltpu.CompilerParams(vmem_limit_bytes=8 * 1024 * 1024),
     )(tiles)
 
 
@@ -240,8 +233,8 @@
     theirs = swap_sides(candidates)
     shifted = [shift(own, step) for step in range(1, planes)]
     slots, picks, clean = prepare(shards, candidates, lengths, passages)
-    clean, *shifted = lax.optimization_barrier((clean, *reversed(shifted)))
-    blocks = [own, *reversed(shifted)]
+    clean, *shifted = lax.optimization_barrier((clean, *shifted))
+    blocks = [own, *shifted]
     far = swap_sides(pack(theirs, blocks))
     tiles = score(near_kernel, planes, planes, 1, clean, slots, picks, clean, *blocks)
     far, tiles = lax.optimization_barrier((far, tiles))

time: 29.2 us -> 29.2 us (level)
  waiting for transfers between devices: 1.62 us -> 3.47 us
  blocking collectives: 11.4 us -> 10.5 us
  starting transfers between devices: 10 us -> 9.11 us
    ppermute x3, waiting for transfers between devices: 0.27 us -> 2.36 us  [shift(): lax.ppermute(x, 'psg', [(j, (j + 2 * step) % shards) for j in range(shard...]
    ppermute x3, starting transfers between devices: 6.96 us -> 6.06 us  [shift(): lax.ppermute(x, 'psg', [(j, (j + 2 * step) % shards) for j in range(shard...]
    all_to_all x1, blocking collectives: 11.4 us -> 10.5 us  [per_device(): lax.all_to_all(tiles, 'psg', split_axis=0, concat_axis=0, tiled=True)]
  transfers between devices with their start and end apart: 5 -> 5, of which waited for: 4 -> 2; matrix products, arithmetic and copies ran while one was open for 0% -> 0% of each run, Pallas kernels for 12% -> 12%
where the time goes in v14:
time: 29.2 us; the launch traced here: 29.1 us
  blocking collectives  10.5 us (36%)
  starting transfers between devices  9.11 us (31%)
  Pallas kernels  5.96 us (20%)
  waiting for transfers between devices  3.47 us (12%)
    all_to_all x1, blocking collectives, per_device(): lax.all_to_all(tiles, 'psg', split_axis=0, concat_axis=0, tiled=True)  10.5 us
    ppermute x3, starting transfers between devices, shift(): lax.ppermute(x, 'psg', [(j, (j + 2 * step) % shards) for j in range(shard...  6.06 us
    pallas_call x2, Pallas kernels, score(): pl.pallas_call(kernel, out_shape=jax.ShapeDtypeStruct((tiles, QB + 1, LAN...  3.13 us
    ppermute x2, starting transfers between devices, swap_sides(): return lax.ppermute(x, 'psg', [(j, j ^ 1) for j in range(shards)])  3.05 us
    ppermute x3, waiting for transfers between devices, shift(): lax.ppermute(x, 'psg', [(j, (j + 2 * step) % shards) for j in range(shard...  2.36 us
    pallas_call x1, Pallas kernels, prepare(): pl.pallas_call(prepare_kernel, out_shape=[jax.ShapeDtypeStruct((shards, L...  1.8 us
    ppermute x2, waiting for transfers between devices, swap_sides(): return lax.ppermute(x, 'psg', [(j, j ^ 1) for j in range(shards)])  1.11 us
    pallas_call x1, Pallas kernels, place(): pl.pallas_call(place_kernel, out_shape=jax.ShapeDtypeStruct((shards, QB,...  0.81 us
  transfers between devices with their start and end apart: 5, of which 2 were waited for; matrix products, arithmetic and copies ran while one was open for 0% of the time, Pallas kernels for 12%

profile of v14, /device:TPU:0, one launch (start us, length us, event | category | flops | bytes accessed | tf_op | source)
XLA Modules:
  0.0 29.1 jit_solution(3611737638139178561)
XLA Ops:
  0.0 0.0 copy-start
  0.0 5.0 %collective-permute-start.2 = (bf16[256,128]{1,0:T(8,128)(2,1)}, bf16[256,128]{1,0:T(8,128)(2,1)S(1)}, u32[]{:S(2)}, u32[]{:S(2)}) collective-permute-start(bf16[256,128]{1,0:T(8,128)(2,1)} %bitcast.5), channel_id=1, source_target_pairs={{0,12},{2,14},{4,0},{6,2},{8,4},{10,6},{12,8},{14,10},{1,13},{3,15... | collective-permute-start | bytes 196616 | tf_op jit(solution)/shard_map/ppermute | solution.py:231
  5.1 0.0 collective-permute-start.1
  5.1 1.0 %collective-permute-start = (bf16[256,128]{1,0:T(8,128)(2,1)}, bf16[256,128]{1,0:T(8,128)(2,1)S(1)}, u32[]{:S(2)}, u32[]{:S(2)}) collective-permute-start(bf16[256,128]{1,0:T(8,128)(2,1)} %bitcast.7), channel_id=1, source_target_pairs={{0,4},{2,6},{4,8},{6,10},{8,12},{10,14},{12,0},{14,2},{1,5},{3,7},... | collective-permute-start | bytes 196616 | tf_op jit(solution)/shard_map/ppermute | solution.py:231
  6.1 1.5 %collective-permute-start.3 = (s32[8,32]{1,0:T(8,128)}, s32[8,32]{1,0:T(8,128)S(1)}, u32[]{:S(2)}, u32[]{:S(2)}) collective-permute-start(s32[8,32]{1,0:T(8,128)} %bitcast.10), channel_id=1, source_target_pairs={{0,2},{2,0},{4,6},{6,4},{8,10},{10,8},{12,14},{14,12},{1,3},{3,1},... | collective-permute-start | bytes 3080 | tf_op jit(solution)/shard_map/ppermute | solution.py:228
  7.6 1.8 %shard_map.46 = (f32[8,128]{1,0:T(8,128)S(1)}, s32[8,128]{1,0:T(8,128)S(1)}, bf16[128,64,128]{2,1,0:T(8,128)(2,1)S(1)}) custom-call(s32[8,32]{1,0:T(8,128)} %bitcast.11, s32[128]{0:T(128)} %len_hbm.1, bf16[128,64,128]{2,1,0:T(8,128)(2,1)} %p_hbm.1), custom_call_target="tpu_custom_call" | custom-call | flops 1048576 | bytes 2097152 | tf_op jit(solution)/shard_map/pallas_call | solution.py:73
  9.4 0.0 collective-permute-done.2.refs_3_
  9.4 2.4 %collective-permute-done.1.refs_2_ = bf16[256,128]{1,0:T(8,128)(2,1)S(1)} collective-permute-done((bf16[256,128]{1,0:T(8,128)(2,1)}, bf16[256,128]{1,0:T(8,128)(2,1)S(1)}, u32[]{:S(2)}, u32[]{:S(2)}) %collective-permute-start.1) | collective-permute-done | bytes 65568 | tf_op jit(solution)/shard_map/ppermute | solution.py:231
  11.7 0.0 collective-permute-done.refs_1_
  11.7 0.0 collective-permute-done.3.cand_ref
  11.7 0.0 copy-done
  11.7 0.2 shard_map.47
  12.0 1.6 %collective-permute-start.4 = (bf16[256,128]{1,0:T(8,128)(2,1)S(1)}, bf16[256,128]{1,0:T(8,128)(2,1)S(1)}, u32[]{:S(2)}, u32[]{:S(2)}) collective-permute-start(bf16[256,128]{1,0:T(8,128)(2,1)S(1)} %shard_map.47), channel_id=1, source_target_pairs={{0,2},{2,0},{4,6},{6,4},{8,10},{10,8},{12,14},{14,12},{1,3},{3,1},... | collective-permute-start | bytes 196616 | tf_op jit(solution)/shard_map/ppermute | solution.py:228
  13.5 1.7 %shard_map.48.earlier_ref = f32[4,3,128]{2,1,0:T(4,128)S(1)} custom-call(f32[8,128]{1,0:T(8,128)S(1)} %get-tuple-element.14.slots_ref, s32[8,128]{1,0:T(8,128)S(1)} %get-tuple-element.20.picks_ref, bf16[128,64,128]{2,1,0:T(8,128)(2,1)S(1)} %get-tuple-element.16.p_ref, bf16[256,128]{1,0:T(8,128)(2,1)S(1)} %bitcast.9, ...), custom_call_target="tpu_custom_call" | custom-call | flops 536870912 | bytes 2097152 | tf_op jit(solution)/shard_map/pallas_call | solution.py:186
  15.2 1.1 %collective-permute-done.4.sel_ref = bf16[256,128]{1,0:T(8,128)(2,1)S(1)} collective-permute-done((bf16[256,128]{1,0:T(8,128)(2,1)S(1)}, bf16[256,128]{1,0:T(8,128)(2,1)S(1)}, u32[]{:S(2)}, u32[]{:S(2)}) %collective-permute-start.4) | collective-permute-done | bytes 65568 | tf_op jit(solution)/shard_map/ppermute | solution.py:228
  16.3 1.5 %shard_map.49 = f32[8,3,128]{2,1,0:T(4,128)S(1)} custom-call(f32[8,128]{1,0:T(8,128)S(1)} %get-tuple-element.14.slots_ref, bf16[128,64,128]{2,1,0:T(8,128)(2,1)S(1)} %get-tuple-element.16.p_ref, bf16[256,128]{1,0:T(8,128)(2,1)S(1)} %collective-permute-done.4.sel_ref, f32[4,3,128]{2,1,0:T(4,128)S(1)} %shard_map.48.earlier_ref), custom_call_target="tpu_custom_call" | custom-call | flops 536870912 | bytes 2097152 | tf_op jit(solution)/shard_map/pallas_call | solution.py:186
  17.8 10.5 %all_to_all.5.in_ref = f32[8,3,128]{2,1,0:T(4,128)S(1)} all-to-all(f32[8,3,128]{2,1,0:T(4,128)S(1)} %shard_map.49), channel_id=1, replica_groups=mesh['grp'=2,'psg'=8,'qry'=2] {'psg'}, dimensions={0} | all-to-all | bytes 24576 | tf_op jit(solution)/shard_map/all_to_all | solution.py:263
  28.3 0.8 %shard_map.50 = f32[8,2,16,32]{3,2,1,0:T(8,128)} custom-call(f32[8,3,128]{2,1,0:T(4,128)S(1)} %all_to_all.5.in_ref), custom_call_target="tpu_custom_call" | custom-call | tf_op jit(solution)/shard_map/pallas_call | solution.py:215
Async XLA Ops:
  0.0 11.7 %copy-start = (bf16[8,32,128]{2,1,0:T(8,128)(2,1)S(1)}, bf16[8,32,128]{2,1,0:T(8,128)(2,1)}, u32[]{:S(2)}) copy-start(bf16[8,32,128]{2,1,0:T(8,128)(2,1)} %param.4) | copy-start | bytes 196612
  0.0 9.4 %collective-permute-start.2 = (bf16[256,128]{1,0:T(8,128)(2,1)}, bf16[256,128]{1,0:T(8,128)(2,1)S(1)}, u32[]{:S(2)}, u32[]{:S(2)}) collective-permute-start(bf16[256,128]{1,0:T(8,128)(2,1)} %bitcast.5), channel_id=1, source_target_pairs={{0,12},{2,14},{4,0},{6,2},{8,4},{10,6},{12,8},{14,10},{1,13},{3,15... | collective-permute-start | bytes 196616 | tf_op jit(solution)/shard_map/ppermute | solution.py:231
  5.1 6.7 %collective-permute-start.1 = (bf16[256,128]{1,0:T(8,128)(2,1)}, bf16[256,128]{1,0:T(8,128)(2,1)S(1)}, u32[]{:S(2)}, u32[]{:S(2)}) collective-permute-start(bf16[256,128]{1,0:T(8,128)(2,1)} %bitcast.6), channel_id=1, source_target_pairs={{0,8},{2,10},{4,12},{6,14},{8,0},{10,2},{12,4},{14,6},{1,9},{3,11}... | collective-permute-start | bytes 196616 | tf_op jit(solution)/shard_map/ppermute | solution.py:231
  5.1 6.7 %collective-permute-start = (bf16[256,128]{1,0:T(8,128)(2,1)}, bf16[256,128]{1,0:T(8,128)(2,1)S(1)}, u32[]{:S(2)}, u32[]{:S(2)}) collective-permute-start(bf16[256,128]{1,0:T(8,128)(2,1)} %bitcast.7), channel_id=1, source_target_pairs={{0,4},{2,6},{4,8},{6,10},{8,12},{10,14},{12,0},{14,2},{1,5},{3,7},... | collective-permute-start | bytes 196616 | tf_op jit(solution)/shard_map/ppermute | solution.py:231
  6.1 5.7 %collective-permute-start.3 = (s32[8,32]{1,0:T(8,128)}, s32[8,32]{1,0:T(8,128)S(1)}, u32[]{:S(2)}, u32[]{:S(2)}) collective-permute-start(s32[8,32]{1,0:T(8,128)} %bitcast.10), channel_id=1, source_target_pairs={{0,2},{2,0},{4,6},{6,4},{8,10},{10,8},{12,14},{14,12},{1,3},{3,1},... | collective-permute-start | bytes 3080 | tf_op jit(solution)/shard_map/ppermute | solution.py:228
  12.0 4.3 %collective-permute-start.4 = (bf16[256,128]{1,0:T(8,128)(2,1)S(1)}, bf16[256,128]{1,0:T(8,128)(2,1)S(1)}, u32[]{:S(2)}, u32[]{:S(2)}) collective-permute-start(bf16[256,128]{1,0:T(8,128)(2,1)S(1)} %shard_map.47), channel_id=1, source_target_pairs={{0,2},{2,0},{4,6},{6,4},{8,10},{10,8},{12,14},{14,12},{1,3},{3,1},... | collective-permute-start | bytes 196616 | tf_op jit(solution)/shard_map/ppermute | solution.py:228

commit v15 on v14

--- a/solution.py
+++ b/solution.py
@@ -99,22 +99,21 @@
     return q_ref[pl.ds(pick * QB * QT, QB * QT), :]
 
 
-def pack_kernel(cand_ref, *refs):
+def pack_kernel(steps, planes, cand_ref, *refs):
     q_refs, out_ref = refs[:-1], refs[-1]
     me = lax.axis_index("psg")
-    planes = len(q_refs)
     cand = cand_ref[...]
     owner = cand // QBD
     block = cand - owner * QBD
-    for n in range(planes):
-        pick = jnp.max(jnp.where(owner == near_owner(me, n, planes), block, 0))
+    for n, step in enumerate(steps):
+        pick = jnp.max(jnp.where(owner == near_owner(me, step, planes), block, 0))
         out_ref[n * QB * QT:(n + 1) * QB * QT, :] = q_refs[n][pl.ds(pick * QB * QT, QB * QT), :]
 
 
-def pack(candidates, blocks):
+def pack(steps, planes, candidates, blocks):
     vmem = pl.BlockSpec(memory_space=pltpu.VMEM)
     return pl.pallas_call(
-        pack_kernel,
+        functools.partial(pack_kernel, steps, planes),
         out_shape=jax.ShapeDtypeStruct((len(blocks) * QB * QT, DIM), blocks[0].dtype),
         in_specs=[vmem] * (1 + len(blocks)),
         out_specs=vmem,
@@ -122,17 +121,8 @@
     )(candidates, *blocks)
 
 
-def score_picked(sel_ref, p_ref, max_ref):
-    count = p_ref.shape[0]
-    sel = sel_ref[...]
-    tokens = sel.shape[0]
-    piece = 2 * GROUP
-    for g in range(0, count, piece):
-        left = p_ref[g:g + piece].reshape(piece * PT, DIM)
-        dots = lax.dot_general(left, sel, (((1,), (1,)), ((), ())), preferred_element_type=jnp.float32)
-        max_ref[g:g + piece, :] = jnp.max(dots.reshape(piece, PT, tokens), axis=1)
-
-    best = max_ref[...]
+def sum_tokens(best):
+    tokens = best.shape[1]
     high = best.astype(jnp.bfloat16)
     rest = best - high.astype(jnp.float32)
     mid = rest.astype(jnp.bfloat16)
@@ -147,53 +137,98 @@
     return total * (1.0 / QT)
 
 
+def best_tokens(left_of, sel, max_ref):
+    count, tokens = max_ref.shape
+    piece = 2 * GROUP
+    for g in range(0, count, piece):
+        dots = lax.dot_general(left_of(g, piece), sel, (((1,), (1,)), ((), ())), preferred_element_type=jnp.float32)
+        max_ref[g:g + piece, :] = jnp.max(dots.reshape(piece, PT, tokens), axis=1)
+    return max_ref[...]
+
+
+def score_picked(sel, p_ref, max_ref):
+    def left_of(g, piece):
+        return p_ref[g:g + piece].reshape(piece * PT, DIM)
+
+    return sum_tokens(best_tokens(left_of, sel, max_ref))
+
+
+def score_picked_few(sel, p_ref, wide_ref, max_ref):
+    tokens, half = sel.shape[0], p_ref.shape[0] // 2
+    wide_ref[...] = jnp.zeros_like(wide_ref)
+    wide_ref[0:tokens, 0:DIM] = sel
+    wide_ref[tokens:, DIM:] = sel
+
+    def left_of(g, piece):
+        return jnp.concatenate(
+            [p_ref[h + g:h + g + piece].reshape(piece * PT, DIM) for h in (0, half)], axis=1
+        )
+
+    best = best_tokens(left_of, wide_ref[...], max_ref)
+    return jnp.concatenate([sum_tokens(best[:, :tokens]), sum_tokens(best[:, tokens:])], axis=1)
+
+
+def put(out_ref, place, total, n, slots_ref, owner):
+    out_ref[place, 0:QB, :] = total[n * QB:(n + 1) * QB]
+    out_ref[place, QB:QB + 1, :] = slots_ref[pl.ds(owner, 1), :]
+
+
 def near_kernel(slots_ref, picks_ref, p_ref, *refs):
     q_refs, (out_ref, sel_ref, max_ref) = refs[:-3], refs[-3:]
     me = lax.axis_index("psg")
     owners = [near_owner(me, n, len(q_refs)) for n in range(len(q_refs))]
     for n, owner in enumerate(owners):
         sel_ref[n * QB * QT:(n + 1) * QB * QT, :] = picked(picks_ref, owner, q_refs[n])
-    total = score_picked(sel_ref, p_ref, max_ref)
+    total = score_picked(sel_ref[...], p_ref, max_ref)
     for n, owner in enumerate(owners):
-        out_ref[n, 0:QB, :] = total[n * QB:(n + 1) * QB]
-        out_ref[n, QB:QB + 1, :] = slots_ref[pl.ds(owner, 1), :]
-
-
-def far_kernel(slots_ref, p_ref, sel_ref, earlier_ref, out_ref, max_ref):
+        put(out_ref, n, total, n, slots_ref, owner)
+
+
+def some_far_kernel(steps, planes, slots_ref, p_ref, sel_ref, out_ref, wide_ref, max_ref):
     me = lax.axis_index("psg")
-    planes = earlier_ref.shape[0]
-    total = score_picked(sel_ref, p_ref, max_ref)
-    for n in range(planes):
-        owner = near_owner(me, n, planes)
-        out_ref[owner] = earlier_ref[n]
-        out_ref[owner ^ 1, 0:QB, :] = total[n * QB:(n + 1) * QB]
-        out_ref[owner ^ 1, QB:QB + 1, :] = slots_ref[pl.ds(owner ^ 1, 1), :]
+    total = score_picked_few(sel_ref[...], p_ref, wide_ref, max_ref)
+    for n, step in enumerate(steps):
+        put(out_ref, n, total, n, slots_ref, near_owner(me, step, planes) ^ 1)
+
+
+def last_far_kernel(steps, planes, slots_ref, p_ref, sel_ref, near_ref, far_ref, out_ref, wide_ref, max_ref):
+    me = lax.axis_index("psg")
+    total = score_picked_few(sel_ref[...], p_ref, wide_ref, max_ref)
+    for n, step in enumerate(steps):
+        owner = near_owner(me, step, planes) ^ 1
+        put(out_ref, owner, total, n, slots_ref, owner)
+    others = [step for step in range(planes) if step not in steps]
+    for step in range(planes):
+        out_ref[near_owner(me, step, planes)] = near_ref[step]
+    for n, step in enumerate(others):
+        out_ref[near_owner(me, step, planes) ^ 1] = far_ref[n]
 
 
 def all_kernel(slots_ref, picks_ref, p_ref, q_ref, out_ref, sel_ref, max_ref):
     some = q_ref.shape[0]
     for n in range(some):
         sel_ref[n * QB * QT:(n + 1) * QB * QT, :] = picked(picks_ref, n, q_ref.at[n])
-    total = score_picked(sel_ref, p_ref, max_ref)
+    total = score_picked(sel_ref[...], p_ref, max_ref)
     for n in range(some):
-        out_ref[n, 0:QB, :] = total[n * QB:(n + 1) * QB]
-        out_ref[n, QB:QB + 1, :] = slots_ref[n:n + 1, :]
-
-
-def score(kernel, tiles, some, selects, passages, *more):
-    count = passages.shape[0]
+        put(out_ref, n, total, n, slots_ref, n)
+
+
+def score(kernel, tiles, some, few, passages, *more):
+    count, tokens = passages.shape[0], some * QB * QT
     vmem = pl.BlockSpec(memory_space=pltpu.VMEM)
+    if few:
+        scratch = [pltpu.VMEM((2 * tokens, 2 * DIM), jnp.bfloat16), pltpu.VMEM((count // 2, 2 * tokens), jnp.float32)]
+    else:
+        scratch = [pltpu.VMEM((tokens, DIM), jnp.bfloat16), pltpu.VMEM((count, tokens), jnp.float32)]
     return pl.pallas_call(
         kernel,
         out_shape=jax.ShapeDtypeStruct((tiles, QB + 1, LANES), jnp.float32),
         in_specs=[vmem] * len(more),
         out_specs=vmem,
-        scratch_shapes=[pltpu.VMEM((some * QB * QT, DIM), jnp.bfloat16)] * selects + [
-            pltpu.VMEM((count, some * QB * QT), jnp.float32),
-        ],
+        scratch_shapes=scratch,
         compiler_params=pltpu.CompilerParams(vmem_limit_bytes=32 * 1024 * 1024),
         cost_estimate=pl.CostEstimate(
-            flops=2 * passages.size * some * QB * QT, bytes_accessed=2 * passages.size, transcendentals=0
+            flops=2 * passages.size * tokens, bytes_accessed=2 * passages.size, transcendentals=0
         ),
     )(*more)
 
@@ -233,12 +268,25 @@
     theirs = swap_sides(candidates)
     shifted = [shift(own, step) for step in range(1, planes)]
     slots, picks, clean = prepare(shards, candidates, lengths, passages)
-    clean, *shifted = lax.optimization_barrier((clean, *shifted))
-    blocks = [own, *shifted]
-    far = swap_sides(pack(theirs, blocks))
-    tiles = score(near_kernel, planes, planes, 1, clean, slots, picks, clean, *blocks)
-    far, tiles = lax.optimization_barrier((far, tiles))
-    return score(far_kernel, shards, planes, 0, clean, slots, clean, far, tiles)
+    clean, *early = lax.optimization_barrier((clean, *reversed(shifted[:planes // 2 - 1])))
+    early, late = [own, *reversed(early)], shifted[planes // 2 - 1:]
+    steps = list(range(planes))
+    first, last = steps[:planes // 2], steps[planes // 2:]
+    packed = pack(first, planes, theirs, early)
+    first_far = swap_sides(packed)
+    *late, _ = lax.optimization_barrier((*reversed(late), packed))
+    late = late[::-1]
+    last_far = swap_sides(pack(last, planes, theirs, late))
+    near_tiles = score(near_kernel, planes, planes, False, clean, slots, picks, clean, *early, *late)
+    first_far, near_tiles = lax.optimization_barrier((first_far, near_tiles))
+    far_tiles = score(
+        functools.partial(some_far_kernel, first, planes), len(first), len(first), True, clean, slots, clean, first_far
+    )
+    last_far, far_tiles = lax.optimization_barrier((last_far, far_tiles))
+    return score(
+        functools.partial(last_far_kernel, last, planes), shards, len(last), True, clean,
+        slots, clean, last_far, near_tiles, far_tiles,
+    )
 
 
 def by_gather(own, shards, candidates, lengths, passages):
@@ -247,7 +295,7 @@
     some = min(shards, 8)
 
     def score_some(items):
-        return score(all_kernel, some, some, 1, clean, items[0], items[1], clean, items[2])
+        return score(all_kernel, some, some, False, clean, items[0], items[1], clean, items[2])
 
     parts = [x.reshape(shards // some, some, *x.shape[1:]) for x in (slots, picks, gathered)]
     return lax.map(score_some, parts).reshape(shards, QB + 1, LANES)
@@ -256,7 +304,7 @@
 def per_device(queries, passages, lengths, candidates):
     shards = lax.axis_size("psg")
     rows = passages.shape[0] // PBS
-    form = by_planes if shards in (4, 8) else by_gather
+    form = by_planes if shards == 8 else by_gather
     tiles = form(
         queries.reshape(QBD * QB * QT, DIM), shards, candidates.reshape(rows, KB), lengths, passages
     )

time: 29.2 us -> 28.3 us (0.969)
  waiting for transfers between devices: 3.47 us -> 1.22 us
  starting transfers between devices: 9.11 us -> 10.6 us
  blocking collectives: 10.5 us -> 9.58 us
  Pallas kernels: 5.96 us -> 6.69 us
    ppermute x3, waiting for transfers between devices: 2.36 us -> 0.01 us  [shift(): lax.ppermute(x, 'psg', [(j, (j + 2 * step) % shards) for j in range(shard...]
    all_to_all x1, blocking collectives: 10.5 us -> 9.58 us  [per_device(): lax.all_to_all(tiles, 'psg', split_axis=0, concat_axis=0, tiled=True)]
    ppermute x3, starting transfers between devices: 6.06 us -> 6.96 us  [shift(): lax.ppermute(x, 'psg', [(j, (j + 2 * step) % shards) for j in range(shard...]
    ppermute x2 -> x3, starting transfers between devices: 3.05 us -> 3.65 us  [swap_sides(): return lax.ppermute(x, 'psg', [(j, j ^ 1) for j in range(shards)])]
    pallas_call x2 -> x3, Pallas kernels: 3.13 us -> 3.66 us  [score(): pl.pallas_call(kernel, out_shape=jax.ShapeDtypeStruct((tiles, QB + 1, LAN...]
    ppermute x2 -> x3, waiting for transfers between devices: 1.11 us -> 1.21 us  [swap_sides(): return lax.ppermute(x, 'psg', [(j, j ^ 1) for j in range(shards)])]
  transfers between devices with their start and end apart: 5 -> 6, of which waited for: 2 -> 2; matrix products, arithmetic and copies ran while one was open for 0% -> 0% of each run, Pallas kernels for 12% -> 17%
where the time goes in v15:
time: 28.3 us; the launch traced here: 28.1 us
  starting transfers between devices  10.6 us (37%)
  blocking collectives  9.58 us (34%)
  Pallas kernels  6.69 us (24%)
  waiting for transfers between devices  1.22 us (4%)
    all_to_all x1, blocking collectives, per_device(): lax.all_to_all(tiles, 'psg', split_axis=0, concat_axis=0, tiled=True)  9.58 us
    ppermute x3, starting transfers between devices, shift(): lax.ppermute(x, 'psg', [(j, (j + 2 * step) % shards) for j in range(shard...  6.96 us
    pallas_call x3, Pallas kernels, score(): pl.pallas_call(kernel, out_shape=jax.ShapeDtypeStruct((tiles, QB + 1, LAN...  3.66 us
    ppermute x3, starting transfers between devices, swap_sides(): return lax.ppermute(x, 'psg', [(j, j ^ 1) for j in range(shards)])  3.65 us
    pallas_call x1, Pallas kernels, prepare(): pl.pallas_call(prepare_kernel, out_shape=[jax.ShapeDtypeStruct((shards, L...  1.8 us
    ppermute x3, waiting for transfers between devices, swap_sides(): return lax.ppermute(x, 'psg', [(j, j ^ 1) for j in range(shards)])  1.21 us
    pallas_call x1, Pallas kernels, place(): pl.pallas_call(place_kernel, out_shape=jax.ShapeDtypeStruct((shards, QB,...  0.81 us
  transfers between devices with their start and end apart: 6, of which 2 were waited for; matrix products, arithmetic and copies ran while one was open for 0% of the time, Pallas kernels for 17%

profile of v15, /device:TPU:0, one launch (start us, length us, event | category | flops | bytes accessed | tf_op | source)
XLA Modules:
  0.0 28.1 jit_solution(6954360779657939870)
XLA Ops:
  0.0 0.0 copy-start
  0.0 3.0 %collective-permute-start = (bf16[256,128]{1,0:T(8,128)(2,1)}, bf16[256,128]{1,0:T(8,128)(2,1)S(1)}, u32[]{:S(2)}, u32[]{:S(2)}) collective-permute-start(bf16[256,128]{1,0:T(8,128)(2,1)} %bitcast.5), channel_id=1, source_target_pairs={{0,4},{2,6},{4,8},{6,10},{8,12},{10,14},{12,0},{14,2},{1,5},{3,7},... | collective-permute-start | bytes 196616 | tf_op jit(solution)/shard_map/ppermute | solution.py:266
  3.0 2.6 %collective-permute-start.3 = (bf16[256,128]{1,0:T(8,128)(2,1)}, bf16[256,128]{1,0:T(8,128)(2,1)S(1)}, u32[]{:S(2)}, u32[]{:S(2)}) collective-permute-start(bf16[256,128]{1,0:T(8,128)(2,1)} %bitcast.6), channel_id=1, source_target_pairs={{0,8},{2,10},{4,12},{6,14},{8,0},{10,2},{12,4},{14,6},{1,9},{3,11}... | collective-permute-start | bytes 196616 | tf_op jit(solution)/shard_map/ppermute | solution.py:266
  5.6 1.3 %collective-permute-start.2 = (bf16[256,128]{1,0:T(8,128)(2,1)}, bf16[256,128]{1,0:T(8,128)(2,1)S(1)}, u32[]{:S(2)}, u32[]{:S(2)}) collective-permute-start(bf16[256,128]{1,0:T(8,128)(2,1)} %bitcast.7), channel_id=1, source_target_pairs={{0,12},{2,14},{4,0},{6,2},{8,4},{10,6},{12,8},{14,10},{1,13},{3,15... | collective-permute-start | bytes 196616 | tf_op jit(solution)/shard_map/ppermute | solution.py:266
  7.0 1.5 %collective-permute-start.1 = (s32[8,32]{1,0:T(8,128)}, s32[8,32]{1,0:T(8,128)S(1)}, u32[]{:S(2)}, u32[]{:S(2)}) collective-permute-start(s32[8,32]{1,0:T(8,128)} %bitcast.10), channel_id=1, source_target_pairs={{0,2},{2,0},{4,6},{6,4},{8,10},{10,8},{12,14},{14,12},{1,3},{3,1},... | collective-permute-start | bytes 3080 | tf_op jit(solution)/shard_map/ppermute | solution.py:263
  8.5 1.8 %shard_map.46 = (f32[8,128]{1,0:T(8,128)S(1)}, s32[8,128]{1,0:T(8,128)S(1)}, bf16[128,64,128]{2,1,0:T(8,128)(2,1)S(1)}) custom-call(s32[8,32]{1,0:T(8,128)} %bitcast.11, s32[128]{0:T(128)} %len_hbm.1, bf16[128,64,128]{2,1,0:T(8,128)(2,1)} %p_hbm.1), custom_call_target="tpu_custom_call" | custom-call | flops 1048576 | bytes 2097152 | tf_op jit(solution)/shard_map/pallas_call | solution.py:73
  10.3 0.0 collective-permute-done.refs_1_
  10.3 0.5 %collective-permute-done.1.cand_ref = s32[8,32]{1,0:T(8,128)S(1)} collective-permute-done((s32[8,32]{1,0:T(8,128)}, s32[8,32]{1,0:T(8,128)S(1)}, u32[]{:S(2)}, u32[]{:S(2)}) %collective-permute-start.1) | collective-permute-done | bytes 1056 | tf_op jit(solution)/shard_map/ppermute | solution.py:263
  10.8 0.0 copy-done
  10.8 0.2 shard_map.47
  11.0 1.6 %collective-permute-start.5 = (bf16[128,128]{1,0:T(8,128)(2,1)S(1)}, bf16[128,128]{1,0:T(8,128)(2,1)S(1)}, u32[]{:S(2)}, u32[]{:S(2)}) collective-permute-start(bf16[128,128]{1,0:T(8,128)(2,1)S(1)} %shard_map.47), channel_id=1, source_target_pairs={{0,2},{2,0},{4,6},{6,4},{8,10},{10,8},{12,14},{14,12},{1,3},{3,1},... | collective-permute-start | bytes 98312 | tf_op jit(solution)/shard_map/ppermute | solution.py:263
  12.6 0.0 collective-permute-done.3.refs_0_.refs_2_
  12.6 0.0 collective-permute-done.2.refs_1_.refs_3_
  12.6 0.2 shard_map.48
  12.8 0.6 %collective-permute-start.4 = (bf16[128,128]{1,0:T(8,128)(2,1)S(1)}, bf16[128,128]{1,0:T(8,128)(2,1)S(1)}, u32[]{:S(2)}, u32[]{:S(2)}) collective-permute-start(bf16[128,128]{1,0:T(8,128)(2,1)S(1)} %shard_map.48), channel_id=1, source_target_pairs={{0,2},{2,0},{4,6},{6,4},{8,10},{10,8},{12,14},{14,12},{1,3},{3,1},... | collective-permute-start | bytes 98312 | tf_op jit(solution)/shard_map/ppermute | solution.py:263
  13.4 1.7 %shard_map.49.near_ref = f32[4,3,128]{2,1,0:T(4,128)S(1)} custom-call(f32[8,128]{1,0:T(8,128)S(1)} %get-tuple-element.16.slots_ref, s32[8,128]{1,0:T(8,128)S(1)} %get-tuple-element.22.picks_ref, bf16[128,64,128]{2,1,0:T(8,128)(2,1)S(1)} %get-tuple-element.18.p_ref, bf16[256,128]{1,0:T(8,128)(2,1)S(1)} %bitcast.9, ...), custom_call_target="tpu_custom_call" | custom-call | flops 536870912 | bytes 2097152 | tf_op jit(solution)/shard_map/pallas_call | solution.py:223
  15.1 0.0 collective-permute-done.5.sel_ref
  15.1 1.0 %shard_map.50.far_ref = f32[2,3,128]{2,1,0:T(4,128)S(1)} custom-call(f32[8,128]{1,0:T(8,128)S(1)} %get-tuple-element.16.slots_ref, bf16[128,64,128]{2,1,0:T(8,128)(2,1)S(1)} %get-tuple-element.18.p_ref, bf16[128,128]{1,0:T(8,128)(2,1)S(1)} %collective-permute-done.5.sel_ref), custom_call_target="tpu_custom_call" | custom-call | flops 268435456 | bytes 2097152 | tf_op jit(solution)/shard_map/pallas_call | solution.py:223
  16.1 0.7 %collective-permute-done.4.sel_ref = bf16[128,128]{1,0:T(8,128)(2,1)S(1)} collective-permute-done((bf16[128,128]{1,0:T(8,128)(2,1)S(1)}, bf16[128,128]{1,0:T(8,128)(2,1)S(1)}, u32[]{:S(2)}, u32[]{:S(2)}) %collective-permute-start.4) | collective-permute-done | bytes 32800 | tf_op jit(solution)/shard_map/ppermute | solution.py:263
  16.8 1.0 %shard_map.51 = f32[8,3,128]{2,1,0:T(4,128)S(1)} custom-call(f32[8,128]{1,0:T(8,128)S(1)} %get-tuple-element.16.slots_ref, bf16[128,64,128]{2,1,0:T(8,128)(2,1)S(1)} %get-tuple-element.18.p_ref, bf16[128,128]{1,0:T(8,128)(2,1)S(1)} %collective-permute-done.4.sel_ref, f32[4,3,128]{2,1,0:T(4,128)S(1)} %shard_map.49.near_ref, f32[2,3,128]{2,1,0:T(4,128)S(1)} %shard_map.50.far_ref), custom_call_target="tpu_custom_call" | custom-call | flops 268435456 | bytes 2097152 | tf_op jit(solution)/shard_map/pallas_call | solution.py:223
  17.8 9.6 %all_to_all.5.in_ref = f32[8,3,128]{2,1,0:T(4,128)S(1)} all-to-all(f32[8,3,128]{2,1,0:T(4,128)S(1)} %shard_map.51), channel_id=1, replica_groups=mesh['grp'=2,'psg'=8,'qry'=2] {'psg'}, dimensions={0} | all-to-all | bytes 24576 | tf_op jit(solution)/shard_map/all_to_all | solution.py:311
  27.3 0.8 %shard_map.52 = f32[8,2,16,32]{3,2,1,0:T(8,128)} custom-call(f32[8,3,128]{2,1,0:T(4,128)S(1)} %all_to_all.5.in_ref), custom_call_target="tpu_custom_call" | custom-call | tf_op jit(solution)/shard_map/pallas_call | solution.py:250
Async XLA Ops:
  0.0 10.8 %copy-start = (bf16[8,32,128]{2,1,0:T(8,128)(2,1)S(1)}, bf16[8,32,128]{2,1,0:T(8,128)(2,1)}, u32[]{:S(2)}) copy-start(bf16[8,32,128]{2,1,0:T(8,128)(2,1)} %param.4) | copy-start | bytes 196612
  0.0 10.3 %collective-permute-start = (bf16[256,128]{1,0:T(8,128)(2,1)}, bf16[256,128]{1,0:T(8,128)(2,1)S(1)}, u32[]{:S(2)}, u32[]{:S(2)}) collective-permute-start(bf16[256,128]{1,0:T(8,128)(2,1)} %bitcast.5), channel_id=1, source_target_pairs={{0,4},{2,6},{4,8},{6,10},{8,12},{10,14},{12,0},{14,2},{1,5},{3,7},... | collective-permute-start | bytes 196616 | tf_op jit(solution)/shard_map/ppermute | solution.py:266
  3.0 9.5 %collective-permute-start.3 = (bf16[256,128]{1,0:T(8,128)(2,1)}, bf16[256,128]{1,0:T(8,128)(2,1)S(1)}, u32[]{:S(2)}, u32[]{:S(2)}) collective-permute-start(bf16[256,128]{1,0:T(8,128)(2,1)} %bitcast.6), channel_id=1, source_target_pairs={{0,8},{2,10},{4,12},{6,14},{8,0},{10,2},{12,4},{14,6},{1,9},{3,11}... | collective-permute-start | bytes 196616 | tf_op jit(solution)/shard_map/ppermute | solution.py:266
  5.6 7.0 %collective-permute-start.2 = (bf16[256,128]{1,0:T(8,128)(2,1)}, bf16[256,128]{1,0:T(8,128)(2,1)S(1)}, u32[]{:S(2)}, u32[]{:S(2)}) collective-permute-start(bf16[256,128]{1,0:T(8,128)(2,1)} %bitcast.7), channel_id=1, source_target_pairs={{0,12},{2,14},{4,0},{6,2},{8,4},{10,6},{12,8},{14,10},{1,13},{3,15... | collective-permute-start | bytes 196616 | tf_op jit(solution)/shard_map/ppermute | solution.py:266
  7.0 3.8 %collective-permute-start.1 = (s32[8,32]{1,0:T(8,128)}, s32[8,32]{1,0:T(8,128)S(1)}, u32[]{:S(2)}, u32[]{:S(2)}) collective-permute-start(s32[8,32]{1,0:T(8,128)} %bitcast.10), channel_id=1, source_target_pairs={{0,2},{2,0},{4,6},{6,4},{8,10},{10,8},{12,14},{14,12},{1,3},{3,1},... | collective-permute-start | bytes 3080 | tf_op jit(solution)/shard_map/ppermute | solution.py:263
  11.0 4.1 %collective-permute-start.5 = (bf16[128,128]{1,0:T(8,128)(2,1)S(1)}, bf16[128,128]{1,0:T(8,128)(2,1)S(1)}, u32[]{:S(2)}, u32[]{:S(2)}) collective-permute-start(bf16[128,128]{1,0:T(8,128)(2,1)S(1)} %shard_map.47), channel_id=1, source_target_pairs={{0,2},{2,0},{4,6},{6,4},{8,10},{10,8},{12,14},{14,12},{1,3},{3,1},... | collective-permute-start | bytes 98312 | tf_op jit(solution)/shard_map/ppermute | solution.py:263
  12.8 4.0 %collective-permute-start.4 = (bf16[128,128]{1,0:T(8,128)(2,1)S(1)}, bf16[128,128]{1,0:T(8,128)(2,1)S(1)}, u32[]{:S(2)}, u32[]{:S(2)}) collective-permute-start(bf16[128,128]{1,0:T(8,128)(2,1)S(1)} %shard_map.48), channel_id=1, source_target_pairs={{0,2},{2,0},{4,6},{6,4},{8,10},{10,8},{12,14},{14,12},{1,3},{3,1},... | collective-permute-start | bytes 98312 | tf_op jit(solution)/shard_map/ppermute | solution.py:263

commit v16 on v15

--- a/solution.py
+++ b/solution.py
@@ -164,8 +164,9 @@
             [p_ref[h + g:h + g + piece].reshape(piece * PT, DIM) for h in (0, half)], axis=1
         )
 
-    best = best_tokens(left_of, wide_ref[...], max_ref)
-    return jnp.concatenate([sum_tokens(best[:, :tokens]), sum_tokens(best[:, tokens:])], axis=1)
+    total = sum_tokens(best_tokens(left_of, wide_ref[...], max_ref))
+    queries = tokens // QT
+    return jnp.concatenate([total[:queries], total[queries:]], axis=1)
 
 
 def put(out_ref, place, total, n, slots_ref, owner):
@@ -173,35 +174,29 @@
     out_ref[place, QB:QB + 1, :] = slots_ref[pl.ds(owner, 1), :]
 
 
-def near_kernel(slots_ref, picks_ref, p_ref, *refs):
-    q_refs, (out_ref, sel_ref, max_ref) = refs[:-3], refs[-3:]
+def most_kernel(steps, planes, slots_ref, picks_ref, p_ref, far_ref, *refs):
+    q_refs, (out_ref, sel_ref, max_ref, wide_ref, few_max_ref) = refs[:-5], refs[-5:]
     me = lax.axis_index("psg")
-    owners = [near_owner(me, n, len(q_refs)) for n in range(len(q_refs))]
+    owners = [near_owner(me, n, planes) for n in range(planes)]
     for n, owner in enumerate(owners):
         sel_ref[n * QB * QT:(n + 1) * QB * QT, :] = picked(picks_ref, owner, q_refs[n])
     total = score_picked(sel_ref[...], p_ref, max_ref)
     for n, owner in enumerate(owners):
         put(out_ref, n, total, n, slots_ref, owner)
-
-
-def some_far_kernel(steps, planes, slots_ref, p_ref, sel_ref, out_ref, wide_ref, max_ref):
+    total = score_picked_few(far_ref[...], p_ref, wide_ref, few_max_ref)
+    for n, step in enumerate(steps):
+        put(out_ref, planes + n, total, n, slots_ref, owners[step] ^ 1)
+
+
+def last_kernel(steps, planes, slots_ref, p_ref, far_ref, earlier_ref, out_ref, wide_ref, few_max_ref):
     me = lax.axis_index("psg")
-    total = score_picked_few(sel_ref[...], p_ref, wide_ref, max_ref)
+    owners = [near_owner(me, n, planes) for n in range(planes)]
+    total = score_picked_few(far_ref[...], p_ref, wide_ref, few_max_ref)
     for n, step in enumerate(steps):
-        put(out_ref, n, total, n, slots_ref, near_owner(me, step, planes) ^ 1)
-
-
-def last_far_kernel(steps, planes, slots_ref, p_ref, sel_ref, near_ref, far_ref, out_ref, wide_ref, max_ref):
-    me = lax.axis_index("psg")
-    total = score_picked_few(sel_ref[...], p_ref, wide_ref, max_ref)
-    for n, step in enumerate(steps):
-        owner = near_owner(me, step, planes) ^ 1
-        put(out_ref, owner, total, n, slots_ref, owner)
+        put(out_ref, owners[step] ^ 1, total, n, slots_ref, owners[step] ^ 1)
     others = [step for step in range(planes) if step not in steps]
-    for step in range(planes):
-        out_ref[near_owner(me, step, planes)] = near_ref[step]
-    for n, step in enumerate(others):
-        out_ref[near_owner(me, step, planes) ^ 1] = far_ref[n]
+    for n, owner in enumerate(owners + [owners[step] ^ 1 for step in others]):
+        out_ref[owner] = earlier_ref[n]
 
 
 def all_kernel(slots_ref, picks_ref, p_ref, q_ref, out_ref, sel_ref, max_ref):
@@ -216,10 +211,12 @@
 def score(kernel, tiles, some, few, passages, *more):
     count, tokens = passages.shape[0], some * QB * QT
     vmem = pl.BlockSpec(memory_space=pltpu.VMEM)
+    scratch = []
+    if some:
+        scratch += [pltpu.VMEM((tokens, DIM), jnp.bfloat16), pltpu.VMEM((count, tokens), jnp.float32)]
     if few:
-        scratch = [pltpu.VMEM((2 * tokens, 2 * DIM), jnp.bfloat16), pltpu.VMEM((count // 2, 2 * tokens), jnp.float32)]
-    else:
-        scratch = [pltpu.VMEM((tokens, DIM), jnp.bfloat16), pltpu.VMEM((count, tokens), jnp.float32)]
+        wide = 2 * few * QB * QT
+        scratch += [pltpu.VMEM((wide, 2 * DIM), jnp.bfloat16), pltpu.VMEM((count // 2, wide), jnp.float32)]
     return pl.pallas_call(
         kernel,
         out_shape=jax.ShapeDtypeStruct((tiles, QB + 1, LANES), jnp.float32),
@@ -228,7 +225,7 @@
         scratch_shapes=scratch,
         compiler_params=pltpu.CompilerParams(vmem_limit_bytes=32 * 1024 * 1024),
         cost_estimate=pl.CostEstimate(
-            flops=2 * passages.size * tokens, bytes_accessed=2 * passages.size, transcendentals=0
+            flops=2 * passages.size * (some + few) * QB * QT, bytes_accessed=2 * passages.size, transcendentals=0
         ),
     )(*more)
 
@@ -268,25 +265,20 @@
     theirs = swap_sides(candidates)
     shifted = [shift(own, step) for step in range(1, planes)]
     slots, picks, clean = prepare(shards, candidates, lengths, passages)
-    clean, *early = lax.optimization_barrier((clean, *reversed(shifted[:planes // 2 - 1])))
-    early, late = [own, *reversed(early)], shifted[planes // 2 - 1:]
-    steps = list(range(planes))
-    first, last = steps[:planes // 2], steps[planes // 2:]
+    half = planes // 2
+    clean, *early = lax.optimization_barrier((clean, *reversed(shifted[:half - 1])))
+    early, late = [own, *reversed(early)], shifted[half - 1:]
+    first, last = list(range(half)), list(range(half, planes))
     packed = pack(first, planes, theirs, early)
     first_far = swap_sides(packed)
-    *late, _ = lax.optimization_barrier((*reversed(late), packed))
-    late = late[::-1]
+    *late, _ = lax.optimization_barrier((*late, packed))
     last_far = swap_sides(pack(last, planes, theirs, late))
-    near_tiles = score(near_kernel, planes, planes, False, clean, slots, picks, clean, *early, *late)
-    first_far, near_tiles = lax.optimization_barrier((first_far, near_tiles))
-    far_tiles = score(
-        functools.partial(some_far_kernel, first, planes), len(first), len(first), True, clean, slots, clean, first_far
+    tiles = score(
+        functools.partial(most_kernel, first, planes), planes + half, planes, half, clean,
+        slots, picks, clean, first_far, *early, *late,
     )
-    last_far, far_tiles = lax.optimization_barrier((last_far, far_tiles))
-    return score(
-        functools.partial(last_far_kernel, last, planes), shards, len(last), True, clean,
-        slots, clean, last_far, near_tiles, far_tiles,
-    )
+    last_far, tiles = lax.optimization_barrier((last_far, tiles))
+    return score(functools.partial(last_kernel, last, planes), shards, 0, half, clean, slots, clean, last_far, tiles)
 
 
 def by_gather(own, shards, candidates, lengths, passages):
@@ -295,7 +287,7 @@
     some = min(shards, 8)
 
     def score_some(items):
-        return score(all_kernel, some, some, False, clean, items[0], items[1], clean, items[2])
+        return score(all_kernel, some, some, 0, clean, items[0], items[1], clean, items[2])
 
     parts = [x.reshape(shards // some, some, *x.shape[1:]) for x in (slots, picks, gathered)]
     return lax.map(score_some, parts).reshape(shards, QB + 1, LANES)

time: 28.3 us -> 28.8 us (1.018)
  waiting for transfers between devices: 1.22 us -> 2.12 us
  blocking collectives: 9.58 us -> 9.28 us
    ppermute x3, waiting for transfers between devices: 1.21 us -> 2.11 us  [swap_sides(): return lax.ppermute(x, 'psg', [(j, j ^ 1) for j in range(shards)])]
    all_to_all x1, blocking collectives: 9.58 us -> 9.28 us  [per_device(): lax.all_to_all(tiles, 'psg', split_axis=0, concat_axis=0, tiled=True)]
    pallas_call x3 -> x2, Pallas kernels: 3.66 us -> 3.54 us  [score(): pl.pallas_call(kernel, out_shape=jax.ShapeDtypeStruct((tiles, QB + 1, LAN...]
where the time goes in v16:
time: 28.8 us; the launch traced here: 28.6 us
  starting transfers between devices  10.6 us (37%)
  blocking collectives  9.28 us (32%)
  Pallas kernels  6.57 us (23%)
  waiting for transfers between devices  2.12 us (7%)
    all_to_all x1, blocking collectives, per_device(): lax.all_to_all(tiles, 'psg', split_axis=0, concat_axis=0, tiled=True)  9.28 us
    ppermute x3, starting transfers between devices, shift(): lax.ppermute(x, 'psg', [(j, (j + 2 * step) % shards) for j in range(shard...  6.96 us
    ppermute x3, starting transfers between devices, swap_sides(): return lax.ppermute(x, 'psg', [(j, j ^ 1) for j in range(shards)])  3.65 us
    pallas_call x2, Pallas kernels, score(): pl.pallas_call(kernel, out_shape=jax.ShapeDtypeStruct((tiles, QB + 1, LAN...  3.54 us
    ppermute x3, waiting for transfers between devices, swap_sides(): return lax.ppermute(x, 'psg', [(j, j ^ 1) for j in range(shards)])  2.11 us
    pallas_call x1, Pallas kernels, prepare(): pl.pallas_call(prepare_kernel, out_shape=[jax.ShapeDtypeStruct((shards, L...  1.8 us
    pallas_call x1, Pallas kernels, place(): pl.pallas_call(place_kernel, out_shape=jax.ShapeDtypeStruct((shards, QB,...  0.81 us
  transfers between devices with their start and end apart: 6, of which 2 were waited for; matrix products, arithmetic and copies ran while one was open for 0% of the time, Pallas kernels for 17%

profile of v16, /device:TPU:0, one launch (start us, length us, event | category | flops | bytes accessed | tf_op | source)
XLA Modules:
  0.0 28.6 jit_solution(9576551796491989060)
XLA Ops:
  0.0 0.0 copy-start
  0.0 3.0 %collective-permute-start = (bf16[256,128]{1,0:T(8,128)(2,1)}, bf16[256,128]{1,0:T(8,128)(2,1)S(1)}, u32[]{:S(2)}, u32[]{:S(2)}) collective-permute-start(bf16[256,128]{1,0:T(8,128)(2,1)} %bitcast.5), channel_id=1, source_target_pairs={{0,4},{2,6},{4,8},{6,10},{8,12},{10,14},{12,0},{14,2},{1,5},{3,7},... | collective-permute-start | bytes 196616 | tf_op jit(solution)/shard_map/ppermute | solution.py:263
  3.0 2.6 %collective-permute-start.2 = (bf16[256,128]{1,0:T(8,128)(2,1)}, bf16[256,128]{1,0:T(8,128)(2,1)S(1)}, u32[]{:S(2)}, u32[]{:S(2)}) collective-permute-start(bf16[256,128]{1,0:T(8,128)(2,1)} %bitcast.6), channel_id=1, source_target_pairs={{0,8},{2,10},{4,12},{6,14},{8,0},{10,2},{12,4},{14,6},{1,9},{3,11}... | collective-permute-start | bytes 196616 | tf_op jit(solution)/shard_map/ppermute | solution.py:263
  5.6 1.3 %collective-permute-start.3 = (bf16[256,128]{1,0:T(8,128)(2,1)}, bf16[256,128]{1,0:T(8,128)(2,1)S(1)}, u32[]{:S(2)}, u32[]{:S(2)}) collective-permute-start(bf16[256,128]{1,0:T(8,128)(2,1)} %bitcast.7), channel_id=1, source_target_pairs={{0,12},{2,14},{4,0},{6,2},{8,4},{10,6},{12,8},{14,10},{1,13},{3,15... | collective-permute-start | bytes 196616 | tf_op jit(solution)/shard_map/ppermute | solution.py:263
  7.0 1.5 %collective-permute-start.1 = (s32[8,32]{1,0:T(8,128)}, s32[8,32]{1,0:T(8,128)S(1)}, u32[]{:S(2)}, u32[]{:S(2)}) collective-permute-start(s32[8,32]{1,0:T(8,128)} %bitcast.10), channel_id=1, source_target_pairs={{0,2},{2,0},{4,6},{6,4},{8,10},{10,8},{12,14},{14,12},{1,3},{3,1},... | collective-permute-start | bytes 3080 | tf_op jit(solution)/shard_map/ppermute | solution.py:260
  8.5 1.8 %shard_map.46 = (f32[8,128]{1,0:T(8,128)S(1)}, s32[8,128]{1,0:T(8,128)S(1)}, bf16[128,64,128]{2,1,0:T(8,128)(2,1)S(1)}) custom-call(s32[8,32]{1,0:T(8,128)} %bitcast.11, s32[128]{0:T(128)} %len_hbm.1, bf16[128,64,128]{2,1,0:T(8,128)(2,1)} %p_hbm.1), custom_call_target="tpu_custom_call" | custom-call | flops 1048576 | bytes 2097152 | tf_op jit(solution)/shard_map/pallas_call | solution.py:73
  10.3 0.0 collective-permute-done.refs_1_
  10.3 0.5 %collective-permute-done.1.cand_ref = s32[8,32]{1,0:T(8,128)S(1)} collective-permute-done((s32[8,32]{1,0:T(8,128)}, s32[8,32]{1,0:T(8,128)S(1)}, u32[]{:S(2)}, u32[]{:S(2)}) %collective-permute-start.1) | collective-permute-done | bytes 1056 | tf_op jit(solution)/shard_map/ppermute | solution.py:260
  10.8 0.0 copy-done
  10.8 0.2 shard_map.47
  11.0 1.6 %collective-permute-start.5 = (bf16[128,128]{1,0:T(8,128)(2,1)S(1)}, bf16[128,128]{1,0:T(8,128)(2,1)S(1)}, u32[]{:S(2)}, u32[]{:S(2)}) collective-permute-start(bf16[128,128]{1,0:T(8,128)(2,1)S(1)} %shard_map.47), channel_id=1, source_target_pairs={{0,2},{2,0},{4,6},{6,4},{8,10},{10,8},{12,14},{14,12},{1,3},{3,1},... | collective-permute-start | bytes 98312 | tf_op jit(solution)/shard_map/ppermute | solution.py:260
  12.6 0.0 collective-permute-done.2.refs_0_.refs_2_
  12.6 0.0 collective-permute-done.3.refs_1_.refs_3_
  12.6 0.2 shard_map.48
  12.8 0.6 %collective-permute-start.4 = (bf16[128,128]{1,0:T(8,128)(2,1)S(1)}, bf16[128,128]{1,0:T(8,128)(2,1)S(1)}, u32[]{:S(2)}, u32[]{:S(2)}) collective-permute-start(bf16[128,128]{1,0:T(8,128)(2,1)S(1)} %shard_map.48), channel_id=1, source_target_pairs={{0,2},{2,0},{4,6},{6,4},{8,10},{10,8},{12,14},{14,12},{1,3},{3,1},... | collective-permute-start | bytes 98312 | tf_op jit(solution)/shard_map/ppermute | solution.py:260
  13.4 1.6 %collective-permute-done.5.far_ref = bf16[128,128]{1,0:T(8,128)(2,1)S(1)} collective-permute-done((bf16[128,128]{1,0:T(8,128)(2,1)S(1)}, bf16[128,128]{1,0:T(8,128)(2,1)S(1)}, u32[]{:S(2)}, u32[]{:S(2)}) %collective-permute-start.5) | collective-permute-done | bytes 32800 | tf_op jit(solution)/shard_map/ppermute | solution.py:260
  15.0 2.5 %shard_map.49.earlier_ref = f32[6,3,128]{2,1,0:T(4,128)S(1)} custom-call(f32[8,128]{1,0:T(8,128)S(1)} %get-tuple-element.14.slots_ref, s32[8,128]{1,0:T(8,128)S(1)} %get-tuple-element.20.picks_ref, bf16[128,64,128]{2,1,0:T(8,128)(2,1)S(1)} %get-tuple-element.16.p_ref, bf16[128,128]{1,0:T(8,128)(2,1)S(1)} %collective-permute-done.5.far_ref, ...), custom_call_target="tpu_custom_call" | custom-call | flops 805306368 | bytes 2097152 | tf_op jit(solution)/shard_map/pallas_call | solution.py:220
  17.5 0.0 collective-permute-done.4.far_ref
  17.5 1.0 %shard_map.50 = f32[8,3,128]{2,1,0:T(4,128)S(1)} custom-call(f32[8,128]{1,0:T(8,128)S(1)} %get-tuple-element.14.slots_ref, bf16[128,64,128]{2,1,0:T(8,128)(2,1)S(1)} %get-tuple-element.16.p_ref, bf16[128,128]{1,0:T(8,128)(2,1)S(1)} %collective-permute-done.4.far_ref, f32[6,3,128]{2,1,0:T(4,128)S(1)} %shard_map.49.earlier_ref), custom_call_target="tpu_custom_call" | custom-call | flops 268435456 | bytes 2097152 | tf_op jit(solution)/shard_map/pallas_call | solution.py:220
  18.5 9.3 %all_to_all.5.in_ref = f32[8,3,128]{2,1,0:T(4,128)S(1)} all-to-all(f32[8,3,128]{2,1,0:T(4,128)S(1)} %shard_map.50), channel_id=1, replica_groups=mesh['grp'=2,'psg'=8,'qry'=2] {'psg'}, dimensions={0} | all-to-all | bytes 24576 | tf_op jit(solution)/shard_map/all_to_all | solution.py:303
  27.8 0.8 %shard_map.51 = f32[8,2,16,32]{3,2,1,0:T(8,128)} custom-call(f32[8,3,128]{2,1,0:T(4,128)S(1)} %all_to_all.5.in_ref), custom_call_target="tpu_custom_call" | custom-call | tf_op jit(solution)/shard_map/pallas_call | solution.py:247
Async XLA Ops:
  0.0 10.8 %copy-start = (bf16[8,32,128]{2,1,0:T(8,128)(2,1)S(1)}, bf16[8,32,128]{2,1,0:T(8,128)(2,1)}, u32[]{:S(2)}) copy-start(bf16[8,32,128]{2,1,0:T(8,128)(2,1)} %param.4) | copy-start | bytes 196612
  0.0 10.3 %collective-permute-start = (bf16[256,128]{1,0:T(8,128)(2,1)}, bf16[256,128]{1,0:T(8,128)(2,1)S(1)}, u32[]{:S(2)}, u32[]{:S(2)}) collective-permute-start(bf16[256,128]{1,0:T(8,128)(2,1)} %bitcast.5), channel_id=1, source_target_pairs={{0,4},{2,6},{4,8},{6,10},{8,12},{10,14},{12,0},{14,2},{1,5},{3,7},... | collective-permute-start | bytes 196616 | tf_op jit(solution)/shard_map/ppermute | solution.py:263
  3.0 9.5 %collective-permute-start.2 = (bf16[256,128]{1,0:T(8,128)(2,1)}, bf16[256,128]{1,0:T(8,128)(2,1)S(1)}, u32[]{:S(2)}, u32[]{:S(2)}) collective-permute-start(bf16[256,128]{1,0:T(8,128)(2,1)} %bitcast.6), channel_id=1, source_target_pairs={{0,8},{2,10},{4,12},{6,14},{8,0},{10,2},{12,4},{14,6},{1,9},{3,11}... | collective-permute-start | bytes 196616 | tf_op jit(solution)/shard_map/ppermute | solution.py:263
  5.6 7.0 %collective-permute-start.3 = (bf16[256,128]{1,0:T(8,128)(2,1)}, bf16[256,128]{1,0:T(8,128)(2,1)S(1)}, u32[]{:S(2)}, u32[]{:S(2)}) collective-permute-start(bf16[256,128]{1,0:T(8,128)(2,1)} %bitcast.7), channel_id=1, source_target_pairs={{0,12},{2,14},{4,0},{6,2},{8,4},{10,6},{12,8},{14,10},{1,13},{3,15... | collective-permute-start | bytes 196616 | tf_op jit(solution)/shard_map/ppermute | solution.py:263
  7.0 3.8 %collective-permute-start.1 = (s32[8,32]{1,0:T(8,128)}, s32[8,32]{1,0:T(8,128)S(1)}, u32[]{:S(2)}, u32[]{:S(2)}) collective-permute-start(s32[8,32]{1,0:T(8,128)} %bitcast.10), channel_id=1, source_target_pairs={{0,2},{2,0},{4,6},{6,4},{8,10},{10,8},{12,14},{14,12},{1,3},{3,1},... | collective-permute-start | bytes 3080 | tf_op jit(solution)/shard_map/ppermute | solution.py:260
  11.0 4.0 %collective-permute-start.5 = (bf16[128,128]{1,0:T(8,128)(2,1)S(1)}, bf16[128,128]{1,0:T(8,128)(2,1)S(1)}, u32[]{:S(2)}, u32[]{:S(2)}) collective-permute-start(bf16[128,128]{1,0:T(8,128)(2,1)S(1)} %shard_map.47), channel_id=1, source_target_pairs={{0,2},{2,0},{4,6},{6,4},{8,10},{10,8},{12,14},{14,12},{1,3},{3,1},... | collective-permute-start | bytes 98312 | tf_op jit(solution)/shard_map/ppermute | solution.py:260
  12.8 4.7 %collective-permute-start.4 = (bf16[128,128]{1,0:T(8,128)(2,1)S(1)}, bf16[128,128]{1,0:T(8,128)(2,1)S(1)}, u32[]{:S(2)}, u32[]{:S(2)}) collective-permute-start(bf16[128,128]{1,0:T(8,128)(2,1)S(1)} %shard_map.48), channel_id=1, source_target_pairs={{0,2},{2,0},{4,6},{6,4},{8,10},{10,8},{12,14},{14,12},{1,3},{3,1},... | collective-permute-start | bytes 98312 | tf_op jit(solution)/shard_map/ppermute | solution.py:260

commit v17 on v15

--- a/solution.py
+++ b/solution.py
@@ -16,6 +16,7 @@
 KB = 32
 LANES = 128
 GROUP = 8
+PACK = 16
 
 
 def prepare_kernel(
@@ -55,15 +56,18 @@
         slots_ref[o:o + 1, :] = jnp.sum(jnp.where(upto <= lane, 1.0, 0.0), axis=0, keepdims=True)
 
     fetch_len.wait()
-    u = lax.broadcasted_iota(jnp.int32, (PT, LANES), 0)
+    u = lax.broadcasted_iota(jnp.int32, (PT, LANES), 0).astype(jnp.int16)
 
     @pl.loop(0, groups)
     def _(g):
         fetch(g).wait()
         for i in range(GROUP):
             p = g * GROUP + i
-            tokens = raw_ref[p].astype(jnp.float32)
-            clean_ref[p] = jnp.where(u < len_ref[p], tokens, tokens[0:1]).astype(jnp.bfloat16)
+            tokens = raw_ref[p]
+            first = jnp.broadcast_to(tokens[0:PACK].astype(jnp.float32)[0:1], (PACK, LANES)).astype(jnp.bfloat16)
+            limit = jnp.full((PACK, LANES), len_ref[p], jnp.int32).astype(jnp.int16)
+            live = u < jnp.concatenate([limit] * (PT // PACK))
+            clean_ref[p] = jnp.where(live, tokens, jnp.concatenate([first] * (PT // PACK)))
 
 
 def prepare(shards, candidates, lengths, passages):
@@ -164,8 +168,9 @@
             [p_ref[h + g:h + g + piece].reshape(piece * PT, DIM) for h in (0, half)], axis=1
         )
 
-    best = best_tokens(left_of, wide_ref[...], max_ref)
-    return jnp.concatenate([sum_tokens(best[:, :tokens]), sum_tokens(best[:, tokens:])], axis=1)
+    total = sum_tokens(best_tokens(left_of, wide_ref[...], max_ref))
+    queries = tokens // QT
+    return jnp.concatenate([total[:queries], total[queries:]], axis=1)
 
 
 def put(out_ref, place, total, n, slots_ref, owner):

time: 28.3 us -> 28.3 us (level)
  no operation moved by 1% of the time
where the time goes in v17:
time: 28.3 us; the launch traced here: 28.1 us
  starting transfers between devices  10.6 us (37%)
  blocking collectives  9.6 us (34%)
  Pallas kernels  6.66 us (24%)
  waiting for transfers between devices  1.24 us (4%)
    all_to_all x1, blocking collectives, per_device(): lax.all_to_all(tiles, 'psg', split_axis=0, concat_axis=0, tiled=True)  9.6 us
    ppermute x3, starting transfers between devices, shift(): lax.ppermute(x, 'psg', [(j, (j + 2 * step) % shards) for j in range(shard...  6.96 us
    ppermute x3, starting transfers between devices, swap_sides(): return lax.ppermute(x, 'psg', [(j, j ^ 1) for j in range(shards)])  3.65 us
    pallas_call x3, Pallas kernels, score(): pl.pallas_call(kernel, out_shape=jax.ShapeDtypeStruct((tiles, QB + 1, LAN...  3.63 us
    pallas_call x1, Pallas kernels, prepare(): pl.pallas_call(prepare_kernel, out_shape=[jax.ShapeDtypeStruct((shards, L...  1.79 us
    ppermute x3, waiting for transfers between devices, swap_sides(): return lax.ppermute(x, 'psg', [(j, j ^ 1) for j in range(shards)])  1.23 us
    pallas_call x1, Pallas kernels, place(): pl.pallas_call(place_kernel, out_shape=jax.ShapeDtypeStruct((shards, QB,...  0.81 us
  transfers between devices with their start and end apart: 6, of which 2 were waited for; matrix products, arithmetic and copies ran while one was open for 0% of the time, Pallas kernels for 17%

profile of v17, /device:TPU:0, one launch (start us, length us, event | category | flops | bytes accessed | tf_op | source)
XLA Modules:
  0.0 28.1 jit_solution(7303263490740971803)
XLA Ops:
  0.0 0.0 copy-start
  0.0 3.0 %collective-permute-start = (bf16[256,128]{1,0:T(8,128)(2,1)}, bf16[256,128]{1,0:T(8,128)(2,1)S(1)}, u32[]{:S(2)}, u32[]{:S(2)}) collective-permute-start(bf16[256,128]{1,0:T(8,128)(2,1)} %bitcast.5), channel_id=1, source_target_pairs={{0,4},{2,6},{4,8},{6,10},{8,12},{10,14},{12,0},{14,2},{1,5},{3,7},... | collective-permute-start | bytes 196616 | tf_op jit(solution)/shard_map/ppermute | solution.py:271
  3.0 2.6 %collective-permute-start.3 = (bf16[256,128]{1,0:T(8,128)(2,1)}, bf16[256,128]{1,0:T(8,128)(2,1)S(1)}, u32[]{:S(2)}, u32[]{:S(2)}) collective-permute-start(bf16[256,128]{1,0:T(8,128)(2,1)} %bitcast.6), channel_id=1, source_target_pairs={{0,8},{2,10},{4,12},{6,14},{8,0},{10,2},{12,4},{14,6},{1,9},{3,11}... | collective-permute-start | bytes 196616 | tf_op jit(solution)/shard_map/ppermute | solution.py:271
  5.6 1.3 %collective-permute-start.2 = (bf16[256,128]{1,0:T(8,128)(2,1)}, bf16[256,128]{1,0:T(8,128)(2,1)S(1)}, u32[]{:S(2)}, u32[]{:S(2)}) collective-permute-start(bf16[256,128]{1,0:T(8,128)(2,1)} %bitcast.7), channel_id=1, source_target_pairs={{0,12},{2,14},{4,0},{6,2},{8,4},{10,6},{12,8},{14,10},{1,13},{3,15... | collective-permute-start | bytes 196616 | tf_op jit(solution)/shard_map/ppermute | solution.py:271
  7.0 1.5 %collective-permute-start.1 = (s32[8,32]{1,0:T(8,128)}, s32[8,32]{1,0:T(8,128)S(1)}, u32[]{:S(2)}, u32[]{:S(2)}) collective-permute-start(s32[8,32]{1,0:T(8,128)} %bitcast.10), channel_id=1, source_target_pairs={{0,2},{2,0},{4,6},{6,4},{8,10},{10,8},{12,14},{14,12},{1,3},{3,1},... | collective-permute-start | bytes 3080 | tf_op jit(solution)/shard_map/ppermute | solution.py:268
  8.5 1.8 %shard_map.46 = (f32[8,128]{1,0:T(8,128)S(1)}, s32[8,128]{1,0:T(8,128)S(1)}, bf16[128,64,128]{2,1,0:T(8,128)(2,1)S(1)}) custom-call(s32[8,32]{1,0:T(8,128)} %bitcast.11, s32[128]{0:T(128)} %len_hbm.1, bf16[128,64,128]{2,1,0:T(8,128)(2,1)} %p_hbm.1), custom_call_target="tpu_custom_call" | custom-call | flops 1048576 | bytes 2097152 | tf_op jit(solution)/shard_map/pallas_call | solution.py:77
  10.3 0.0 collective-permute-done.refs_1_
  10.3 0.5 %collective-permute-done.1.cand_ref = s32[8,32]{1,0:T(8,128)S(1)} collective-permute-done((s32[8,32]{1,0:T(8,128)}, s32[8,32]{1,0:T(8,128)S(1)}, u32[]{:S(2)}, u32[]{:S(2)}) %collective-permute-start.1) | collective-permute-done | bytes 1056 | tf_op jit(solution)/shard_map/ppermute | solution.py:268
  10.8 0.0 copy-done
  10.8 0.2 shard_map.47
  11.0 1.6 %collective-permute-start.5 = (bf16[128,128]{1,0:T(8,128)(2,1)S(1)}, bf16[128,128]{1,0:T(8,128)(2,1)S(1)}, u32[]{:S(2)}, u32[]{:S(2)}) collective-permute-start(bf16[128,128]{1,0:T(8,128)(2,1)S(1)} %shard_map.47), channel_id=1, source_target_pairs={{0,2},{2,0},{4,6},{6,4},{8,10},{10,8},{12,14},{14,12},{1,3},{3,1},... | collective-permute-start | bytes 98312 | tf_op jit(solution)/shard_map/ppermute | solution.py:268
  12.6 0.0 collective-permute-done.3.refs_0_.refs_2_
  12.6 0.0 collective-permute-done.2.refs_1_.refs_3_
  12.6 0.2 shard_map.48
  12.8 0.6 %collective-permute-start.4 = (bf16[128,128]{1,0:T(8,128)(2,1)S(1)}, bf16[128,128]{1,0:T(8,128)(2,1)S(1)}, u32[]{:S(2)}, u32[]{:S(2)}) collective-permute-start(bf16[128,128]{1,0:T(8,128)(2,1)S(1)} %shard_map.48), channel_id=1, source_target_pairs={{0,2},{2,0},{4,6},{6,4},{8,10},{10,8},{12,14},{14,12},{1,3},{3,1},... | collective-permute-start | bytes 98312 | tf_op jit(solution)/shard_map/ppermute | solution.py:268
  13.4 1.7 %shard_map.49.near_ref = f32[4,3,128]{2,1,0:T(4,128)S(1)} custom-call(f32[8,128]{1,0:T(8,128)S(1)} %get-tuple-element.16.slots_ref, s32[8,128]{1,0:T(8,128)S(1)} %get-tuple-element.22.picks_ref, bf16[128,64,128]{2,1,0:T(8,128)(2,1)S(1)} %get-tuple-element.18.p_ref, bf16[256,128]{1,0:T(8,128)(2,1)S(1)} %bitcast.9, ...), custom_call_target="tpu_custom_call" | custom-call | flops 536870912 | bytes 2097152 | tf_op jit(solution)/shard_map/pallas_call | solution.py:228
  15.1 0.0 collective-permute-done.5.sel_ref
  15.1 1.0 %shard_map.50.far_ref = f32[2,3,128]{2,1,0:T(4,128)S(1)} custom-call(f32[8,128]{1,0:T(8,128)S(1)} %get-tuple-element.16.slots_ref, bf16[128,64,128]{2,1,0:T(8,128)(2,1)S(1)} %get-tuple-element.18.p_ref, bf16[128,128]{1,0:T(8,128)(2,1)S(1)} %collective-permute-done.5.sel_ref), custom_call_target="tpu_custom_call" | custom-call | flops 268435456 | bytes 2097152 | tf_op jit(solution)/shard_map/pallas_call | solution.py:228
  16.1 0.7 %collective-permute-done.4.sel_ref = bf16[128,128]{1,0:T(8,128)(2,1)S(1)} collective-permute-done((bf16[128,128]{1,0:T(8,128)(2,1)S(1)}, bf16[128,128]{1,0:T(8,128)(2,1)S(1)}, u32[]{:S(2)}, u32[]{:S(2)}) %collective-permute-start.4) | collective-permute-done | bytes 32800 | tf_op jit(solution)/shard_map/ppermute | solution.py:268
  16.8 1.0 %shard_map.51 = f32[8,3,128]{2,1,0:T(4,128)S(1)} custom-call(f32[8,128]{1,0:T(8,128)S(1)} %get-tuple-element.16.slots_ref, bf16[128,64,128]{2,1,0:T(8,128)(2,1)S(1)} %get-tuple-element.18.p_ref, bf16[128,128]{1,0:T(8,128)(2,1)S(1)} %collective-permute-done.4.sel_ref, f32[4,3,128]{2,1,0:T(4,128)S(1)} %shard_map.49.near_ref, f32[2,3,128]{2,1,0:T(4,128)S(1)} %shard_map.50.far_ref), custom_call_target="tpu_custom_call" | custom-call | flops 268435456 | bytes 2097152 | tf_op jit(solution)/shard_map/pallas_call | solution.py:228
  17.7 9.6 %all_to_all.5.in_ref = f32[8,3,128]{2,1,0:T(4,128)S(1)} all-to-all(f32[8,3,128]{2,1,0:T(4,128)S(1)} %shard_map.51), channel_id=1, replica_groups=mesh['grp'=2,'psg'=8,'qry'=2] {'psg'}, dimensions={0} | all-to-all | bytes 24576 | tf_op jit(solution)/shard_map/all_to_all | solution.py:316
  27.3 0.8 %shard_map.52 = f32[8,2,16,32]{3,2,1,0:T(8,128)} custom-call(f32[8,3,128]{2,1,0:T(4,128)S(1)} %all_to_all.5.in_ref), custom_call_target="tpu_custom_call" | custom-call | tf_op jit(solution)/shard_map/pallas_call | solution.py:255
Async XLA Ops:
  0.0 10.8 %copy-start = (bf16[8,32,128]{2,1,0:T(8,128)(2,1)S(1)}, bf16[8,32,128]{2,1,0:T(8,128)(2,1)}, u32[]{:S(2)}) copy-start(bf16[8,32,128]{2,1,0:T(8,128)(2,1)} %param.4) | copy-start | bytes 196612
  0.0 10.3 %collective-permute-start = (bf16[256,128]{1,0:T(8,128)(2,1)}, bf16[256,128]{1,0:T(8,128)(2,1)S(1)}, u32[]{:S(2)}, u32[]{:S(2)}) collective-permute-start(bf16[256,128]{1,0:T(8,128)(2,1)} %bitcast.5), channel_id=1, source_target_pairs={{0,4},{2,6},{4,8},{6,10},{8,12},{10,14},{12,0},{14,2},{1,5},{3,7},... | collective-permute-start | bytes 196616 | tf_op jit(solution)/shard_map/ppermute | solution.py:271
  3.0 9.5 %collective-permute-start.3 = (bf16[256,128]{1,0:T(8,128)(2,1)}, bf16[256,128]{1,0:T(8,128)(2,1)S(1)}, u32[]{:S(2)}, u32[]{:S(2)}) collective-permute-start(bf16[256,128]{1,0:T(8,128)(2,1)} %bitcast.6), channel_id=1, source_target_pairs={{0,8},{2,10},{4,12},{6,14},{8,0},{10,2},{12,4},{14,6},{1,9},{3,11}... | collective-permute-start | bytes 196616 | tf_op jit(solution)/shard_map/ppermute | solution.py:271
  5.6 7.0 %collective-permute-start.2 = (bf16[256,128]{1,0:T(8,128)(2,1)}, bf16[256,128]{1,0:T(8,128)(2,1)S(1)}, u32[]{:S(2)}, u32[]{:S(2)}) collective-permute-start(bf16[256,128]{1,0:T(8,128)(2,1)} %bitcast.7), channel_id=1, source_target_pairs={{0,12},{2,14},{4,0},{6,2},{8,4},{10,6},{12,8},{14,10},{1,13},{3,15... | collective-permute-start | bytes 196616 | tf_op jit(solution)/shard_map/ppermute | solution.py:271
  7.0 3.8 %collective-permute-start.1 = (s32[8,32]{1,0:T(8,128)}, s32[8,32]{1,0:T(8,128)S(1)}, u32[]{:S(2)}, u32[]{:S(2)}) collective-permute-start(s32[8,32]{1,0:T(8,128)} %bitcast.10), channel_id=1, source_target_pairs={{0,2},{2,0},{4,6},{6,4},{8,10},{10,8},{12,14},{14,12},{1,3},{3,1},... | collective-permute-start | bytes 3080 | tf_op jit(solution)/shard_map/ppermute | solution.py:268
  11.0 4.1 %collective-permute-start.5 = (bf16[128,128]{1,0:T(8,128)(2,1)S(1)}, bf16[128,128]{1,0:T(8,128)(2,1)S(1)}, u32[]{:S(2)}, u32[]{:S(2)}) collective-permute-start(bf16[128,128]{1,0:T(8,128)(2,1)S(1)} %shard_map.47), channel_id=1, source_target_pairs={{0,2},{2,0},{4,6},{6,4},{8,10},{10,8},{12,14},{14,12},{1,3},{3,1},... | collective-permute-start | bytes 98312 | tf_op jit(solution)/shard_map/ppermute | solution.py:268
  12.8 4.0 %collective-permute-start.4 = (bf16[128,128]{1,0:T(8,128)(2,1)S(1)}, bf16[128,128]{1,0:T(8,128)(2,1)S(1)}, u32[]{:S(2)}, u32[]{:S(2)}) collective-permute-start(bf16[128,128]{1,0:T(8,128)(2,1)S(1)} %shard_map.48), channel_id=1, source_target_pairs={{0,2},{2,0},{4,6},{6,4},{8,10},{10,8},{12,14},{14,12},{1,3},{3,1},... | collective-permute-start | bytes 98312 | tf_op jit(solution)/shard_map/ppermute | solution.py:268

commit v18 on v15

--- a/solution.py
+++ b/solution.py
@@ -164,8 +164,9 @@
             [p_ref[h + g:h + g + piece].reshape(piece * PT, DIM) for h in (0, half)], axis=1
         )
 
-    best = best_tokens(left_of, wide_ref[...], max_ref)
-    return jnp.concatenate([sum_tokens(best[:, :tokens]), sum_tokens(best[:, tokens:])], axis=1)
+    total = sum_tokens(best_tokens(left_of, wide_ref[...], max_ref))
+    queries = tokens // QT
+    return jnp.concatenate([total[:queries], total[queries:]], axis=1)
 
 
 def put(out_ref, place, total, n, slots_ref, owner):
@@ -274,8 +275,7 @@
     first, last = steps[:planes // 2], steps[planes // 2:]
     packed = pack(first, planes, theirs, early)
     first_far = swap_sides(packed)
-    *late, _ = lax.optimization_barrier((*reversed(late), packed))
-    late = late[::-1]
+    *late, _ = lax.optimization_barrier((*late, packed))
     last_far = swap_sides(pack(last, planes, theirs, late))
     near_tiles = score(near_kernel, planes, planes, False, clean, slots, picks, clean, *early, *late)
     first_far, near_tiles = lax.optimization_barrier((first_far, near_tiles))

time: 28.3 us -> 28.5 us (level)
  blocking collectives: 9.58 us -> 10.4 us
  waiting for transfers between devices: 1.22 us -> 0.52 us
    ppermute x3, starting transfers between devices: 3.65 us -> 4.57 us  [swap_sides(): return lax.ppermute(x, 'psg', [(j, j ^ 1) for j in range(shards)])]
    ppermute x3, starting transfers between devices: 6.96 us -> 6.06 us  [shift(): lax.ppermute(x, 'psg', [(j, (j + 2 * step) % shards) for j in range(shard...]
    all_to_all x1, blocking collectives: 9.58 us -> 10.4 us  [per_device(): lax.all_to_all(tiles, 'psg', split_axis=0, concat_axis=0, tiled=True)]
    ppermute x3, waiting for transfers between devices: 1.21 us -> 0.52 us  [swap_sides(): return lax.ppermute(x, 'psg', [(j, j ^ 1) for j in range(shards)])]
  transfers between devices with their start and end apart: 6 -> 6, of which waited for: 2 -> 1; matrix products, arithmetic and copies ran while one was open for 0% -> 0% of each run, Pallas kernels for 17% -> 17%
where the time goes in v18:
time: 28.5 us; the launch traced here: 28.3 us
  starting transfers between devices  10.6 us (37%)
  blocking collectives  10.4 us (36%)
  Pallas kernels  6.69 us (23%)
  waiting for transfers between devices  0.52 us (2%)
    all_to_all x1, blocking collectives, per_device(): lax.all_to_all(tiles, 'psg', split_axis=0, concat_axis=0, tiled=True)  10.4 us
    ppermute x3, starting transfers between devices, shift(): lax.ppermute(x, 'psg', [(j, (j + 2 * step) % shards) for j in range(shard...  6.06 us
    ppermute x3, starting transfers between devices, swap_sides(): return lax.ppermute(x, 'psg', [(j, j ^ 1) for j in range(shards)])  4.57 us
    pallas_call x3, Pallas kernels, score(): pl.pallas_call(kernel, out_shape=jax.ShapeDtypeStruct((tiles, QB + 1, LAN...  3.66 us
    pallas_call x1, Pallas kernels, prepare(): pl.pallas_call(prepare_kernel, out_shape=[jax.ShapeDtypeStruct((shards, L...  1.8 us
    pallas_call x1, Pallas kernels, place(): pl.pallas_call(place_kernel, out_shape=jax.ShapeDtypeStruct((shards, QB,...  0.81 us
  transfers between devices with their start and end apart: 6, of which 1 were waited for; matrix products, arithmetic and copies ran while one was open for 0% of the time, Pallas kernels for 17%

profile of v18, /device:TPU:0, one launch (start us, length us, event | category | flops | bytes accessed | tf_op | source)
XLA Modules:
  0.0 28.3 jit_solution(9596506217747116094)
XLA Ops:
  0.0 0.0 copy-start
  0.0 3.0 %collective-permute-start = (bf16[256,128]{1,0:T(8,128)(2,1)}, bf16[256,128]{1,0:T(8,128)(2,1)S(1)}, u32[]{:S(2)}, u32[]{:S(2)}) collective-permute-start(bf16[256,128]{1,0:T(8,128)(2,1)} %bitcast.5), channel_id=1, source_target_pairs={{0,4},{2,6},{4,8},{6,10},{8,12},{10,14},{12,0},{14,2},{1,5},{3,7},... | collective-permute-start | bytes 196616 | tf_op jit(solution)/shard_map/ppermute | solution.py:267
  3.0 2.1 %collective-permute-start.3 = (bf16[256,128]{1,0:T(8,128)(2,1)}, bf16[256,128]{1,0:T(8,128)(2,1)S(1)}, u32[]{:S(2)}, u32[]{:S(2)}) collective-permute-start(bf16[256,128]{1,0:T(8,128)(2,1)} %bitcast.6), channel_id=1, source_target_pairs={{0,12},{2,14},{4,0},{6,2},{8,4},{10,6},{12,8},{14,10},{1,13},{3,15... | collective-permute-start | bytes 196616 | tf_op jit(solution)/shard_map/ppermute | solution.py:267
  5.1 1.0 %collective-permute-start.2 = (bf16[256,128]{1,0:T(8,128)(2,1)}, bf16[256,128]{1,0:T(8,128)(2,1)S(1)}, u32[]{:S(2)}, u32[]{:S(2)}) collective-permute-start(bf16[256,128]{1,0:T(8,128)(2,1)} %bitcast.7), channel_id=1, source_target_pairs={{0,8},{2,10},{4,12},{6,14},{8,0},{10,2},{12,4},{14,6},{1,9},{3,11}... | collective-permute-start | bytes 196616 | tf_op jit(solution)/shard_map/ppermute | solution.py:267
  6.1 1.5 %collective-permute-start.1 = (s32[8,32]{1,0:T(8,128)}, s32[8,32]{1,0:T(8,128)S(1)}, u32[]{:S(2)}, u32[]{:S(2)}) collective-permute-start(s32[8,32]{1,0:T(8,128)} %bitcast.10), channel_id=1, source_target_pairs={{0,2},{2,0},{4,6},{6,4},{8,10},{10,8},{12,14},{14,12},{1,3},{3,1},... | collective-permute-start | bytes 3080 | tf_op jit(solution)/shard_map/ppermute | solution.py:264
  7.6 1.8 %shard_map.46 = (f32[8,128]{1,0:T(8,128)S(1)}, s32[8,128]{1,0:T(8,128)S(1)}, bf16[128,64,128]{2,1,0:T(8,128)(2,1)S(1)}) custom-call(s32[8,32]{1,0:T(8,128)} %bitcast.11, s32[128]{0:T(128)} %len_hbm.1, bf16[128,64,128]{2,1,0:T(8,128)(2,1)} %p_hbm.1), custom_call_target="tpu_custom_call" | custom-call | flops 1048576 | bytes 2097152 | tf_op jit(solution)/shard_map/pallas_call | solution.py:73
  9.4 0.0 collective-permute-done.refs_1_
  9.4 0.5 %collective-permute-done.1.cand_ref = s32[8,32]{1,0:T(8,128)S(1)} collective-permute-done((s32[8,32]{1,0:T(8,128)}, s32[8,32]{1,0:T(8,128)S(1)}, u32[]{:S(2)}, u32[]{:S(2)}) %collective-permute-start.1) | collective-permute-done | bytes 1056 | tf_op jit(solution)/shard_map/ppermute | solution.py:264
  9.9 0.0 copy-done
  9.9 0.2 shard_map.47
  10.1 1.6 %collective-permute-start.5 = (bf16[128,128]{1,0:T(8,128)(2,1)S(1)}, bf16[128,128]{1,0:T(8,128)(2,1)S(1)}, u32[]{:S(2)}, u32[]{:S(2)}) collective-permute-start(bf16[128,128]{1,0:T(8,128)(2,1)S(1)} %shard_map.47), channel_id=1, source_target_pairs={{0,2},{2,0},{4,6},{6,4},{8,10},{10,8},{12,14},{14,12},{1,3},{3,1},... | collective-permute-start | bytes 98312 | tf_op jit(solution)/shard_map/ppermute | solution.py:264
  11.7 0.0 collective-permute-done.3.refs_1_.refs_3_
  11.7 0.0 collective-permute-done.2.refs_0_.refs_2_
  11.7 0.2 shard_map.48
  11.9 1.5 %collective-permute-start.4 = (bf16[128,128]{1,0:T(8,128)(2,1)S(1)}, bf16[128,128]{1,0:T(8,128)(2,1)S(1)}, u32[]{:S(2)}, u32[]{:S(2)}) collective-permute-start(bf16[128,128]{1,0:T(8,128)(2,1)S(1)} %shard_map.48), channel_id=1, source_target_pairs={{0,2},{2,0},{4,6},{6,4},{8,10},{10,8},{12,14},{14,12},{1,3},{3,1},... | collective-permute-start | bytes 98312 | tf_op jit(solution)/shard_map/ppermute | solution.py:264
  13.4 1.7 %shard_map.49.near_ref = f32[4,3,128]{2,1,0:T(4,128)S(1)} custom-call(f32[8,128]{1,0:T(8,128)S(1)} %get-tuple-element.16.slots_ref, s32[8,128]{1,0:T(8,128)S(1)} %get-tuple-element.22.picks_ref, bf16[128,64,128]{2,1,0:T(8,128)(2,1)S(1)} %get-tuple-element.18.p_ref, bf16[256,128]{1,0:T(8,128)(2,1)S(1)} %bitcast.9, ...), custom_call_target="tpu_custom_call" | custom-call | flops 536870912 | bytes 2097152 | tf_op jit(solution)/shard_map/pallas_call | solution.py:224
  15.1 0.0 collective-permute-done.5.sel_ref
  15.1 1.0 %shard_map.50.far_ref = f32[2,3,128]{2,1,0:T(4,128)S(1)} custom-call(f32[8,128]{1,0:T(8,128)S(1)} %get-tuple-element.16.slots_ref, bf16[128,64,128]{2,1,0:T(8,128)(2,1)S(1)} %get-tuple-element.18.p_ref, bf16[128,128]{1,0:T(8,128)(2,1)S(1)} %collective-permute-done.5.sel_ref), custom_call_target="tpu_custom_call" | custom-call | flops 268435456 | bytes 2097152 | tf_op jit(solution)/shard_map/pallas_call | solution.py:224
  16.1 0.0 collective-permute-done.4.sel_ref
  16.1 1.0 %shard_map.51 = f32[8,3,128]{2,1,0:T(4,128)S(1)} custom-call(f32[8,128]{1,0:T(8,128)S(1)} %get-tuple-element.16.slots_ref, bf16[128,64,128]{2,1,0:T(8,128)(2,1)S(1)} %get-tuple-element.18.p_ref, bf16[128,128]{1,0:T(8,128)(2,1)S(1)} %collective-permute-done.4.sel_ref, f32[4,3,128]{2,1,0:T(4,128)S(1)} %shard_map.49.near_ref, f32[2,3,128]{2,1,0:T(4,128)S(1)} %shard_map.50.far_ref), custom_call_target="tpu_custom_call" | custom-call | flops 268435456 | bytes 2097152 | tf_op jit(solution)/shard_map/pallas_call | solution.py:224
  17.1 10.4 %all_to_all.5.in_ref = f32[8,3,128]{2,1,0:T(4,128)S(1)} all-to-all(f32[8,3,128]{2,1,0:T(4,128)S(1)} %shard_map.51), channel_id=1, replica_groups=mesh['grp'=2,'psg'=8,'qry'=2] {'psg'}, dimensions={0} | all-to-all | bytes 24576 | tf_op jit(solution)/shard_map/all_to_all | solution.py:311
  27.5 0.8 %shard_map.52 = f32[8,2,16,32]{3,2,1,0:T(8,128)} custom-call(f32[8,3,128]{2,1,0:T(4,128)S(1)} %all_to_all.5.in_ref), custom_call_target="tpu_custom_call" | custom-call | tf_op jit(solution)/shard_map/pallas_call | solution.py:251
Async XLA Ops:
  0.0 9.9 %copy-start = (bf16[8,32,128]{2,1,0:T(8,128)(2,1)S(1)}, bf16[8,32,128]{2,1,0:T(8,128)(2,1)}, u32[]{:S(2)}) copy-start(bf16[8,32,128]{2,1,0:T(8,128)(2,1)} %param.4) | copy-start | bytes 196612
  0.0 9.4 %collective-permute-start = (bf16[256,128]{1,0:T(8,128)(2,1)}, bf16[256,128]{1,0:T(8,128)(2,1)S(1)}, u32[]{:S(2)}, u32[]{:S(2)}) collective-permute-start(bf16[256,128]{1,0:T(8,128)(2,1)} %bitcast.5), channel_id=1, source_target_pairs={{0,4},{2,6},{4,8},{6,10},{8,12},{10,14},{12,0},{14,2},{1,5},{3,7},... | collective-permute-start | bytes 196616 | tf_op jit(solution)/shard_map/ppermute | solution.py:267
  3.0 8.6 %collective-permute-start.3 = (bf16[256,128]{1,0:T(8,128)(2,1)}, bf16[256,128]{1,0:T(8,128)(2,1)S(1)}, u32[]{:S(2)}, u32[]{:S(2)}) collective-permute-start(bf16[256,128]{1,0:T(8,128)(2,1)} %bitcast.6), channel_id=1, source_target_pairs={{0,12},{2,14},{4,0},{6,2},{8,4},{10,6},{12,8},{14,10},{1,13},{3,15... | collective-permute-start | bytes 196616 | tf_op jit(solution)/shard_map/ppermute | solution.py:267
  5.1 6.6 %collective-permute-start.2 = (bf16[256,128]{1,0:T(8,128)(2,1)}, bf16[256,128]{1,0:T(8,128)(2,1)S(1)}, u32[]{:S(2)}, u32[]{:S(2)}) collective-permute-start(bf16[256,128]{1,0:T(8,128)(2,1)} %bitcast.7), channel_id=1, source_target_pairs={{0,8},{2,10},{4,12},{6,14},{8,0},{10,2},{12,4},{14,6},{1,9},{3,11}... | collective-permute-start | bytes 196616 | tf_op jit(solution)/shard_map/ppermute | solution.py:267
  6.1 3.8 %collective-permute-start.1 = (s32[8,32]{1,0:T(8,128)}, s32[8,32]{1,0:T(8,128)S(1)}, u32[]{:S(2)}, u32[]{:S(2)}) collective-permute-start(s32[8,32]{1,0:T(8,128)} %bitcast.10), channel_id=1, source_target_pairs={{0,2},{2,0},{4,6},{6,4},{8,10},{10,8},{12,14},{14,12},{1,3},{3,1},... | collective-permute-start | bytes 3080 | tf_op jit(solution)/shard_map/ppermute | solution.py:264
  10.1 5.0 %collective-permute-start.5 = (bf16[128,128]{1,0:T(8,128)(2,1)S(1)}, bf16[128,128]{1,0:T(8,128)(2,1)S(1)}, u32[]{:S(2)}, u32[]{:S(2)}) collective-permute-start(bf16[128,128]{1,0:T(8,128)(2,1)S(1)} %shard_map.47), channel_id=1, source_target_pairs={{0,2},{2,0},{4,6},{6,4},{8,10},{10,8},{12,14},{14,12},{1,3},{3,1},... | collective-permute-start | bytes 98312 | tf_op jit(solution)/shard_map/ppermute | solution.py:264
  11.9 4.2 %collective-permute-start.4 = (bf16[128,128]{1,0:T(8,128)(2,1)S(1)}, bf16[128,128]{1,0:T(8,128)(2,1)S(1)}, u32[]{:S(2)}, u32[]{:S(2)}) collective-permute-start(bf16[128,128]{1,0:T(8,128)(2,1)S(1)} %shard_map.48), channel_id=1, source_target_pairs={{0,2},{2,0},{4,6},{6,4},{8,10},{10,8},{12,14},{14,12},{1,3},{3,1},... | collective-permute-start | bytes 98312 | tf_op jit(solution)/shard_map/ppermute | solution.py:264

commit v19 on v18

--- a/solution.py
+++ b/solution.py
@@ -269,15 +269,17 @@
     theirs = swap_sides(candidates)
     shifted = [shift(own, step) for step in range(1, planes)]
     slots, picks, clean = prepare(shards, candidates, lengths, passages)
-    clean, *early = lax.optimization_barrier((clean, *reversed(shifted[:planes // 2 - 1])))
-    early, late = [own, *reversed(early)], shifted[planes // 2 - 1:]
-    steps = list(range(planes))
-    first, last = steps[:planes // 2], steps[planes // 2:]
-    packed = pack(first, planes, theirs, early)
+    first = [0, planes // 2]
+    last = [step for step in range(planes) if step not in first]
+    clean, shifted[first[1] - 1] = lax.optimization_barrier((clean, shifted[first[1] - 1]))
+    blocks = [own, *shifted]
+    packed = pack(first, planes, theirs, [blocks[step] for step in first])
     first_far = swap_sides(packed)
-    *late, _ = lax.optimization_barrier((*late, packed))
-    last_far = swap_sides(pack(last, planes, theirs, late))
-    near_tiles = score(near_kernel, planes, planes, False, clean, slots, picks, clean, *early, *late)
+    *late, _ = lax.optimization_barrier((*[blocks[step] for step in reversed(last)], packed))
+    for step, block in zip(reversed(last), late):
+        blocks[step] = block
+    last_far = swap_sides(pack(last, planes, theirs, [blocks[step] for step in last]))
+    near_tiles = score(near_kernel, planes, planes, False, clean, slots, picks, clean, *blocks)
     first_far, near_tiles = lax.optimization_barrier((first_far, near_tiles))
     far_tiles = score(
         functools.partial(some_far_kernel, first, planes), len(first), len(first), True, clean, slots, clean, first_far

time: 28.5 us -> 28.9 us (1.014)
  blocking collectives: 10.4 us -> 9.27 us
  starting transfers between devices: 10.6 us -> 11.5 us
  waiting for transfers between devices: 0.52 us -> 1.24 us
    ppermute x3, starting transfers between devices: 6.06 us -> 7.86 us  [shift(): lax.ppermute(x, 'psg', [(j, (j + 2 * step) % shards) for j in range(shard...]
    all_to_all x1, blocking collectives: 10.4 us -> 9.27 us  [per_device(): lax.all_to_all(tiles, 'psg', split_axis=0, concat_axis=0, tiled=True)]
    ppermute x3, starting transfers between devices: 4.57 us -> 3.65 us  [swap_sides(): return lax.ppermute(x, 'psg', [(j, j ^ 1) for j in range(shards)])]
    ppermute x3, waiting for transfers between devices: 0.52 us -> 1.23 us  [swap_sides(): return lax.ppermute(x, 'psg', [(j, j ^ 1) for j in range(shards)])]
  transfers between devices with their start and end apart: 6 -> 6, of which waited for: 1 -> 2; matrix products, arithmetic and copies ran while one was open for 0% -> 0% of each run, Pallas kernels for 17% -> 17%
where the time goes in v19:
time: 28.9 us; the launch traced here: 28.7 us
  starting transfers between devices  11.5 us (40%)
  blocking collectives  9.27 us (32%)
  Pallas kernels  6.65 us (23%)
  waiting for transfers between devices  1.24 us (4%)
    all_to_all x1, blocking collectives, per_device(): lax.all_to_all(tiles, 'psg', split_axis=0, concat_axis=0, tiled=True)  9.27 us
    ppermute x3, starting transfers between devices, shift(): lax.ppermute(x, 'psg', [(j, (j + 2 * step) % shards) for j in range(shard...  7.86 us
    ppermute x3, starting transfers between devices, swap_sides(): return lax.ppermute(x, 'psg', [(j, j ^ 1) for j in range(shards)])  3.65 us
    pallas_call x3, Pallas kernels, score(): pl.pallas_call(kernel, out_shape=jax.ShapeDtypeStruct((tiles, QB + 1, LAN...  3.62 us
    pallas_call x1, Pallas kernels, prepare(): pl.pallas_call(prepare_kernel, out_shape=[jax.ShapeDtypeStruct((shards, L...  1.8 us
    ppermute x3, waiting for transfers between devices, swap_sides(): return lax.ppermute(x, 'psg', [(j, j ^ 1) for j in range(shards)])  1.23 us
    pallas_call x1, Pallas kernels, place(): pl.pallas_call(place_kernel, out_shape=jax.ShapeDtypeStruct((shards, QB,...  0.81 us
  transfers between devices with their start and end apart: 6, of which 2 were waited for; matrix products, arithmetic and copies ran while one was open for 0% of the time, Pallas kernels for 17%

profile of v19, /device:TPU:0, one launch (start us, length us, event | category | flops | bytes accessed | tf_op | source)
XLA Modules:
  0.0 28.7 jit_solution(2903818778644819703)
XLA Ops:
  0.0 0.0 copy-start
  0.0 4.0 %collective-permute-start = (bf16[256,128]{1,0:T(8,128)(2,1)}, bf16[256,128]{1,0:T(8,128)(2,1)S(1)}, u32[]{:S(2)}, u32[]{:S(2)}) collective-permute-start(bf16[256,128]{1,0:T(8,128)(2,1)} %bitcast.5), channel_id=1, source_target_pairs={{0,8},{2,10},{4,12},{6,14},{8,0},{10,2},{12,4},{14,6},{1,9},{3,11}... | collective-permute-start | bytes 196616 | tf_op jit(solution)/shard_map/ppermute | solution.py:267
  4.0 1.6 %collective-permute-start.3 = (bf16[256,128]{1,0:T(8,128)(2,1)}, bf16[256,128]{1,0:T(8,128)(2,1)S(1)}, u32[]{:S(2)}, u32[]{:S(2)}) collective-permute-start(bf16[256,128]{1,0:T(8,128)(2,1)} %bitcast.6), channel_id=1, source_target_pairs={{0,4},{2,6},{4,8},{6,10},{8,12},{10,14},{12,0},{14,2},{1,5},{3,7},... | collective-permute-start | bytes 196616 | tf_op jit(solution)/shard_map/ppermute | solution.py:267
  5.6 2.2 %collective-permute-start.2 = (bf16[256,128]{1,0:T(8,128)(2,1)}, bf16[256,128]{1,0:T(8,128)(2,1)S(1)}, u32[]{:S(2)}, u32[]{:S(2)}) collective-permute-start(bf16[256,128]{1,0:T(8,128)(2,1)} %bitcast.7), channel_id=1, source_target_pairs={{0,12},{2,14},{4,0},{6,2},{8,4},{10,6},{12,8},{14,10},{1,13},{3,15... | collective-permute-start | bytes 196616 | tf_op jit(solution)/shard_map/ppermute | solution.py:267
  7.9 1.5 %collective-permute-start.1 = (s32[8,32]{1,0:T(8,128)}, s32[8,32]{1,0:T(8,128)S(1)}, u32[]{:S(2)}, u32[]{:S(2)}) collective-permute-start(s32[8,32]{1,0:T(8,128)} %bitcast.10), channel_id=1, source_target_pairs={{0,2},{2,0},{4,6},{6,4},{8,10},{10,8},{12,14},{14,12},{1,3},{3,1},... | collective-permute-start | bytes 3080 | tf_op jit(solution)/shard_map/ppermute | solution.py:264
  9.4 1.8 %shard_map.46 = (f32[8,128]{1,0:T(8,128)S(1)}, s32[8,128]{1,0:T(8,128)S(1)}, bf16[128,64,128]{2,1,0:T(8,128)(2,1)S(1)}) custom-call(s32[8,32]{1,0:T(8,128)} %bitcast.11, s32[128]{0:T(128)} %len_hbm.1, bf16[128,64,128]{2,1,0:T(8,128)(2,1)} %p_hbm.1), custom_call_target="tpu_custom_call" | custom-call | flops 1048576 | bytes 2097152 | tf_op jit(solution)/shard_map/pallas_call | solution.py:73
  11.2 0.0 collective-permute-done.refs_1_.refs_2_
  11.2 0.5 %collective-permute-done.1.cand_ref = s32[8,32]{1,0:T(8,128)S(1)} collective-permute-done((s32[8,32]{1,0:T(8,128)}, s32[8,32]{1,0:T(8,128)S(1)}, u32[]{:S(2)}, u32[]{:S(2)}) %collective-permute-start.1) | collective-permute-done | bytes 1056 | tf_op jit(solution)/shard_map/ppermute | solution.py:264
  11.7 0.0 copy-done
  11.7 0.2 shard_map.47
  11.9 1.6 %collective-permute-start.5 = (bf16[128,128]{1,0:T(8,128)(2,1)S(1)}, bf16[128,128]{1,0:T(8,128)(2,1)S(1)}, u32[]{:S(2)}, u32[]{:S(2)}) collective-permute-start(bf16[128,128]{1,0:T(8,128)(2,1)S(1)} %shard_map.47), channel_id=1, source_target_pairs={{0,2},{2,0},{4,6},{6,4},{8,10},{10,8},{12,14},{14,12},{1,3},{3,1},... | collective-permute-start | bytes 98312 | tf_op jit(solution)/shard_map/ppermute | solution.py:264
  13.5 0.0 collective-permute-done.3.refs_0_.refs_1_
  13.5 0.0 collective-permute-done.2.refs_1_.refs_3_
  13.5 0.2 shard_map.48
  13.7 0.6 %collective-permute-start.4 = (bf16[128,128]{1,0:T(8,128)(2,1)S(1)}, bf16[128,128]{1,0:T(8,128)(2,1)S(1)}, u32[]{:S(2)}, u32[]{:S(2)}) collective-permute-start(bf16[128,128]{1,0:T(8,128)(2,1)S(1)} %shard_map.48), channel_id=1, source_target_pairs={{0,2},{2,0},{4,6},{6,4},{8,10},{10,8},{12,14},{14,12},{1,3},{3,1},... | collective-permute-start | bytes 98312 | tf_op jit(solution)/shard_map/ppermute | solution.py:264
  14.3 1.7 %shard_map.49.near_ref = f32[4,3,128]{2,1,0:T(4,128)S(1)} custom-call(f32[8,128]{1,0:T(8,128)S(1)} %get-tuple-element.16.slots_ref, s32[8,128]{1,0:T(8,128)S(1)} %get-tuple-element.22.picks_ref, bf16[128,64,128]{2,1,0:T(8,128)(2,1)S(1)} %get-tuple-element.18.p_ref, bf16[256,128]{1,0:T(8,128)(2,1)S(1)} %bitcast.9, ...), custom_call_target="tpu_custom_call" | custom-call | flops 536870912 | bytes 2097152 | tf_op jit(solution)/shard_map/pallas_call | solution.py:224
  16.0 0.0 collective-permute-done.5.sel_ref
  16.0 1.0 %shard_map.50.far_ref = f32[2,3,128]{2,1,0:T(4,128)S(1)} custom-call(f32[8,128]{1,0:T(8,128)S(1)} %get-tuple-element.16.slots_ref, bf16[128,64,128]{2,1,0:T(8,128)(2,1)S(1)} %get-tuple-element.18.p_ref, bf16[128,128]{1,0:T(8,128)(2,1)S(1)} %collective-permute-done.5.sel_ref), custom_call_target="tpu_custom_call" | custom-call | flops 268435456 | bytes 2097152 | tf_op jit(solution)/shard_map/pallas_call | solution.py:224
  17.0 0.7 %collective-permute-done.4.sel_ref = bf16[128,128]{1,0:T(8,128)(2,1)S(1)} collective-permute-done((bf16[128,128]{1,0:T(8,128)(2,1)S(1)}, bf16[128,128]{1,0:T(8,128)(2,1)S(1)}, u32[]{:S(2)}, u32[]{:S(2)}) %collective-permute-start.4) | collective-permute-done | bytes 32800 | tf_op jit(solution)/shard_map/ppermute | solution.py:264
  17.7 1.0 %shard_map.51 = f32[8,3,128]{2,1,0:T(4,128)S(1)} custom-call(f32[8,128]{1,0:T(8,128)S(1)} %get-tuple-element.16.slots_ref, bf16[128,64,128]{2,1,0:T(8,128)(2,1)S(1)} %get-tuple-element.18.p_ref, bf16[128,128]{1,0:T(8,128)(2,1)S(1)} %collective-permute-done.4.sel_ref, f32[4,3,128]{2,1,0:T(4,128)S(1)} %shard_map.49.near_ref, f32[2,3,128]{2,1,0:T(4,128)S(1)} %shard_map.50.far_ref), custom_call_target="tpu_custom_call" | custom-call | flops 268435456 | bytes 2097152 | tf_op jit(solution)/shard_map/pallas_call | solution.py:224
  18.6 9.3 %all_to_all.5.in_ref = f32[8,3,128]{2,1,0:T(4,128)S(1)} all-to-all(f32[8,3,128]{2,1,0:T(4,128)S(1)} %shard_map.51), channel_id=1, replica_groups=mesh['grp'=2,'psg'=8,'qry'=2] {'psg'}, dimensions={0} | all-to-all | bytes 24576 | tf_op jit(solution)/shard_map/all_to_all | solution.py:313
  27.9 0.8 %shard_map.52 = f32[8,2,16,32]{3,2,1,0:T(8,128)} custom-call(f32[8,3,128]{2,1,0:T(4,128)S(1)} %all_to_all.5.in_ref), custom_call_target="tpu_custom_call" | custom-call | tf_op jit(solution)/shard_map/pallas_call | solution.py:251
Async XLA Ops:
  0.0 11.7 %copy-start = (bf16[8,32,128]{2,1,0:T(8,128)(2,1)S(1)}, bf16[8,32,128]{2,1,0:T(8,128)(2,1)}, u32[]{:S(2)}) copy-start(bf16[8,32,128]{2,1,0:T(8,128)(2,1)} %param.4) | copy-start | bytes 196612
  0.0 11.2 %collective-permute-start = (bf16[256,128]{1,0:T(8,128)(2,1)}, bf16[256,128]{1,0:T(8,128)(2,1)S(1)}, u32[]{:S(2)}, u32[]{:S(2)}) collective-permute-start(bf16[256,128]{1,0:T(8,128)(2,1)} %bitcast.5), channel_id=1, source_target_pairs={{0,8},{2,10},{4,12},{6,14},{8,0},{10,2},{12,4},{14,6},{1,9},{3,11}... | collective-permute-start | bytes 196616 | tf_op jit(solution)/shard_map/ppermute | solution.py:267
  4.0 9.4 %collective-permute-start.3 = (bf16[256,128]{1,0:T(8,128)(2,1)}, bf16[256,128]{1,0:T(8,128)(2,1)S(1)}, u32[]{:S(2)}, u32[]{:S(2)}) collective-permute-start(bf16[256,128]{1,0:T(8,128)(2,1)} %bitcast.6), channel_id=1, source_target_pairs={{0,4},{2,6},{4,8},{6,10},{8,12},{10,14},{12,0},{14,2},{1,5},{3,7},... | collective-permute-start | bytes 196616 | tf_op jit(solution)/shard_map/ppermute | solution.py:267
  5.6 7.9 %collective-permute-start.2 = (bf16[256,128]{1,0:T(8,128)(2,1)}, bf16[256,128]{1,0:T(8,128)(2,1)S(1)}, u32[]{:S(2)}, u32[]{:S(2)}) collective-permute-start(bf16[256,128]{1,0:T(8,128)(2,1)} %bitcast.7), channel_id=1, source_target_pairs={{0,12},{2,14},{4,0},{6,2},{8,4},{10,6},{12,8},{14,10},{1,13},{3,15... | collective-permute-start | bytes 196616 | tf_op jit(solution)/shard_map/ppermute | solution.py:267
  7.9 3.8 %collective-permute-start.1 = (s32[8,32]{1,0:T(8,128)}, s32[8,32]{1,0:T(8,128)S(1)}, u32[]{:S(2)}, u32[]{:S(2)}) collective-permute-start(s32[8,32]{1,0:T(8,128)} %bitcast.10), channel_id=1, source_target_pairs={{0,2},{2,0},{4,6},{6,4},{8,10},{10,8},{12,14},{14,12},{1,3},{3,1},... | collective-permute-start | bytes 3080 | tf_op jit(solution)/shard_map/ppermute | solution.py:264
  11.9 4.1 %collective-permute-start.5 = (bf16[128,128]{1,0:T(8,128)(2,1)S(1)}, bf16[128,128]{1,0:T(8,128)(2,1)S(1)}, u32[]{:S(2)}, u32[]{:S(2)}) collective-permute-start(bf16[128,128]{1,0:T(8,128)(2,1)S(1)} %shard_map.47), channel_id=1, source_target_pairs={{0,2},{2,0},{4,6},{6,4},{8,10},{10,8},{12,14},{14,12},{1,3},{3,1},... | collective-permute-start | bytes 98312 | tf_op jit(solution)/shard_map/ppermute | solution.py:264
  13.7 4.0 %collective-permute-start.4 = (bf16[128,128]{1,0:T(8,128)(2,1)S(1)}, bf16[128,128]{1,0:T(8,128)(2,1)S(1)}, u32[]{:S(2)}, u32[]{:S(2)}) collective-permute-start(bf16[128,128]{1,0:T(8,128)(2,1)S(1)} %shard_map.48), channel_id=1, source_target_pairs={{0,2},{2,0},{4,6},{6,4},{8,10},{10,8},{12,14},{14,12},{1,3},{3,1},... | collective-permute-start | bytes 98312 | tf_op jit(solution)/shard_map/ppermute | solution.py:264

commit v20 on v18

--- a/solution.py
+++ b/solution.py
@@ -124,22 +124,19 @@
 def sum_tokens(best):
     tokens = best.shape[1]
     high = best.astype(jnp.bfloat16)
-    rest = best - high.astype(jnp.float32)
-    mid = rest.astype(jnp.bfloat16)
-    low = (rest - mid.astype(jnp.float32)).astype(jnp.bfloat16)
-    parts = jnp.concatenate([low, mid, high], axis=1)
+    low = (best - high.astype(jnp.float32)).astype(jnp.bfloat16)
+    parts = jnp.concatenate([low, high], axis=1)
     query = lax.broadcasted_iota(jnp.int32, (tokens // QT, tokens), 0)
     token = lax.broadcasted_iota(jnp.int32, (tokens // QT, tokens), 1)
     ones = jnp.where(token // QT == query, 1.0, 0.0).astype(jnp.bfloat16)
     total = lax.dot_general(
-        jnp.concatenate([ones] * 3, axis=1), parts, (((1,), (1,)), ((), ())), preferred_element_type=jnp.float32
+        jnp.concatenate([ones] * 2, axis=1), parts, (((1,), (1,)), ((), ())), preferred_element_type=jnp.float32
     )
     return total * (1.0 / QT)
 
 
-def best_tokens(left_of, sel, max_ref):
+def best_tokens(left_of, sel, max_ref, piece):
     count, tokens = max_ref.shape
-    piece = 2 * GROUP
     for g in range(0, count, piece):
         dots = lax.dot_general(left_of(g, piece), sel, (((1,), (1,)), ((), ())), preferred_element_type=jnp.float32)
         max_ref[g:g + piece, :] = jnp.max(dots.reshape(piece, PT, tokens), axis=1)
@@ -150,7 +147,7 @@
     def left_of(g, piece):
         return p_ref[g:g + piece].reshape(piece * PT, DIM)
 
-    return sum_tokens(best_tokens(left_of, sel, max_ref))
+    return sum_tokens(best_tokens(left_of, sel, max_ref, 2 * GROUP))
 
 
 def score_picked_few(sel, p_ref, wide_ref, max_ref):
@@ -164,7 +161,7 @@
             [p_ref[h + g:h + g + piece].reshape(piece * PT, DIM) for h in (0, half)], axis=1
         )
 
-    total = sum_tokens(best_tokens(left_of, wide_ref[...], max_ref))
+    total = sum_tokens(best_tokens(left_of, wide_ref[...], max_ref, GROUP))
     queries = tokens // QT
     return jnp.concatenate([total[:queries], total[queries:]], axis=1)
 
@@ -275,7 +272,8 @@
     first, last = steps[:planes // 2], steps[planes // 2:]
     packed = pack(first, planes, theirs, early)
     first_far = swap_sides(packed)
-    *late, _ = lax.optimization_barrier((*late, packed))
+    *late, _ = lax.optimization_barrier((*reversed(late), packed))
+    late = late[::-1]
     last_far = swap_sides(pack(last, planes, theirs, late))
     near_tiles = score(near_kernel, planes, planes, False, clean, slots, picks, clean, *early, *late)
     first_far, near_tiles = lax.optimization_barrier((first_far, near_tiles))

time: 28.5 us -> 28.3 us (level)
  blocking collectives: 10.4 us -> 9.58 us
  waiting for transfers between devices: 0.52 us -> 1.33 us
    ppermute x3, starting transfers between devices: 4.57 us -> 3.65 us  [swap_sides(): return lax.ppermute(x, 'psg', [(j, j ^ 1) for j in range(shards)])]
    ppermute x3, starting transfers between devices: 6.06 us -> 6.96 us  [shift(): lax.ppermute(x, 'psg', [(j, (j + 2 * step) % shards) for j in range(shard...]
    all_to_all x1, blocking collectives: 10.4 us -> 9.58 us  [per_device(): lax.all_to_all(tiles, 'psg', split_axis=0, concat_axis=0, tiled=True)]
    ppermute x3, waiting for transfers between devices: 0.52 us -> 1.32 us  [swap_sides(): return lax.ppermute(x, 'psg', [(j, j ^ 1) for j in range(shards)])]
  transfers between devices with their start and end apart: 6 -> 6, of which waited for: 1 -> 2; matrix products, arithmetic and copies ran while one was open for 0% -> 0% of each run, Pallas kernels for 17% -> 17%
where the time goes in v20:
time: 28.3 us; the launch traced here: 28.1 us
  starting transfers between devices  10.6 us (37%)
  blocking collectives  9.58 us (34%)
  Pallas kernels  6.56 us (23%)
  waiting for transfers between devices  1.33 us (5%)
    all_to_all x1, blocking collectives, per_device(): lax.all_to_all(tiles, 'psg', split_axis=0, concat_axis=0, tiled=True)  9.58 us
    ppermute x3, starting transfers between devices, shift(): lax.ppermute(x, 'psg', [(j, (j + 2 * step) % shards) for j in range(shard...  6.96 us
    ppermute x3, starting transfers between devices, swap_sides(): return lax.ppermute(x, 'psg', [(j, j ^ 1) for j in range(shards)])  3.65 us
    pallas_call x3, Pallas kernels, score(): pl.pallas_call(kernel, out_shape=jax.ShapeDtypeStruct((tiles, QB + 1, LAN...  3.53 us
    pallas_call x1, Pallas kernels, prepare(): pl.pallas_call(prepare_kernel, out_shape=[jax.ShapeDtypeStruct((shards, L...  1.8 us
    ppermute x3, waiting for transfers between devices, swap_sides(): return lax.ppermute(x, 'psg', [(j, j ^ 1) for j in range(shards)])  1.32 us
    pallas_call x1, Pallas kernels, place(): pl.pallas_call(place_kernel, out_shape=jax.ShapeDtypeStruct((shards, QB,...  0.81 us
  transfers between devices with their start and end apart: 6, of which 2 were waited for; matrix products, arithmetic and copies ran while one was open for 0% of the time, Pallas kernels for 17%

profile of v20, /device:TPU:0, one launch (start us, length us, event | category | flops | bytes accessed | tf_op | source)
XLA Modules:
  0.0 28.1 jit_solution(7547360328137089454)
XLA Ops:
  0.0 0.0 copy-start
  0.0 3.0 %collective-permute-start = (bf16[256,128]{1,0:T(8,128)(2,1)}, bf16[256,128]{1,0:T(8,128)(2,1)S(1)}, u32[]{:S(2)}, u32[]{:S(2)}) collective-permute-start(bf16[256,128]{1,0:T(8,128)(2,1)} %bitcast.5), channel_id=1, source_target_pairs={{0,4},{2,6},{4,8},{6,10},{8,12},{10,14},{12,0},{14,2},{1,5},{3,7},... | collective-permute-start | bytes 196616 | tf_op jit(solution)/shard_map/ppermute | solution.py:264
  3.0 2.6 %collective-permute-start.3 = (bf16[256,128]{1,0:T(8,128)(2,1)}, bf16[256,128]{1,0:T(8,128)(2,1)S(1)}, u32[]{:S(2)}, u32[]{:S(2)}) collective-permute-start(bf16[256,128]{1,0:T(8,128)(2,1)} %bitcast.6), channel_id=1, source_target_pairs={{0,8},{2,10},{4,12},{6,14},{8,0},{10,2},{12,4},{14,6},{1,9},{3,11}... | collective-permute-start | bytes 196616 | tf_op jit(solution)/shard_map/ppermute | solution.py:264
  5.6 1.3 %collective-permute-start.2 = (bf16[256,128]{1,0:T(8,128)(2,1)}, bf16[256,128]{1,0:T(8,128)(2,1)S(1)}, u32[]{:S(2)}, u32[]{:S(2)}) collective-permute-start(bf16[256,128]{1,0:T(8,128)(2,1)} %bitcast.7), channel_id=1, source_target_pairs={{0,12},{2,14},{4,0},{6,2},{8,4},{10,6},{12,8},{14,10},{1,13},{3,15... | collective-permute-start | bytes 196616 | tf_op jit(solution)/shard_map/ppermute | solution.py:264
  7.0 1.5 %collective-permute-start.1 = (s32[8,32]{1,0:T(8,128)}, s32[8,32]{1,0:T(8,128)S(1)}, u32[]{:S(2)}, u32[]{:S(2)}) collective-permute-start(s32[8,32]{1,0:T(8,128)} %bitcast.10), channel_id=1, source_target_pairs={{0,2},{2,0},{4,6},{6,4},{8,10},{10,8},{12,14},{14,12},{1,3},{3,1},... | collective-permute-start | bytes 3080 | tf_op jit(solution)/shard_map/ppermute | solution.py:261
  8.5 1.8 %shard_map.46 = (f32[8,128]{1,0:T(8,128)S(1)}, s32[8,128]{1,0:T(8,128)S(1)}, bf16[128,64,128]{2,1,0:T(8,128)(2,1)S(1)}) custom-call(s32[8,32]{1,0:T(8,128)} %bitcast.11, s32[128]{0:T(128)} %len_hbm.1, bf16[128,64,128]{2,1,0:T(8,128)(2,1)} %p_hbm.1), custom_call_target="tpu_custom_call" | custom-call | flops 1048576 | bytes 2097152 | tf_op jit(solution)/shard_map/pallas_call | solution.py:73
  10.3 0.0 collective-permute-done.refs_1_
  10.3 0.5 %collective-permute-done.1.cand_ref = s32[8,32]{1,0:T(8,128)S(1)} collective-permute-done((s32[8,32]{1,0:T(8,128)}, s32[8,32]{1,0:T(8,128)S(1)}, u32[]{:S(2)}, u32[]{:S(2)}) %collective-permute-start.1) | collective-permute-done | bytes 1056 | tf_op jit(solution)/shard_map/ppermute | solution.py:261
  10.8 0.0 copy-done
  10.8 0.2 shard_map.47
  11.0 1.6 %collective-permute-start.5 = (bf16[128,128]{1,0:T(8,128)(2,1)S(1)}, bf16[128,128]{1,0:T(8,128)(2,1)S(1)}, u32[]{:S(2)}, u32[]{:S(2)}) collective-permute-start(bf16[128,128]{1,0:T(8,128)(2,1)S(1)} %shard_map.47), channel_id=1, source_target_pairs={{0,2},{2,0},{4,6},{6,4},{8,10},{10,8},{12,14},{14,12},{1,3},{3,1},... | collective-permute-start | bytes 98312 | tf_op jit(solution)/shard_map/ppermute | solution.py:261
  12.6 0.0 collective-permute-done.3.refs_0_.refs_2_
  12.6 0.0 collective-permute-done.2.refs_1_.refs_3_
  12.6 0.2 shard_map.48
  12.8 0.6 %collective-permute-start.4 = (bf16[128,128]{1,0:T(8,128)(2,1)S(1)}, bf16[128,128]{1,0:T(8,128)(2,1)S(1)}, u32[]{:S(2)}, u32[]{:S(2)}) collective-permute-start(bf16[128,128]{1,0:T(8,128)(2,1)S(1)} %shard_map.48), channel_id=1, source_target_pairs={{0,2},{2,0},{4,6},{6,4},{8,10},{10,8},{12,14},{14,12},{1,3},{3,1},... | collective-permute-start | bytes 98312 | tf_op jit(solution)/shard_map/ppermute | solution.py:261
  13.4 1.6 %shard_map.49.near_ref = f32[4,3,128]{2,1,0:T(4,128)S(1)} custom-call(f32[8,128]{1,0:T(8,128)S(1)} %get-tuple-element.16.slots_ref, s32[8,128]{1,0:T(8,128)S(1)} %get-tuple-element.22.picks_ref, bf16[128,64,128]{2,1,0:T(8,128)(2,1)S(1)} %get-tuple-element.18.p_ref, bf16[256,128]{1,0:T(8,128)(2,1)S(1)} %bitcast.9, ...), custom_call_target="tpu_custom_call" | custom-call | flops 536870912 | bytes 2097152 | tf_op jit(solution)/shard_map/pallas_call | solution.py:221
  15.0 0.0 collective-permute-done.5.sel_ref
  15.0 1.0 %shard_map.50.far_ref = f32[2,3,128]{2,1,0:T(4,128)S(1)} custom-call(f32[8,128]{1,0:T(8,128)S(1)} %get-tuple-element.16.slots_ref, bf16[128,64,128]{2,1,0:T(8,128)(2,1)S(1)} %get-tuple-element.18.p_ref, bf16[128,128]{1,0:T(8,128)(2,1)S(1)} %collective-permute-done.5.sel_ref), custom_call_target="tpu_custom_call" | custom-call | flops 268435456 | bytes 2097152 | tf_op jit(solution)/shard_map/pallas_call | solution.py:221
  16.0 0.8 %collective-permute-done.4.sel_ref = bf16[128,128]{1,0:T(8,128)(2,1)S(1)} collective-permute-done((bf16[128,128]{1,0:T(8,128)(2,1)S(1)}, bf16[128,128]{1,0:T(8,128)(2,1)S(1)}, u32[]{:S(2)}, u32[]{:S(2)}) %collective-permute-start.4) | collective-permute-done | bytes 32800 | tf_op jit(solution)/shard_map/ppermute | solution.py:261
  16.8 1.0 %shard_map.51 = f32[8,3,128]{2,1,0:T(4,128)S(1)} custom-call(f32[8,128]{1,0:T(8,128)S(1)} %get-tuple-element.16.slots_ref, bf16[128,64,128]{2,1,0:T(8,128)(2,1)S(1)} %get-tuple-element.18.p_ref, bf16[128,128]{1,0:T(8,128)(2,1)S(1)} %collective-permute-done.4.sel_ref, f32[4,3,128]{2,1,0:T(4,128)S(1)} %shard_map.49.near_ref, f32[2,3,128]{2,1,0:T(4,128)S(1)} %shard_map.50.far_ref), custom_call_target="tpu_custom_call" | custom-call | flops 268435456 | bytes 2097152 | tf_op jit(solution)/shard_map/pallas_call | solution.py:221
  17.7 9.6 %all_to_all.5.in_ref = f32[8,3,128]{2,1,0:T(4,128)S(1)} all-to-all(f32[8,3,128]{2,1,0:T(4,128)S(1)} %shard_map.51), channel_id=1, replica_groups=mesh['grp'=2,'psg'=8,'qry'=2] {'psg'}, dimensions={0} | all-to-all | bytes 24576 | tf_op jit(solution)/shard_map/all_to_all | solution.py:309
  27.3 0.8 %shard_map.52 = f32[8,2,16,32]{3,2,1,0:T(8,128)} custom-call(f32[8,3,128]{2,1,0:T(4,128)S(1)} %all_to_all.5.in_ref), custom_call_target="tpu_custom_call" | custom-call | tf_op jit(solution)/shard_map/pallas_call | solution.py:248
Async XLA Ops:
  0.0 10.8 %copy-start = (bf16[8,32,128]{2,1,0:T(8,128)(2,1)S(1)}, bf16[8,32,128]{2,1,0:T(8,128)(2,1)}, u32[]{:S(2)}) copy-start(bf16[8,32,128]{2,1,0:T(8,128)(2,1)} %param.4) | copy-start | bytes 196612
  0.0 10.3 %collective-permute-start = (bf16[256,128]{1,0:T(8,128)(2,1)}, bf16[256,128]{1,0:T(8,128)(2,1)S(1)}, u32[]{:S(2)}, u32[]{:S(2)}) collective-permute-start(bf16[256,128]{1,0:T(8,128)(2,1)} %bitcast.5), channel_id=1, source_target_pairs={{0,4},{2,6},{4,8},{6,10},{8,12},{10,14},{12,0},{14,2},{1,5},{3,7},... | collective-permute-start | bytes 196616 | tf_op jit(solution)/shard_map/ppermute | solution.py:264
  3.0 9.5 %collective-permute-start.3 = (bf16[256,128]{1,0:T(8,128)(2,1)}, bf16[256,128]{1,0:T(8,128)(2,1)S(1)}, u32[]{:S(2)}, u32[]{:S(2)}) collective-permute-start(bf16[256,128]{1,0:T(8,128)(2,1)} %bitcast.6), channel_id=1, source_target_pairs={{0,8},{2,10},{4,12},{6,14},{8,0},{10,2},{12,4},{14,6},{1,9},{3,11}... | collective-permute-start | bytes 196616 | tf_op jit(solution)/shard_map/ppermute | solution.py:264
  5.6 7.0 %collective-permute-start.2 = (bf16[256,128]{1,0:T(8,128)(2,1)}, bf16[256,128]{1,0:T(8,128)(2,1)S(1)}, u32[]{:S(2)}, u32[]{:S(2)}) collective-permute-start(bf16[256,128]{1,0:T(8,128)(2,1)} %bitcast.7), channel_id=1, source_target_pairs={{0,12},{2,14},{4,0},{6,2},{8,4},{10,6},{12,8},{14,10},{1,13},{3,15... | collective-permute-start | bytes 196616 | tf_op jit(solution)/shard_map/ppermute | solution.py:264
  7.0 3.8 %collective-permute-start.1 = (s32[8,32]{1,0:T(8,128)}, s32[8,32]{1,0:T(8,128)S(1)}, u32[]{:S(2)}, u32[]{:S(2)}) collective-permute-start(s32[8,32]{1,0:T(8,128)} %bitcast.10), channel_id=1, source_target_pairs={{0,2},{2,0},{4,6},{6,4},{8,10},{10,8},{12,14},{14,12},{1,3},{3,1},... | collective-permute-start | bytes 3080 | tf_op jit(solution)/shard_map/ppermute | solution.py:261
  11.0 4.0 %collective-permute-start.5 = (bf16[128,128]{1,0:T(8,128)(2,1)S(1)}, bf16[128,128]{1,0:T(8,128)(2,1)S(1)}, u32[]{:S(2)}, u32[]{:S(2)}) collective-permute-start(bf16[128,128]{1,0:T(8,128)(2,1)S(1)} %shard_map.47), channel_id=1, source_target_pairs={{0,2},{2,0},{4,6},{6,4},{8,10},{10,8},{12,14},{14,12},{1,3},{3,1},... | collective-permute-start | bytes 98312 | tf_op jit(solution)/shard_map/ppermute | solution.py:261
  12.8 4.0 %collective-permute-start.4 = (bf16[128,128]{1,0:T(8,128)(2,1)S(1)}, bf16[128,128]{1,0:T(8,128)(2,1)S(1)}, u32[]{:S(2)}, u32[]{:S(2)}) collective-permute-start(bf16[128,128]{1,0:T(8,128)(2,1)S(1)} %shard_map.48), channel_id=1, source_target_pairs={{0,2},{2,0},{4,6},{6,4},{8,10},{10,8},{12,14},{14,12},{1,3},{3,1},... | collective-permute-start | bytes 98312 | tf_op jit(solution)/shard_map/ppermute | solution.py:261

commit v21 on v20

--- a/solution.py
+++ b/solution.py
@@ -124,13 +124,15 @@
 def sum_tokens(best):
     tokens = best.shape[1]
     high = best.astype(jnp.bfloat16)
-    low = (best - high.astype(jnp.float32)).astype(jnp.bfloat16)
-    parts = jnp.concatenate([low, high], axis=1)
+    rest = best - high.astype(jnp.float32)
+    mid = rest.astype(jnp.bfloat16)
+    low = (rest - mid.astype(jnp.float32)).astype(jnp.bfloat16)
+    parts = jnp.concatenate([low, mid, high], axis=1)
     query = lax.broadcasted_iota(jnp.int32, (tokens // QT, tokens), 0)
     token = lax.broadcasted_iota(jnp.int32, (tokens // QT, tokens), 1)
     ones = jnp.where(token // QT == query, 1.0, 0.0).astype(jnp.bfloat16)
     total = lax.dot_general(
-        jnp.concatenate([ones] * 2, axis=1), parts, (((1,), (1,)), ((), ())), preferred_element_type=jnp.float32
+        jnp.concatenate([ones] * 3, axis=1), parts, (((1,), (1,)), ((), ())), preferred_element_type=jnp.float32
     )
     return total * (1.0 / QT)
 

time: 28.3 us -> 28.3 us (level)
  no operation moved by 1% of the time
where the time goes in v21:
time: 28.3 us; the launch traced here: 28.1 us
  starting transfers between devices  10.6 us (37%)
  blocking collectives  9.59 us (34%)
  Pallas kernels  6.65 us (23%)
  waiting for transfers between devices  1.24 us (4%)
    all_to_all x1, blocking collectives, per_device(): lax.all_to_all(tiles, 'psg', split_axis=0, concat_axis=0, tiled=True)  9.59 us
    ppermute x3, starting transfers between devices, shift(): lax.ppermute(x, 'psg', [(j, (j + 2 * step) % shards) for j in range(shard...  6.96 us
    ppermute x3, starting transfers between devices, swap_sides(): return lax.ppermute(x, 'psg', [(j, j ^ 1) for j in range(shards)])  3.65 us
    pallas_call x3, Pallas kernels, score(): pl.pallas_call(kernel, out_shape=jax.ShapeDtypeStruct((tiles, QB + 1, LAN...  3.62 us
    pallas_call x1, Pallas kernels, prepare(): pl.pallas_call(prepare_kernel, out_shape=[jax.ShapeDtypeStruct((shards, L...  1.8 us
    ppermute x3, waiting for transfers between devices, swap_sides(): return lax.ppermute(x, 'psg', [(j, j ^ 1) for j in range(shards)])  1.23 us
    pallas_call x1, Pallas kernels, place(): pl.pallas_call(place_kernel, out_shape=jax.ShapeDtypeStruct((shards, QB,...  0.81 us
  transfers between devices with their start and end apart: 6, of which 2 were waited for; matrix products, arithmetic and copies ran while one was open for 0% of the time, Pallas kernels for 17%

profile of v21, /device:TPU:0, one launch (start us, length us, event | category | flops | bytes accessed | tf_op | source)
XLA Modules:
  0.0 28.1 jit_solution(18426479474214988784)
XLA Ops:
  0.0 0.0 copy-start
  0.0 3.0 %collective-permute-start = (bf16[256,128]{1,0:T(8,128)(2,1)}, bf16[256,128]{1,0:T(8,128)(2,1)S(1)}, u32[]{:S(2)}, u32[]{:S(2)}) collective-permute-start(bf16[256,128]{1,0:T(8,128)(2,1)} %bitcast.5), channel_id=1, source_target_pairs={{0,4},{2,6},{4,8},{6,10},{8,12},{10,14},{12,0},{14,2},{1,5},{3,7},... | collective-permute-start | bytes 196616 | tf_op jit(solution)/shard_map/ppermute | solution.py:266
  3.0 2.6 %collective-permute-start.3 = (bf16[256,128]{1,0:T(8,128)(2,1)}, bf16[256,128]{1,0:T(8,128)(2,1)S(1)}, u32[]{:S(2)}, u32[]{:S(2)}) collective-permute-start(bf16[256,128]{1,0:T(8,128)(2,1)} %bitcast.6), channel_id=1, source_target_pairs={{0,8},{2,10},{4,12},{6,14},{8,0},{10,2},{12,4},{14,6},{1,9},{3,11}... | collective-permute-start | bytes 196616 | tf_op jit(solution)/shard_map/ppermute | solution.py:266
  5.6 1.3 %collective-permute-start.2 = (bf16[256,128]{1,0:T(8,128)(2,1)}, bf16[256,128]{1,0:T(8,128)(2,1)S(1)}, u32[]{:S(2)}, u32[]{:S(2)}) collective-permute-start(bf16[256,128]{1,0:T(8,128)(2,1)} %bitcast.7), channel_id=1, source_target_pairs={{0,12},{2,14},{4,0},{6,2},{8,4},{10,6},{12,8},{14,10},{1,13},{3,15... | collective-permute-start | bytes 196616 | tf_op jit(solution)/shard_map/ppermute | solution.py:266
  7.0 1.5 %collective-permute-start.1 = (s32[8,32]{1,0:T(8,128)}, s32[8,32]{1,0:T(8,128)S(1)}, u32[]{:S(2)}, u32[]{:S(2)}) collective-permute-start(s32[8,32]{1,0:T(8,128)} %bitcast.10), channel_id=1, source_target_pairs={{0,2},{2,0},{4,6},{6,4},{8,10},{10,8},{12,14},{14,12},{1,3},{3,1},... | collective-permute-start | bytes 3080 | tf_op jit(solution)/shard_map/ppermute | solution.py:263
  8.5 1.8 %shard_map.46 = (f32[8,128]{1,0:T(8,128)S(1)}, s32[8,128]{1,0:T(8,128)S(1)}, bf16[128,64,128]{2,1,0:T(8,128)(2,1)S(1)}) custom-call(s32[8,32]{1,0:T(8,128)} %bitcast.11, s32[128]{0:T(128)} %len_hbm.1, bf16[128,64,128]{2,1,0:T(8,128)(2,1)} %p_hbm.1), custom_call_target="tpu_custom_call" | custom-call | flops 1048576 | bytes 2097152 | tf_op jit(solution)/shard_map/pallas_call | solution.py:73
  10.3 0.0 collective-permute-done.refs_1_
  10.3 0.5 %collective-permute-done.1.cand_ref = s32[8,32]{1,0:T(8,128)S(1)} collective-permute-done((s32[8,32]{1,0:T(8,128)}, s32[8,32]{1,0:T(8,128)S(1)}, u32[]{:S(2)}, u32[]{:S(2)}) %collective-permute-start.1) | collective-permute-done | bytes 1056 | tf_op jit(solution)/shard_map/ppermute | solution.py:263
  10.8 0.0 copy-done
  10.8 0.2 shard_map.47
  11.0 1.6 %collective-permute-start.5 = (bf16[128,128]{1,0:T(8,128)(2,1)S(1)}, bf16[128,128]{1,0:T(8,128)(2,1)S(1)}, u32[]{:S(2)}, u32[]{:S(2)}) collective-permute-start(bf16[128,128]{1,0:T(8,128)(2,1)S(1)} %shard_map.47), channel_id=1, source_target_pairs={{0,2},{2,0},{4,6},{6,4},{8,10},{10,8},{12,14},{14,12},{1,3},{3,1},... | collective-permute-start | bytes 98312 | tf_op jit(solution)/shard_map/ppermute | solution.py:263
  12.6 0.0 collective-permute-done.3.refs_0_.refs_2_
  12.6 0.0 collective-permute-done.2.refs_1_.refs_3_
  12.6 0.2 shard_map.48
  12.8 0.6 %collective-permute-start.4 = (bf16[128,128]{1,0:T(8,128)(2,1)S(1)}, bf16[128,128]{1,0:T(8,128)(2,1)S(1)}, u32[]{:S(2)}, u32[]{:S(2)}) collective-permute-start(bf16[128,128]{1,0:T(8,128)(2,1)S(1)} %shard_map.48), channel_id=1, source_target_pairs={{0,2},{2,0},{4,6},{6,4},{8,10},{10,8},{12,14},{14,12},{1,3},{3,1},... | collective-permute-start | bytes 98312 | tf_op jit(solution)/shard_map/ppermute | solution.py:263
  13.4 1.7 %shard_map.49.near_ref = f32[4,3,128]{2,1,0:T(4,128)S(1)} custom-call(f32[8,128]{1,0:T(8,128)S(1)} %get-tuple-element.16.slots_ref, s32[8,128]{1,0:T(8,128)S(1)} %get-tuple-element.22.picks_ref, bf16[128,64,128]{2,1,0:T(8,128)(2,1)S(1)} %get-tuple-element.18.p_ref, bf16[256,128]{1,0:T(8,128)(2,1)S(1)} %bitcast.9, ...), custom_call_target="tpu_custom_call" | custom-call | flops 536870912 | bytes 2097152 | tf_op jit(solution)/shard_map/pallas_call | solution.py:223
  15.1 0.0 collective-permute-done.5.sel_ref
  15.1 1.0 %shard_map.50.far_ref = f32[2,3,128]{2,1,0:T(4,128)S(1)} custom-call(f32[8,128]{1,0:T(8,128)S(1)} %get-tuple-element.16.slots_ref, bf16[128,64,128]{2,1,0:T(8,128)(2,1)S(1)} %get-tuple-element.18.p_ref, bf16[128,128]{1,0:T(8,128)(2,1)S(1)} %collective-permute-done.5.sel_ref), custom_call_target="tpu_custom_call" | custom-call | flops 268435456 | bytes 2097152 | tf_op jit(solution)/shard_map/pallas_call | solution.py:223
  16.1 0.7 %collective-permute-done.4.sel_ref = bf16[128,128]{1,0:T(8,128)(2,1)S(1)} collective-permute-done((bf16[128,128]{1,0:T(8,128)(2,1)S(1)}, bf16[128,128]{1,0:T(8,128)(2,1)S(1)}, u32[]{:S(2)}, u32[]{:S(2)}) %collective-permute-start.4) | collective-permute-done | bytes 32800 | tf_op jit(solution)/shard_map/ppermute | solution.py:263
  16.8 1.0 %shard_map.51 = f32[8,3,128]{2,1,0:T(4,128)S(1)} custom-call(f32[8,128]{1,0:T(8,128)S(1)} %get-tuple-element.16.slots_ref, bf16[128,64,128]{2,1,0:T(8,128)(2,1)S(1)} %get-tuple-element.18.p_ref, bf16[128,128]{1,0:T(8,128)(2,1)S(1)} %collective-permute-done.4.sel_ref, f32[4,3,128]{2,1,0:T(4,128)S(1)} %shard_map.49.near_ref, f32[2,3,128]{2,1,0:T(4,128)S(1)} %shard_map.50.far_ref), custom_call_target="tpu_custom_call" | custom-call | flops 268435456 | bytes 2097152 | tf_op jit(solution)/shard_map/pallas_call | solution.py:223
  17.7 9.6 %all_to_all.5.in_ref = f32[8,3,128]{2,1,0:T(4,128)S(1)} all-to-all(f32[8,3,128]{2,1,0:T(4,128)S(1)} %shard_map.51), channel_id=1, replica_groups=mesh['grp'=2,'psg'=8,'qry'=2] {'psg'}, dimensions={0} | all-to-all | bytes 24576 | tf_op jit(solution)/shard_map/all_to_all | solution.py:311
  27.3 0.8 %shard_map.52 = f32[8,2,16,32]{3,2,1,0:T(8,128)} custom-call(f32[8,3,128]{2,1,0:T(4,128)S(1)} %all_to_all.5.in_ref), custom_call_target="tpu_custom_call" | custom-call | tf_op jit(solution)/shard_map/pallas_call | solution.py:250
Async XLA Ops:
  0.0 10.8 %copy-start = (bf16[8,32,128]{2,1,0:T(8,128)(2,1)S(1)}, bf16[8,32,128]{2,1,0:T(8,128)(2,1)}, u32[]{:S(2)}) copy-start(bf16[8,32,128]{2,1,0:T(8,128)(2,1)} %param.4) | copy-start | bytes 196612
  0.0 10.3 %collective-permute-start = (bf16[256,128]{1,0:T(8,128)(2,1)}, bf16[256,128]{1,0:T(8,128)(2,1)S(1)}, u32[]{:S(2)}, u32[]{:S(2)}) collective-permute-start(bf16[256,128]{1,0:T(8,128)(2,1)} %bitcast.5), channel_id=1, source_target_pairs={{0,4},{2,6},{4,8},{6,10},{8,12},{10,14},{12,0},{14,2},{1,5},{3,7},... | collective-permute-start | bytes 196616 | tf_op jit(solution)/shard_map/ppermute | solution.py:266
  3.0 9.5 %collective-permute-start.3 = (bf16[256,128]{1,0:T(8,128)(2,1)}, bf16[256,128]{1,0:T(8,128)(2,1)S(1)}, u32[]{:S(2)}, u32[]{:S(2)}) collective-permute-start(bf16[256,128]{1,0:T(8,128)(2,1)} %bitcast.6), channel_id=1, source_target_pairs={{0,8},{2,10},{4,12},{6,14},{8,0},{10,2},{12,4},{14,6},{1,9},{3,11}... | collective-permute-start | bytes 196616 | tf_op jit(solution)/shard_map/ppermute | solution.py:266
  5.6 7.0 %collective-permute-start.2 = (bf16[256,128]{1,0:T(8,128)(2,1)}, bf16[256,128]{1,0:T(8,128)(2,1)S(1)}, u32[]{:S(2)}, u32[]{:S(2)}) collective-permute-start(bf16[256,128]{1,0:T(8,128)(2,1)} %bitcast.7), channel_id=1, source_target_pairs={{0,12},{2,14},{4,0},{6,2},{8,4},{10,6},{12,8},{14,10},{1,13},{3,15... | collective-permute-start | bytes 196616 | tf_op jit(solution)/shard_map/ppermute | solution.py:266
  7.0 3.8 %collective-permute-start.1 = (s32[8,32]{1,0:T(8,128)}, s32[8,32]{1,0:T(8,128)S(1)}, u32[]{:S(2)}, u32[]{:S(2)}) collective-permute-start(s32[8,32]{1,0:T(8,128)} %bitcast.10), channel_id=1, source_target_pairs={{0,2},{2,0},{4,6},{6,4},{8,10},{10,8},{12,14},{14,12},{1,3},{3,1},... | collective-permute-start | bytes 3080 | tf_op jit(solution)/shard_map/ppermute | solution.py:263
  11.0 4.1 %collective-permute-start.5 = (bf16[128,128]{1,0:T(8,128)(2,1)S(1)}, bf16[128,128]{1,0:T(8,128)(2,1)S(1)}, u32[]{:S(2)}, u32[]{:S(2)}) collective-permute-start(bf16[128,128]{1,0:T(8,128)(2,1)S(1)} %shard_map.47), channel_id=1, source_target_pairs={{0,2},{2,0},{4,6},{6,4},{8,10},{10,8},{12,14},{14,12},{1,3},{3,1},... | collective-permute-start | bytes 98312 | tf_op jit(solution)/shard_map/ppermute | solution.py:263
  12.8 4.0 %collective-permute-start.4 = (bf16[128,128]{1,0:T(8,128)(2,1)S(1)}, bf16[128,128]{1,0:T(8,128)(2,1)S(1)}, u32[]{:S(2)}, u32[]{:S(2)}) collective-permute-start(bf16[128,128]{1,0:T(8,128)(2,1)S(1)} %shard_map.48), channel_id=1, source_target_pairs={{0,2},{2,0},{4,6},{6,4},{8,10},{10,8},{12,14},{14,12},{1,3},{3,1},... | collective-permute-start | bytes 98312 | tf_op jit(solution)/shard_map/ppermute | solution.py:263

commit v22 on v19

--- a/solution.py
+++ b/solution.py
@@ -137,9 +137,8 @@
     return total * (1.0 / QT)
 
 
-def best_tokens(left_of, sel, max_ref):
+def best_tokens(left_of, sel, max_ref, piece):
     count, tokens = max_ref.shape
-    piece = 2 * GROUP
     for g in range(0, count, piece):
         dots = lax.dot_general(left_of(g, piece), sel, (((1,), (1,)), ((), ())), preferred_element_type=jnp.float32)
         max_ref[g:g + piece, :] = jnp.max(dots.reshape(piece, PT, tokens), axis=1)
@@ -150,7 +149,7 @@
     def left_of(g, piece):
         return p_ref[g:g + piece].reshape(piece * PT, DIM)
 
-    return sum_tokens(best_tokens(left_of, sel, max_ref))
+    return sum_tokens(best_tokens(left_of, sel, max_ref, 2 * GROUP))
 
 
 def score_picked_few(sel, p_ref, wide_ref, max_ref):
@@ -164,7 +163,7 @@
             [p_ref[h + g:h + g + piece].reshape(piece * PT, DIM) for h in (0, half)], axis=1
         )
 
-    total = sum_tokens(best_tokens(left_of, wide_ref[...], max_ref))
+    total = sum_tokens(best_tokens(left_of, wide_ref[...], max_ref, GROUP))
     queries = tokens // QT
     return jnp.concatenate([total[:queries], total[queries:]], axis=1)
 
@@ -275,8 +274,8 @@
     blocks = [own, *shifted]
     packed = pack(first, planes, theirs, [blocks[step] for step in first])
     first_far = swap_sides(packed)
-    *late, _ = lax.optimization_barrier((*[blocks[step] for step in reversed(last)], packed))
-    for step, block in zip(reversed(last), late):
+    *late, _ = lax.optimization_barrier((*[blocks[step] for step in last], packed))
+    for step, block in zip(last, late):
         blocks[step] = block
     last_far = swap_sides(pack(last, planes, theirs, [blocks[step] for step in last]))
     near_tiles = score(near_kernel, planes, planes, False, clean, slots, picks, clean, *blocks)

time: 28.9 us -> 28.9 us (level)
  blocking collectives: 9.27 us -> 10.9 us
  starting transfers between devices: 11.5 us -> 10.7 us
  waiting for transfers between devices: 1.24 us -> 0.52 us
    ppermute x3, starting transfers between devices: 7.86 us -> 6.06 us  [shift(): lax.ppermute(x, 'psg', [(j, (j + 2 * step) % shards) for j in range(shard...]
    all_to_all x1, blocking collectives: 9.27 us -> 10.9 us  [per_device(): lax.all_to_all(tiles, 'psg', split_axis=0, concat_axis=0, tiled=True)]
    ppermute x3, starting transfers between devices: 3.65 us -> 4.59 us  [swap_sides(): return lax.ppermute(x, 'psg', [(j, j ^ 1) for j in range(shards)])]
    ppermute x3, waiting for transfers between devices: 1.23 us -> 0.52 us  [swap_sides(): return lax.ppermute(x, 'psg', [(j, j ^ 1) for j in range(shards)])]
  transfers between devices with their start and end apart: 6 -> 6, of which waited for: 2 -> 1; matrix products, arithmetic and copies ran while one was open for 0% -> 0% of each run, Pallas kernels for 17% -> 17%
where the time goes in v22:
time: 28.9 us; the launch traced here: 28.8 us
  blocking collectives  10.9 us (38%)
  starting transfers between devices  10.7 us (37%)
  Pallas kernels  6.67 us (23%)
  waiting for transfers between devices  0.52 us (2%)
    all_to_all x1, blocking collectives, per_device(): lax.all_to_all(tiles, 'psg', split_axis=0, concat_axis=0, tiled=True)  10.9 us
    ppermute x3, starting transfers between devices, shift(): lax.ppermute(x, 'psg', [(j, (j + 2 * step) % shards) for j in range(shard...  6.06 us
    ppermute x3, starting transfers between devices, swap_sides(): return lax.ppermute(x, 'psg', [(j, j ^ 1) for j in range(shards)])  4.59 us
    pallas_call x3, Pallas kernels, score(): pl.pallas_call(kernel, out_shape=jax.ShapeDtypeStruct((tiles, QB + 1, LAN...  3.64 us
    pallas_call x1, Pallas kernels, prepare(): pl.pallas_call(prepare_kernel, out_shape=[jax.ShapeDtypeStruct((shards, L...  1.8 us
    pallas_call x1, Pallas kernels, place(): pl.pallas_call(place_kernel, out_shape=jax.ShapeDtypeStruct((shards, QB,...  0.81 us
  transfers between devices with their start and end apart: 6, of which 1 were waited for; matrix products, arithmetic and copies ran while one was open for 0% of the time, Pallas kernels for 17%

profile of v22, /device:TPU:0, one launch (start us, length us, event | category | flops | bytes accessed | tf_op | source)
XLA Modules:
  0.0 28.8 jit_solution(1059336956482173172)
XLA Ops:
  0.0 0.0 copy-start
  0.0 4.0 %collective-permute-start = (bf16[256,128]{1,0:T(8,128)(2,1)}, bf16[256,128]{1,0:T(8,128)(2,1)S(1)}, u32[]{:S(2)}, u32[]{:S(2)}) collective-permute-start(bf16[256,128]{1,0:T(8,128)(2,1)} %bitcast.5), channel_id=1, source_target_pairs={{0,8},{2,10},{4,12},{6,14},{8,0},{10,2},{12,4},{14,6},{1,9},{3,11}... | collective-permute-start | bytes 196616 | tf_op jit(solution)/shard_map/ppermute | solution.py:266
  4.0 1.3 %collective-permute-start.3 = (bf16[256,128]{1,0:T(8,128)(2,1)}, bf16[256,128]{1,0:T(8,128)(2,1)S(1)}, u32[]{:S(2)}, u32[]{:S(2)}) collective-permute-start(bf16[256,128]{1,0:T(8,128)(2,1)} %bitcast.6), channel_id=1, source_target_pairs={{0,12},{2,14},{4,0},{6,2},{8,4},{10,6},{12,8},{14,10},{1,13},{3,15... | collective-permute-start | bytes 196616 | tf_op jit(solution)/shard_map/ppermute | solution.py:266
  5.4 0.7 %collective-permute-start.2 = (bf16[256,128]{1,0:T(8,128)(2,1)}, bf16[256,128]{1,0:T(8,128)(2,1)S(1)}, u32[]{:S(2)}, u32[]{:S(2)}) collective-permute-start(bf16[256,128]{1,0:T(8,128)(2,1)} %bitcast.7), channel_id=1, source_target_pairs={{0,4},{2,6},{4,8},{6,10},{8,12},{10,14},{12,0},{14,2},{1,5},{3,7},... | collective-permute-start | bytes 196616 | tf_op jit(solution)/shard_map/ppermute | solution.py:266
  6.1 1.5 %collective-permute-start.1 = (s32[8,32]{1,0:T(8,128)}, s32[8,32]{1,0:T(8,128)S(1)}, u32[]{:S(2)}, u32[]{:S(2)}) collective-permute-start(s32[8,32]{1,0:T(8,128)} %bitcast.10), channel_id=1, source_target_pairs={{0,2},{2,0},{4,6},{6,4},{8,10},{10,8},{12,14},{14,12},{1,3},{3,1},... | collective-permute-start | bytes 3080 | tf_op jit(solution)/shard_map/ppermute | solution.py:263
  7.6 1.8 %shard_map.46 = (f32[8,128]{1,0:T(8,128)S(1)}, s32[8,128]{1,0:T(8,128)S(1)}, bf16[128,64,128]{2,1,0:T(8,128)(2,1)S(1)}) custom-call(s32[8,32]{1,0:T(8,128)} %bitcast.11, s32[128]{0:T(128)} %len_hbm.1, bf16[128,64,128]{2,1,0:T(8,128)(2,1)} %p_hbm.1), custom_call_target="tpu_custom_call" | custom-call | flops 1048576 | bytes 2097152 | tf_op jit(solution)/shard_map/pallas_call | solution.py:73
  9.4 0.0 collective-permute-done.refs_1_.refs_2_
  9.4 0.5 %collective-permute-done.1.cand_ref = s32[8,32]{1,0:T(8,128)S(1)} collective-permute-done((s32[8,32]{1,0:T(8,128)}, s32[8,32]{1,0:T(8,128)S(1)}, u32[]{:S(2)}, u32[]{:S(2)}) %collective-permute-start.1) | collective-permute-done | bytes 1056 | tf_op jit(solution)/shard_map/ppermute | solution.py:263
  9.9 0.0 copy-done
  9.9 0.2 shard_map.47
  10.1 1.6 %collective-permute-start.5 = (bf16[128,128]{1,0:T(8,128)(2,1)S(1)}, bf16[128,128]{1,0:T(8,128)(2,1)S(1)}, u32[]{:S(2)}, u32[]{:S(2)}) collective-permute-start(bf16[128,128]{1,0:T(8,128)(2,1)S(1)} %shard_map.47), channel_id=1, source_target_pairs={{0,2},{2,0},{4,6},{6,4},{8,10},{10,8},{12,14},{14,12},{1,3},{3,1},... | collective-permute-start | bytes 98312 | tf_op jit(solution)/shard_map/ppermute | solution.py:263
  11.7 0.0 collective-permute-done.3.refs_1_.refs_3_
  11.7 0.0 collective-permute-done.2.refs_0_.refs_1_
  11.7 0.2 shard_map.48
  11.9 1.5 %collective-permute-start.4 = (bf16[128,128]{1,0:T(8,128)(2,1)S(1)}, bf16[128,128]{1,0:T(8,128)(2,1)S(1)}, u32[]{:S(2)}, u32[]{:S(2)}) collective-permute-start(bf16[128,128]{1,0:T(8,128)(2,1)S(1)} %shard_map.48), channel_id=1, source_target_pairs={{0,2},{2,0},{4,6},{6,4},{8,10},{10,8},{12,14},{14,12},{1,3},{3,1},... | collective-permute-start | bytes 98312 | tf_op jit(solution)/shard_map/ppermute | solution.py:263
  13.4 1.7 %shard_map.49.near_ref = f32[4,3,128]{2,1,0:T(4,128)S(1)} custom-call(f32[8,128]{1,0:T(8,128)S(1)} %get-tuple-element.16.slots_ref, s32[8,128]{1,0:T(8,128)S(1)} %get-tuple-element.22.picks_ref, bf16[128,64,128]{2,1,0:T(8,128)(2,1)S(1)} %get-tuple-element.18.p_ref, bf16[256,128]{1,0:T(8,128)(2,1)S(1)} %bitcast.9, ...), custom_call_target="tpu_custom_call" | custom-call | flops 536870912 | bytes 2097152 | tf_op jit(solution)/shard_map/pallas_call | solution.py:223
  15.1 0.0 collective-permute-done.5.sel_ref
  15.1 1.0 %shard_map.50.far_ref = f32[2,3,128]{2,1,0:T(4,128)S(1)} custom-call(f32[8,128]{1,0:T(8,128)S(1)} %get-tuple-element.16.slots_ref, bf16[128,64,128]{2,1,0:T(8,128)(2,1)S(1)} %get-tuple-element.18.p_ref, bf16[128,128]{1,0:T(8,128)(2,1)S(1)} %collective-permute-done.5.sel_ref), custom_call_target="tpu_custom_call" | custom-call | flops 268435456 | bytes 2097152 | tf_op jit(solution)/shard_map/pallas_call | solution.py:223
  16.1 0.0 collective-permute-done.4.sel_ref
  16.1 1.0 %shard_map.51 = f32[8,3,128]{2,1,0:T(4,128)S(1)} custom-call(f32[8,128]{1,0:T(8,128)S(1)} %get-tuple-element.16.slots_ref, bf16[128,64,128]{2,1,0:T(8,128)(2,1)S(1)} %get-tuple-element.18.p_ref, bf16[128,128]{1,0:T(8,128)(2,1)S(1)} %collective-permute-done.4.sel_ref, f32[4,3,128]{2,1,0:T(4,128)S(1)} %shard_map.49.near_ref, f32[2,3,128]{2,1,0:T(4,128)S(1)} %shard_map.50.far_ref), custom_call_target="tpu_custom_call" | custom-call | flops 268435456 | bytes 2097152 | tf_op jit(solution)/shard_map/pallas_call | solution.py:223
  17.1 10.9 %all_to_all.5.in_ref = f32[8,3,128]{2,1,0:T(4,128)S(1)} all-to-all(f32[8,3,128]{2,1,0:T(4,128)S(1)} %shard_map.51), channel_id=1, replica_groups=mesh['grp'=2,'psg'=8,'qry'=2] {'psg'}, dimensions={0} | all-to-all | bytes 24576 | tf_op jit(solution)/shard_map/all_to_all | solution.py:312
  27.9 0.8 %shard_map.52 = f32[8,2,16,32]{3,2,1,0:T(8,128)} custom-call(f32[8,3,128]{2,1,0:T(4,128)S(1)} %all_to_all.5.in_ref), custom_call_target="tpu_custom_call" | custom-call | tf_op jit(solution)/shard_map/pallas_call | solution.py:250
Async XLA Ops:
  0.0 9.9 %copy-start = (bf16[8,32,128]{2,1,0:T(8,128)(2,1)S(1)}, bf16[8,32,128]{2,1,0:T(8,128)(2,1)}, u32[]{:S(2)}) copy-start(bf16[8,32,128]{2,1,0:T(8,128)(2,1)} %param.4) | copy-start | bytes 196612
  0.0 9.4 %collective-permute-start = (bf16[256,128]{1,0:T(8,128)(2,1)}, bf16[256,128]{1,0:T(8,128)(2,1)S(1)}, u32[]{:S(2)}, u32[]{:S(2)}) collective-permute-start(bf16[256,128]{1,0:T(8,128)(2,1)} %bitcast.5), channel_id=1, source_target_pairs={{0,8},{2,10},{4,12},{6,14},{8,0},{10,2},{12,4},{14,6},{1,9},{3,11}... | collective-permute-start | bytes 196616 | tf_op jit(solution)/shard_map/ppermute | solution.py:266
  4.0 7.6 %collective-permute-start.3 = (bf16[256,128]{1,0:T(8,128)(2,1)}, bf16[256,128]{1,0:T(8,128)(2,1)S(1)}, u32[]{:S(2)}, u32[]{:S(2)}) collective-permute-start(bf16[256,128]{1,0:T(8,128)(2,1)} %bitcast.6), channel_id=1, source_target_pairs={{0,12},{2,14},{4,0},{6,2},{8,4},{10,6},{12,8},{14,10},{1,13},{3,15... | collective-permute-start | bytes 196616 | tf_op jit(solution)/shard_map/ppermute | solution.py:266
  5.4 6.3 %collective-permute-start.2 = (bf16[256,128]{1,0:T(8,128)(2,1)}, bf16[256,128]{1,0:T(8,128)(2,1)S(1)}, u32[]{:S(2)}, u32[]{:S(2)}) collective-permute-start(bf16[256,128]{1,0:T(8,128)(2,1)} %bitcast.7), channel_id=1, source_target_pairs={{0,4},{2,6},{4,8},{6,10},{8,12},{10,14},{12,0},{14,2},{1,5},{3,7},... | collective-permute-start | bytes 196616 | tf_op jit(solution)/shard_map/ppermute | solution.py:266
  6.1 3.8 %collective-permute-start.1 = (s32[8,32]{1,0:T(8,128)}, s32[8,32]{1,0:T(8,128)S(1)}, u32[]{:S(2)}, u32[]{:S(2)}) collective-permute-start(s32[8,32]{1,0:T(8,128)} %bitcast.10), channel_id=1, source_target_pairs={{0,2},{2,0},{4,6},{6,4},{8,10},{10,8},{12,14},{14,12},{1,3},{3,1},... | collective-permute-start | bytes 3080 | tf_op jit(solution)/shard_map/ppermute | solution.py:263
  10.1 5.0 %collective-permute-start.5 = (bf16[128,128]{1,0:T(8,128)(2,1)S(1)}, bf16[128,128]{1,0:T(8,128)(2,1)S(1)}, u32[]{:S(2)}, u32[]{:S(2)}) collective-permute-start(bf16[128,128]{1,0:T(8,128)(2,1)S(1)} %shard_map.47), channel_id=1, source_target_pairs={{0,2},{2,0},{4,6},{6,4},{8,10},{10,8},{12,14},{14,12},{1,3},{3,1},... | collective-permute-start | bytes 98312 | tf_op jit(solution)/shard_map/ppermute | solution.py:263
  11.9 4.2 %collective-permute-start.4 = (bf16[128,128]{1,0:T(8,128)(2,1)S(1)}, bf16[128,128]{1,0:T(8,128)(2,1)S(1)}, u32[]{:S(2)}, u32[]{:S(2)}) collective-permute-start(bf16[128,128]{1,0:T(8,128)(2,1)S(1)} %shard_map.48), channel_id=1, source_target_pairs={{0,2},{2,0},{4,6},{6,4},{8,10},{10,8},{12,14},{14,12},{1,3},{3,1},... | collective-permute-start | bytes 98312 | tf_op jit(solution)/shard_map/ppermute | solution.py:263

commit v23 on v21

--- a/solution.py
+++ b/solution.py
@@ -16,6 +16,7 @@
 KB = 32
 LANES = 128
 GROUP = 8
+TILE = 4
 
 
 def prepare_kernel(
@@ -199,9 +200,9 @@
         put(out_ref, owner, total, n, slots_ref, owner)
     others = [step for step in range(planes) if step not in steps]
     for step in range(planes):
-        out_ref[near_owner(me, step, planes)] = near_ref[step]
+        out_ref[near_owner(me, step, planes), 0:QB + 1, :] = near_ref[step]
     for n, step in enumerate(others):
-        out_ref[near_owner(me, step, planes) ^ 1] = far_ref[n]
+        out_ref[near_owner(me, step, planes) ^ 1, 0:QB + 1, :] = far_ref[n]
 
 
 def all_kernel(slots_ref, picks_ref, p_ref, q_ref, out_ref, sel_ref, max_ref):
@@ -213,7 +214,7 @@
         put(out_ref, n, total, n, slots_ref, n)
 
 
-def score(kernel, tiles, some, few, passages, *more):
+def score(kernel, tiles, some, few, passages, *more, tile_rows=QB + 1):
     count, tokens = passages.shape[0], some * QB * QT
     vmem = pl.BlockSpec(memory_space=pltpu.VMEM)
     if few:
@@ -222,7 +223,7 @@
         scratch = [pltpu.VMEM((tokens, DIM), jnp.bfloat16), pltpu.VMEM((count, tokens), jnp.float32)]
     return pl.pallas_call(
         kernel,
-        out_shape=jax.ShapeDtypeStruct((tiles, QB + 1, LANES), jnp.float32),
+        out_shape=jax.ShapeDtypeStruct((tiles, tile_rows, LANES), jnp.float32),
         in_specs=[vmem] * len(more),
         out_specs=vmem,
         scratch_shapes=scratch,
@@ -237,10 +238,11 @@
     slots = out_ref.shape[-1]
     m = lax.broadcasted_iota(jnp.int32, (PBS, LANES), 0)
     for j in range(in_ref.shape[0]):
-        row = in_ref[j, QB:QB + 1, :].astype(jnp.int32)
+        tile_ref = in_ref.at[j, lax.axis_index("psg")] if len(in_ref.shape) == 4 else in_ref.at[j]
+        row = tile_ref[QB:QB + 1, :].astype(jnp.int32)
         where = jnp.minimum(row * PBS, LANES - PBS) + m
         for i in range(QB):
-            tile = jnp.broadcast_to(in_ref[j, i:i + 1, :], (PBS, LANES))
+            tile = jnp.broadcast_to(tile_ref[i:i + 1, :], (PBS, LANES))
             out_ref[j, i] = jnp.take_along_axis(tile, where, axis=1)[:, :slots]
 
 
@@ -256,7 +258,7 @@
     )(tiles)
 
 
-def by_planes(own, shards, candidates, lengths, passages):
+def by_planes(own, shards, slot_count, candidates, lengths, passages):
     planes = shards // 2
 
     def swap_sides(x):
@@ -283,13 +285,15 @@
         functools.partial(some_far_kernel, first, planes), len(first), len(first), True, clean, slots, clean, first_far
     )
     last_far, far_tiles = lax.optimization_barrier((last_far, far_tiles))
-    return score(
+    tiles = score(
         functools.partial(last_far_kernel, last, planes), shards, len(last), True, clean,
-        slots, clean, last_far, near_tiles, far_tiles,
-    )
-
-
-def by_gather(own, shards, candidates, lengths, passages):
+        slots, clean, last_far, near_tiles, far_tiles, tile_rows=TILE,
+    )
+    tiles = lax.all_gather(tiles.reshape(shards * TILE, LANES), "psg", axis=0, tiled=True)
+    return place(tiles.reshape(shards, shards, TILE, LANES), slot_count)
+
+
+def by_gather(own, shards, slot_count, candidates, lengths, passages):
     slots, picks, clean = prepare(shards, candidates, lengths, passages)
     gathered = lax.all_gather(own, "psg", axis=0)
     some = min(shards, 8)
@@ -298,18 +302,19 @@
         return score(all_kernel, some, some, False, clean, items[0], items[1], clean, items[2])
 
     parts = [x.reshape(shards // some, some, *x.shape[1:]) for x in (slots, picks, gathered)]
-    return lax.map(score_some, parts).reshape(shards, QB + 1, LANES)
+    tiles = lax.map(score_some, parts).reshape(shards, QB + 1, LANES)
+    return place(lax.all_to_all(tiles, "psg", split_axis=0, concat_axis=0, tiled=True), slot_count)
 
 
 def per_device(queries, passages, lengths, candidates):
     shards = lax.axis_size("psg")
     rows = passages.shape[0] // PBS
     form = by_planes if shards == 8 else by_gather
-    tiles = form(
-        queries.reshape(QBD * QB * QT, DIM), shards, candidates.reshape(rows, KB), lengths, passages
-    )
-    tiles = lax.all_to_all(tiles, "psg", split_axis=0, concat_axis=0, tiled=True)
-    return place(tiles, rows * KB // shards).transpose(0, 3, 1, 2)[None]
+    placed = form(
+        queries.reshape(QBD * QB * QT, DIM), shards, rows * KB // shards,
+        candidates.reshape(rows, KB), lengths, passages,
+    )
+    return placed.transpose(0, 3, 1, 2)[None]
 
 
 def solution(mesh):

time: 28.3 us -> 49.3 us (1.74)
  blocking collectives: 9.59 us -> 30.6 us
    all_gather x0 -> x1, blocking collectives: none -> 30.6 us  [by_planes(): lax.all_gather(tiles.reshape(shards * TILE, LANES), 'psg', axis=0, tiled=...]
    all_to_all x1 -> x0, blocking collectives: 9.59 us -> none  [per_device(): lax.all_to_all(tiles, 'psg', split_axis=0, concat_axis=0, tiled=True)]
  transfers between devices with their start and end apart: 6 -> 6, of which waited for: 2 -> 2; matrix products, arithmetic and copies ran while one was open for 0% -> 0% of each run, Pallas kernels for 17% -> 10%
where the time goes in v23:
time: 49.3 us; the launch traced here: 49.1 us
  blocking collectives  30.6 us (62%)
  starting transfers between devices  10.6 us (22%)
  Pallas kernels  6.66 us (14%)
  waiting for transfers between devices  1.24 us (3%)
    all_gather x1, blocking collectives, by_planes(): lax.all_gather(tiles.reshape(shards * TILE, LANES), 'psg', axis=0, tiled=...  30.6 us
    ppermute x3, starting transfers between devices, shift(): lax.ppermute(x, 'psg', [(j, (j + 2 * step) % shards) for j in range(shard...  6.96 us
    ppermute x3, starting transfers between devices, swap_sides(): return lax.ppermute(x, 'psg', [(j, j ^ 1) for j in range(shards)])  3.65 us
    pallas_call x3, Pallas kernels, score(): pl.pallas_call(kernel, out_shape=jax.ShapeDtypeStruct((tiles, tile_rows,...  3.62 us
    pallas_call x1, Pallas kernels, prepare(): pl.pallas_call(prepare_kernel, out_shape=[jax.ShapeDtypeStruct((shards, L...  1.8 us
    ppermute x3, waiting for transfers between devices, swap_sides(): return lax.ppermute(x, 'psg', [(j, j ^ 1) for j in range(shards)])  1.23 us
  transfers between devices with their start and end apart: 6, of which 2 were waited for; matrix products, arithmetic and copies ran while one was open for 0% of the time, Pallas kernels for 10%

profile of v23, /device:TPU:0, one launch (start us, length us, event | category | flops | bytes accessed | tf_op | source)
XLA Modules:
  0.0 49.1 jit_solution(8214454053981476260)
XLA Ops:
  0.0 0.0 copy-start
  0.0 3.0 %collective-permute-start = (bf16[256,128]{1,0:T(8,128)(2,1)}, bf16[256,128]{1,0:T(8,128)(2,1)S(1)}, u32[]{:S(2)}, u32[]{:S(2)}) collective-permute-start(bf16[256,128]{1,0:T(8,128)(2,1)} %bitcast.8), channel_id=1, source_target_pairs={{0,4},{2,6},{4,8},{6,10},{8,12},{10,14},{12,0},{14,2},{1,5},{3,7},... | collective-permute-start | bytes 196616 | tf_op jit(solution)/shard_map/ppermute | solution.py:268
  3.0 2.6 %collective-permute-start.3 = (bf16[256,128]{1,0:T(8,128)(2,1)}, bf16[256,128]{1,0:T(8,128)(2,1)S(1)}, u32[]{:S(2)}, u32[]{:S(2)}) collective-permute-start(bf16[256,128]{1,0:T(8,128)(2,1)} %bitcast.9), channel_id=1, source_target_pairs={{0,8},{2,10},{4,12},{6,14},{8,0},{10,2},{12,4},{14,6},{1,9},{3,11}... | collective-permute-start | bytes 196616 | tf_op jit(solution)/shard_map/ppermute | solution.py:268
  5.6 1.3 %collective-permute-start.2 = (bf16[256,128]{1,0:T(8,128)(2,1)}, bf16[256,128]{1,0:T(8,128)(2,1)S(1)}, u32[]{:S(2)}, u32[]{:S(2)}) collective-permute-start(bf16[256,128]{1,0:T(8,128)(2,1)} %bitcast.10), channel_id=1, source_target_pairs={{0,12},{2,14},{4,0},{6,2},{8,4},{10,6},{12,8},{14,10},{1,13},{3,15... | collective-permute-start | bytes 196616 | tf_op jit(solution)/shard_map/ppermute | solution.py:268
  7.0 1.5 %collective-permute-start.1 = (s32[8,32]{1,0:T(8,128)}, s32[8,32]{1,0:T(8,128)S(1)}, u32[]{:S(2)}, u32[]{:S(2)}) collective-permute-start(s32[8,32]{1,0:T(8,128)} %bitcast.14), channel_id=1, source_target_pairs={{0,2},{2,0},{4,6},{6,4},{8,10},{10,8},{12,14},{14,12},{1,3},{3,1},... | collective-permute-start | bytes 3080 | tf_op jit(solution)/shard_map/ppermute | solution.py:265
  8.5 1.8 %shard_map.46 = (f32[8,128]{1,0:T(8,128)S(1)}, s32[8,128]{1,0:T(8,128)S(1)}, bf16[128,64,128]{2,1,0:T(8,128)(2,1)S(1)}) custom-call(s32[8,32]{1,0:T(8,128)} %bitcast.15, s32[128]{0:T(128)} %len_hbm.1, bf16[128,64,128]{2,1,0:T(8,128)(2,1)} %p_hbm.1), custom_call_target="tpu_custom_call" | custom-call | flops 1048576 | bytes 2097152 | tf_op jit(solution)/shard_map/pallas_call | solution.py:74
  10.3 0.0 collective-permute-done.refs_1_
  10.3 0.5 %collective-permute-done.1.cand_ref = s32[8,32]{1,0:T(8,128)S(1)} collective-permute-done((s32[8,32]{1,0:T(8,128)}, s32[8,32]{1,0:T(8,128)S(1)}, u32[]{:S(2)}, u32[]{:S(2)}) %collective-permute-start.1) | collective-permute-done | bytes 1056 | tf_op jit(solution)/shard_map/ppermute | solution.py:265
  10.8 0.0 copy-done
  10.8 0.2 shard_map.47
  11.0 1.6 %collective-permute-start.5 = (bf16[128,128]{1,0:T(8,128)(2,1)S(1)}, bf16[128,128]{1,0:T(8,128)(2,1)S(1)}, u32[]{:S(2)}, u32[]{:S(2)}) collective-permute-start(bf16[128,128]{1,0:T(8,128)(2,1)S(1)} %shard_map.47), channel_id=1, source_target_pairs={{0,2},{2,0},{4,6},{6,4},{8,10},{10,8},{12,14},{14,12},{1,3},{3,1},... | collective-permute-start | bytes 98312 | tf_op jit(solution)/shard_map/ppermute | solution.py:265
  12.6 0.0 collective-permute-done.3.refs_0_.refs_2_
  12.6 0.0 collective-permute-done.2.refs_1_.refs_3_
  12.6 0.2 shard_map.48
  12.8 0.6 %collective-permute-start.4 = (bf16[128,128]{1,0:T(8,128)(2,1)S(1)}, bf16[128,128]{1,0:T(8,128)(2,1)S(1)}, u32[]{:S(2)}, u32[]{:S(2)}) collective-permute-start(bf16[128,128]{1,0:T(8,128)(2,1)S(1)} %shard_map.48), channel_id=1, source_target_pairs={{0,2},{2,0},{4,6},{6,4},{8,10},{10,8},{12,14},{14,12},{1,3},{3,1},... | collective-permute-start | bytes 98312 | tf_op jit(solution)/shard_map/ppermute | solution.py:265
  13.4 1.7 %shard_map.49.near_ref = f32[4,3,128]{2,1,0:T(4,128)S(1)} custom-call(f32[8,128]{1,0:T(8,128)S(1)} %get-tuple-element.16.slots_ref, s32[8,128]{1,0:T(8,128)S(1)} %get-tuple-element.22.picks_ref, bf16[128,64,128]{2,1,0:T(8,128)(2,1)S(1)} %get-tuple-element.18.p_ref, bf16[256,128]{1,0:T(8,128)(2,1)S(1)} %bitcast.12, ...), custom_call_target="tpu_custom_call" | custom-call | flops 536870912 | bytes 2097152 | tf_op jit(solution)/shard_map/pallas_call | solution.py:224
  15.1 0.0 collective-permute-done.5.sel_ref
  15.1 1.0 %shard_map.50.far_ref = f32[2,3,128]{2,1,0:T(4,128)S(1)} custom-call(f32[8,128]{1,0:T(8,128)S(1)} %get-tuple-element.16.slots_ref, bf16[128,64,128]{2,1,0:T(8,128)(2,1)S(1)} %get-tuple-element.18.p_ref, bf16[128,128]{1,0:T(8,128)(2,1)S(1)} %collective-permute-done.5.sel_ref), custom_call_target="tpu_custom_call" | custom-call | flops 268435456 | bytes 2097152 | tf_op jit(solution)/shard_map/pallas_call | solution.py:224
  16.1 0.7 %collective-permute-done.4.sel_ref = bf16[128,128]{1,0:T(8,128)(2,1)S(1)} collective-permute-done((bf16[128,128]{1,0:T(8,128)(2,1)S(1)}, bf16[128,128]{1,0:T(8,128)(2,1)S(1)}, u32[]{:S(2)}, u32[]{:S(2)}) %collective-permute-start.4) | collective-permute-done | bytes 32800 | tf_op jit(solution)/shard_map/ppermute | solution.py:265
  16.8 1.0 %shard_map.51 = f32[8,4,128]{2,1,0:T(4,128)S(1)} custom-call(f32[8,128]{1,0:T(8,128)S(1)} %get-tuple-element.16.slots_ref, bf16[128,64,128]{2,1,0:T(8,128)(2,1)S(1)} %get-tuple-element.18.p_ref, bf16[128,128]{1,0:T(8,128)(2,1)S(1)} %collective-permute-done.4.sel_ref, f32[4,3,128]{2,1,0:T(4,128)S(1)} %shard_map.49.near_ref, f32[2,3,128]{2,1,0:T(4,128)S(1)} %shard_map.50.far_ref), custom_call_target="tpu_custom_call" | custom-call | flops 268435456 | bytes 2097152 | tf_op jit(solution)/shard_map/pallas_call | solution.py:224
  17.7 30.6 %all_gather.3 = f32[256,128]{1,0:T(8,128)S(1)} all-gather(f32[32,128]{1,0:T(8,128)S(1)} %bitcast.13), channel_id=1, replica_groups=mesh['grp'=2,'psg'=8,'qry'=2] {'psg'}, dimensions={0}, use_global_device_ids=true | all-gather | bytes 147456 | tf_op jit(solution)/shard_map/all_gather | solution.py:292
  48.3 0.8 %shard_map.52 = f32[8,2,16,32]{3,2,1,0:T(8,128)} custom-call(f32[8,8,4,128]{3,2,1,0:T(4,128)S(1)} %bitcast.7), custom_call_target="tpu_custom_call" | custom-call | tf_op jit(solution)/shard_map/pallas_call | solution.py:252
Async XLA Ops:
  0.0 10.8 %copy-start = (bf16[8,32,128]{2,1,0:T(8,128)(2,1)S(1)}, bf16[8,32,128]{2,1,0:T(8,128)(2,1)}, u32[]{:S(2)}) copy-start(bf16[8,32,128]{2,1,0:T(8,128)(2,1)} %param.4) | copy-start | bytes 196612
  0.0 10.3 %collective-permute-start = (bf16[256,128]{1,0:T(8,128)(2,1)}, bf16[256,128]{1,0:T(8,128)(2,1)S(1)}, u32[]{:S(2)}, u32[]{:S(2)}) collective-permute-start(bf16[256,128]{1,0:T(8,128)(2,1)} %bitcast.8), channel_id=1, source_target_pairs={{0,4},{2,6},{4,8},{6,10},{8,12},{10,14},{12,0},{14,2},{1,5},{3,7},... | collective-permute-start | bytes 196616 | tf_op jit(solution)/shard_map/ppermute | solution.py:268
  3.0 9.5 %collective-permute-start.3 = (bf16[256,128]{1,0:T(8,128)(2,1)}, bf16[256,128]{1,0:T(8,128)(2,1)S(1)}, u32[]{:S(2)}, u32[]{:S(2)}) collective-permute-start(bf16[256,128]{1,0:T(8,128)(2,1)} %bitcast.9), channel_id=1, source_target_pairs={{0,8},{2,10},{4,12},{6,14},{8,0},{10,2},{12,4},{14,6},{1,9},{3,11}... | collective-permute-start | bytes 196616 | tf_op jit(solution)/shard_map/ppermute | solution.py:268
  5.6 7.0 %collective-permute-start.2 = (bf16[256,128]{1,0:T(8,128)(2,1)}, bf16[256,128]{1,0:T(8,128)(2,1)S(1)}, u32[]{:S(2)}, u32[]{:S(2)}) collective-permute-start(bf16[256,128]{1,0:T(8,128)(2,1)} %bitcast.10), channel_id=1, source_target_pairs={{0,12},{2,14},{4,0},{6,2},{8,4},{10,6},{12,8},{14,10},{1,13},{3,15... | collective-permute-start | bytes 196616 | tf_op jit(solution)/shard_map/ppermute | solution.py:268
  7.0 3.8 %collective-permute-start.1 = (s32[8,32]{1,0:T(8,128)}, s32[8,32]{1,0:T(8,128)S(1)}, u32[]{:S(2)}, u32[]{:S(2)}) collective-permute-start(s32[8,32]{1,0:T(8,128)} %bitcast.14), channel_id=1, source_target_pairs={{0,2},{2,0},{4,6},{6,4},{8,10},{10,8},{12,14},{14,12},{1,3},{3,1},... | collective-permute-start | bytes 3080 | tf_op jit(solution)/shard_map/ppermute | solution.py:265
  11.0 4.1 %collective-permute-start.5 = (bf16[128,128]{1,0:T(8,128)(2,1)S(1)}, bf16[128,128]{1,0:T(8,128)(2,1)S(1)}, u32[]{:S(2)}, u32[]{:S(2)}) collective-permute-start(bf16[128,128]{1,0:T(8,128)(2,1)S(1)} %shard_map.47), channel_id=1, source_target_pairs={{0,2},{2,0},{4,6},{6,4},{8,10},{10,8},{12,14},{14,12},{1,3},{3,1},... | collective-permute-start | bytes 98312 | tf_op jit(solution)/shard_map/ppermute | solution.py:265
  12.8 4.0 %collective-permute-start.4 = (bf16[128,128]{1,0:T(8,128)(2,1)S(1)}, bf16[128,128]{1,0:T(8,128)(2,1)S(1)}, u32[]{:S(2)}, u32[]{:S(2)}) collective-permute-start(bf16[128,128]{1,0:T(8,128)(2,1)S(1)} %shard_map.48), channel_id=1, source_target_pairs={{0,2},{2,0},{4,6},{6,4},{8,10},{10,8},{12,14},{14,12},{1,3},{3,1},... | collective-permute-start | bytes 98312 | tf_op jit(solution)/shard_map/ppermute | solution.py:265

commit v24 on v17

--- a/solution.py
+++ b/solution.py
@@ -16,34 +16,40 @@
 KB = 32
 LANES = 128
 GROUP = 8
-PACK = 16
-
-
-def prepare_kernel(
-    cand_hbm, len_hbm, p_hbm, slots_ref, picks_ref, clean_ref, cand_ref, len_ref, raw_ref, sems
-):
-    rows = cand_ref.shape[0]
-    shards = slots_ref.shape[0]
+
+
+def clean_passages(len_hbm, p_hbm, clean_ref, len_ref, raw_ref, sems, meanwhile=lambda: None):
     groups = p_hbm.shape[0] // GROUP
 
     def fetch(g):
         part = pl.ds(g * GROUP, GROUP)
         return pltpu.make_async_copy(p_hbm.at[part], raw_ref.at[part], sems.at[g])
 
-    fetch_cand = pltpu.make_async_copy(cand_hbm, cand_ref, sems.at[groups])
-    fetch_len = pltpu.make_async_copy(len_hbm, len_ref, sems.at[groups + 1])
-    fetch_cand.start()
+    fetch_len = pltpu.make_async_copy(len_hbm, len_ref, sems.at[groups])
     fetch_len.start()
     for g in range(groups):
         fetch(g).start()
-
-    fetch_cand.wait()
+    meanwhile()
+    fetch_len.wait()
+    u = lax.broadcasted_iota(jnp.int32, (PT, LANES), 0)
+
+    @pl.loop(0, groups)
+    def _(g):
+        fetch(g).wait()
+        for i in range(GROUP):
+            p = g * GROUP + i
+            tokens = raw_ref[p].astype(jnp.float32)
+            clean_ref[p] = jnp.where(u < len_ref[p], tokens, tokens[0:1]).astype(jnp.bfloat16)
+
+
+def read_candidates(cand_ref, slots_ref, picks_ref):
+    rows = cand_ref.shape[0]
     cand = cand_ref[...]
     owner = cand // QBD
     block = cand - owner * QBD
     lane = lax.broadcasted_iota(jnp.int32, (rows, LANES), 1).astype(jnp.float32)
     sub = lax.broadcasted_iota(jnp.int32, (rows, LANES), 0)
-    for o in range(shards):
+    for o in range(slots_ref.shape[0]):
         mine = owner == o
         named = jnp.max(jnp.where(mine, block, 0), axis=1, keepdims=True)
         picks_ref[o:o + 1, :] = jnp.broadcast_to(jnp.max(named, axis=0, keepdims=True), (1, LANES))
@@ -55,43 +61,78 @@
             step *= 2
         slots_ref[o:o + 1, :] = jnp.sum(jnp.where(upto <= lane, 1.0, 0.0), axis=0, keepdims=True)
 
-    fetch_len.wait()
-    u = lax.broadcasted_iota(jnp.int32, (PT, LANES), 0).astype(jnp.int16)
-
-    @pl.loop(0, groups)
-    def _(g):
-        fetch(g).wait()
-        for i in range(GROUP):
-            p = g * GROUP + i
-            tokens = raw_ref[p]
-            first = jnp.broadcast_to(tokens[0:PACK].astype(jnp.float32)[0:1], (PACK, LANES)).astype(jnp.bfloat16)
-            limit = jnp.full((PACK, LANES), len_ref[p], jnp.int32).astype(jnp.int16)
-            live = u < jnp.concatenate([limit] * (PT // PACK))
-            clean_ref[p] = jnp.where(live, tokens, jnp.concatenate([first] * (PT // PACK)))
-
-
-def prepare(shards, candidates, lengths, passages):
+
+def prepare_early_kernel(len_hbm, p_hbm, clean_ref, *scratch):
+    @pl.when(lax.axis_index("qry") % 2 == 1)
+    def _():
+        clean_passages(len_hbm, p_hbm, clean_ref, *scratch)
+
+
+def prepare_kernel(early, cand_hbm, len_hbm, p_hbm, *refs):
+    early_refs, (slots_ref, picks_ref, clean_ref, len_ref, raw_ref, sems, cand_ref) = refs[:early], refs[early:]
+    fetch_cand = pltpu.make_async_copy(cand_hbm, cand_ref, sems.at[sems.shape[0] - 1])
+    fetch_cand.start()
+
+    def candidates():
+        fetch_cand.wait()
+        read_candidates(cand_ref, slots_ref, picks_ref)
+
+    def now():
+        clean_passages(len_hbm, p_hbm, clean_ref, len_ref, raw_ref, sems, candidates)
+
+    if not early:
+        now()
+        return
+    odd = lax.axis_index("qry") % 2 == 1
+    pl.when(jnp.logical_not(odd))(now)
+
+    @pl.when(odd)
+    def _():
+        candidates()
+
+        @pl.loop(0, clean_ref.shape[0] // GROUP)
+        def _(g):
+            part = pl.ds(g * GROUP, GROUP)
+            clean_ref[part] = early_refs[0][part]
+
+
+def prepare_scratch(lengths, passages):
+    return [
+        pltpu.SMEM(lengths.shape, lengths.dtype),
+        pltpu.VMEM(passages.shape, passages.dtype),
+        pltpu.SemaphoreType.DMA((passages.shape[0] // GROUP + 2,)),
+    ]
+
+
+def prepare_early(lengths, passages):
+    hbm = pl.BlockSpec(memory_space=pltpu.HBM)
+    return pl.pallas_call(
+        prepare_early_kernel,
+        out_shape=jax.ShapeDtypeStruct(passages.shape, passages.dtype),
+        in_specs=[hbm] * 2,
+        out_specs=pl.BlockSpec(memory_space=pltpu.VMEM),
+        scratch_shapes=prepare_scratch(lengths, passages),
+        compiler_params=pltpu.CompilerParams(vmem_limit_bytes=24 * 1024 * 1024),
+    )(*[pltpu.with_memory_space_constraint(x, pltpu.HBM) for x in (lengths, passages)])
+
+
+def prepare(shards, candidates, lengths, passages, *early):
     hbm = pl.BlockSpec(memory_space=pltpu.HBM)
     vmem = pl.BlockSpec(memory_space=pltpu.VMEM)
     operands = [pltpu.with_memory_space_constraint(x, pltpu.HBM) for x in (candidates, lengths, passages)]
     return pl.pallas_call(
-        prepare_kernel,
+        functools.partial(prepare_kernel, len(early)),
         out_shape=[
             jax.ShapeDtypeStruct((shards, LANES), jnp.float32),
             jax.ShapeDtypeStruct((shards, LANES), jnp.int32),
             jax.ShapeDtypeStruct(passages.shape, passages.dtype),
         ],
-        in_specs=[hbm] * 3,
+        in_specs=[hbm] * 3 + [vmem] * len(early),
         out_specs=[vmem] * 3,
-        scratch_shapes=[
-            pltpu.VMEM(candidates.shape, candidates.dtype),
-            pltpu.SMEM(lengths.shape, lengths.dtype),
-            pltpu.VMEM(passages.shape, passages.dtype),
-            pltpu.SemaphoreType.DMA((passages.shape[0] // GROUP + 2,)),
-        ],
+        scratch_shapes=prepare_scratch(lengths, passages) + [pltpu.VMEM(candidates.shape, candidates.dtype)],
         compiler_params=pltpu.CompilerParams(vmem_limit_bytes=24 * 1024 * 1024),
         cost_estimate=pl.CostEstimate(flops=passages.size, bytes_accessed=2 * passages.size, transcendentals=0),
-    )(*operands)
+    )(*operands, *early)
 
 
 def near_owner(me, step, planes):
@@ -141,9 +182,8 @@
     return total * (1.0 / QT)
 
 
-def best_tokens(left_of, sel, max_ref):
+def best_tokens(left_of, sel, max_ref, piece):
     count, tokens = max_ref.shape
-    piece = 2 * GROUP
     for g in range(0, count, piece):
         dots = lax.dot_general(left_of(g, piece), sel, (((1,), (1,)), ((), ())), preferred_element_type=jnp.float32)
         max_ref[g:g + piece, :] = jnp.max(dots.reshape(piece, PT, tokens), axis=1)
@@ -154,7 +194,7 @@
     def left_of(g, piece):
         return p_ref[g:g + piece].reshape(piece * PT, DIM)
 
-    return sum_tokens(best_tokens(left_of, sel, max_ref))
+    return sum_tokens(best_tokens(left_of, sel, max_ref, 2 * GROUP))
 
 
 def score_picked_few(sel, p_ref, wide_ref, max_ref):
@@ -168,7 +208,7 @@
             [p_ref[h + g:h + g + piece].reshape(piece * PT, DIM) for h in (0, half)], axis=1
         )
 
-    total = sum_tokens(best_tokens(left_of, wide_ref[...], max_ref))
+    total = sum_tokens(best_tokens(left_of, wide_ref[...], max_ref, GROUP))
     queries = tokens // QT
     return jnp.concatenate([total[:queries], total[queries:]], axis=1)
 
@@ -271,16 +311,16 @@
         return lax.ppermute(x, "psg", [(j, (j + 2 * step) % shards) for j in range(shards)])
 
     theirs = swap_sides(candidates)
-    shifted = [shift(own, step) for step in range(1, planes)]
-    slots, picks, clean = prepare(shards, candidates, lengths, passages)
+    sent, prepared = lax.optimization_barrier((own, prepare_early(lengths, passages)))
+    shifted = [shift(own if step == 1 else sent, step) for step in range(1, planes)]
+    slots, picks, clean = prepare(shards, candidates, lengths, passages, prepared)
     clean, *early = lax.optimization_barrier((clean, *reversed(shifted[:planes // 2 - 1])))
     early, late = [own, *reversed(early)], shifted[planes // 2 - 1:]
     steps = list(range(planes))
     first, last = steps[:planes // 2], steps[planes // 2:]
     packed = pack(first, planes, theirs, early)
     first_far = swap_sides(packed)
-    *late, _ = lax.optimization_barrier((*reversed(late), packed))
-    late = late[::-1]
+    *late, _ = lax.optimization_barrier((*late, packed))
     last_far = swap_sides(pack(last, planes, theirs, late))
     near_tiles = score(near_kernel, planes, planes, False, clean, slots, picks, clean, *early, *late)
     first_far, near_tiles = lax.optimization_barrier((first_far, near_tiles))

time: 28.3 us -> 29.3 us (1.035)
  blocking collectives: 9.6 us -> 10.5 us
    all_to_all x1, blocking collectives: 9.6 us -> 10.5 us  [per_device(): lax.all_to_all(tiles, 'psg', split_axis=0, concat_axis=0, tiled=True)]
    pallas_call x1 -> x2, Pallas kernels: 1.79 us -> 1.96 us  [the longest x1 1.8 us: prepare(): pl.pallas_call(functools.partial(prepare_kernel, len(early)), out_shape=[...]
where the time goes in v24:
time: 29.3 us; the launch traced here: 29.1 us
  starting transfers between devices  10.7 us (37%)
  blocking collectives  10.5 us (36%)
  Pallas kernels  6.81 us (23%)
  waiting for transfers between devices  1.03 us (4%)
    all_to_all x1, blocking collectives, per_device(): lax.all_to_all(tiles, 'psg', split_axis=0, concat_axis=0, tiled=True)  10.5 us
    ppermute x3, starting transfers between devices, shift(): lax.ppermute(x, 'psg', [(j, (j + 2 * step) % shards) for j in range(shard...  7.03 us
    ppermute x3, starting transfers between devices, swap_sides(): return lax.ppermute(x, 'psg', [(j, j ^ 1) for j in range(shards)])  3.65 us
    pallas_call x3, Pallas kernels, score(): pl.pallas_call(kernel, out_shape=jax.ShapeDtypeStruct((tiles, QB + 1, LAN...  3.62 us
    pallas_call x1, Pallas kernels, prepare(): pl.pallas_call(functools.partial(prepare_kernel, len(early)), out_shape=[...  1.8 us
    ppermute x3, waiting for transfers between devices, swap_sides(): return lax.ppermute(x, 'psg', [(j, j ^ 1) for j in range(shards)])  1.02 us
    pallas_call x1, Pallas kernels, place(): pl.pallas_call(place_kernel, out_shape=jax.ShapeDtypeStruct((shards, QB,...  0.81 us
  transfers between devices with their start and end apart: 6, of which 2 were waited for; matrix products, arithmetic and copies ran while one was open for 0% of the time, Pallas kernels for 17%

profile of v24, /device:TPU:0, one launch (start us, length us, event | category | flops | bytes accessed | tf_op | source)
XLA Modules:
  0.0 29.1 jit_solution(12158927957392371513)
XLA Ops:
  0.0 0.0 copy-start
  0.0 0.0 copy-start.1
  0.0 3.0 %collective-permute-start = (bf16[256,128]{1,0:T(8,128)(2,1)}, bf16[256,128]{1,0:T(8,128)(2,1)S(1)}, u32[]{:S(2)}, u32[]{:S(2)}) collective-permute-start(bf16[256,128]{1,0:T(8,128)(2,1)} %bitcast.5), channel_id=1, source_target_pairs={{0,4},{2,6},{4,8},{6,10},{8,12},{10,14},{12,0},{14,2},{1,5},{3,7},... | collective-permute-start | bytes 196616 | tf_op jit(solution)/shard_map/ppermute | solution.py:311
  3.0 0.2 shard_map.46.refs_0_
  3.2 0.0 copy-done
  3.2 2.7 %collective-permute-start.2 = (bf16[256,128]{1,0:T(8,128)(2,1)S(1)}, bf16[256,128]{1,0:T(8,128)(2,1)S(1)}, u32[]{:S(2)}, u32[]{:S(2)}) collective-permute-start(bf16[256,128]{1,0:T(8,128)(2,1)S(1)} %bitcast.6), channel_id=1, source_target_pairs={{0,8},{2,10},{4,12},{6,14},{8,0},{10,2},{12,4},{14,6},{1,9},{3,11}... | collective-permute-start | bytes 196616 | tf_op jit(solution)/shard_map/ppermute | solution.py:311
  5.9 1.3 %collective-permute-start.3 = (bf16[256,128]{1,0:T(8,128)(2,1)S(1)}, bf16[256,128]{1,0:T(8,128)(2,1)S(1)}, u32[]{:S(2)}, u32[]{:S(2)}) collective-permute-start(bf16[256,128]{1,0:T(8,128)(2,1)S(1)} %bitcast.7), channel_id=1, source_target_pairs={{0,12},{2,14},{4,0},{6,2},{8,4},{10,6},{12,8},{14,10},{1,13},{3,15... | collective-permute-start | bytes 196616 | tf_op jit(solution)/shard_map/ppermute | solution.py:311
  7.2 0.0 copy-done.1
  7.2 1.5 %collective-permute-start.1 = (s32[8,32]{1,0:T(8,128)S(1)}, s32[8,32]{1,0:T(8,128)S(1)}, u32[]{:S(2)}, u32[]{:S(2)}) collective-permute-start(s32[8,32]{1,0:T(8,128)S(1)} %bitcast.11), channel_id=1, source_target_pairs={{0,2},{2,0},{4,6},{6,4},{8,10},{10,8},{12,14},{14,12},{1,3},{3,1},... | collective-permute-start | bytes 3080 | tf_op jit(solution)/shard_map/ppermute | solution.py:308
  8.7 1.8 %shard_map.47 = (f32[8,128]{1,0:T(8,128)S(1)}, s32[8,128]{1,0:T(8,128)S(1)}, bf16[128,64,128]{2,1,0:T(8,128)(2,1)S(1)}) custom-call(s32[8,32]{1,0:T(8,128)} %bitcast.10, s32[128]{0:T(128)} %len_hbm.3, bf16[128,64,128]{2,1,0:T(8,128)(2,1)} %p_hbm.3, bf16[128,64,128]{2,1,0:T(8,128)(2,1)S(1)} %shard_map.46.refs_0_), custom_call_target="tpu_custom_call" | custom-call | flops 1048576 | bytes 2097152 | tf_op jit(solution)/shard_map/pallas_call | solution.py:123
  10.5 0.0 collective-permute-done.refs_1_
  10.5 0.3 %collective-permute-done.1.cand_ref = s32[8,32]{1,0:T(8,128)S(1)} collective-permute-done((s32[8,32]{1,0:T(8,128)S(1)}, s32[8,32]{1,0:T(8,128)S(1)}, u32[]{:S(2)}, u32[]{:S(2)}) %collective-permute-start.1) | collective-permute-done | bytes 1056 | tf_op jit(solution)/shard_map/ppermute | solution.py:308
  10.8 0.2 shard_map.48
  11.0 1.6 %collective-permute-start.5 = (bf16[128,128]{1,0:T(8,128)(2,1)S(1)}, bf16[128,128]{1,0:T(8,128)(2,1)S(1)}, u32[]{:S(2)}, u32[]{:S(2)}) collective-permute-start(bf16[128,128]{1,0:T(8,128)(2,1)S(1)} %shard_map.48), channel_id=1, source_target_pairs={{0,2},{2,0},{4,6},{6,4},{8,10},{10,8},{12,14},{14,12},{1,3},{3,1},... | collective-permute-start | bytes 98312 | tf_op jit(solution)/shard_map/ppermute | solution.py:308
  12.6 0.0 collective-permute-done.2.refs_0_.refs_2_
  12.6 0.0 collective-permute-done.3.refs_1_.refs_3_
  12.6 0.2 shard_map.49
  12.8 0.6 %collective-permute-start.4 = (bf16[128,128]{1,0:T(8,128)(2,1)S(1)}, bf16[128,128]{1,0:T(8,128)(2,1)S(1)}, u32[]{:S(2)}, u32[]{:S(2)}) collective-permute-start(bf16[128,128]{1,0:T(8,128)(2,1)S(1)} %shard_map.49), channel_id=1, source_target_pairs={{0,2},{2,0},{4,6},{6,4},{8,10},{10,8},{12,14},{14,12},{1,3},{3,1},... | collective-permute-start | bytes 98312 | tf_op jit(solution)/shard_map/ppermute | solution.py:308
  13.4 1.7 %shard_map.50.near_ref = f32[4,3,128]{2,1,0:T(4,128)S(1)} custom-call(f32[8,128]{1,0:T(8,128)S(1)} %get-tuple-element.19.slots_ref, s32[8,128]{1,0:T(8,128)S(1)} %get-tuple-element.26.picks_ref, bf16[128,64,128]{2,1,0:T(8,128)(2,1)S(1)} %get-tuple-element.21.p_ref, bf16[256,128]{1,0:T(8,128)(2,1)S(1)} %bitcast.9, ...), custom_call_target="tpu_custom_call" | custom-call | flops 536870912 | bytes 2097152 | tf_op jit(solution)/shard_map/pallas_call | solution.py:268
  15.1 0.0 collective-permute-done.5.sel_ref
  15.1 1.0 %shard_map.51.far_ref = f32[2,3,128]{2,1,0:T(4,128)S(1)} custom-call(f32[8,128]{1,0:T(8,128)S(1)} %get-tuple-element.19.slots_ref, bf16[128,64,128]{2,1,0:T(8,128)(2,1)S(1)} %get-tuple-element.21.p_ref, bf16[128,128]{1,0:T(8,128)(2,1)S(1)} %collective-permute-done.5.sel_ref), custom_call_target="tpu_custom_call" | custom-call | flops 268435456 | bytes 2097152 | tf_op jit(solution)/shard_map/pallas_call | solution.py:268
  16.1 0.7 %collective-permute-done.4.sel_ref = bf16[128,128]{1,0:T(8,128)(2,1)S(1)} collective-permute-done((bf16[128,128]{1,0:T(8,128)(2,1)S(1)}, bf16[128,128]{1,0:T(8,128)(2,1)S(1)}, u32[]{:S(2)}, u32[]{:S(2)}) %collective-permute-start.4) | collective-permute-done | bytes 32800 | tf_op jit(solution)/shard_map/ppermute | solution.py:308
  16.8 1.0 %shard_map.52 = f32[8,3,128]{2,1,0:T(4,128)S(1)} custom-call(f32[8,128]{1,0:T(8,128)S(1)} %get-tuple-element.19.slots_ref, bf16[128,64,128]{2,1,0:T(8,128)(2,1)S(1)} %get-tuple-element.21.p_ref, bf16[128,128]{1,0:T(8,128)(2,1)S(1)} %collective-permute-done.4.sel_ref, f32[4,3,128]{2,1,0:T(4,128)S(1)} %shard_map.50.near_ref, f32[2,3,128]{2,1,0:T(4,128)S(1)} %shard_map.51.far_ref), custom_call_target="tpu_custom_call" | custom-call | flops 268435456 | bytes 2097152 | tf_op jit(solution)/shard_map/pallas_call | solution.py:268
  17.8 10.5 %all_to_all.5.in_ref = f32[8,3,128]{2,1,0:T(4,128)S(1)} all-to-all(f32[8,3,128]{2,1,0:T(4,128)S(1)} %shard_map.52), channel_id=1, replica_groups=mesh['grp'=2,'psg'=8,'qry'=2] {'psg'}, dimensions={0} | all-to-all | bytes 24576 | tf_op jit(solution)/shard_map/all_to_all | solution.py:356
  28.3 0.8 %shard_map.53 = f32[8,2,16,32]{3,2,1,0:T(8,128)} custom-call(f32[8,3,128]{2,1,0:T(4,128)S(1)} %all_to_all.5.in_ref), custom_call_target="tpu_custom_call" | custom-call | tf_op jit(solution)/shard_map/pallas_call | solution.py:295
Async XLA Ops:
  0.0 3.2 %copy-start = (bf16[8,32,128]{2,1,0:T(8,128)(2,1)S(1)}, bf16[8,32,128]{2,1,0:T(8,128)(2,1)}, u32[]{:S(2)}) copy-start(bf16[8,32,128]{2,1,0:T(8,128)(2,1)} %param.4) | copy-start | bytes 196612
  0.0 7.2 %copy-start.1 = (s32[1,8,32]{2,1,0:T(8,128)S(1)}, s32[1,8,32]{2,1,0:T(8,128)}, u32[]{:S(2)}) copy-start(s32[1,8,32]{2,1,0:T(8,128)} %param.7) | copy-start | bytes 3076
  0.0 10.5 %collective-permute-start = (bf16[256,128]{1,0:T(8,128)(2,1)}, bf16[256,128]{1,0:T(8,128)(2,1)S(1)}, u32[]{:S(2)}, u32[]{:S(2)}) collective-permute-start(bf16[256,128]{1,0:T(8,128)(2,1)} %bitcast.5), channel_id=1, source_target_pairs={{0,4},{2,6},{4,8},{6,10},{8,12},{10,14},{12,0},{14,2},{1,5},{3,7},... | collective-permute-start | bytes 196616 | tf_op jit(solution)/shard_map/ppermute | solution.py:311
  3.2 9.4 %collective-permute-start.2 = (bf16[256,128]{1,0:T(8,128)(2,1)S(1)}, bf16[256,128]{1,0:T(8,128)(2,1)S(1)}, u32[]{:S(2)}, u32[]{:S(2)}) collective-permute-start(bf16[256,128]{1,0:T(8,128)(2,1)S(1)} %bitcast.6), channel_id=1, source_target_pairs={{0,8},{2,10},{4,12},{6,14},{8,0},{10,2},{12,4},{14,6},{1,9},{3,11}... | collective-permute-start | bytes 196616 | tf_op jit(solution)/shard_map/ppermute | solution.py:311
  5.9 6.7 %collective-permute-start.3 = (bf16[256,128]{1,0:T(8,128)(2,1)S(1)}, bf16[256,128]{1,0:T(8,128)(2,1)S(1)}, u32[]{:S(2)}, u32[]{:S(2)}) collective-permute-start(bf16[256,128]{1,0:T(8,128)(2,1)S(1)} %bitcast.7), channel_id=1, source_target_pairs={{0,12},{2,14},{4,0},{6,2},{8,4},{10,6},{12,8},{14,10},{1,13},{3,15... | collective-permute-start | bytes 196616 | tf_op jit(solution)/shard_map/ppermute | solution.py:311
  7.2 3.6 %collective-permute-start.1 = (s32[8,32]{1,0:T(8,128)S(1)}, s32[8,32]{1,0:T(8,128)S(1)}, u32[]{:S(2)}, u32[]{:S(2)}) collective-permute-start(s32[8,32]{1,0:T(8,128)S(1)} %bitcast.11), channel_id=1, source_target_pairs={{0,2},{2,0},{4,6},{6,4},{8,10},{10,8},{12,14},{14,12},{1,3},{3,1},... | collective-permute-start | bytes 3080 | tf_op jit(solution)/shard_map/ppermute | solution.py:308
  11.0 4.1 %collective-permute-start.5 = (bf16[128,128]{1,0:T(8,128)(2,1)S(1)}, bf16[128,128]{1,0:T(8,128)(2,1)S(1)}, u32[]{:S(2)}, u32[]{:S(2)}) collective-permute-start(bf16[128,128]{1,0:T(8,128)(2,1)S(1)} %shard_map.48), channel_id=1, source_target_pairs={{0,2},{2,0},{4,6},{6,4},{8,10},{10,8},{12,14},{14,12},{1,3},{3,1},... | collective-permute-start | bytes 98312 | tf_op jit(solution)/shard_map/ppermute | solution.py:308
  12.8 4.0 %collective-permute-start.4 = (bf16[128,128]{1,0:T(8,128)(2,1)S(1)}, bf16[128,128]{1,0:T(8,128)(2,1)S(1)}, u32[]{:S(2)}, u32[]{:S(2)}) collective-permute-start(bf16[128,128]{1,0:T(8,128)(2,1)S(1)} %shard_map.49), channel_id=1, source_target_pairs={{0,2},{2,0},{4,6},{6,4},{8,10},{10,8},{12,14},{14,12},{1,3},{3,1},... | collective-permute-start | bytes 98312 | tf_op jit(solution)/shard_map/ppermute | solution.py:308

commit v25 on v22

--- a/solution.py
+++ b/solution.py
@@ -91,7 +91,7 @@
 
 
 def near_owner(me, step, planes):
-    return lax.rem((me >> 1) + planes - step, planes) << 1 | me & 1
+    return me ^ 2 * step
 
 
 def picked(picks_ref, owner, q_ref):
@@ -263,7 +263,7 @@
         return lax.ppermute(x, "psg", [(j, j ^ 1) for j in range(shards)])
 
     def shift(x, step):
-        return lax.ppermute(x, "psg", [(j, (j + 2 * step) % shards) for j in range(shards)])
+        return lax.ppermute(x, "psg", [(j, j ^ 2 * step) for j in range(shards)])
 
     theirs = swap_sides(candidates)
     shifted = [shift(own, step) for step in range(1, planes)]

time: 28.9 us -> 29 us (level)
  starting transfers between devices: 10.7 us -> 9.56 us
  blocking collectives: 10.9 us -> 11.6 us
  waiting for transfers between devices: 0.52 us -> 0.94 us
    all_to_all x1, blocking collectives: 10.9 us -> 11.6 us  [per_device(): lax.all_to_all(tiles, 'psg', split_axis=0, concat_axis=0, tiled=True)]
    ppermute x3, starting transfers between devices: 4.59 us -> 3.95 us  [swap_sides(): return lax.ppermute(x, 'psg', [(j, j ^ 1) for j in range(shards)])]
    ppermute x3, starting transfers between devices: 6.06 us -> 5.62 us  [shift(): return lax.ppermute(x, 'psg', [(j, j ^ 2 * step) for j in range(shards)])]
    ppermute x3, waiting for transfers between devices: 0.52 us -> 0.94 us  [swap_sides(): return lax.ppermute(x, 'psg', [(j, j ^ 1) for j in range(shards)])]
  transfers between devices with their start and end apart: 6 -> 6, of which waited for: 1 -> 2; matrix products, arithmetic and copies ran while one was open for 0% -> 0% of each run, Pallas kernels for 17% -> 17%
where the time goes in v25:
time: 29 us; the launch traced here: 28.8 us
  blocking collectives  11.6 us (40%)
  starting transfers between devices  9.56 us (33%)
  Pallas kernels  6.65 us (23%)
  waiting for transfers between devices  0.94 us (3%)
    all_to_all x1, blocking collectives, per_device(): lax.all_to_all(tiles, 'psg', split_axis=0, concat_axis=0, tiled=True)  11.6 us
    ppermute x3, starting transfers between devices, shift(): return lax.ppermute(x, 'psg', [(j, j ^ 2 * step) for j in range(shards)])  5.62 us
    ppermute x3, starting transfers between devices, swap_sides(): return lax.ppermute(x, 'psg', [(j, j ^ 1) for j in range(shards)])  3.95 us
    pallas_call x3, Pallas kernels, score(): pl.pallas_call(kernel, out_shape=jax.ShapeDtypeStruct((tiles, QB + 1, LAN...  3.62 us
    pallas_call x1, Pallas kernels, prepare(): pl.pallas_call(prepare_kernel, out_shape=[jax.ShapeDtypeStruct((shards, L...  1.8 us
    ppermute x3, waiting for transfers between devices, swap_sides(): return lax.ppermute(x, 'psg', [(j, j ^ 1) for j in range(shards)])  0.94 us
    pallas_call x1, Pallas kernels, place(): pl.pallas_call(place_kernel, out_shape=jax.ShapeDtypeStruct((shards, QB,...  0.81 us
  transfers between devices with their start and end apart: 6, of which 2 were waited for; matrix products, arithmetic and copies ran while one was open for 0% of the time, Pallas kernels for 17%

profile of v25, /device:TPU:0, one launch (start us, length us, event | category | flops | bytes accessed | tf_op | source)
XLA Modules:
  0.0 28.8 jit_solution(1054854683849983217)
XLA Ops:
  0.0 0.0 copy-start
  0.0 4.0 %collective-permute-start = (bf16[256,128]{1,0:T(8,128)(2,1)}, bf16[256,128]{1,0:T(8,128)(2,1)S(1)}, u32[]{:S(2)}, u32[]{:S(2)}) collective-permute-start(bf16[256,128]{1,0:T(8,128)(2,1)} %bitcast.5), channel_id=1, source_target_pairs={{0,8},{2,10},{4,12},{6,14},{8,0},{10,2},{12,4},{14,6},{1,9},{3,11}... | collective-permute-start | bytes 196616 | tf_op jit(solution)/shard_map/ppermute | solution.py:266
  4.0 1.3 %collective-permute-start.3 = (bf16[256,128]{1,0:T(8,128)(2,1)}, bf16[256,128]{1,0:T(8,128)(2,1)S(1)}, u32[]{:S(2)}, u32[]{:S(2)}) collective-permute-start(bf16[256,128]{1,0:T(8,128)(2,1)} %bitcast.6), channel_id=1, source_target_pairs={{0,12},{2,14},{4,8},{6,10},{8,4},{10,6},{12,0},{14,2},{1,13},{3,15... | collective-permute-start | bytes 196616 | tf_op jit(solution)/shard_map/ppermute | solution.py:266
  5.4 0.2 collective-permute-start.2
  5.6 1.5 %collective-permute-start.1 = (s32[8,32]{1,0:T(8,128)}, s32[8,32]{1,0:T(8,128)S(1)}, u32[]{:S(2)}, u32[]{:S(2)}) collective-permute-start(s32[8,32]{1,0:T(8,128)} %bitcast.10), channel_id=1, source_target_pairs={{0,2},{2,0},{4,6},{6,4},{8,10},{10,8},{12,14},{14,12},{1,3},{3,1},... | collective-permute-start | bytes 3080 | tf_op jit(solution)/shard_map/ppermute | solution.py:263
  7.1 1.8 %shard_map.46 = (f32[8,128]{1,0:T(8,128)S(1)}, s32[8,128]{1,0:T(8,128)S(1)}, bf16[128,64,128]{2,1,0:T(8,128)(2,1)S(1)}) custom-call(s32[8,32]{1,0:T(8,128)} %bitcast.11, s32[128]{0:T(128)} %len_hbm.1, bf16[128,64,128]{2,1,0:T(8,128)(2,1)} %p_hbm.1), custom_call_target="tpu_custom_call" | custom-call | flops 1048576 | bytes 2097152 | tf_op jit(solution)/shard_map/pallas_call | solution.py:73
  8.9 0.0 collective-permute-done.refs_1_.refs_2_
  8.9 0.5 %collective-permute-done.1.cand_ref = s32[8,32]{1,0:T(8,128)S(1)} collective-permute-done((s32[8,32]{1,0:T(8,128)}, s32[8,32]{1,0:T(8,128)S(1)}, u32[]{:S(2)}, u32[]{:S(2)}) %collective-permute-start.1) | collective-permute-done | bytes 1056 | tf_op jit(solution)/shard_map/ppermute | solution.py:263
  9.4 0.0 copy-done
  9.4 0.2 shard_map.47
  9.7 1.6 %collective-permute-start.5 = (bf16[128,128]{1,0:T(8,128)(2,1)S(1)}, bf16[128,128]{1,0:T(8,128)(2,1)S(1)}, u32[]{:S(2)}, u32[]{:S(2)}) collective-permute-start(bf16[128,128]{1,0:T(8,128)(2,1)S(1)} %shard_map.47), channel_id=1, source_target_pairs={{0,2},{2,0},{4,6},{6,4},{8,10},{10,8},{12,14},{14,12},{1,3},{3,1},... | collective-permute-start | bytes 98312 | tf_op jit(solution)/shard_map/ppermute | solution.py:263
  11.2 0.0 collective-permute-done.3.refs_1_.refs_3_
  11.2 0.0 collective-permute-done.2.refs_0_.refs_1_
  11.2 0.2 shard_map.48
  11.4 0.9 %collective-permute-start.4 = (bf16[128,128]{1,0:T(8,128)(2,1)S(1)}, bf16[128,128]{1,0:T(8,128)(2,1)S(1)}, u32[]{:S(2)}, u32[]{:S(2)}) collective-permute-start(bf16[128,128]{1,0:T(8,128)(2,1)S(1)} %shard_map.48), channel_id=1, source_target_pairs={{0,2},{2,0},{4,6},{6,4},{8,10},{10,8},{12,14},{14,12},{1,3},{3,1},... | collective-permute-start | bytes 98312 | tf_op jit(solution)/shard_map/ppermute | solution.py:263
  12.3 1.7 %shard_map.49.near_ref = f32[4,3,128]{2,1,0:T(4,128)S(1)} custom-call(f32[8,128]{1,0:T(8,128)S(1)} %get-tuple-element.16.slots_ref, s32[8,128]{1,0:T(8,128)S(1)} %get-tuple-element.22.picks_ref, bf16[128,64,128]{2,1,0:T(8,128)(2,1)S(1)} %get-tuple-element.18.p_ref, bf16[256,128]{1,0:T(8,128)(2,1)S(1)} %bitcast.9, ...), custom_call_target="tpu_custom_call" | custom-call | flops 536870912 | bytes 2097152 | tf_op jit(solution)/shard_map/pallas_call | solution.py:223
  14.0 0.0 collective-permute-done.5.sel_ref
  14.0 1.0 %shard_map.50.far_ref = f32[2,3,128]{2,1,0:T(4,128)S(1)} custom-call(f32[8,128]{1,0:T(8,128)S(1)} %get-tuple-element.16.slots_ref, bf16[128,64,128]{2,1,0:T(8,128)(2,1)S(1)} %get-tuple-element.18.p_ref, bf16[128,128]{1,0:T(8,128)(2,1)S(1)} %collective-permute-done.5.sel_ref), custom_call_target="tpu_custom_call" | custom-call | flops 268435456 | bytes 2097152 | tf_op jit(solution)/shard_map/pallas_call | solution.py:223
  15.0 0.4 %collective-permute-done.4.sel_ref = bf16[128,128]{1,0:T(8,128)(2,1)S(1)} collective-permute-done((bf16[128,128]{1,0:T(8,128)(2,1)S(1)}, bf16[128,128]{1,0:T(8,128)(2,1)S(1)}, u32[]{:S(2)}, u32[]{:S(2)}) %collective-permute-start.4) | collective-permute-done | bytes 32800 | tf_op jit(solution)/shard_map/ppermute | solution.py:263
  15.4 1.0 %shard_map.51 = f32[8,3,128]{2,1,0:T(4,128)S(1)} custom-call(f32[8,128]{1,0:T(8,128)S(1)} %get-tuple-element.16.slots_ref, bf16[128,64,128]{2,1,0:T(8,128)(2,1)S(1)} %get-tuple-element.18.p_ref, bf16[128,128]{1,0:T(8,128)(2,1)S(1)} %collective-permute-done.4.sel_ref, f32[4,3,128]{2,1,0:T(4,128)S(1)} %shard_map.49.near_ref, f32[2,3,128]{2,1,0:T(4,128)S(1)} %shard_map.50.far_ref), custom_call_target="tpu_custom_call" | custom-call | flops 268435456 | bytes 2097152 | tf_op jit(solution)/shard_map/pallas_call | solution.py:223
  16.4 11.6 %all_to_all.5.in_ref = f32[8,3,128]{2,1,0:T(4,128)S(1)} all-to-all(f32[8,3,128]{2,1,0:T(4,128)S(1)} %shard_map.51), channel_id=1, replica_groups=mesh['grp'=2,'psg'=8,'qry'=2] {'psg'}, dimensions={0} | all-to-all | bytes 24576 | tf_op jit(solution)/shard_map/all_to_all | solution.py:312
  28.0 0.8 %shard_map.52 = f32[8,2,16,32]{3,2,1,0:T(8,128)} custom-call(f32[8,3,128]{2,1,0:T(4,128)S(1)} %all_to_all.5.in_ref), custom_call_target="tpu_custom_call" | custom-call | tf_op jit(solution)/shard_map/pallas_call | solution.py:250
Async XLA Ops:
  0.0 9.4 %copy-start = (bf16[8,32,128]{2,1,0:T(8,128)(2,1)S(1)}, bf16[8,32,128]{2,1,0:T(8,128)(2,1)}, u32[]{:S(2)}) copy-start(bf16[8,32,128]{2,1,0:T(8,128)(2,1)} %param.4) | copy-start | bytes 196612
  0.0 8.9 %collective-permute-start = (bf16[256,128]{1,0:T(8,128)(2,1)}, bf16[256,128]{1,0:T(8,128)(2,1)S(1)}, u32[]{:S(2)}, u32[]{:S(2)}) collective-permute-start(bf16[256,128]{1,0:T(8,128)(2,1)} %bitcast.5), channel_id=1, source_target_pairs={{0,8},{2,10},{4,12},{6,14},{8,0},{10,2},{12,4},{14,6},{1,9},{3,11}... | collective-permute-start | bytes 196616 | tf_op jit(solution)/shard_map/ppermute | solution.py:266
  4.0 7.2 %collective-permute-start.3 = (bf16[256,128]{1,0:T(8,128)(2,1)}, bf16[256,128]{1,0:T(8,128)(2,1)S(1)}, u32[]{:S(2)}, u32[]{:S(2)}) collective-permute-start(bf16[256,128]{1,0:T(8,128)(2,1)} %bitcast.6), channel_id=1, source_target_pairs={{0,12},{2,14},{4,8},{6,10},{8,4},{10,6},{12,0},{14,2},{1,13},{3,15... | collective-permute-start | bytes 196616 | tf_op jit(solution)/shard_map/ppermute | solution.py:266
  5.4 5.8 %collective-permute-start.2 = (bf16[256,128]{1,0:T(8,128)(2,1)}, bf16[256,128]{1,0:T(8,128)(2,1)S(1)}, u32[]{:S(2)}, u32[]{:S(2)}) collective-permute-start(bf16[256,128]{1,0:T(8,128)(2,1)} %bitcast.7), channel_id=1, source_target_pairs={{0,4},{2,6},{4,0},{6,2},{8,12},{10,14},{12,8},{14,10},{1,5},{3,7},... | collective-permute-start | bytes 196616 | tf_op jit(solution)/shard_map/ppermute | solution.py:266
  5.6 3.8 %collective-permute-start.1 = (s32[8,32]{1,0:T(8,128)}, s32[8,32]{1,0:T(8,128)S(1)}, u32[]{:S(2)}, u32[]{:S(2)}) collective-permute-start(s32[8,32]{1,0:T(8,128)} %bitcast.10), channel_id=1, source_target_pairs={{0,2},{2,0},{4,6},{6,4},{8,10},{10,8},{12,14},{14,12},{1,3},{3,1},... | collective-permute-start | bytes 3080 | tf_op jit(solution)/shard_map/ppermute | solution.py:263
  9.7 4.4 %collective-permute-start.5 = (bf16[128,128]{1,0:T(8,128)(2,1)S(1)}, bf16[128,128]{1,0:T(8,128)(2,1)S(1)}, u32[]{:S(2)}, u32[]{:S(2)}) collective-permute-start(bf16[128,128]{1,0:T(8,128)(2,1)S(1)} %shard_map.47), channel_id=1, source_target_pairs={{0,2},{2,0},{4,6},{6,4},{8,10},{10,8},{12,14},{14,12},{1,3},{3,1},... | collective-permute-start | bytes 98312 | tf_op jit(solution)/shard_map/ppermute | solution.py:263
  11.4 4.0 %collective-permute-start.4 = (bf16[128,128]{1,0:T(8,128)(2,1)S(1)}, bf16[128,128]{1,0:T(8,128)(2,1)S(1)}, u32[]{:S(2)}, u32[]{:S(2)}) collective-permute-start(bf16[128,128]{1,0:T(8,128)(2,1)S(1)} %shard_map.48), channel_id=1, source_target_pairs={{0,2},{2,0},{4,6},{6,4},{8,10},{10,8},{12,14},{14,12},{1,3},{3,1},... | collective-permute-start | bytes 98312 | tf_op jit(solution)/shard_map/ppermute | solution.py:263

commit v26 on v25

--- a/solution.py
+++ b/solution.py
@@ -274,8 +274,8 @@
     blocks = [own, *shifted]
     packed = pack(first, planes, theirs, [blocks[step] for step in first])
     first_far = swap_sides(packed)
-    *late, _ = lax.optimization_barrier((*[blocks[step] for step in last], packed))
-    for step, block in zip(last, late):
+    *late, _ = lax.optimization_barrier((*[blocks[step] for step in reversed(last)], packed))
+    for step, block in zip(reversed(last), late):
         blocks[step] = block
     last_far = swap_sides(pack(last, planes, theirs, [blocks[step] for step in last]))
     near_tiles = score(near_kernel, planes, planes, False, clean, slots, picks, clean, *blocks)

time: 29 us -> 29.1 us (level)
  starting transfers between devices: 9.56 us -> 10.7 us
  blocking collectives: 11.6 us -> 10.8 us
    ppermute x3, starting transfers between devices: 3.95 us -> 5.04 us  [swap_sides(): return lax.ppermute(x, 'psg', [(j, j ^ 1) for j in range(shards)])]
    all_to_all x1, blocking collectives: 11.6 us -> 10.8 us  [per_device(): lax.all_to_all(tiles, 'psg', split_axis=0, concat_axis=0, tiled=True)]
    ppermute x3, waiting for transfers between devices: 0.94 us -> 0.3 us  [swap_sides(): return lax.ppermute(x, 'psg', [(j, j ^ 1) for j in range(shards)])]
    ppermute x3, waiting for transfers between devices: 0.01 us -> 0.46 us  [shift(): return lax.ppermute(x, 'psg', [(j, j ^ 2 * step) for j in range(shards)])]
where the time goes in v26:
time: 29.1 us; the launch traced here: 28.9 us
  blocking collectives  10.8 us (37%)
  starting transfers between devices  10.7 us (37%)
  Pallas kernels  6.67 us (23%)
  waiting for transfers between devices  0.75 us (3%)
    all_to_all x1, blocking collectives, per_device(): lax.all_to_all(tiles, 'psg', split_axis=0, concat_axis=0, tiled=True)  10.8 us
    ppermute x3, starting transfers between devices, shift(): return lax.ppermute(x, 'psg', [(j, j ^ 2 * step) for j in range(shards)])  5.62 us
    ppermute x3, starting transfers between devices, swap_sides(): return lax.ppermute(x, 'psg', [(j, j ^ 1) for j in range(shards)])  5.04 us
    pallas_call x3, Pallas kernels, score(): pl.pallas_call(kernel, out_shape=jax.ShapeDtypeStruct((tiles, QB + 1, LAN...  3.65 us
    pallas_call x1, Pallas kernels, prepare(): pl.pallas_call(prepare_kernel, out_shape=[jax.ShapeDtypeStruct((shards, L...  1.8 us
    pallas_call x1, Pallas kernels, place(): pl.pallas_call(place_kernel, out_shape=jax.ShapeDtypeStruct((shards, QB,...  0.81 us
  transfers between devices with their start and end apart: 6, of which 2 were waited for; matrix products, arithmetic and copies ran while one was open for 0% of the time, Pallas kernels for 17%

profile of v26, /device:TPU:0, one launch (start us, length us, event | category | flops | bytes accessed | tf_op | source)
XLA Modules:
  0.0 28.9 jit_solution(3050916980770233136)
XLA Ops:
  0.0 0.0 copy-start
  0.0 4.0 %collective-permute-start = (bf16[256,128]{1,0:T(8,128)(2,1)}, bf16[256,128]{1,0:T(8,128)(2,1)S(1)}, u32[]{:S(2)}, u32[]{:S(2)}) collective-permute-start(bf16[256,128]{1,0:T(8,128)(2,1)} %bitcast.5), channel_id=1, source_target_pairs={{0,8},{2,10},{4,12},{6,14},{8,0},{10,2},{12,4},{14,6},{1,9},{3,11}... | collective-permute-start | bytes 196616 | tf_op jit(solution)/shard_map/ppermute | solution.py:266
  4.0 1.6 %collective-permute-start.3 = (bf16[256,128]{1,0:T(8,128)(2,1)}, bf16[256,128]{1,0:T(8,128)(2,1)S(1)}, u32[]{:S(2)}, u32[]{:S(2)}) collective-permute-start(bf16[256,128]{1,0:T(8,128)(2,1)} %bitcast.6), channel_id=1, source_target_pairs={{0,4},{2,6},{4,0},{6,2},{8,12},{10,14},{12,8},{14,10},{1,5},{3,7},... | collective-permute-start | bytes 196616 | tf_op jit(solution)/shard_map/ppermute | solution.py:266
  5.6 0.0 collective-permute-start.2
  5.6 1.7 %collective-permute-start.1 = (s32[8,32]{1,0:T(8,128)}, s32[8,32]{1,0:T(8,128)S(1)}, u32[]{:S(2)}, u32[]{:S(2)}) collective-permute-start(s32[8,32]{1,0:T(8,128)} %bitcast.10), channel_id=1, source_target_pairs={{0,2},{2,0},{4,6},{6,4},{8,10},{10,8},{12,14},{14,12},{1,3},{3,1},... | collective-permute-start | bytes 3080 | tf_op jit(solution)/shard_map/ppermute | solution.py:263
  7.3 1.8 %shard_map.46 = (f32[8,128]{1,0:T(8,128)S(1)}, s32[8,128]{1,0:T(8,128)S(1)}, bf16[128,64,128]{2,1,0:T(8,128)(2,1)S(1)}) custom-call(s32[8,32]{1,0:T(8,128)} %bitcast.11, s32[128]{0:T(128)} %len_hbm.1, bf16[128,64,128]{2,1,0:T(8,128)(2,1)} %p_hbm.1), custom_call_target="tpu_custom_call" | custom-call | flops 1048576 | bytes 2097152 | tf_op jit(solution)/shard_map/pallas_call | solution.py:73
  9.1 0.0 collective-permute-done.refs_1_.refs_2_
  9.1 0.3 %collective-permute-done.1.cand_ref = s32[8,32]{1,0:T(8,128)S(1)} collective-permute-done((s32[8,32]{1,0:T(8,128)}, s32[8,32]{1,0:T(8,128)S(1)}, u32[]{:S(2)}, u32[]{:S(2)}) %collective-permute-start.1) | collective-permute-done | bytes 1056 | tf_op jit(solution)/shard_map/ppermute | solution.py:263
  9.4 0.0 copy-done
  9.4 0.2 shard_map.47
  9.7 1.8 %collective-permute-start.5 = (bf16[128,128]{1,0:T(8,128)(2,1)S(1)}, bf16[128,128]{1,0:T(8,128)(2,1)S(1)}, u32[]{:S(2)}, u32[]{:S(2)}) collective-permute-start(bf16[128,128]{1,0:T(8,128)(2,1)S(1)} %shard_map.47), channel_id=1, source_target_pairs={{0,2},{2,0},{4,6},{6,4},{8,10},{10,8},{12,14},{14,12},{1,3},{3,1},... | collective-permute-start | bytes 98312 | tf_op jit(solution)/shard_map/ppermute | solution.py:263
  11.4 0.0 collective-permute-done.3.refs_0_.refs_1_
  11.4 0.5 %collective-permute-done.2.refs_1_.refs_3_ = bf16[256,128]{1,0:T(8,128)(2,1)S(1)} collective-permute-done((bf16[256,128]{1,0:T(8,128)(2,1)}, bf16[256,128]{1,0:T(8,128)(2,1)S(1)}, u32[]{:S(2)}, u32[]{:S(2)}) %collective-permute-start.2) | collective-permute-done | bytes 65568 | tf_op jit(solution)/shard_map/ppermute | solution.py:266
  11.9 0.2 shard_map.48
  12.1 1.6 %collective-permute-start.4 = (bf16[128,128]{1,0:T(8,128)(2,1)S(1)}, bf16[128,128]{1,0:T(8,128)(2,1)S(1)}, u32[]{:S(2)}, u32[]{:S(2)}) collective-permute-start(bf16[128,128]{1,0:T(8,128)(2,1)S(1)} %shard_map.48), channel_id=1, source_target_pairs={{0,2},{2,0},{4,6},{6,4},{8,10},{10,8},{12,14},{14,12},{1,3},{3,1},... | collective-permute-start | bytes 98312 | tf_op jit(solution)/shard_map/ppermute | solution.py:263
  13.7 1.7 %shard_map.49.near_ref = f32[4,3,128]{2,1,0:T(4,128)S(1)} custom-call(f32[8,128]{1,0:T(8,128)S(1)} %get-tuple-element.16.slots_ref, s32[8,128]{1,0:T(8,128)S(1)} %get-tuple-element.22.picks_ref, bf16[128,64,128]{2,1,0:T(8,128)(2,1)S(1)} %get-tuple-element.18.p_ref, bf16[256,128]{1,0:T(8,128)(2,1)S(1)} %bitcast.9, ...), custom_call_target="tpu_custom_call" | custom-call | flops 536870912 | bytes 2097152 | tf_op jit(solution)/shard_map/pallas_call | solution.py:223
  15.3 0.0 collective-permute-done.5.sel_ref
  15.3 1.0 %shard_map.50.far_ref = f32[2,3,128]{2,1,0:T(4,128)S(1)} custom-call(f32[8,128]{1,0:T(8,128)S(1)} %get-tuple-element.16.slots_ref, bf16[128,64,128]{2,1,0:T(8,128)(2,1)S(1)} %get-tuple-element.18.p_ref, bf16[128,128]{1,0:T(8,128)(2,1)S(1)} %collective-permute-done.5.sel_ref), custom_call_target="tpu_custom_call" | custom-call | flops 268435456 | bytes 2097152 | tf_op jit(solution)/shard_map/pallas_call | solution.py:223
  16.3 0.0 collective-permute-done.4.sel_ref
  16.3 1.0 %shard_map.51 = f32[8,3,128]{2,1,0:T(4,128)S(1)} custom-call(f32[8,128]{1,0:T(8,128)S(1)} %get-tuple-element.16.slots_ref, bf16[128,64,128]{2,1,0:T(8,128)(2,1)S(1)} %get-tuple-element.18.p_ref, bf16[128,128]{1,0:T(8,128)(2,1)S(1)} %collective-permute-done.4.sel_ref, f32[4,3,128]{2,1,0:T(4,128)S(1)} %shard_map.49.near_ref, f32[2,3,128]{2,1,0:T(4,128)S(1)} %shard_map.50.far_ref), custom_call_target="tpu_custom_call" | custom-call | flops 268435456 | bytes 2097152 | tf_op jit(solution)/shard_map/pallas_call | solution.py:223
  17.3 10.8 %all_to_all.5.in_ref = f32[8,3,128]{2,1,0:T(4,128)S(1)} all-to-all(f32[8,3,128]{2,1,0:T(4,128)S(1)} %shard_map.51), channel_id=1, replica_groups=mesh['grp'=2,'psg'=8,'qry'=2] {'psg'}, dimensions={0} | all-to-all | bytes 24576 | tf_op jit(solution)/shard_map/all_to_all | solution.py:312
  28.1 0.8 %shard_map.52 = f32[8,2,16,32]{3,2,1,0:T(8,128)} custom-call(f32[8,3,128]{2,1,0:T(4,128)S(1)} %all_to_all.5.in_ref), custom_call_target="tpu_custom_call" | custom-call | tf_op jit(solution)/shard_map/pallas_call | solution.py:250
Async XLA Ops:
  0.0 9.4 %copy-start = (bf16[8,32,128]{2,1,0:T(8,128)(2,1)S(1)}, bf16[8,32,128]{2,1,0:T(8,128)(2,1)}, u32[]{:S(2)}) copy-start(bf16[8,32,128]{2,1,0:T(8,128)(2,1)} %param.4) | copy-start | bytes 196612
  0.0 9.1 %collective-permute-start = (bf16[256,128]{1,0:T(8,128)(2,1)}, bf16[256,128]{1,0:T(8,128)(2,1)S(1)}, u32[]{:S(2)}, u32[]{:S(2)}) collective-permute-start(bf16[256,128]{1,0:T(8,128)(2,1)} %bitcast.5), channel_id=1, source_target_pairs={{0,8},{2,10},{4,12},{6,14},{8,0},{10,2},{12,4},{14,6},{1,9},{3,11}... | collective-permute-start | bytes 196616 | tf_op jit(solution)/shard_map/ppermute | solution.py:266
  4.0 7.4 %collective-permute-start.3 = (bf16[256,128]{1,0:T(8,128)(2,1)}, bf16[256,128]{1,0:T(8,128)(2,1)S(1)}, u32[]{:S(2)}, u32[]{:S(2)}) collective-permute-start(bf16[256,128]{1,0:T(8,128)(2,1)} %bitcast.6), channel_id=1, source_target_pairs={{0,4},{2,6},{4,0},{6,2},{8,12},{10,14},{12,8},{14,10},{1,5},{3,7},... | collective-permute-start | bytes 196616 | tf_op jit(solution)/shard_map/ppermute | solution.py:266
  5.6 6.3 %collective-permute-start.2 = (bf16[256,128]{1,0:T(8,128)(2,1)}, bf16[256,128]{1,0:T(8,128)(2,1)S(1)}, u32[]{:S(2)}, u32[]{:S(2)}) collective-permute-start(bf16[256,128]{1,0:T(8,128)(2,1)} %bitcast.7), channel_id=1, source_target_pairs={{0,12},{2,14},{4,8},{6,10},{8,4},{10,6},{12,0},{14,2},{1,13},{3,15... | collective-permute-start | bytes 196616 | tf_op jit(solution)/shard_map/ppermute | solution.py:266
  5.6 3.8 %collective-permute-start.1 = (s32[8,32]{1,0:T(8,128)}, s32[8,32]{1,0:T(8,128)S(1)}, u32[]{:S(2)}, u32[]{:S(2)}) collective-permute-start(s32[8,32]{1,0:T(8,128)} %bitcast.10), channel_id=1, source_target_pairs={{0,2},{2,0},{4,6},{6,4},{8,10},{10,8},{12,14},{14,12},{1,3},{3,1},... | collective-permute-start | bytes 3080 | tf_op jit(solution)/shard_map/ppermute | solution.py:263
  9.7 5.7 %collective-permute-start.5 = (bf16[128,128]{1,0:T(8,128)(2,1)S(1)}, bf16[128,128]{1,0:T(8,128)(2,1)S(1)}, u32[]{:S(2)}, u32[]{:S(2)}) collective-permute-start(bf16[128,128]{1,0:T(8,128)(2,1)S(1)} %shard_map.47), channel_id=1, source_target_pairs={{0,2},{2,0},{4,6},{6,4},{8,10},{10,8},{12,14},{14,12},{1,3},{3,1},... | collective-permute-start | bytes 98312 | tf_op jit(solution)/shard_map/ppermute | solution.py:263
  12.1 4.2 %collective-permute-start.4 = (bf16[128,128]{1,0:T(8,128)(2,1)S(1)}, bf16[128,128]{1,0:T(8,128)(2,1)S(1)}, u32[]{:S(2)}, u32[]{:S(2)}) collective-permute-start(bf16[128,128]{1,0:T(8,128)(2,1)S(1)} %shard_map.48), channel_id=1, source_target_pairs={{0,2},{2,0},{4,6},{6,4},{8,10},{10,8},{12,14},{14,12},{1,3},{3,1},... | collective-permute-start | bytes 98312 | tf_op jit(solution)/shard_map/ppermute | solution.py:263

commit v27 on v25

--- a/solution.py
+++ b/solution.py
@@ -268,12 +268,11 @@
     theirs = swap_sides(candidates)
     shifted = [shift(own, step) for step in range(1, planes)]
     slots, picks, clean = prepare(shards, candidates, lengths, passages)
-    first = [0, planes // 2]
-    last = [step for step in range(planes) if step not in first]
-    clean, shifted[first[1] - 1] = lax.optimization_barrier((clean, shifted[first[1] - 1]))
+    first, last = [0], [2, 3, 1]
+    theirs, clean = lax.optimization_barrier((theirs, clean))
+    packed = pack(first, planes, theirs, [own])
+    first_far = swap_sides(packed)
     blocks = [own, *shifted]
-    packed = pack(first, planes, theirs, [blocks[step] for step in first])
-    first_far = swap_sides(packed)
     *late, _ = lax.optimization_barrier((*[blocks[step] for step in last], packed))
     for step, block in zip(last, late):
         blocks[step] = block

time: 29 us -> 29.1 us (level)
  blocking collectives: 11.6 us -> 11 us
  Pallas kernels: 6.65 us -> 7.15 us
    all_to_all x1, blocking collectives: 11.6 us -> 11 us  [per_device(): lax.all_to_all(tiles, 'psg', split_axis=0, concat_axis=0, tiled=True)]
    pallas_call x3, Pallas kernels: 3.62 us -> 4.12 us  [score(): pl.pallas_call(kernel, out_shape=jax.ShapeDtypeStruct((tiles, QB + 1, LAN...]
where the time goes in v27:
time: 29.1 us; the launch traced here: 28.9 us
  blocking collectives  11 us (38%)
  starting transfers between devices  9.56 us (33%)
  Pallas kernels  7.15 us (25%)
  waiting for transfers between devices  1.18 us (4%)
    all_to_all x1, blocking collectives, per_device(): lax.all_to_all(tiles, 'psg', split_axis=0, concat_axis=0, tiled=True)  11 us
    ppermute x3, starting transfers between devices, shift(): return lax.ppermute(x, 'psg', [(j, j ^ 2 * step) for j in range(shards)])  5.62 us
    pallas_call x3, Pallas kernels, score(): pl.pallas_call(kernel, out_shape=jax.ShapeDtypeStruct((tiles, QB + 1, LAN...  4.12 us
    ppermute x3, starting transfers between devices, swap_sides(): return lax.ppermute(x, 'psg', [(j, j ^ 1) for j in range(shards)])  3.94 us
    pallas_call x1, Pallas kernels, prepare(): pl.pallas_call(prepare_kernel, out_shape=[jax.ShapeDtypeStruct((shards, L...  1.8 us
    ppermute x3, waiting for transfers between devices, swap_sides(): return lax.ppermute(x, 'psg', [(j, j ^ 1) for j in range(shards)])  1.17 us
    pallas_call x1, Pallas kernels, place(): pl.pallas_call(place_kernel, out_shape=jax.ShapeDtypeStruct((shards, QB,...  0.81 us
  transfers between devices with their start and end apart: 6, of which 2 were waited for; matrix products, arithmetic and copies ran while one was open for 0% of the time, Pallas kernels for 17%

profile of v27, /device:TPU:0, one launch (start us, length us, event | category | flops | bytes accessed | tf_op | source)
XLA Modules:
  0.0 28.9 jit_solution(5477968799677387958)
XLA Ops:
  0.0 0.0 copy-start
  0.0 4.0 %collective-permute-start.1 = (bf16[256,128]{1,0:T(8,128)(2,1)}, bf16[256,128]{1,0:T(8,128)(2,1)S(1)}, u32[]{:S(2)}, u32[]{:S(2)}) collective-permute-start(bf16[256,128]{1,0:T(8,128)(2,1)} %bitcast.5), channel_id=1, source_target_pairs={{0,8},{2,10},{4,12},{6,14},{8,0},{10,2},{12,4},{14,6},{1,9},{3,11}... | collective-permute-start | bytes 196616 | tf_op jit(solution)/shard_map/ppermute | solution.py:266
  4.0 1.3 %collective-permute-start.2 = (bf16[256,128]{1,0:T(8,128)(2,1)}, bf16[256,128]{1,0:T(8,128)(2,1)S(1)}, u32[]{:S(2)}, u32[]{:S(2)}) collective-permute-start(bf16[256,128]{1,0:T(8,128)(2,1)} %bitcast.6), channel_id=1, source_target_pairs={{0,12},{2,14},{4,8},{6,10},{8,4},{10,6},{12,0},{14,2},{1,13},{3,15... | collective-permute-start | bytes 196616 | tf_op jit(solution)/shard_map/ppermute | solution.py:266
  5.4 0.2 collective-permute-start.3
  5.6 1.5 %collective-permute-start = (s32[8,32]{1,0:T(8,128)}, s32[8,32]{1,0:T(8,128)S(1)}, u32[]{:S(2)}, u32[]{:S(2)}) collective-permute-start(s32[8,32]{1,0:T(8,128)} %bitcast.10), channel_id=1, source_target_pairs={{0,2},{2,0},{4,6},{6,4},{8,10},{10,8},{12,14},{14,12},{1,3},{3,1},... | collective-permute-start | bytes 3080 | tf_op jit(solution)/shard_map/ppermute | solution.py:263
  7.1 1.8 %shard_map.46 = (f32[8,128]{1,0:T(8,128)S(1)}, s32[8,128]{1,0:T(8,128)S(1)}, bf16[128,64,128]{2,1,0:T(8,128)(2,1)S(1)}) custom-call(s32[8,32]{1,0:T(8,128)} %bitcast.11, s32[128]{0:T(128)} %len_hbm.1, bf16[128,64,128]{2,1,0:T(8,128)(2,1)} %p_hbm.1), custom_call_target="tpu_custom_call" | custom-call | flops 1048576 | bytes 2097152 | tf_op jit(solution)/shard_map/pallas_call | solution.py:73
  8.9 0.5 %collective-permute-done.cand_ref = s32[8,32]{1,0:T(8,128)S(1)} collective-permute-done((s32[8,32]{1,0:T(8,128)}, s32[8,32]{1,0:T(8,128)S(1)}, u32[]{:S(2)}, u32[]{:S(2)}) %collective-permute-start) | collective-permute-done | bytes 1056 | tf_op jit(solution)/shard_map/ppermute | solution.py:263
  9.4 0.0 copy-done
  9.4 0.2 shard_map.47
  9.7 1.6 %collective-permute-start.5 = (bf16[64,128]{1,0:T(8,128)(2,1)S(1)}, bf16[64,128]{1,0:T(8,128)(2,1)S(1)}, u32[]{:S(2)}, u32[]{:S(2)}) collective-permute-start(bf16[64,128]{1,0:T(8,128)(2,1)S(1)} %shard_map.47), channel_id=1, source_target_pairs={{0,2},{2,0},{4,6},{6,4},{8,10},{10,8},{12,14},{14,12},{1,3},{3,1},... | collective-permute-start | bytes 49160 | tf_op jit(solution)/shard_map/ppermute | solution.py:263
  11.2 0.0 collective-permute-done.1.refs_0_.refs_2_
  11.2 0.0 collective-permute-done.2.refs_1_.refs_3_
  11.2 0.0 collective-permute-done.3.refs_2_.refs_1_
  11.2 0.2 shard_map.48
  11.5 0.9 %collective-permute-start.4 = (bf16[192,128]{1,0:T(8,128)(2,1)S(1)}, bf16[192,128]{1,0:T(8,128)(2,1)S(1)}, u32[]{:S(2)}, u32[]{:S(2)}) collective-permute-start(bf16[192,128]{1,0:T(8,128)(2,1)S(1)} %shard_map.48), channel_id=1, source_target_pairs={{0,2},{2,0},{4,6},{6,4},{8,10},{10,8},{12,14},{14,12},{1,3},{3,1},... | collective-permute-start | bytes 147464 | tf_op jit(solution)/shard_map/ppermute | solution.py:263
  12.3 1.7 %shard_map.49.near_ref = f32[4,3,128]{2,1,0:T(4,128)S(1)} custom-call(f32[8,128]{1,0:T(8,128)S(1)} %get-tuple-element.17.slots_ref, s32[8,128]{1,0:T(8,128)S(1)} %get-tuple-element.24.picks_ref, bf16[128,64,128]{2,1,0:T(8,128)(2,1)S(1)} %get-tuple-element.19.p_ref, bf16[256,128]{1,0:T(8,128)(2,1)S(1)} %bitcast.9, ...), custom_call_target="tpu_custom_call" | custom-call | flops 536870912 | bytes 2097152 | tf_op jit(solution)/shard_map/pallas_call | solution.py:223
  14.0 0.0 collective-permute-done.5.sel_ref
  14.0 0.9 %shard_map.50.far_ref = f32[1,3,128]{2,1,0:T(4,128)S(1)} custom-call(f32[8,128]{1,0:T(8,128)S(1)} %get-tuple-element.17.slots_ref, bf16[128,64,128]{2,1,0:T(8,128)(2,1)S(1)} %get-tuple-element.19.p_ref, bf16[64,128]{1,0:T(8,128)(2,1)S(1)} %collective-permute-done.5.sel_ref), custom_call_target="tpu_custom_call" | custom-call | flops 134217728 | bytes 2097152 | tf_op jit(solution)/shard_map/pallas_call | solution.py:223
  15.0 0.6 %collective-permute-done.4.sel_ref = bf16[192,128]{1,0:T(8,128)(2,1)S(1)} collective-permute-done((bf16[192,128]{1,0:T(8,128)(2,1)S(1)}, bf16[192,128]{1,0:T(8,128)(2,1)S(1)}, u32[]{:S(2)}, u32[]{:S(2)}) %collective-permute-start.4) | collective-permute-done | bytes 49184 | tf_op jit(solution)/shard_map/ppermute | solution.py:263
  15.6 1.5 %shard_map.51 = f32[8,3,128]{2,1,0:T(4,128)S(1)} custom-call(f32[8,128]{1,0:T(8,128)S(1)} %get-tuple-element.17.slots_ref, bf16[128,64,128]{2,1,0:T(8,128)(2,1)S(1)} %get-tuple-element.19.p_ref, bf16[192,128]{1,0:T(8,128)(2,1)S(1)} %collective-permute-done.4.sel_ref, f32[4,3,128]{2,1,0:T(4,128)S(1)} %shard_map.49.near_ref, f32[1,3,128]{2,1,0:T(4,128)S(1)} %shard_map.50.far_ref), custom_call_target="tpu_custom_call" | custom-call | flops 402653184 | bytes 2097152 | tf_op jit(solution)/shard_map/pallas_call | solution.py:223
  17.1 11.0 %all_to_all.5.in_ref = f32[8,3,128]{2,1,0:T(4,128)S(1)} all-to-all(f32[8,3,128]{2,1,0:T(4,128)S(1)} %shard_map.51), channel_id=1, replica_groups=mesh['grp'=2,'psg'=8,'qry'=2] {'psg'}, dimensions={0} | all-to-all | bytes 24576 | tf_op jit(solution)/shard_map/all_to_all | solution.py:311
  28.1 0.8 %shard_map.52 = f32[8,2,16,32]{3,2,1,0:T(8,128)} custom-call(f32[8,3,128]{2,1,0:T(4,128)S(1)} %all_to_all.5.in_ref), custom_call_target="tpu_custom_call" | custom-call | tf_op jit(solution)/shard_map/pallas_call | solution.py:250
Async XLA Ops:
  0.0 9.4 %copy-start = (bf16[8,32,128]{2,1,0:T(8,128)(2,1)S(1)}, bf16[8,32,128]{2,1,0:T(8,128)(2,1)}, u32[]{:S(2)}) copy-start(bf16[8,32,128]{2,1,0:T(8,128)(2,1)} %param.4) | copy-start | bytes 196612
  0.0 11.2 %collective-permute-start.1 = (bf16[256,128]{1,0:T(8,128)(2,1)}, bf16[256,128]{1,0:T(8,128)(2,1)S(1)}, u32[]{:S(2)}, u32[]{:S(2)}) collective-permute-start(bf16[256,128]{1,0:T(8,128)(2,1)} %bitcast.5), channel_id=1, source_target_pairs={{0,8},{2,10},{4,12},{6,14},{8,0},{10,2},{12,4},{14,6},{1,9},{3,11}... | collective-permute-start | bytes 196616 | tf_op jit(solution)/shard_map/ppermute | solution.py:266
  4.0 7.2 %collective-permute-start.2 = (bf16[256,128]{1,0:T(8,128)(2,1)}, bf16[256,128]{1,0:T(8,128)(2,1)S(1)}, u32[]{:S(2)}, u32[]{:S(2)}) collective-permute-start(bf16[256,128]{1,0:T(8,128)(2,1)} %bitcast.6), channel_id=1, source_target_pairs={{0,12},{2,14},{4,8},{6,10},{8,4},{10,6},{12,0},{14,2},{1,13},{3,15... | collective-permute-start | bytes 196616 | tf_op jit(solution)/shard_map/ppermute | solution.py:266
  5.4 5.8 %collective-permute-start.3 = (bf16[256,128]{1,0:T(8,128)(2,1)}, bf16[256,128]{1,0:T(8,128)(2,1)S(1)}, u32[]{:S(2)}, u32[]{:S(2)}) collective-permute-start(bf16[256,128]{1,0:T(8,128)(2,1)} %bitcast.7), channel_id=1, source_target_pairs={{0,4},{2,6},{4,0},{6,2},{8,12},{10,14},{12,8},{14,10},{1,5},{3,7},... | collective-permute-start | bytes 196616 | tf_op jit(solution)/shard_map/ppermute | solution.py:266
  5.6 3.8 %collective-permute-start = (s32[8,32]{1,0:T(8,128)}, s32[8,32]{1,0:T(8,128)S(1)}, u32[]{:S(2)}, u32[]{:S(2)}) collective-permute-start(s32[8,32]{1,0:T(8,128)} %bitcast.10), channel_id=1, source_target_pairs={{0,2},{2,0},{4,6},{6,4},{8,10},{10,8},{12,14},{14,12},{1,3},{3,1},... | collective-permute-start | bytes 3080 | tf_op jit(solution)/shard_map/ppermute | solution.py:263
  9.7 4.4 %collective-permute-start.5 = (bf16[64,128]{1,0:T(8,128)(2,1)S(1)}, bf16[64,128]{1,0:T(8,128)(2,1)S(1)}, u32[]{:S(2)}, u32[]{:S(2)}) collective-permute-start(bf16[64,128]{1,0:T(8,128)(2,1)S(1)} %shard_map.47), channel_id=1, source_target_pairs={{0,2},{2,0},{4,6},{6,4},{8,10},{10,8},{12,14},{14,12},{1,3},{3,1},... | collective-permute-start | bytes 49160 | tf_op jit(solution)/shard_map/ppermute | solution.py:263
  11.5 4.2 %collective-permute-start.4 = (bf16[192,128]{1,0:T(8,128)(2,1)S(1)}, bf16[192,128]{1,0:T(8,128)(2,1)S(1)}, u32[]{:S(2)}, u32[]{:S(2)}) collective-permute-start(bf16[192,128]{1,0:T(8,128)(2,1)S(1)} %shard_map.48), channel_id=1, source_target_pairs={{0,2},{2,0},{4,6},{6,4},{8,10},{10,8},{12,14},{14,12},{1,3},{3,1},... | collective-permute-start | bytes 147464 | tf_op jit(solution)/shard_map/ppermute | solution.py:263

commit v28 on v21

--- a/solution.py
+++ b/solution.py
@@ -91,7 +91,7 @@
 
 
 def near_owner(me, step, planes):
-    return lax.rem((me >> 1) + planes - step, planes) << 1 | me & 1
+    return me ^ 2 * step
 
 
 def picked(picks_ref, owner, q_ref):
@@ -263,7 +263,7 @@
         return lax.ppermute(x, "psg", [(j, j ^ 1) for j in range(shards)])
 
     def shift(x, step):
-        return lax.ppermute(x, "psg", [(j, (j + 2 * step) % shards) for j in range(shards)])
+        return lax.ppermute(x, "psg", [(j, j ^ 2 * step) for j in range(shards)])
 
     theirs = swap_sides(candidates)
     shifted = [shift(own, step) for step in range(1, planes)]
@@ -274,8 +274,7 @@
     first, last = steps[:planes // 2], steps[planes // 2:]
     packed = pack(first, planes, theirs, early)
     first_far = swap_sides(packed)
-    *late, _ = lax.optimization_barrier((*reversed(late), packed))
-    late = late[::-1]
+    *late, _ = lax.optimization_barrier((*late, packed))
     last_far = swap_sides(pack(last, planes, theirs, late))
     near_tiles = score(near_kernel, planes, planes, False, clean, slots, picks, clean, *early, *late)
     first_far, near_tiles = lax.optimization_barrier((first_far, near_tiles))

time: 28.3 us -> 29.3 us (1.035)
  blocking collectives: 9.59 us -> 10.7 us
  starting transfers between devices: 10.6 us -> 10.2 us
    ppermute x3, starting transfers between devices: 6.96 us -> 5.62 us  [shift(): return lax.ppermute(x, 'psg', [(j, j ^ 2 * step) for j in range(shards)])]
    all_to_all x1, blocking collectives: 9.59 us -> 10.7 us  [per_device(): lax.all_to_all(tiles, 'psg', split_axis=0, concat_axis=0, tiled=True)]
    ppermute x3, starting transfers between devices: 3.65 us -> 4.6 us  [swap_sides(): return lax.ppermute(x, 'psg', [(j, j ^ 1) for j in range(shards)])]
    ppermute x3, waiting for transfers between devices: 0.01 us -> 0.96 us  [shift(): return lax.ppermute(x, 'psg', [(j, j ^ 2 * step) for j in range(shards)])]
    ppermute x3, waiting for transfers between devices: 1.23 us -> 0.52 us  [swap_sides(): return lax.ppermute(x, 'psg', [(j, j ^ 1) for j in range(shards)])]
where the time goes in v28:
time: 29.3 us; the launch traced here: 29.1 us
  blocking collectives  10.7 us (37%)
  starting transfers between devices  10.2 us (35%)
  Pallas kernels  6.67 us (23%)
  waiting for transfers between devices  1.48 us (5%)
    all_to_all x1, blocking collectives, per_device(): lax.all_to_all(tiles, 'psg', split_axis=0, concat_axis=0, tiled=True)  10.7 us
    ppermute x3, starting transfers between devices, shift(): return lax.ppermute(x, 'psg', [(j, j ^ 2 * step) for j in range(shards)])  5.62 us
    ppermute x3, starting transfers between devices, swap_sides(): return lax.ppermute(x, 'psg', [(j, j ^ 1) for j in range(shards)])  4.6 us
    pallas_call x3, Pallas kernels, score(): pl.pallas_call(kernel, out_shape=jax.ShapeDtypeStruct((tiles, QB + 1, LAN...  3.64 us
    pallas_call x1, Pallas kernels, prepare(): pl.pallas_call(prepare_kernel, out_shape=[jax.ShapeDtypeStruct((shards, L...  1.8 us
    ppermute x3, waiting for transfers between devices, shift(): return lax.ppermute(x, 'psg', [(j, j ^ 2 * step) for j in range(shards)])  0.96 us
    pallas_call x1, Pallas kernels, place(): pl.pallas_call(place_kernel, out_shape=jax.ShapeDtypeStruct((shards, QB,...  0.81 us
  transfers between devices with their start and end apart: 6, of which 2 were waited for; matrix products, arithmetic and copies ran while one was open for 0% of the time, Pallas kernels for 17%

profile of v28, /device:TPU:0, one launch (start us, length us, event | category | flops | bytes accessed | tf_op | source)
XLA Modules:
  0.0 29.1 jit_solution(6606004420751401762)
XLA Ops:
  0.0 0.0 copy-start
  0.0 3.0 %collective-permute-start = (bf16[256,128]{1,0:T(8,128)(2,1)}, bf16[256,128]{1,0:T(8,128)(2,1)S(1)}, u32[]{:S(2)}, u32[]{:S(2)}) collective-permute-start(bf16[256,128]{1,0:T(8,128)(2,1)} %bitcast.5), channel_id=1, source_target_pairs={{0,4},{2,6},{4,0},{6,2},{8,12},{10,14},{12,8},{14,10},{1,5},{3,7},... | collective-permute-start | bytes 196616 | tf_op jit(solution)/shard_map/ppermute | solution.py:266
  3.0 2.5 %collective-permute-start.3 = (bf16[256,128]{1,0:T(8,128)(2,1)}, bf16[256,128]{1,0:T(8,128)(2,1)S(1)}, u32[]{:S(2)}, u32[]{:S(2)}) collective-permute-start(bf16[256,128]{1,0:T(8,128)(2,1)} %bitcast.6), channel_id=1, source_target_pairs={{0,12},{2,14},{4,8},{6,10},{8,4},{10,6},{12,0},{14,2},{1,13},{3,15... | collective-permute-start | bytes 196616 | tf_op jit(solution)/shard_map/ppermute | solution.py:266
  5.5 0.1 collective-permute-start.2
  5.6 1.5 %collective-permute-start.1 = (s32[8,32]{1,0:T(8,128)}, s32[8,32]{1,0:T(8,128)S(1)}, u32[]{:S(2)}, u32[]{:S(2)}) collective-permute-start(s32[8,32]{1,0:T(8,128)} %bitcast.10), channel_id=1, source_target_pairs={{0,2},{2,0},{4,6},{6,4},{8,10},{10,8},{12,14},{14,12},{1,3},{3,1},... | collective-permute-start | bytes 3080 | tf_op jit(solution)/shard_map/ppermute | solution.py:263
  7.1 1.8 %shard_map.46 = (f32[8,128]{1,0:T(8,128)S(1)}, s32[8,128]{1,0:T(8,128)S(1)}, bf16[128,64,128]{2,1,0:T(8,128)(2,1)S(1)}) custom-call(s32[8,32]{1,0:T(8,128)} %bitcast.11, s32[128]{0:T(128)} %len_hbm.1, bf16[128,64,128]{2,1,0:T(8,128)(2,1)} %p_hbm.1), custom_call_target="tpu_custom_call" | custom-call | flops 1048576 | bytes 2097152 | tf_op jit(solution)/shard_map/pallas_call | solution.py:73
  8.9 0.0 collective-permute-done.refs_1_
  8.9 0.5 %collective-permute-done.1.cand_ref = s32[8,32]{1,0:T(8,128)S(1)} collective-permute-done((s32[8,32]{1,0:T(8,128)}, s32[8,32]{1,0:T(8,128)S(1)}, u32[]{:S(2)}, u32[]{:S(2)}) %collective-permute-start.1) | collective-permute-done | bytes 1056 | tf_op jit(solution)/shard_map/ppermute | solution.py:263
  9.4 0.0 copy-done
  9.4 0.2 shard_map.47
  9.7 1.6 %collective-permute-start.5 = (bf16[128,128]{1,0:T(8,128)(2,1)S(1)}, bf16[128,128]{1,0:T(8,128)(2,1)S(1)}, u32[]{:S(2)}, u32[]{:S(2)}) collective-permute-start(bf16[128,128]{1,0:T(8,128)(2,1)S(1)} %shard_map.47), channel_id=1, source_target_pairs={{0,2},{2,0},{4,6},{6,4},{8,10},{10,8},{12,14},{14,12},{1,3},{3,1},... | collective-permute-start | bytes 98312 | tf_op jit(solution)/shard_map/ppermute | solution.py:263
  11.2 0.0 collective-permute-done.3.refs_1_.refs_3_
  11.2 1.0 %collective-permute-done.2.refs_0_.refs_2_ = bf16[256,128]{1,0:T(8,128)(2,1)S(1)} collective-permute-done((bf16[256,128]{1,0:T(8,128)(2,1)}, bf16[256,128]{1,0:T(8,128)(2,1)S(1)}, u32[]{:S(2)}, u32[]{:S(2)}) %collective-permute-start.2) | collective-permute-done | bytes 65568 | tf_op jit(solution)/shard_map/ppermute | solution.py:266
  12.2 0.2 shard_map.48
  12.4 1.6 %collective-permute-start.4 = (bf16[128,128]{1,0:T(8,128)(2,1)S(1)}, bf16[128,128]{1,0:T(8,128)(2,1)S(1)}, u32[]{:S(2)}, u32[]{:S(2)}) collective-permute-start(bf16[128,128]{1,0:T(8,128)(2,1)S(1)} %shard_map.48), channel_id=1, source_target_pairs={{0,2},{2,0},{4,6},{6,4},{8,10},{10,8},{12,14},{14,12},{1,3},{3,1},... | collective-permute-start | bytes 98312 | tf_op jit(solution)/shard_map/ppermute | solution.py:263
  14.0 1.7 %shard_map.49.near_ref = f32[4,3,128]{2,1,0:T(4,128)S(1)} custom-call(f32[8,128]{1,0:T(8,128)S(1)} %get-tuple-element.16.slots_ref, s32[8,128]{1,0:T(8,128)S(1)} %get-tuple-element.22.picks_ref, bf16[128,64,128]{2,1,0:T(8,128)(2,1)S(1)} %get-tuple-element.18.p_ref, bf16[256,128]{1,0:T(8,128)(2,1)S(1)} %bitcast.9, ...), custom_call_target="tpu_custom_call" | custom-call | flops 536870912 | bytes 2097152 | tf_op jit(solution)/shard_map/pallas_call | solution.py:223
  15.6 0.0 collective-permute-done.5.sel_ref
  15.6 1.0 %shard_map.50.far_ref = f32[2,3,128]{2,1,0:T(4,128)S(1)} custom-call(f32[8,128]{1,0:T(8,128)S(1)} %get-tuple-element.16.slots_ref, bf16[128,64,128]{2,1,0:T(8,128)(2,1)S(1)} %get-tuple-element.18.p_ref, bf16[128,128]{1,0:T(8,128)(2,1)S(1)} %collective-permute-done.5.sel_ref), custom_call_target="tpu_custom_call" | custom-call | flops 268435456 | bytes 2097152 | tf_op jit(solution)/shard_map/pallas_call | solution.py:223
  16.6 0.0 collective-permute-done.4.sel_ref
  16.6 1.0 %shard_map.51 = f32[8,3,128]{2,1,0:T(4,128)S(1)} custom-call(f32[8,128]{1,0:T(8,128)S(1)} %get-tuple-element.16.slots_ref, bf16[128,64,128]{2,1,0:T(8,128)(2,1)S(1)} %get-tuple-element.18.p_ref, bf16[128,128]{1,0:T(8,128)(2,1)S(1)} %collective-permute-done.4.sel_ref, f32[4,3,128]{2,1,0:T(4,128)S(1)} %shard_map.49.near_ref, f32[2,3,128]{2,1,0:T(4,128)S(1)} %shard_map.50.far_ref), custom_call_target="tpu_custom_call" | custom-call | flops 268435456 | bytes 2097152 | tf_op jit(solution)/shard_map/pallas_call | solution.py:223
  17.6 10.7 %all_to_all.5.in_ref = f32[8,3,128]{2,1,0:T(4,128)S(1)} all-to-all(f32[8,3,128]{2,1,0:T(4,128)S(1)} %shard_map.51), channel_id=1, replica_groups=mesh['grp'=2,'psg'=8,'qry'=2] {'psg'}, dimensions={0} | all-to-all | bytes 24576 | tf_op jit(solution)/shard_map/all_to_all | solution.py:310
  28.3 0.8 %shard_map.52 = f32[8,2,16,32]{3,2,1,0:T(8,128)} custom-call(f32[8,3,128]{2,1,0:T(4,128)S(1)} %all_to_all.5.in_ref), custom_call_target="tpu_custom_call" | custom-call | tf_op jit(solution)/shard_map/pallas_call | solution.py:250
Async XLA Ops:
  0.0 9.4 %copy-start = (bf16[8,32,128]{2,1,0:T(8,128)(2,1)S(1)}, bf16[8,32,128]{2,1,0:T(8,128)(2,1)}, u32[]{:S(2)}) copy-start(bf16[8,32,128]{2,1,0:T(8,128)(2,1)} %param.4) | copy-start | bytes 196612
  0.0 8.9 %collective-permute-start = (bf16[256,128]{1,0:T(8,128)(2,1)}, bf16[256,128]{1,0:T(8,128)(2,1)S(1)}, u32[]{:S(2)}, u32[]{:S(2)}) collective-permute-start(bf16[256,128]{1,0:T(8,128)(2,1)} %bitcast.5), channel_id=1, source_target_pairs={{0,4},{2,6},{4,0},{6,2},{8,12},{10,14},{12,8},{14,10},{1,5},{3,7},... | collective-permute-start | bytes 196616 | tf_op jit(solution)/shard_map/ppermute | solution.py:266
  3.0 8.2 %collective-permute-start.3 = (bf16[256,128]{1,0:T(8,128)(2,1)}, bf16[256,128]{1,0:T(8,128)(2,1)S(1)}, u32[]{:S(2)}, u32[]{:S(2)}) collective-permute-start(bf16[256,128]{1,0:T(8,128)(2,1)} %bitcast.6), channel_id=1, source_target_pairs={{0,12},{2,14},{4,8},{6,10},{8,4},{10,6},{12,0},{14,2},{1,13},{3,15... | collective-permute-start | bytes 196616 | tf_op jit(solution)/shard_map/ppermute | solution.py:266
  5.5 6.7 %collective-permute-start.2 = (bf16[256,128]{1,0:T(8,128)(2,1)}, bf16[256,128]{1,0:T(8,128)(2,1)S(1)}, u32[]{:S(2)}, u32[]{:S(2)}) collective-permute-start(bf16[256,128]{1,0:T(8,128)(2,1)} %bitcast.7), channel_id=1, source_target_pairs={{0,8},{2,10},{4,12},{6,14},{8,0},{10,2},{12,4},{14,6},{1,9},{3,11}... | collective-permute-start | bytes 196616 | tf_op jit(solution)/shard_map/ppermute | solution.py:266
  5.6 3.8 %collective-permute-start.1 = (s32[8,32]{1,0:T(8,128)}, s32[8,32]{1,0:T(8,128)S(1)}, u32[]{:S(2)}, u32[]{:S(2)}) collective-permute-start(s32[8,32]{1,0:T(8,128)} %bitcast.10), channel_id=1, source_target_pairs={{0,2},{2,0},{4,6},{6,4},{8,10},{10,8},{12,14},{14,12},{1,3},{3,1},... | collective-permute-start | bytes 3080 | tf_op jit(solution)/shard_map/ppermute | solution.py:263
  9.7 6.0 %collective-permute-start.5 = (bf16[128,128]{1,0:T(8,128)(2,1)S(1)}, bf16[128,128]{1,0:T(8,128)(2,1)S(1)}, u32[]{:S(2)}, u32[]{:S(2)}) collective-permute-start(bf16[128,128]{1,0:T(8,128)(2,1)S(1)} %shard_map.47), channel_id=1, source_target_pairs={{0,2},{2,0},{4,6},{6,4},{8,10},{10,8},{12,14},{14,12},{1,3},{3,1},... | collective-permute-start | bytes 98312 | tf_op jit(solution)/shard_map/ppermute | solution.py:263
  12.4 4.2 %collective-permute-start.4 = (bf16[128,128]{1,0:T(8,128)(2,1)S(1)}, bf16[128,128]{1,0:T(8,128)(2,1)S(1)}, u32[]{:S(2)}, u32[]{:S(2)}) collective-permute-start(bf16[128,128]{1,0:T(8,128)(2,1)S(1)} %shard_map.48), channel_id=1, source_target_pairs={{0,2},{2,0},{4,6},{6,4},{8,10},{10,8},{12,14},{14,12},{1,3},{3,1},... | collective-permute-start | bytes 98312 | tf_op jit(solution)/shard_map/ppermute | solution.py:263

commit v29 on v21

--- a/solution.py
+++ b/solution.py
@@ -163,7 +163,7 @@
             [p_ref[h + g:h + g + piece].reshape(piece * PT, DIM) for h in (0, half)], axis=1
         )
 
-    total = sum_tokens(best_tokens(left_of, wide_ref[...], max_ref, GROUP))
+    total = sum_tokens(best_tokens(left_of, wide_ref[...], max_ref, 2 * GROUP))
     queries = tokens // QT
     return jnp.concatenate([total[:queries], total[queries:]], axis=1)
 

time: 28.3 us -> 28.3 us (level)
  no operation moved by 1% of the time
where the time goes in v29:
time: 28.3 us; the launch traced here: 28.1 us
  starting transfers between devices  10.6 us (37%)
  blocking collectives  9.6 us (34%)
  Pallas kernels  6.66 us (24%)
  waiting for transfers between devices  1.23 us (4%)
    all_to_all x1, blocking collectives, per_device(): lax.all_to_all(tiles, 'psg', split_axis=0, concat_axis=0, tiled=True)  9.6 us
    ppermute x3, starting transfers between devices, shift(): lax.ppermute(x, 'psg', [(j, (j + 2 * step) % shards) for j in range(shard...  6.96 us
    ppermute x3, starting transfers between devices, swap_sides(): return lax.ppermute(x, 'psg', [(j, j ^ 1) for j in range(shards)])  3.65 us
    pallas_call x3, Pallas kernels, score(): pl.pallas_call(kernel, out_shape=jax.ShapeDtypeStruct((tiles, QB + 1, LAN...  3.63 us
    pallas_call x1, Pallas kernels, prepare(): pl.pallas_call(prepare_kernel, out_shape=[jax.ShapeDtypeStruct((shards, L...  1.8 us
    ppermute x3, waiting for transfers between devices, swap_sides(): return lax.ppermute(x, 'psg', [(j, j ^ 1) for j in range(shards)])  1.22 us
    pallas_call x1, Pallas kernels, place(): pl.pallas_call(place_kernel, out_shape=jax.ShapeDtypeStruct((shards, QB,...  0.81 us
  transfers between devices with their start and end apart: 6, of which 2 were waited for; matrix products, arithmetic and copies ran while one was open for 0% of the time, Pallas kernels for 17%

profile of v29, /device:TPU:0, one launch (start us, length us, event | category | flops | bytes accessed | tf_op | source)
XLA Modules:
  0.0 28.1 jit_solution(6284580603884006988)
XLA Ops:
  0.0 0.0 copy-start
  0.0 3.0 %collective-permute-start = (bf16[256,128]{1,0:T(8,128)(2,1)}, bf16[256,128]{1,0:T(8,128)(2,1)S(1)}, u32[]{:S(2)}, u32[]{:S(2)}) collective-permute-start(bf16[256,128]{1,0:T(8,128)(2,1)} %bitcast.5), channel_id=1, source_target_pairs={{0,4},{2,6},{4,8},{6,10},{8,12},{10,14},{12,0},{14,2},{1,5},{3,7},... | collective-permute-start | bytes 196616 | tf_op jit(solution)/shard_map/ppermute | solution.py:266
  3.0 2.6 %collective-permute-start.3 = (bf16[256,128]{1,0:T(8,128)(2,1)}, bf16[256,128]{1,0:T(8,128)(2,1)S(1)}, u32[]{:S(2)}, u32[]{:S(2)}) collective-permute-start(bf16[256,128]{1,0:T(8,128)(2,1)} %bitcast.6), channel_id=1, source_target_pairs={{0,8},{2,10},{4,12},{6,14},{8,0},{10,2},{12,4},{14,6},{1,9},{3,11}... | collective-permute-start | bytes 196616 | tf_op jit(solution)/shard_map/ppermute | solution.py:266
  5.6 1.3 %collective-permute-start.2 = (bf16[256,128]{1,0:T(8,128)(2,1)}, bf16[256,128]{1,0:T(8,128)(2,1)S(1)}, u32[]{:S(2)}, u32[]{:S(2)}) collective-permute-start(bf16[256,128]{1,0:T(8,128)(2,1)} %bitcast.7), channel_id=1, source_target_pairs={{0,12},{2,14},{4,0},{6,2},{8,4},{10,6},{12,8},{14,10},{1,13},{3,15... | collective-permute-start | bytes 196616 | tf_op jit(solution)/shard_map/ppermute | solution.py:266
  7.0 1.5 %collective-permute-start.1 = (s32[8,32]{1,0:T(8,128)}, s32[8,32]{1,0:T(8,128)S(1)}, u32[]{:S(2)}, u32[]{:S(2)}) collective-permute-start(s32[8,32]{1,0:T(8,128)} %bitcast.10), channel_id=1, source_target_pairs={{0,2},{2,0},{4,6},{6,4},{8,10},{10,8},{12,14},{14,12},{1,3},{3,1},... | collective-permute-start | bytes 3080 | tf_op jit(solution)/shard_map/ppermute | solution.py:263
  8.5 1.8 %shard_map.46 = (f32[8,128]{1,0:T(8,128)S(1)}, s32[8,128]{1,0:T(8,128)S(1)}, bf16[128,64,128]{2,1,0:T(8,128)(2,1)S(1)}) custom-call(s32[8,32]{1,0:T(8,128)} %bitcast.11, s32[128]{0:T(128)} %len_hbm.1, bf16[128,64,128]{2,1,0:T(8,128)(2,1)} %p_hbm.1), custom_call_target="tpu_custom_call" | custom-call | flops 1048576 | bytes 2097152 | tf_op jit(solution)/shard_map/pallas_call | solution.py:73
  10.3 0.0 collective-permute-done.refs_1_
  10.3 0.5 %collective-permute-done.1.cand_ref = s32[8,32]{1,0:T(8,128)S(1)} collective-permute-done((s32[8,32]{1,0:T(8,128)}, s32[8,32]{1,0:T(8,128)S(1)}, u32[]{:S(2)}, u32[]{:S(2)}) %collective-permute-start.1) | collective-permute-done | bytes 1056 | tf_op jit(solution)/shard_map/ppermute | solution.py:263
  10.8 0.0 copy-done
  10.8 0.2 shard_map.47
  11.0 1.6 %collective-permute-start.5 = (bf16[128,128]{1,0:T(8,128)(2,1)S(1)}, bf16[128,128]{1,0:T(8,128)(2,1)S(1)}, u32[]{:S(2)}, u32[]{:S(2)}) collective-permute-start(bf16[128,128]{1,0:T(8,128)(2,1)S(1)} %shard_map.47), channel_id=1, source_target_pairs={{0,2},{2,0},{4,6},{6,4},{8,10},{10,8},{12,14},{14,12},{1,3},{3,1},... | collective-permute-start | bytes 98312 | tf_op jit(solution)/shard_map/ppermute | solution.py:263
  12.6 0.0 collective-permute-done.3.refs_0_.refs_2_
  12.6 0.0 collective-permute-done.2.refs_1_.refs_3_
  12.6 0.2 shard_map.48
  12.8 0.6 %collective-permute-start.4 = (bf16[128,128]{1,0:T(8,128)(2,1)S(1)}, bf16[128,128]{1,0:T(8,128)(2,1)S(1)}, u32[]{:S(2)}, u32[]{:S(2)}) collective-permute-start(bf16[128,128]{1,0:T(8,128)(2,1)S(1)} %shard_map.48), channel_id=1, source_target_pairs={{0,2},{2,0},{4,6},{6,4},{8,10},{10,8},{12,14},{14,12},{1,3},{3,1},... | collective-permute-start | bytes 98312 | tf_op jit(solution)/shard_map/ppermute | solution.py:263
  13.4 1.7 %shard_map.49.near_ref = f32[4,3,128]{2,1,0:T(4,128)S(1)} custom-call(f32[8,128]{1,0:T(8,128)S(1)} %get-tuple-element.16.slots_ref, s32[8,128]{1,0:T(8,128)S(1)} %get-tuple-element.22.picks_ref, bf16[128,64,128]{2,1,0:T(8,128)(2,1)S(1)} %get-tuple-element.18.p_ref, bf16[256,128]{1,0:T(8,128)(2,1)S(1)} %bitcast.9, ...), custom_call_target="tpu_custom_call" | custom-call | flops 536870912 | bytes 2097152 | tf_op jit(solution)/shard_map/pallas_call | solution.py:223
  15.1 0.0 collective-permute-done.5.sel_ref
  15.1 1.0 %shard_map.50.far_ref = f32[2,3,128]{2,1,0:T(4,128)S(1)} custom-call(f32[8,128]{1,0:T(8,128)S(1)} %get-tuple-element.16.slots_ref, bf16[128,64,128]{2,1,0:T(8,128)(2,1)S(1)} %get-tuple-element.18.p_ref, bf16[128,128]{1,0:T(8,128)(2,1)S(1)} %collective-permute-done.5.sel_ref), custom_call_target="tpu_custom_call" | custom-call | flops 268435456 | bytes 2097152 | tf_op jit(solution)/shard_map/pallas_call | solution.py:223
  16.1 0.7 %collective-permute-done.4.sel_ref = bf16[128,128]{1,0:T(8,128)(2,1)S(1)} collective-permute-done((bf16[128,128]{1,0:T(8,128)(2,1)S(1)}, bf16[128,128]{1,0:T(8,128)(2,1)S(1)}, u32[]{:S(2)}, u32[]{:S(2)}) %collective-permute-start.4) | collective-permute-done | bytes 32800 | tf_op jit(solution)/shard_map/ppermute | solution.py:263
  16.8 1.0 %shard_map.51 = f32[8,3,128]{2,1,0:T(4,128)S(1)} custom-call(f32[8,128]{1,0:T(8,128)S(1)} %get-tuple-element.16.slots_ref, bf16[128,64,128]{2,1,0:T(8,128)(2,1)S(1)} %get-tuple-element.18.p_ref, bf16[128,128]{1,0:T(8,128)(2,1)S(1)} %collective-permute-done.4.sel_ref, f32[4,3,128]{2,1,0:T(4,128)S(1)} %shard_map.49.near_ref, f32[2,3,128]{2,1,0:T(4,128)S(1)} %shard_map.50.far_ref), custom_call_target="tpu_custom_call" | custom-call | flops 268435456 | bytes 2097152 | tf_op jit(solution)/shard_map/pallas_call | solution.py:223
  17.7 9.6 %all_to_all.5.in_ref = f32[8,3,128]{2,1,0:T(4,128)S(1)} all-to-all(f32[8,3,128]{2,1,0:T(4,128)S(1)} %shard_map.51), channel_id=1, replica_groups=mesh['grp'=2,'psg'=8,'qry'=2] {'psg'}, dimensions={0} | all-to-all | bytes 24576 | tf_op jit(solution)/shard_map/all_to_all | solution.py:311
  27.3 0.8 %shard_map.52 = f32[8,2,16,32]{3,2,1,0:T(8,128)} custom-call(f32[8,3,128]{2,1,0:T(4,128)S(1)} %all_to_all.5.in_ref), custom_call_target="tpu_custom_call" | custom-call | tf_op jit(solution)/shard_map/pallas_call | solution.py:250
Async XLA Ops:
  0.0 10.8 %copy-start = (bf16[8,32,128]{2,1,0:T(8,128)(2,1)S(1)}, bf16[8,32,128]{2,1,0:T(8,128)(2,1)}, u32[]{:S(2)}) copy-start(bf16[8,32,128]{2,1,0:T(8,128)(2,1)} %param.4) | copy-start | bytes 196612
  0.0 10.3 %collective-permute-start = (bf16[256,128]{1,0:T(8,128)(2,1)}, bf16[256,128]{1,0:T(8,128)(2,1)S(1)}, u32[]{:S(2)}, u32[]{:S(2)}) collective-permute-start(bf16[256,128]{1,0:T(8,128)(2,1)} %bitcast.5), channel_id=1, source_target_pairs={{0,4},{2,6},{4,8},{6,10},{8,12},{10,14},{12,0},{14,2},{1,5},{3,7},... | collective-permute-start | bytes 196616 | tf_op jit(solution)/shard_map/ppermute | solution.py:266
  3.0 9.5 %collective-permute-start.3 = (bf16[256,128]{1,0:T(8,128)(2,1)}, bf16[256,128]{1,0:T(8,128)(2,1)S(1)}, u32[]{:S(2)}, u32[]{:S(2)}) collective-permute-start(bf16[256,128]{1,0:T(8,128)(2,1)} %bitcast.6), channel_id=1, source_target_pairs={{0,8},{2,10},{4,12},{6,14},{8,0},{10,2},{12,4},{14,6},{1,9},{3,11}... | collective-permute-start | bytes 196616 | tf_op jit(solution)/shard_map/ppermute | solution.py:266
  5.6 7.0 %collective-permute-start.2 = (bf16[256,128]{1,0:T(8,128)(2,1)}, bf16[256,128]{1,0:T(8,128)(2,1)S(1)}, u32[]{:S(2)}, u32[]{:S(2)}) collective-permute-start(bf16[256,128]{1,0:T(8,128)(2,1)} %bitcast.7), channel_id=1, source_target_pairs={{0,12},{2,14},{4,0},{6,2},{8,4},{10,6},{12,8},{14,10},{1,13},{3,15... | collective-permute-start | bytes 196616 | tf_op jit(solution)/shard_map/ppermute | solution.py:266
  7.0 3.8 %collective-permute-start.1 = (s32[8,32]{1,0:T(8,128)}, s32[8,32]{1,0:T(8,128)S(1)}, u32[]{:S(2)}, u32[]{:S(2)}) collective-permute-start(s32[8,32]{1,0:T(8,128)} %bitcast.10), channel_id=1, source_target_pairs={{0,2},{2,0},{4,6},{6,4},{8,10},{10,8},{12,14},{14,12},{1,3},{3,1},... | collective-permute-start | bytes 3080 | tf_op jit(solution)/shard_map/ppermute | solution.py:263
  11.0 4.1 %collective-permute-start.5 = (bf16[128,128]{1,0:T(8,128)(2,1)S(1)}, bf16[128,128]{1,0:T(8,128)(2,1)S(1)}, u32[]{:S(2)}, u32[]{:S(2)}) collective-permute-start(bf16[128,128]{1,0:T(8,128)(2,1)S(1)} %shard_map.47), channel_id=1, source_target_pairs={{0,2},{2,0},{4,6},{6,4},{8,10},{10,8},{12,14},{14,12},{1,3},{3,1},... | collective-permute-start | bytes 98312 | tf_op jit(solution)/shard_map/ppermute | solution.py:263
  12.8 4.0 %collective-permute-start.4 = (bf16[128,128]{1,0:T(8,128)(2,1)S(1)}, bf16[128,128]{1,0:T(8,128)(2,1)S(1)}, u32[]{:S(2)}, u32[]{:S(2)}) collective-permute-start(bf16[128,128]{1,0:T(8,128)(2,1)S(1)} %shard_map.48), channel_id=1, source_target_pairs={{0,2},{2,0},{4,6},{6,4},{8,10},{10,8},{12,14},{14,12},{1,3},{3,1},... | collective-permute-start | bytes 98312 | tf_op jit(solution)/shard_map/ppermute | solution.py:263
